TPU v7x, 32 devices: a whole 2x2x4 slice. The times are simulated.
32 devices in a mesh: dp: 2 (over x), blk: 4 (over y, core), tensor: 4 (over z).
Axes of the slice: x: 2, y: 2, z: 4, core: 2. Of those that a mesh axis runs over, the one named last changes fastest.
Arguments:
- tokens: bfloat16 [8, 512, 768], P('dp', 'blk'), may hold values from -6 to 6
- bucket_ids: int32 [8], P('dp'), may hold values from 0 to 2, as said below
- seq_lengths: int32 [8, 4], P('dp'), may hold values from 0 to 512, as said below
- w_query: bfloat16 [768, 768], P(None, 'tensor'), may hold values from -0.21875 to 0.21875
- b_query: float32 [768], P('tensor'), may hold values from -3 to 3
- w_key: bfloat16 [768, 768], P(None, 'tensor'), may hold values from -0.21875 to 0.21875
- w_value: bfloat16 [768, 768], P(None, 'tensor'), may hold values from -0.21875 to 0.21875
- b_value: float32 [768], P('tensor'), may hold values from -3 to 3
- w_out: bfloat16 [768, 768], P('tensor'), may hold values from -1.25 to 1.25
- b_out: float32 [768], replicated, may hold values from -3 to 3
- norm1_gain: float32 [768], replicated, may hold values from 0.25 to 1.75
- norm1_bias: float32 [768], replicated, may hold values from -3 to 3
- w_inner: bfloat16 [768, 3072], P(None, 'tensor'), may hold values from -0.21875 to 0.21875
- b_inner: float32 [3072], P('tensor'), may hold values from -3 to 3
- w_outer: bfloat16 [3072, 768], P('tensor'), may hold values from -0.109375 to 0.109375
- b_outer: float32 [768], replicated, may hold values from -3 to 3
- norm2_gain: float32 [768], replicated, may hold values from 0.25 to 1.75
- norm2_bias: float32 [768], replicated, may hold values from -3 to 3
- cotangent: bfloat16 [8, 512, 768], P('dp', 'blk'), may hold values from -6 to 6
Outputs:
- output: bfloat16 [8, 512, 768], P('dp', 'blk')
- d_tokens: bfloat16 [8, 512, 768], P('dp', 'blk')
- g_w_query: float32 [768, 768], P(None, 'tensor')
- g_b_query: float32 [768], P('tensor')
- g_w_key: float32 [768, 768], P(None, 'tensor')
- g_w_value: float32 [768, 768], P(None, 'tensor')
- g_b_value: float32 [768], P('tensor')
- g_w_out: float32 [768, 768], P('tensor')
- g_b_out: float32 [768], replicated
- g_norm1_gain: float32 [768], replicated
- g_norm1_bias: float32 [768], replicated
- g_w_inner: float32 [768, 3072], P(None, 'tensor')
- g_b_inner: float32 [3072], P('tensor')
- g_w_outer: float32 [3072, 768], P('tensor')
- g_b_outer: float32 [768], replicated
- g_norm2_gain: float32 [768], replicated
- g_norm2_bias: float32 [768], replicated
Inputs may be any that keep to these rules, and one draw needn't show every extreme that they name: `bucket_ids`: A row's slots hold 128 * 2**id positions each. Among the 4 rows of each index of dp at least one, drawn from the seed, has id 2. `seq_lengths`: entry s is the length of the sequence in slot s of the row, from a quarter of the slot's positions to all of them; entries for slots past the row's end are 0. The row of id 2 named above has length 512 in slot 0.
All inputs are finite; a program needn't handle non-finite values.
Results may differ from a plain program's by a relative error of at most 0.03.
Values may be sent and summed in bfloat16 or wider, within the bound.
No kernel may reach another device: no remote copies, remote signals or barrier semaphores. Data moves between devices by JAX's collectives and lax.ppermute only.
A program may use at most 128 MiB of HBM per device.

v0:
```python
import jax
import jax.numpy as jnp
from jax import lax
from jax.sharding import PartitionSpec as P

HEAD_DIM = 64


norm_eps = 1e-12


def layer_norm(resid, gain, shift):
    center = resid - jnp.mean(resid, axis=-1, keepdims=True)
    spread = jnp.mean(center * center, axis=-1, keepdims=True)
    return center * lax.rsqrt(spread + norm_eps) * gain + shift


def gelu_exact(values):
    return jax.nn.gelu(values, approximate=False)


def slot_groups(bucket, lengths, start, count, block_len):
    positions = start + jnp.arange(count, dtype=jnp.int32)
    factor = jnp.where(bucket == 0, 1, jnp.where(bucket == 1, 2, 4)).astype(jnp.int32)
    slot_size = (block_len * factor)[:, None]
    slot_index = positions[None, :] // slot_size
    within = positions[None, :] - slot_index * slot_size
    slot_ids = jnp.arange(lengths.shape[1], dtype=jnp.int32)
    chosen = jnp.sum(jnp.where(slot_index[:, :, None] == slot_ids, lengths[:, None, :], 0), axis=-1)
    return slot_index * 2 + jnp.where(within < chosen, 0, 1)


def forward_dot(left, right):
    return jnp.dot(left, right, preferred_element_type=jnp.float32)


def over_tokens(left, right):
    return lax.dot_general(
        left, right, (((0,), (0,)), ((), ())), preferred_element_type=jnp.float32
    )


def by_transpose(left, right):
    return lax.dot_general(
        left, right, (((1,), (1,)), ((), ())), preferred_element_type=jnp.float32
    )


def body(
    tokens,
    bucket_ids,
    seq_lengths,
    w_query,
    b_query,
    w_key,
    w_value,
    b_value,
    w_out,
    b_out,
    norm1_gain,
    norm1_bias,
    w_inner,
    b_inner,
    w_outer,
    b_outer,
    norm2_gain,
    norm2_bias,
    cotangent,
):
    row_count, block_len, model_width = tokens.shape
    token_count = row_count * block_len
    local_width = w_query.shape[1]
    head_count = local_width // HEAD_DIM
    softmax_scale = HEAD_DIM ** (-0.5)
    first_pos = lax.axis_index("blk") * block_len
    query_groups = slot_groups(bucket_ids, seq_lengths, first_pos, block_len, block_len)
    flat = tokens.reshape(token_count, model_width)
    query = (forward_dot(flat, w_query) + b_query).astype(jnp.bfloat16)
    key_rows = forward_dot(flat, w_key).astype(jnp.bfloat16)
    value_rows = (forward_dot(flat, w_value) + b_value).astype(jnp.bfloat16)
    query_heads = query.reshape(row_count, block_len, head_count, HEAD_DIM)
    key_send = key_rows.reshape(row_count, block_len, local_width)
    value_send = value_rows.reshape(row_count, block_len, local_width)

    def piece_scores(key_piece, start):
        piece_len = key_piece.shape[1]
        key_groups = slot_groups(bucket_ids, seq_lengths, start, piece_len, block_len)
        allowed = (query_groups[:, :, None] == key_groups[:, None, :])[:, None]
        key_heads = key_piece.reshape(row_count, piece_len, head_count, HEAD_DIM)
        scores = (
            jnp.einsum(
                "rqhd,rkhd->rhqk", query_heads, key_heads, preferred_element_type=jnp.float32
            )
            * softmax_scale
        )
        return (allowed, scores, key_heads)

    running_max = jnp.full((row_count, head_count, block_len), -1e30, jnp.float32)
    key_piece = lax.all_gather(key_send, "blk", axis=1, tiled=True)
    value_piece = lax.all_gather(value_send, "blk", axis=1, tiled=True)
    piece_len = key_piece.shape[1]
    allowed, scores, key_heads = piece_scores(key_piece, jnp.int32(0))
    masked = jnp.where(allowed, scores, -1e30)
    new_max = jnp.maximum(running_max, jnp.max(masked, axis=-1))
    weights = jnp.where(allowed, jnp.exp(masked - new_max[..., None]), 0.0)
    running_sum = jnp.sum(weights, axis=-1)
    value_heads = value_piece.reshape(row_count, piece_len, head_count, HEAD_DIM)
    update = jnp.einsum(
        "rhqk,rkhd->rqhd",
        weights.astype(jnp.bfloat16),
        value_heads,
        preferred_element_type=jnp.float32,
    )
    weighted = update
    folded = (new_max, running_sum, weighted)
    running_max, running_sum, weighted = folded
    attended = weighted / jnp.transpose(running_sum, (0, 2, 1))[..., None]
    log_total = running_max + jnp.log(running_sum)
    heads_out = attended.reshape(token_count, local_width).astype(jnp.bfloat16)
    attn_out = (
        lax.psum(forward_dot(heads_out, w_out).astype(jnp.bfloat16), "tensor").astype(jnp.float32)
        + b_out
    )
    resid_one = flat.astype(jnp.float32) + attn_out
    hidden, norm1_back = jax.vjp(layer_norm, resid_one, norm1_gain, norm1_bias)
    hidden_low = hidden.astype(jnp.bfloat16)
    inner = forward_dot(hidden_low, w_inner) + b_inner
    act, act_back = jax.vjp(gelu_exact, inner)
    act_low = act.astype(jnp.bfloat16)
    ffn_out = (
        lax.psum(forward_dot(act_low, w_outer).astype(jnp.bfloat16), "tensor").astype(jnp.float32)
        + b_outer
    )
    result, norm2_back = jax.vjp(layer_norm, hidden + ffn_out, norm2_gain, norm2_bias)
    output = result.astype(jnp.bfloat16).reshape(row_count, block_len, model_width)
    d_res2, g_norm2_gain, g_norm2_bias = norm2_back(
        cotangent.reshape(token_count, model_width).astype(jnp.float32)
    )
    d_ffn = d_res2.astype(jnp.bfloat16)
    g_b_outer = jnp.sum(d_ffn.astype(jnp.float32), axis=0)
    g_w_outer = over_tokens(act_low, d_ffn)
    (d_inner,) = act_back(by_transpose(d_ffn, w_outer))
    d_inner_low = d_inner.astype(jnp.bfloat16)
    g_b_inner = jnp.sum(d_inner_low.astype(jnp.float32), axis=0)
    g_w_inner = over_tokens(hidden_low, d_inner_low)
    d_hidden = (
        lax.psum(by_transpose(d_inner_low, w_inner).astype(jnp.bfloat16), "tensor").astype(
            jnp.float32
        )
        + d_res2
    )
    d_res1, g_norm1_gain, g_norm1_bias = norm1_back(d_hidden)
    d_attn = d_res1.astype(jnp.bfloat16)
    g_b_out = jnp.sum(d_attn.astype(jnp.float32), axis=0)
    g_w_out = over_tokens(heads_out, d_attn)
    d_heads = (
        by_transpose(d_attn, w_out)
        .astype(jnp.bfloat16)
        .reshape(row_count, block_len, head_count, HEAD_DIM)
    )
    delta = jnp.transpose(jnp.sum(d_heads.astype(jnp.float32) * attended, axis=-1), (0, 2, 1))
    key_piece = lax.all_gather(key_send, "blk", axis=1, tiled=True)
    value_piece = lax.all_gather(value_send, "blk", axis=1, tiled=True)
    piece_len = key_piece.shape[1]
    allowed, scores, key_heads = piece_scores(key_piece, jnp.int32(0))
    value_heads = value_piece.reshape(row_count, piece_len, head_count, HEAD_DIM)
    probs = jnp.where(allowed, jnp.exp(scores - log_total[..., None]), 0.0)
    d_probs = jnp.einsum(
        "rqhd,rkhd->rhqk", d_heads, value_heads, preferred_element_type=jnp.float32
    )
    d_scores = (probs * (d_probs - delta[..., None])).astype(jnp.bfloat16)
    d_query_acc = (
        jnp.einsum("rhqk,rkhd->rqhd", d_scores, key_heads, preferred_element_type=jnp.float32)
        * softmax_scale
    )
    key_part = (
        jnp.einsum("rhqk,rqhd->rkhd", d_scores, query_heads, preferred_element_type=jnp.float32)
        * softmax_scale
    )
    value_part = jnp.einsum(
        "rhqk,rqhd->rkhd", probs.astype(jnp.bfloat16), d_heads, preferred_element_type=jnp.float32
    )
    d_key_all = key_part.reshape(row_count, piece_len, local_width)
    d_value_all = value_part.reshape(row_count, piece_len, local_width)
    back_folded = (d_query_acc, d_key_all, d_value_all)
    d_query_acc, d_key_all, d_value_all = back_folded
    d_key_own, d_value_own = (
        lax.psum_scatter(
            d_key_all.astype(jnp.bfloat16), "blk", scatter_dimension=1, tiled=True
        ).astype(jnp.float32),
        lax.psum_scatter(
            d_value_all.astype(jnp.bfloat16), "blk", scatter_dimension=1, tiled=True
        ).astype(jnp.float32),
    )
    d_query_low = d_query_acc.reshape(token_count, local_width).astype(jnp.bfloat16)
    d_key_low = d_key_own.reshape(token_count, local_width).astype(jnp.bfloat16)
    d_value_low = d_value_own.reshape(token_count, local_width).astype(jnp.bfloat16)
    g_b_query = jnp.sum(d_query_low.astype(jnp.float32), axis=0)
    g_w_query = over_tokens(flat, d_query_low)
    g_w_key = over_tokens(flat, d_key_low)
    g_w_value = over_tokens(flat, d_value_low)
    g_b_value = jnp.sum(d_value_low.astype(jnp.float32), axis=0)
    input_part = (
        by_transpose(d_query_low, w_query)
        + by_transpose(d_key_low, w_key)
        + by_transpose(d_value_low, w_value)
    )
    d_input = lax.psum(input_part.astype(jnp.bfloat16), "tensor").astype(jnp.float32) + d_res1
    d_tokens = d_input.astype(jnp.bfloat16).reshape(row_count, block_len, model_width)
    summed = lax.psum(
        (
            g_w_query,
            g_b_query,
            g_w_key,
            g_w_value,
            g_b_value,
            g_w_out,
            g_b_out,
            g_norm1_gain,
            g_norm1_bias,
            g_w_inner,
            g_b_inner,
            g_w_outer,
            g_b_outer,
            g_norm2_gain,
            g_norm2_bias,
        ),
        ("dp", "blk"),
    )
    return (
        output,
        d_tokens,
        summed[0],
        summed[1],
        summed[2],
        summed[3],
        summed[4],
        summed[5],
        summed[6],
        summed[7],
        summed[8],
        summed[9],
        summed[10],
        summed[11],
        summed[12],
        summed[13],
        summed[14],
    )


def solution(mesh):
    return jax.shard_map(
        body,
        mesh=mesh,
        in_specs=(
            P("dp", "blk", None),
            P("dp"),
            P("dp", None),
            P(None, "tensor"),
            P("tensor"),
            P(None, "tensor"),
            P(None, "tensor"),
            P("tensor"),
            P("tensor", None),
            P(),
            P(),
            P(),
            P(None, "tensor"),
            P("tensor"),
            P("tensor", None),
            P(),
            P(),
            P(),
            P("dp", "blk", None),
        ),
        out_specs=(
            P("dp", "blk", None),
            P("dp", "blk", None),
            P(None, "tensor"),
            P("tensor"),
            P(None, "tensor"),
            P(None, "tensor"),
            P("tensor"),
            P("tensor", None),
            P(),
            P(),
            P(),
            P(None, "tensor"),
            P("tensor"),
            P("tensor", None),
            P(),
            P(),
            P(),
        ),
        check_vma=False,
    )
```

profile of v0, /device:TPU:0, one launch (start us, length us, event | category | flops | bytes accessed | tf_op | source)
XLA Modules:
  0.0 583.8 jit_solution(12093206490536530430)
XLA Ops:
  10.6 1.7 fusion.32
  13.4 10.3 %all_gather.9 = bf16[4,512,192]{1,0,2:T(4,128)(2,1)S(1)} all-gather(bf16[4,128,192]{1,0,2:T(4,128)(2,1)S(1)} %reshape.373), channel_id=1, replica_groups=mesh['dp'=2,'blk'=4,'tensor'=4] {'blk'}, dimensions={1}, use_global_device_ids=true | all-gather | bytes 983040 | tf_op jit(solution)/shard_map/all_gather | solution.py:99
  23.8 8.9 %all_gather.8 = bf16[4,512,192]{1,0,2:T(4,128)(2,1)S(1)} all-gather(bf16[4,128,192]{1,0,2:T(4,128)(2,1)S(1)} %reshape.370), channel_id=1, replica_groups=mesh['dp'=2,'blk'=4,'tensor'=4] {'blk'}, dimensions={1}, use_global_device_ids=true | all-gather | bytes 983040 | tf_op jit(solution)/shard_map/all_gather | solution.py:100
  35.7 1.9 fusion.82
  39.8 44.6 %all-reduce.8.cloned.1.call-done = bf16[512,768]{1,0:T(8,128)(2,1)} async-done(((bf16[512,768]{1,0:T(8,128)(2,1)}), bf16[512,768]{1,0:T(8,128)(2,1)}) %all-reduce.8.cloned.1.call-update) | async-done | bytes 786448 | tf_op jit(solution)/shard_map/psum | solution.py:121
  87.1 5.3 multiply_convert_fusion.2
  93.3 1.7 convolution_convert_fusion.1
  95.3 42.8 %all-reduce.10.cloned.1.call-done = bf16[512,768]{1,0:T(8,128)(2,1)} async-done(((bf16[512,768]{1,0:T(8,128)(2,1)}), bf16[512,768]{1,0:T(8,128)(2,1)}) %all-reduce.10.cloned.1.call-update) | async-done | bytes 786448 | tf_op jit(solution)/shard_map/psum | solution.py:131
  146.0 1.8 convert_reduce_fusion.2
  148.7 1.7 convolution_convert_fusion
  151.2 42.4 %all-reduce.12.cloned.1.call-done = bf16[512,768]{1,0:T(8,128)(2,1)} async-done(((bf16[512,768]{1,0:T(8,128)(2,1)}), bf16[512,768]{1,0:T(8,128)(2,1)}) %all-reduce.12.cloned.1.call-update) | async-done | bytes 786448 | tf_op jit(solution)/shard_map/psum | solution.py:147
  193.5 3.1 multiply_reduce_fusion
  200.0 1.7 reshape.376
  201.7 3.7 fusion.22
  205.4 19.1 %copy.81 = bf16[4,512,192]{0,2,1:T(8,128)(2,1)} copy(bf16[4,512,192]{1,2,0:T(8,128)(2,1)} %bitcast.149) | data formatting | bytes 1572864
  224.5 46.3 %reshape.383 = bf16[512,768]{1,0:T(8,128)(2,1)} reshape(bf16[512,192,4]{2,1,0:T(8,128)(2,1)} %bitcast.131) | data formatting | bytes 1572864
  272.0 3.4 multiply_convert_fusion
  277.8 19.1 %copy.79 = bf16[4,512,192]{0,2,1:T(8,128)(2,1)} copy(bf16[4,512,192]{1,2,0:T(8,128)(2,1)} %bitcast.143) | data formatting | bytes 1572864
  297.0 46.3 %reshape.381 = bf16[512,768]{1,0:T(8,128)(2,1)} reshape(bf16[512,192,4]{2,1,0:T(8,128)(2,1)} %bitcast.132) | data formatting | bytes 1572864
  343.3 9.3 %all-reduce.14.cloned.1.call-start = ((), (), s32[]{:S(2)}) async-start(), calls=%async_computation.5 | async-start | bytes 1572864 | tf_op jit(solution)/shard_map/psum | solution.py:208
  352.6 3.7 fusion.83
  356.2 2.3 fusion.71
  360.0 15.3 %reshape.384 = bf16[128,192,4]{2,1,0:T(8,128)(2,1)} reshape(bf16[128,768]{1,0:T(8,128)(2,1)} %reduce-scatter.9.cloned.1.call-done) | data formatting | bytes 393216
  375.3 6.6 %copy.82 = bf16[4,128,192]{1,0,2:T(4,128)(2,1)S(1)} copy(bf16[4,128,192]{0,2,1:T(8,128)(2,1)} %bitcast.133) | data formatting | bytes 393216
  381.9 15.3 %reshape.382 = bf16[128,192,4]{2,1,0:T(8,128)(2,1)} reshape(bf16[128,768]{1,0:T(8,128)(2,1)} %reduce-scatter.7.cloned.1.call-done) | data formatting | bytes 393216
  397.2 6.6 %copy.80 = bf16[4,128,192]{1,0,2:T(4,128)(2,1)S(1)} copy(bf16[4,128,192]{0,2,1:T(8,128)(2,1)} %bitcast.135) | data formatting | bytes 393216
  409.0 6.5 %copy.78 = bf16[4,128,192]{1,2,0:T(8,128)(2,1)S(1)} copy(bf16[4,128,192]{0,2,1:T(8,128)(2,1)} %bitcast.134) | data formatting | bytes 393216 | tf_op jit(solution)/shard_map/reduce_scatter | solution.py:191
  415.5 6.5 %copy.77 = bf16[4,128,192]{1,2,0:T(8,128)(2,1)S(1)} copy(bf16[4,128,192]{0,2,1:T(8,128)(2,1)} %bitcast.136) | data formatting | bytes 393216 | tf_op jit(solution)/shard_map/reduce_scatter | solution.py:188
  426.7 25.3 %all-reduce = (f32[192]{0:T(256)}, f32[192]{0:T(256)}, f32[768]{0:T(1024)}, f32[768]{0:T(1024)}, f32[768]{0:T(1024)}, /*index=5*/f32[768]{0:T(1024)}, f32[768]{0:T(1024)}, f32[768]{0:T(1024)}, f32[768]{0:T(1024)}) all-reduce(f32[192]{0:T(256)S(1)} %reduce_sum.240, ...), channel_id=1, replica_groups=mesh['dp'=2,'blk'=4,'tensor'=4] {'dp','blk'}, use_global_device_ids=true, to_apply=%region_21.23 | all-reduce | flops 5760 | bytes 46080 | tf_op jit(solution)/shard_map/psum | solution.py:210
  452.0 2.3 add_convert_fusion
  454.3 114.0 %all-reduce.16.cloned.1.call-done = (f32[768,192]{0,1:T(8,128)}, f32[768,192]{0,1:T(8,128)}, f32[768,192]{0,1:T(8,128)}, f32[192,768]{1,0:T(8,128)}, f32[768,768]{1,0:T(8,128)}, /*index=5*/f32[768,768]{1,0:T(8,128)}) async-done(((f32[768,192]{0,1:T(8,128)}, f32[768,192]{0,1:T(8,128)}, f32[768,192]{0,1:T(8,128)}, f32[192,768]{1,0:T(8,128)}, f32[768,768]{1,0:T(8,128)}, /*index=5*/f32[768,768]{1,0:T(8,128)}), ...) | async-done | bytes 7077904 | tf_op jit(solution)/shard_map/psum | solution.py:210
  568.3 2.0 copy.136
  (201 shorter events, 47.3 us)
Async XLA Ops:
  7.2 79.9 %copy-start = (bf16[768,768]{1,0:T(8,128)(2,1)S(1)}, bf16[768,768]{1,0:T(8,128)(2,1)}, u32[]{:S(2)}) copy-start(bf16[768,768]{1,0:T(8,128)(2,1)} %param.33) | copy-start | bytes 3538948
  7.2 5.2 copy-start.2
  7.2 5.2 copy-start.37
  7.2 5.2 copy-start.59
  7.2 77.2 %all-reduce.8.cloned.1.call-start = ((), (), s32[]{:S(2)}) async-start(), calls=%async_computation.2 | async-start | bytes 1572864 | tf_op jit(solution)/shard_map/psum | solution.py:121
  12.4 20.7 %copy-start.22 = (bf16[4,128,3,64]{1,0,3,2:T(4,128)(2,1)}, bf16[4,128,3,64]{1,0,3,2:T(4,128)(2,1)S(1)}, u32[]{:S(2)}) copy-start(bf16[4,128,3,64]{1,0,3,2:T(4,128)(2,1)S(1)} %reshape.372) | copy-start | bytes 589828
  23.8 10.2 %copy-start.10 = (bf16[4,512,192]{1,2,0:T(8,128)(2,1)}, bf16[4,512,192]{1,2,0:T(8,128)(2,1)S(1)}, u32[]{:S(2)}) copy-start(bf16[4,512,192]{1,2,0:T(8,128)(2,1)S(1)} %copy.67) | copy-start | bytes 2359300
  35.7 2.7 copy-start.28
  37.6 46.8 %copy-start.46 = (f32[768]{0:T(1024)S(1)}, f32[768]{0:T(1024)}, u32[]{:S(2)}) copy-start(f32[768]{0:T(1024)} %param.30) | copy-start | bytes 9220
  39.7 98.4 %all-reduce.10.cloned.1.call-start = ((), (), s32[]{:S(2)}) async-start(), calls=%async_computation.3 | async-start | bytes 1572864 | tf_op jit(solution)/shard_map/psum | solution.py:131
  87.1 6.2 %copy-start.56 = (bf16[768,768]{1,0:T(8,128)(2,1)S(1)}, bf16[768,768]{1,0:T(8,128)(2,1)}, u32[]{:S(2)}) copy-start(bf16[768,768]{1,0:T(8,128)(2,1)} %param.35) | copy-start | bytes 3538948
  95.0 98.6 %all-reduce.12.cloned.1.call-start = ((), (), s32[]{:S(2)}) async-start(), calls=%async_computation.4 | async-start | bytes 1572864 | tf_op jit(solution)/shard_map/psum | solution.py:147
  143.8 4.0 copy-start.3
  144.6 3.2 copy-start.16
  150.4 209.6 %reduce-scatter.9.cloned.1.call-start = ((), (), s32[]{:S(2)}) async-start(), calls=%async_computation.7 | async-start | bytes 983040
  151.2 45.5 %copy-start.45 = (f32[512]{0:T(512)S(1)}, f32[512]{0:T(512)}, u32[]{:S(2)}) copy-start(f32[512]{0:T(512)} %copy-done.44) | copy-start | bytes 6148
  151.2 45.5 %copy-start.42 = (f32[512]{0:T(512)S(1)}, f32[512]{0:T(512)}, u32[]{:S(2)}) copy-start(f32[512]{0:T(512)} %copy-done.41) | copy-start | bytes 6148
  193.5 3.1 copy-start.4
  193.5 3.1 copy-start.14
  198.7 3.0 copy-start.20
  270.8 111.1 %reduce-scatter.7.cloned.1.call-start = ((), (), s32[]{:S(2)}) async-start(), calls=%async_computation.6 | async-start | bytes 983040
  272.0 4.6 copy-start.23
  343.3 13.0 %copy-start.53 = (f32[768]{0:T(1024)S(1)}, f32[768]{0:T(1024)}, u32[]{:S(2)}) copy-start(f32[768]{0:T(1024)} %param.32) | copy-start | bytes 9220
  343.3 108.7 %all-reduce.14.cloned.1.call-start = ((), (), s32[]{:S(2)}) async-start(), calls=%async_computation.5 | async-start | bytes 1572864 | tf_op jit(solution)/shard_map/psum | solution.py:208
  352.5 3.7 copy-start.33
  359.5 15.8 %copy-start.26 = (bf16[4,128,3,64]{1,0,3,2:T(4,128)(2,1)}, bf16[4,128,3,64]{1,0,3,2:T(4,128)(2,1)S(1)}, u32[]{:S(2)}) copy-start(bf16[4,128,3,64]{1,0,3,2:T(4,128)(2,1)S(1)} %copy.72) | copy-start | bytes 589828
  406.6 161.7 %all-reduce.16.cloned.1.call-start = ((), (), s32[]{:S(2)}) async-start(), calls=%async_computation.8 | async-start | bytes 14155776 | tf_op jit(solution)/shard_map/psum | solution.py:210
  424.3 27.7 %copy-start.6 = (f32[512,768]{1,0:T(8,128)S(1)}, f32[512,768]{1,0:T(8,128)}, u32[]{:S(2)}) copy-start(f32[512,768]{1,0:T(8,128)} %copy-done.5) | copy-start | bytes 4718596
  568.3 2.9 copy-start.35
  568.3 3.7 copy-start.34
  572.8 2.5 copy-start.17
  572.8 3.9 copy-start.1
  (37 other events, 62.0 us)
Sparse Core Ops, SparseCore 0:
  39.8 44.5 all-reduce.7
  95.1 42.9 all-reduce.9
  150.5 42.9 all-reduce.11
  270.9 22.5 reduce-scatter.8
  343.4 22.5 reduce-scatter.6
  406.8 42.9 all-reduce.13
  455.0 113.2 all-reduce.15
where the time goes:
time: 589 us; the launch traced here: 584 us
  waiting for transfers between devices  244 us (41%)
  local copies, waits for them, and re-layouts  208 us (35%)
  blocking collectives  44.5 us (8%)
  matrix products  40.8 us (7%)
  other arithmetic  21.6 us (4%)
  between operations  15 us (3%)
  starting transfers between devices  9.78 us (2%)
    unnamed x138, local copies, waits for them, and re-layouts  192 us
    psum x1, waiting for transfers between devices, body(): lax.psum((g_w_query, g_b_query, g_w_key, g_w_value, g_b_value, g_w_out, g...  114 us
    psum x1, waiting for transfers between devices, body(): lax.psum(forward_dot(heads_out, w_out).astype(jnp.bfloat16), 'tensor')  44.6 us
    psum x1, waiting for transfers between devices, body(): lax.psum(forward_dot(act_low, w_outer).astype(jnp.bfloat16), 'tensor')  42.8 us
    psum x1, waiting for transfers between devices, body(): lax.psum(by_transpose(d_inner_low, w_inner).astype(jnp.bfloat16), 'tensor')  42.4 us
    psum x1, blocking collectives, body(): lax.psum((g_w_query, g_b_query, g_w_key, g_w_value, g_b_value, g_w_out, g...  25.3 us
  transfers between devices with their start and end apart: 7, of which 4 were waited for; matrix products, arithmetic and copies ran while one was open for 21% of the time, Pallas kernels for 0%

commit v1 on v0

v1 whole, which is shorter than its diff:
```python
import functools

import jax
import jax.numpy as jnp
from jax import lax
from jax.experimental import pallas as pl
from jax.experimental.pallas import tpu as pltpu
from jax.sharding import PartitionSpec as P

HEAD_DIM = 64
BLOCK = 128
LANES = 128
SCALE = HEAD_DIM**-0.5
EPS = 1e-12
f32 = jnp.float32
bf16 = jnp.bfloat16
i32 = jnp.int32
MIB = 1 << 20


def nn(a, b):
    return lax.dot_general(a, b, (((1,), (0,)), ((), ())), preferred_element_type=f32)


def nt(a, b):
    return lax.dot_general(a, b, (((1,), (1,)), ((), ())), preferred_element_type=f32)


def tn(a, b):
    return lax.dot_general(a, b, (((0,), (0,)), ((), ())), preferred_element_type=f32)


def mean(v):
    return jnp.mean(v, axis=-1, keepdims=True)


def col_sum(v):
    return jnp.sum(v, axis=0, keepdims=True)


def rows8(*rows):
    width = rows[0].shape[1]
    pad = jnp.zeros((8 - len(rows), width), f32)
    return jnp.concatenate(rows + (pad,), axis=0)


def shape(dims, dtype):
    return jax.ShapeDtypeStruct(dims, dtype)


SMEM = pl.BlockSpec(memory_space=pltpu.SMEM)
VMEM = pl.BlockSpec(memory_space=pltpu.VMEM)


def cost(flops, nbytes, trans=0):
    return pl.CostEstimate(flops=int(flops), bytes_accessed=int(nbytes), transcendentals=int(trans))


def plain(kernel, outs, specs, name, vmem=32, scratch=(), estimate=None):
    return pl.pallas_call(
        kernel,
        out_shape=outs,
        in_specs=specs,
        out_specs=jax.tree.map(lambda _: VMEM, outs),
        scratch_shapes=list(scratch),
        compiler_params=pltpu.CompilerParams(vmem_limit_bytes=vmem * MIB),
        cost_estimate=estimate,
        name=name,
    )


def chunked(kernel, outs, specs, name, vmem=32, scratch=(), estimate=None):
    def whole(s):
        nd = len(s.shape)
        return pl.BlockSpec(s.shape, lambda i, at: (0,) * nd)

    return pl.pallas_call(
        kernel,
        out_shape=outs,
        grid_spec=pltpu.PrefetchScalarGridSpec(
            num_scalar_prefetch=1,
            grid=(1,),
            in_specs=specs,
            out_specs=jax.tree.map(whole, outs),
            scratch_shapes=list(scratch),
        ),
        compiler_params=pltpu.CompilerParams(vmem_limit_bytes=vmem * MIB),
        cost_estimate=estimate,
        name=name,
    )


def whole_of(a):
    nd = a.ndim
    return pl.BlockSpec(a.shape, lambda i, at: (0,) * nd)


def block_of(rows, width):
    return pl.BlockSpec((rows, width), lambda i, at: (at[0], 0))


def kv_kernel(tok, wk, wv, bv, kv, wkv):
    heads = wk.shape[1] // HEAD_DIM
    cols, bias = [], []
    for h in range(heads):
        part = slice(h * HEAD_DIM, (h + 1) * HEAD_DIM)
        cols += [wk[:, part], wv[:, part]]
        bias += [jnp.zeros((1, HEAD_DIM), f32), bv[:, part]]
    both = jnp.concatenate(cols, axis=1)
    wkv[...] = both
    kv[...] = (nn(tok[...], both) + jnp.concatenate(bias, axis=1)).astype(bf16)


def q_kernel(tok, wq, bq, q):
    heads = wq.shape[1] // HEAD_DIM
    full = (nn(tok[...], wq[...]) + bq[...]).astype(bf16) * jnp.asarray(SCALE, bf16)
    zero = jnp.zeros((full.shape[0], HEAD_DIM), bf16)
    cols = []
    for h in range(heads):
        cols += [full[:, h * HEAD_DIM : (h + 1) * HEAD_DIM], zero]
    q[...] = jnp.concatenate(cols, axis=1)


def wout_kernel(n, z, *refs):
    out = refs[n]
    for k in range(n):
        j = lax.rem(z[0] - k + n, n)
        out[pl.ds(pl.multiple_of(j * LANES, LANES), LANES), :] = refs[k][:LANES, :]
        at = n * LANES + j * HEAD_DIM
        out[pl.ds(pl.multiple_of(at, HEAD_DIM), HEAD_DIM), :] = refs[k][LANES:, :]


def attend_kernel(n_blk, bucket, lens, blk, q, *refs):
    kvs, hp, probs = refs[:n_blk], refs[n_blk], refs[n_blk + 1]
    rows = bucket.shape[0]
    heads = q.shape[1] // LANES
    b = blk[0]
    q_at = lax.broadcasted_iota(i32, (BLOCK, 1), 0)
    k_at = lax.broadcasted_iota(i32, (1, BLOCK), 1)
    for r in range(rows):
        bk = bucket[r]
        size = BLOCK << bk
        slot = b >> bk
        limit = lens[r, slot]
        q_in = jnp.where(q_at + (b * BLOCK - slot * size) < limit, 1, 0)
        k_in = []
        for j in range(n_blk):
            kb = b ^ j
            k_slot = kb >> bk
            inside = jnp.where(k_at + (kb * BLOCK - k_slot * size) < limit, 1, 0)
            k_in.append(jnp.where(k_slot == slot, inside, 2))
        allowed = q_in == jnp.concatenate(k_in, axis=1)
        at = slice(r * BLOCK, (r + 1) * BLOCK)
        outs = []
        for h in range(heads):
            lanes = slice(h * LANES, (h + 1) * LANES)
            kvh = jnp.concatenate([kv[at, lanes] for kv in kvs], axis=0)
            scores = jnp.where(allowed, nt(q[at, lanes], kvh), -1e30)
            weights = jnp.exp(scores - jnp.max(scores, axis=-1, keepdims=True))
            total = jnp.sum(weights, axis=-1, keepdims=True)
            p = (weights / total).astype(bf16)
            probs[(r * heads + h) * BLOCK : (r * heads + h + 1) * BLOCK, :] = p
            outs.append(nn(p, kvh)[:, HEAD_DIM:].astype(bf16))
        base = r * (BLOCK + HEAD_DIM)
        hp[base : base + BLOCK, :] = jnp.concatenate(outs[:2], axis=1)
        hp[base + BLOCK : base + BLOCK + HEAD_DIM, :] = jnp.concatenate(
            [outs[2][:HEAD_DIM], outs[2][HEAD_DIM:]], axis=1
        )


def ffn_kernel(n, at, tok, wfull, b_out, g1, b1, w_in, b_in, w_outer, *refs):
    hps = refs[:n]
    part, n1_out, s1_out, low_out, act_out, slope_out, held = refs[n:]
    z = at[1]
    for k in range(n):
        held[lax.rem(z - k + n, n)] = hps[k][...]
    pair = [held[j, :BLOCK, :] for j in range(n)]
    last = [
        jnp.concatenate([held[j, BLOCK:, :HEAD_DIM], held[j, BLOCK:, HEAD_DIM:]], axis=0)
        for j in range(n)
    ]
    attn = nn(jnp.concatenate(pair + last, axis=1), wfull[...])
    resid = tok[...].astype(f32) + (attn + b_out[...])
    center = resid - mean(resid)
    s1 = lax.rsqrt(mean(center * center) + EPS)
    n1 = center * s1
    low = (n1 * g1[...] + b1[...]).astype(bf16)
    inner = nn(low, w_in[...]) + b_in[...]
    cdf = 0.5 * (1.0 + lax.erf(inner * (0.5**0.5)))
    act = (inner * cdf).astype(bf16)
    slope = cdf + inner * (0.3989422804014327 * jnp.exp(-0.5 * inner * inner))
    part[...] = nn(act, w_outer[...]).astype(bf16)
    n1_out[...] = n1
    s1_out[...] = jnp.broadcast_to(s1, s1_out.shape)
    low_out[...] = low
    act_out[...] = act
    slope_out[...] = slope.astype(bf16)


def ffn_back_kernel(
    at, cot, n1, slope, ffn, g1, b1, b_outer, g2, b2, w_in, w_outer,
    out, dres2_out, dffn_out, dinner_out, part, sums,
):
    hidden = n1[...] * g1[...] + b1[...]
    resid = hidden + (ffn[...].astype(f32) + b_outer[...])
    center = resid - mean(resid)
    s2 = lax.rsqrt(mean(center * center) + EPS)
    n2 = center * s2
    out[...] = (n2 * g2[...] + b2[...]).astype(bf16)
    ct = cot[...].astype(f32)
    dn = ct * g2[...]
    dres2 = s2 * (dn - mean(dn) - n2 * mean(dn * n2))
    dffn = dres2.astype(bf16)
    dinner = (nt(dffn, w_outer[...]) * slope[...].astype(f32)).astype(bf16)
    part[...] = nt(dinner, w_in[...]).astype(bf16)
    dres2_out[...] = dres2
    dffn_out[...] = dffn
    dinner_out[...] = dinner
    sums[...] = rows8(
        col_sum(ct * n2), col_sum(ct), col_sum(dffn.astype(f32)), col_sum(dinner.astype(f32))
    )


def attend_back_kernel(n_blk, at, dh, dres2, n1, s1, g1, w_out, q, probs, *refs):
    kvs = refs[:n_blk]
    dres1_out, dattn_out, sums, dq_out, send, keep = refs[n_blk:]
    heads = q.shape[1] // LANES
    dhidden = dh[...].astype(f32) + dres2[...]
    norm = n1[...]
    dn = dhidden * g1[...]
    dres1 = s1[:, :1] * (dn - mean(dn) - norm * mean(dn * norm))
    dattn = dres1.astype(bf16)
    dres1_out[...] = dres1
    dattn_out[...] = dattn
    sums[...] = rows8(col_sum(dhidden * norm), col_sum(dhidden), col_sum(dattn.astype(f32)))
    zero = jnp.zeros((HEAD_DIM, w_out.shape[1]), bf16)
    spread = []
    for h in range(heads):
        spread += [zero, w_out[h * HEAD_DIM : (h + 1) * HEAD_DIM, :]]
    dheads = nt(dattn, jnp.concatenate(spread, axis=0)).astype(bf16)
    dqs = []
    for h in range(heads):
        lanes = slice(h * LANES, (h + 1) * LANES)
        kvh = jnp.concatenate([kv[:, lanes] for kv in kvs], axis=0)
        p = probs[h * BLOCK : (h + 1) * BLOCK, :]
        pf = p.astype(f32)
        dp = nt(dheads[:, lanes], kvh)
        delta = jnp.sum(pf * dp, axis=-1, keepdims=True)
        ds = (pf * (dp - delta)).astype(bf16)
        dqs.append((nn(ds, kvh) * SCALE)[:, :HEAD_DIM].astype(bf16))
        left = jnp.concatenate([q[:, lanes], dheads[:, lanes]], axis=0)
        dkv = tn(left, jnp.concatenate([ds, p], axis=0)).astype(bf16)
        for j in range(n_blk):
            target = keep if j % 2 == 0 else send
            target[j // 2, lanes, :] = dkv[:, j * BLOCK : (j + 1) * BLOCK]
    dq_out[...] = jnp.concatenate(dqs, axis=1)


def input_kernel(dq, keep, recv, far, wq, wkv, part, dkv_t, sums):
    total = keep[0].astype(f32) + recv[0].astype(f32) + far[...].astype(f32)
    low_t = total.astype(bf16)
    low = low_t.T
    part[...] = (nt(dq[...], wq[...]) + nt(low, wkv[...])).astype(bf16)
    dkv_t[...] = low_t
    width = sums.shape[1]
    first = col_sum(dq[...].astype(f32))
    second = col_sum(low.astype(f32))
    sums[...] = rows8(
        jnp.concatenate([first, jnp.zeros((1, width - first.shape[1]), f32)], axis=1),
        jnp.concatenate([second, jnp.zeros((1, width - second.shape[1]), f32)], axis=1),
    )


def ordered_sum(n, z, refs, held):
    for k in range(n):
        held[lax.rem(z - k + n, n)] = refs[k][...]
    total = held[0]
    for j in range(1, n):
        total = total + held[j]
    return total


def pick(first, one, other):
    return jnp.where(first, one, other)


def ffn_grad_kernel(n, at, *refs):
    low, dinner, act, dffn, sums = (refs[i * n : (i + 1) * n] for i in range(5))
    keep, send, held = refs[5 * n :]
    first = at[2] == 0
    tail = ordered_sum(n, at[1], sums, held).astype(bf16)
    a = jnp.concatenate([pick(first, x[...], y[...]) for x, y in zip(low, act)], axis=0)
    b = jnp.concatenate([pick(first, x[...], y[...]) for x, y in zip(dinner, dffn)], axis=0)
    c = jnp.concatenate([pick(first, y[...], x[...]) for x, y in zip(low, act)], axis=0)
    d = jnp.concatenate([pick(first, y[...], x[...]) for x, y in zip(dinner, dffn)], axis=0)
    rows = a.shape[1]
    rest = keep.shape[0] - rows
    tail = jnp.concatenate([tail, jnp.zeros((rest - 8, tail.shape[1]), bf16)], axis=0)
    send[:rows, :] = tn(c, d).astype(bf16)
    send[rows:, :] = tail
    keep[:rows, :] = tn(a, b).astype(bf16)
    keep[rows:, :] = tail


def attend_grad_kernel(n, at, tok, hp, *refs):
    dattn, dq, dkv_t, sums1, sums2 = (refs[i * n : (i + 1) * n] for i in range(5))
    keep, send, held1, held2 = refs[5 * n :]
    z = at[1]
    first = at[2] == 0
    total1 = ordered_sum(n, z, sums1, held1)
    total2 = ordered_sum(n, z, sums2, held2)
    tail = jnp.concatenate([total1, total2], axis=0).astype(bf16)
    toks, heads = [], []
    for k in range(n):
        c = lax.rem(z - k + n, n)
        toks.append(tok[pl.ds(pl.multiple_of(c * BLOCK, BLOCK), BLOCK), :])
        step = BLOCK + HEAD_DIM
        h = hp[pl.ds(pl.multiple_of(c * step, HEAD_DIM), step), :]
        odd = jnp.concatenate([h[BLOCK:, :HEAD_DIM], h[BLOCK:, HEAD_DIM:]], axis=0)
        heads.append(jnp.concatenate([h[:BLOCK, :], odd], axis=1))
    toks = jnp.concatenate(toks, axis=0)
    g_out = tn(jnp.concatenate(heads, axis=0), jnp.concatenate([x[...] for x in dattn], axis=0))
    g_q = tn(jnp.concatenate([x[...] for x in dq], axis=0), toks)
    g_kv = nn(jnp.concatenate([x[...] for x in dkv_t], axis=1), toks)
    one = jnp.concatenate([g_out, g_q], axis=0).astype(bf16)
    two = g_kv.astype(bf16)
    rows = two.shape[0]
    rest = keep.shape[0] - rows
    tail = jnp.concatenate([tail, jnp.zeros((rest - 16, tail.shape[1]), bf16)], axis=0)
    send[:rows, :] = pick(first, two, one)
    send[rows:, :] = tail
    keep[:rows, :] = pick(first, one, two)
    keep[rows:, :] = tail


def gather_kernel(m, i, *refs):
    out = refs[m]
    for s in range(m):
        out[i[0] ^ s] = refs[s][...]


def ffn_final_kernel(at, mine, other, g_in, g_outer, tail):
    first = at[2] == 0
    rows = g_in.shape[0]
    a = mine[...]
    b = other[...]
    g_in[...] = pick(first, a[:rows], b[:rows]).astype(f32)
    g_outer[...] = pick(first, b[:rows], a[:rows]).astype(f32)
    tail[...] = pick(first, a[rows : rows + 16], b[rows : rows + 16]).astype(f32)


def attend_final_kernel(at, mine, other, g_out, g_q, g_k, g_v, tail):
    first = at[2] == 0
    width = g_out.shape[0]
    a = mine[...]
    b = other[...]
    one = pick(first, a, b).astype(f32)
    two = pick(first, b, a).astype(f32)
    g_out[...] = one[:width]
    g_q[...] = one[width : 2 * width].T
    ks, vs = [], []
    for h in range(width // HEAD_DIM):
        ks.append(two[h * LANES : h * LANES + HEAD_DIM])
        vs.append(two[h * LANES + HEAD_DIM : (h + 1) * LANES])
    g_k[...] = jnp.concatenate(ks, axis=0).T
    g_v[...] = jnp.concatenate(vs, axis=0).T
    tail[...] = one[2 * width : 2 * width + 16]


def output_kernel(n, at, *refs):
    out = refs[n]
    for k in range(n):
        out[lax.rem(at[1] - k + n, n)] = refs[k][...]


def solution(mesh):
    n_dp = mesh.shape["dp"]
    n_blk = mesh.shape["blk"]
    n = mesh.shape["tensor"]
    half_blk = n_blk // 2
    m = n_dp * half_blk

    def shift(v, k):
        return lax.ppermute(v, "tensor", [(i, (i + k) % n) for i in range(n)])

    def flip(v, bit):
        return lax.ppermute(v, "blk", [(i, i ^ bit) for i in range(n_blk)])

    def flip_member(v, s):
        perm = []
        for dp in range(n_dp):
            for blk in range(n_blk):
                i = (dp * half_blk + blk // 2) ^ s
                to = (i // half_blk) * n_blk + (i % half_blk) * 2 + blk % 2
                perm.append((dp * n_blk + blk, to))
        return lax.ppermute(v, ("dp", "blk"), perm)

    def sum_grads(keep, send, member, name):
        recv = flip(send, 1)
        rows = keep.shape[0] // m
        width = keep.shape[1]
        keep3 = keep.reshape(m, rows, width)
        recv3 = recv.reshape(m, rows, width)

        def piece(s):
            mine = lax.dynamic_index_in_dim(keep3, member ^ s, 0, keepdims=False)
            theirs = lax.dynamic_index_in_dim(recv3, member ^ s, 0, keepdims=False)
            return mine.astype(f32) + theirs.astype(f32)

        got = [flip_member(piece(s).astype(bf16), s) for s in range(1, m)]
        total = piece(0)
        for part in got:
            total = total + part.astype(f32)
        total = total.astype(bf16)
        every = [total] + [flip_member(total, s) for s in range(1, m)]
        mine = plain(
            functools.partial(gather_kernel, m),
            shape((m, rows, width), bf16),
            [SMEM] + [VMEM] * m,
            name,
        )(member.reshape(1), *every)
        mine = mine.reshape(m * rows, width)
        return mine, flip(mine, 1)

    def body(
        tokens, bucket_ids, seq_lengths, w_query, b_query, w_key, w_value, b_value, w_out, b_out,
        norm1_gain, norm1_bias, w_inner, b_inner, w_outer, b_outer, norm2_gain, norm2_bias,
        cotangent,
    ):
        row_count, block, width = tokens.shape
        count = row_count * block
        local = w_query.shape[1]
        heads = local // HEAD_DIM
        hidden_units = w_inner.shape[1]
        blk = lax.axis_index("blk").astype(i32)
        z = lax.axis_index("tensor").astype(i32)
        member = (lax.axis_index("dp") * half_blk + blk // 2).astype(i32)
        tok = tokens.reshape(count, width)
        cot = cotangent.reshape(count, width)
        row = lambda v: v.reshape(1, -1)
        ats = [jnp.stack([lax.rem(z - k + n, n), z, blk % 2]).astype(i32) for k in range(n)]

        kv, wkv = plain(
            kv_kernel,
            (shape((count, heads * LANES), bf16), shape((width, heads * LANES), bf16)),
            [VMEM] * 4,
            "kv_rows",
            estimate=cost(4 * count * width * local, 3 * MIB),
        )(tok, w_key, w_value, row(b_value))
        kv_far = flip(kv, 2)
        kv_core = flip(kv, 1)
        wouts = [w_out] + [shift(w_out, k) for k in range(1, n)]
        q = plain(
            q_kernel,
            shape((count, heads * LANES), bf16),
            [VMEM] * 3,
            "query_rows",
            estimate=cost(2 * count * width * local, 2 * MIB),
        )(tok, w_query, row(b_query))
        kv_both = flip(kv_far, 1)
        kvs = [kv, kv_core, kv_far, kv_both]
        hp, probs = plain(
            functools.partial(attend_kernel, n_blk),
            (
                shape((row_count * (BLOCK + HEAD_DIM), LANES), bf16),
                shape((row_count * heads * BLOCK, n_blk * BLOCK), bf16),
            ),
            [SMEM] * 3 + [VMEM] * (1 + n_blk),
            "attend",
            estimate=cost(2e9, 4 * MIB),
        )(bucket_ids, seq_lengths, blk.reshape(1), q, *kvs)
        hps = [hp] + [shift(hp, k) for k in range(1, n)]
        wfull = plain(
            functools.partial(wout_kernel, n),
            shape((n * local, width), bf16),
            [SMEM] + [VMEM] * n,
            "all_w_out",
            estimate=cost(0, 3 * MIB),
        )(z.reshape(1), *wouts)

        chunk = lambda w, dt: shape((BLOCK, w), dt)
        order = [k for k in range(1, n)] + [0]

        def ffn(k):
            weights = (wfull, row(b_out), row(norm1_gain), row(norm1_bias), w_inner, row(b_inner), w_outer)
            return chunked(
                functools.partial(ffn_kernel, n),
                (
                    chunk(width, bf16), chunk(width, f32), chunk(LANES, f32), chunk(width, bf16),
                    chunk(hidden_units, bf16), chunk(hidden_units, bf16),
                ),
                [block_of(BLOCK, width)]
                + [whole_of(w) for w in weights]
                + [block_of(BLOCK + HEAD_DIM, LANES)] * n,
                "ffn",
                scratch=[pltpu.VMEM((n, BLOCK + HEAD_DIM, LANES), bf16)],
                estimate=cost(6 * BLOCK * width * width, 5 * MIB),
            )(ats[k], tok, *weights, *hps)

        def scatter_gather(parts, extra=None):
            total = parts[0].astype(f32)
            for k in range(1, n):
                total = total + shift(parts[k], -k).astype(f32)
            if extra is not None:
                total = total + extra
            total = total.astype(bf16)
            return [total] + [shift(total, k) for k in range(1, n)]

        first = {k: ffn(k) for k in order}
        ffns = scatter_gather([first[k][0] for k in range(n)])

        def ffn_back(k):
            _, n1, _, _, _, slope = first[k]
            args = (n1, slope, ffns[k], row(norm1_gain), row(norm1_bias), row(b_outer),
                    row(norm2_gain), row(norm2_bias), w_inner, w_outer)
            return chunked(
                ffn_back_kernel,
                (
                    chunk(width, bf16), chunk(width, f32), chunk(width, bf16),
                    chunk(hidden_units, bf16), chunk(width, bf16), shape((8, width), f32),
                ),
                [block_of(BLOCK, width)] + [whole_of(a) for a in args],
                "ffn_back",
                estimate=cost(4 * BLOCK * width * width, 5 * MIB),
            )(ats[k], cot, *args)

        second = {k: ffn_back(k) for k in [0] + order[:-1]}
        dhs = scatter_gather([second[k][4] for k in range(n)])

        half = width + 16 * m
        half += -half % (16 * m)
        keep1, send1 = chunked(
            functools.partial(ffn_grad_kernel, n),
            (shape((half, width), bf16), shape((half, width), bf16)),
            [pl.BlockSpec((BLOCK, width), lambda i, at: (0, 0))] * (4 * n)
            + [pl.BlockSpec((8, width), lambda i, at: (0, 0))] * n,
            "ffn_grads",
            vmem=48,
            scratch=[pltpu.VMEM((n, 8, width), f32)],
            estimate=cost(4 * count * width * width, 6 * MIB),
        )(
            ats[0],
            *[first[k][3] for k in range(n)],
            *[second[k][3] for k in range(n)],
            *[first[k][4] for k in range(n)],
            *[second[k][2] for k in range(n)],
            *[second[k][5] for k in range(n)],
        )
        mine1, other1 = sum_grads(keep1, send1, member, "gather_ffn_grads")

        def attend_back(k):
            _, n1, s1, _, _, _ = first[k]
            args = (dhs[k], second[k][1], n1, s1, row(norm1_gain), w_out)
            return chunked(
                functools.partial(attend_back_kernel, n_blk),
                (
                    chunk(width, f32), chunk(width, bf16), shape((8, width), f32), chunk(local, bf16),
                    shape((half_blk, heads * LANES, BLOCK), bf16),
                    shape((half_blk, heads * LANES, BLOCK), bf16),
                ),
                [whole_of(a) for a in args]
                + [block_of(BLOCK, heads * LANES), block_of(heads * BLOCK, n_blk * BLOCK)]
                + [block_of(BLOCK, heads * LANES)] * n_blk,
                "attend_back",
                estimate=cost(1e9, 4 * MIB),
            )(ats[k], *args, q, probs, *kvs)

        third = {k: attend_back(k) for k in [0] + order[:-1]}

        def input_part(k):
            _, _, _, dq, send, keep = third[k]
            recv = flip(send, 1)
            out = (keep[1].astype(f32) + recv[1].astype(f32)).astype(bf16)
            far = flip(out, 2)
            return plain(
                input_kernel,
                (chunk(width, bf16), shape((heads * LANES, BLOCK), bf16), shape((8, width), f32)),
                [VMEM] * 6,
                "input_part",
                estimate=cost(6 * BLOCK * width * local, 2 * MIB),
            )(dq, keep, recv, far, w_query, wkv)

        fourth = {k: input_part(k) for k in order}
        d_tok = scatter_gather([fourth[k][0] for k in range(n)], third[0][0])

        rows2 = 2 * local + 16
        rows2 += -rows2 % (16 * m)
        keep2, send2 = plain(
            functools.partial(attend_grad_kernel, n),
            (shape((rows2, width), bf16), shape((rows2, width), bf16)),
            [SMEM] + [VMEM] * (2 + 5 * n),
            "attend_grads",
            vmem=48,
            scratch=[pltpu.VMEM((n, 8, width), f32)] * 2,
            estimate=cost(2 * count * width * 4 * local, 5 * MIB),
        )(
            ats[0], tok, hp,
            *[third[k][1] for k in range(n)],
            *[third[k][3] for k in range(n)],
            *[fourth[k][1] for k in range(n)],
            *[third[k][2] for k in range(n)],
            *[fourth[k][2] for k in range(n)],
        )
        mine2, other2 = sum_grads(keep2, send2, member, "gather_attend_grads")

        assemble = lambda parts, name: plain(
            functools.partial(output_kernel, n),
            shape((row_count, block, width), bf16),
            [SMEM] + [VMEM] * n,
            name,
            estimate=cost(0, 2 * MIB),
        )(ats[0], *parts)
        output = assemble([second[k][0] for k in range(n)], "output_rows")
        d_tokens = assemble(d_tok, "input_grad_rows")

        g_w_inner, g_w_outer, tail1 = plain(
            ffn_final_kernel,
            (shape((width, hidden_units), f32), shape((hidden_units, width), f32), shape((16, width), f32)),
            [SMEM] + [VMEM] * 2,
            "ffn_grads_out",
            estimate=cost(0, 8 * MIB),
        )(ats[0], mine1, other1)
        g_w_out, g_w_query, g_w_key, g_w_value, tail2 = plain(
            attend_final_kernel,
            (shape((local, width), f32),) + (shape((width, local), f32),) * 3 + (shape((16, width), f32),),
            [SMEM] + [VMEM] * 2,
            "attend_grads_out",
            estimate=cost(0, 5 * MIB),
        )(ats[0], mine2, other2)
        g_b_query = tail2[8, :local]
        g_b_value = tail2[9, : heads * LANES].reshape(heads, 2, HEAD_DIM)[:, 1].reshape(local)
        return (
            output, d_tokens, g_w_query, g_b_query, g_w_key, g_w_value, g_b_value, g_w_out,
            tail2[2], tail2[0], tail2[1], g_w_inner, tail1[3], g_w_outer, tail1[2], tail1[0], tail1[1],
        )

    spread, cols, vec, rows_ = P("dp", "blk", None), P(None, "tensor"), P("tensor"), P("tensor", None)
    return jax.shard_map(
        body,
        mesh=mesh,
        in_specs=(
            spread, P("dp"), P("dp", None), cols, vec, cols, cols, vec, rows_, P(), P(), P(),
            cols, vec, rows_, P(), P(), P(), spread,
        ),
        out_specs=(
            spread, spread, cols, vec, cols, cols, vec, rows_, P(), P(), P(), cols, vec, rows_,
            P(), P(), P(),
        ),
        check_vma=False,
    )
```

time: 589 us -> 284 us (0.48)
  local copies, waits for them, and re-layouts: 208 us -> 43 us
  waiting for transfers between devices: 244 us -> 98 us
  starting transfers between devices: 9.78 us -> 77.6 us
  Pallas kernels: 0 us -> 52.5 us
  blocking collectives: 44.5 us -> 0 us
  matrix products: 40.8 us -> 0 us
  other arithmetic: 21.6 us -> 8.26 us
  between operations: 15 us -> 1.93 us
    psum x5 -> x0, waiting for transfers between devices: 244 us -> none  [the longest x1 114 us: body(): lax.psum((g_w_query, g_b_query, g_w_key, g_w_value, g_b_value, g_w_out, g...]
    unnamed x138 -> x258, local copies, waits for them, and re-layouts: 192 us -> 40.4 us
    ppermute x0 -> x51, waiting for transfers between devices: none -> 98 us  [the longest x24 57.2 us: shift(): return lax.ppermute(v, 'tensor', [(i, (i + k) % n) for i in range(n)])]
    ppermute x0 -> x51, starting transfers between devices: none -> 77.6 us  [the longest x24 53.2 us: shift(): return lax.ppermute(v, 'tensor', [(i, (i + k) % n) for i in range(n)])]
    pallas_call x0 -> x28, Pallas kernels: none -> 52.5 us  [the longest x4 13.2 us: attend_back(): chunked(functools.partial(attend_back_kernel, n_blk), (chunk(width, f32),...]
    dot_general x24 -> x0, matrix products: 40.8 us -> none  [the longest x6 10.8 us: forward_dot(): return jnp.dot(left, right, preferred_element_type=jnp.float32)]
    psum x1 -> x0, blocking collectives: 25.3 us -> none  [body(): lax.psum((g_w_query, g_b_query, g_w_key, g_w_value, g_b_value, g_w_out, g...]
    all_gather x2 -> x0, blocking collectives: 19.2 us -> none  [the longest x1 10.3 us: body(): key_piece = lax.all_gather(key_send, 'blk', axis=1, tiled=True)]
  transfers between devices with their start and end apart: 7 -> 51, of which waited for: 4 -> 25; matrix products, arithmetic and copies ran while one was open for 21% -> 5% of each run, Pallas kernels for 0% -> 17%
where the time goes in v1:
time: 284 us; the launch traced here: 281 us
  waiting for transfers between devices  98 us (35%)
  starting transfers between devices  77.6 us (27%)
  Pallas kernels  52.5 us (18%)
  local copies, waits for them, and re-layouts  43 us (15%)
  other arithmetic  8.26 us (3%)
    ppermute x24, waiting for transfers between devices, shift(): return lax.ppermute(v, 'tensor', [(i, (i + k) % n) for i in range(n)])  57.2 us
    ppermute x24, starting transfers between devices, shift(): return lax.ppermute(v, 'tensor', [(i, (i + k) % n) for i in range(n)])  53.2 us
    unnamed x258, local copies, waits for them, and re-layouts  40.4 us
    ppermute x12, waiting for transfers between devices, flip_member(): return lax.ppermute(v, ('dp', 'blk'), perm)  27.4 us
    ppermute x12, starting transfers between devices, flip_member(): return lax.ppermute(v, ('dp', 'blk'), perm)  15.2 us
    ppermute x15, waiting for transfers between devices, flip(): return lax.ppermute(v, 'blk', [(i, i ^ bit) for i in range(n_blk)])  13.4 us
    pallas_call x4, Pallas kernels, attend_back(): chunked(functools.partial(attend_back_kernel, n_blk), (chunk(width, f32),...  13.2 us
    ppermute x15, starting transfers between devices, flip(): return lax.ppermute(v, 'blk', [(i, i ^ bit) for i in range(n_blk)])  9.16 us
  transfers between devices with their start and end apart: 51, of which 25 were waited for; matrix products, arithmetic and copies ran while one was open for 5% of the time, Pallas kernels for 17%

profile of v1, /device:TPU:0, one launch (start us, length us, event | category | flops | bytes accessed | tf_op | source)
XLA Modules:
  0.0 281.2 jit_solution(4720817455763875618)
XLA Ops:
  4.6 3.0 %collective-permute-start.4 = (bf16[512,384]{1,0:T(8,128)(2,1)S(1)}, bf16[512,384]{1,0:T(8,128)(2,1)S(1)}, u32[]{:S(2)}, u32[]{:S(2)}) collective-permute-start(bf16[512,384]{1,0:T(8,128)(2,1)S(1)} %get-tuple-element.114.refs_0_), channel_id=1, source_target_pairs={{0,8},{4,12},{8,0},{12,4},{1,9},{5,13},{9,1},{13,5},{2,10},{6,14},... | collective-permute-start | bytes 1179656 | tf_op jit(solution)/shard_map/ppermute | solution.py:387
  7.6 9.1 %collective-permute-done.4.refs_2_ = bf16[512,384]{1,0:T(8,128)(2,1)S(1)} collective-permute-done((bf16[512,384]{1,0:T(8,128)(2,1)S(1)}, bf16[512,384]{1,0:T(8,128)(2,1)S(1)}, u32[]{:S(2)}, u32[]{:S(2)}) %collective-permute-start.4) | collective-permute-done | bytes 393248 | tf_op jit(solution)/shard_map/ppermute | solution.py:387
  18.5 2.6 collective-permute-start.1
  23.3 4.9 %attend.1 = (bf16[768,128]{1,0:T(8,128)(2,1)S(1)}, bf16[1536,512]{1,0:T(8,128)(2,1)S(1)}) custom-call(s32[4]{0:T(128)S(1)} %copy-done.117, s32[4,4]{1,0:T(4,128)S(1)} %copy-done.116, s32[1]{0:T(128)} %bitcast.5.blk, bf16[512,384]{1,0:T(8,128)(2,1)S(1)} %query_rows.1.q, bf16[512,384]{1,0:T(8,128)(2,1)S(1)} %get-tuple-element.114.refs_0_, ...), custom_call_target="tpu_custom_call" | custom-call | flops 2000000000 | bytes 4194304 | tf_op jit(solution)/shard_map/attend/pallas_call | solution.py:462
  31.9 2.8 %collective-permute-start.8 = (bf16[768,128]{1,0:T(8,128)(2,1)S(1)}, bf16[768,128]{1,0:T(8,128)(2,1)S(1)}, u32[]{:S(2)}, u32[]{:S(2)}) collective-permute-start(bf16[768,128]{1,0:T(8,128)(2,1)S(1)} %get-tuple-element.115.refs_0_.hp), channel_id=1, source_target_pairs={{0,3},{1,0},{2,1},{3,2},{4,7},{5,4},{6,5},{7,6},{8,11},{9,8},{10,9... | collective-permute-start | bytes 589832 | tf_op jit(solution)/shard_map/ppermute | solution.py:384
  34.9 6.7 %collective-permute-done.1.refs_2_ = bf16[192,768]{1,0:T(8,128)(2,1)} collective-permute-done((bf16[192,768]{1,0:T(8,128)(2,1)}, bf16[192,768]{1,0:T(8,128)(2,1)}, u32[]{:S(2)}, u32[]{:S(2)}) %collective-permute-start.1) | collective-permute-done | bytes 294944 | tf_op jit(solution)/shard_map/ppermute | solution.py:384
  42.9 2.8 collective-permute-done.6.refs_1_
  45.7 14.5 %collective-permute-done.7.refs_2_ = bf16[768,128]{1,0:T(8,128)(2,1)S(1)} collective-permute-done((bf16[768,128]{1,0:T(8,128)(2,1)S(1)}, bf16[768,128]{1,0:T(8,128)(2,1)S(1)}, u32[]{:S(2)}, u32[]{:S(2)}) %collective-permute-start.7) | collective-permute-done | bytes 196640 | tf_op jit(solution)/shard_map/ppermute | solution.py:384
  65.4 4.7 %collective-permute-start.11 = (bf16[128,768]{1,0:T(8,128)(2,1)}, bf16[128,768]{1,0:T(8,128)(2,1)}, u32[]{:S(2)}, u32[]{:S(2)}) collective-permute-start(bf16[128,768]{1,0:T(8,128)(2,1)} %get-tuple-element.121), channel_id=1, source_target_pairs={{0,1},{1,2},{2,3},{3,0},{4,5},{5,6},{6,7},{7,4},{8,9},{9,10},{10,1... | collective-permute-start | bytes 589832 | tf_op jit(solution)/shard_map/ppermute | solution.py:384
  94.0 4.6 %collective-permute-done.14.ffn = bf16[128,768]{1,0:T(8,128)(2,1)S(1)} collective-permute-done((bf16[128,768]{1,0:T(8,128)(2,1)S(1)}, bf16[128,768]{1,0:T(8,128)(2,1)S(1)}, u32[]{:S(2)}, u32[]{:S(2)}) %collective-permute-start.14) | collective-permute-done | bytes 196640 | tf_op jit(solution)/shard_map/ppermute | solution.py:384
  101.9 16.4 %collective-permute-start.17 = (bf16[128,768]{1,0:T(8,128)(2,1)S(1)}, bf16[128,768]{1,0:T(8,128)(2,1)S(1)}, u32[]{:S(2)}, u32[]{:S(2)}) collective-permute-start(bf16[128,768]{1,0:T(8,128)(2,1)S(1)} %get-tuple-element.135), channel_id=1, source_target_pairs={{0,1},{1,2},{2,3},{3,0},{4,5},{5,6},{6,7},{7,4},{8,9},{9,10},{10,1... | collective-permute-start | bytes 589832 | tf_op jit(solution)/shard_map/ppermute | solution.py:384
  127.0 3.6 %collective-permute-done.16 = bf16[128,768]{1,0:T(8,128)(2,1)S(1)} collective-permute-done((bf16[128,768]{1,0:T(8,128)(2,1)S(1)}, bf16[128,768]{1,0:T(8,128)(2,1)S(1)}, u32[]{:S(2)}, u32[]{:S(2)}) %collective-permute-start.16) | collective-permute-done | bytes 196640 | tf_op jit(solution)/shard_map/ppermute | solution.py:384
  131.3 4.3 %collective-permute-start.28 = (bf16[128,768]{1,0:T(8,128)(2,1)}, bf16[128,768]{1,0:T(8,128)(2,1)}, u32[]{:S(2)}, u32[]{:S(2)}) collective-permute-start(bf16[128,768]{1,0:T(8,128)(2,1)} %add_convert_fusion.4.dh), channel_id=1, source_target_pairs={{0,3},{1,0},{2,1},{3,2},{4,7},{5,4},{6,5},{7,6},{8,11},{9,8},{10,9... | collective-permute-start | bytes 589832 | tf_op jit(solution)/shard_map/ppermute | solution.py:384
  135.7 3.8 %attend_back.4 = (f32[128,768]{1,0:T(8,128)S(1)}, bf16[128,768]{1,0:T(8,128)(2,1)S(1)}, f32[8,768]{1,0:T(8,128)S(1)}, bf16[128,192]{1,0:T(8,128)(2,1)S(1)}, bf16...) custom-call(s32[3]{0:T(128)S(1)} %add_add_fusion.at, bf16[128,768]{1,0:T(8,128)(2,1)} %add_convert_fusion.4.dh, ...), custom_call_target="tpu_custom_call" | custom-call | flops 1000000000 | bytes 4194304 | tf_op jit(solution)/shard_map/attend_back/pallas_call | solution.py:554
  143.0 3.0 %ffn_grads.1 = (bf16[832,768]{1,0:T(8,128)(2,1)S(1)}, bf16[832,768]{1,0:T(8,128)(2,1)}) custom-call(s32[3]{0:T(128)S(1)} %add_add_fusion.at, bf16[128,768]{1,0:T(8,128)(2,1)S(1)} %get-tuple-element.186.refs_0_, bf16[128,768]{1,0:T(8,128)(2,1)S(1)} %copy-done.113, bf16[128,768]{1,0:T(8,128)(2,1)S(1)} %copy-done.109, bf16[128,768]{1,0:T(8,128)(2,1)S(1)} %copy-done.103, ...), custom_call_target="tpu_custom_call" | custom-call | flops 1207959552 | bytes 6291456 | tf_op jit(solution)/shard_map/ffn_grads/pallas_call | solution.py:532
  153.5 3.1 %attend_back.7 = (f32[128,768]{1,0:T(8,128)}, bf16[128,768]{1,0:T(8,128)(2,1)S(1)}, f32[8,768]{1,0:T(8,128)S(1)}, bf16[128,192]{1,0:T(8,128)(2,1)S(1)}, bf16[2,3...) custom-call(s32[3]{0:T(128)S(1)} %copy-done.95, bf16[128,768]{1,0:T(8,128)(2,1)} %collective-permute-done.28.dh, ...), custom_call_target="tpu_custom_call" | custom-call | flops 1000000000 | bytes 4194304 | tf_op jit(solution)/shard_map/attend_back/pallas_call | solution.py:554
  161.8 3.1 %attend_back.6 = (f32[128,768]{1,0:T(8,128)}, bf16[128,768]{1,0:T(8,128)(2,1)S(1)}, f32[8,768]{1,0:T(8,128)S(1)}, bf16[128,192]{1,0:T(8,128)(2,1)S(1)}, bf16[2,3...) custom-call(s32[3]{0:T(128)S(1)} %copy-done.92, bf16[128,768]{1,0:T(8,128)(2,1)S(1)} %collective-permute-done.24.dh, ...), custom_call_target="tpu_custom_call" | custom-call | flops 1000000000 | bytes 4194304 | tf_op jit(solution)/shard_map/attend_back/pallas_call | solution.py:554
  165.0 3.1 %attend_back.5 = (f32[128,768]{1,0:T(8,128)}, bf16[128,768]{1,0:T(8,128)(2,1)S(1)}, f32[8,768]{1,0:T(8,128)S(1)}, bf16[128,192]{1,0:T(8,128)(2,1)S(1)}, bf16[2,3...) custom-call(s32[3]{0:T(128)S(1)} %copy-done.90, bf16[128,768]{1,0:T(8,128)(2,1)S(1)} %collective-permute-done.20.dh, ...), custom_call_target="tpu_custom_call" | custom-call | flops 1000000000 | bytes 4194304 | tf_op jit(solution)/shard_map/attend_back/pallas_call | solution.py:554
  181.3 4.2 %collective-permute-done.22.far = bf16[384,128]{1,0:T(8,128)(2,1)S(1)} collective-permute-done((bf16[384,128]{1,0:T(8,128)(2,1)S(1)}, bf16[384,128]{1,0:T(8,128)(2,1)S(1)}, u32[]{:S(2)}, u32[]{:S(2)}) %collective-permute-start.22) | collective-permute-done | bytes 98336 | tf_op jit(solution)/shard_map/ppermute | solution.py:387
  189.0 3.0 %collective-permute-done.45 = bf16[208,768]{1,0:T(8,128)(2,1)} collective-permute-done((bf16[208,768]{1,0:T(8,128)(2,1)}, bf16[208,768]{1,0:T(8,128)(2,1)}, u32[]{:S(2)}, u32[]{:S(2)}) %collective-permute-start.45) | collective-permute-done | bytes 319520 | tf_op jit(solution)/shard_map/ppermute | solution.py:396
  198.1 2.5 collective-permute-start.38
  201.2 2.8 %collective-permute-done.47.refs_1_ = bf16[208,768]{1,0:T(8,128)(2,1)S(1)} collective-permute-done((bf16[208,768]{1,0:T(8,128)(2,1)S(1)}, bf16[208,768]{1,0:T(8,128)(2,1)S(1)}, u32[]{:S(2)}, u32[]{:S(2)}) %collective-permute-start.47) | collective-permute-done | bytes 319520 | tf_op jit(solution)/shard_map/ppermute | solution.py:396
  206.5 6.8 %collective-permute-done.49.refs_3_ = bf16[208,768]{1,0:T(8,128)(2,1)S(1)} collective-permute-done((bf16[208,768]{1,0:T(8,128)(2,1)S(1)}, bf16[208,768]{1,0:T(8,128)(2,1)S(1)}, u32[]{:S(2)}, u32[]{:S(2)}) %collective-permute-start.49) | collective-permute-done | bytes 319520 | tf_op jit(solution)/shard_map/ppermute | solution.py:396
  213.5 3.4 %collective-permute-done.38 = bf16[112,768]{1,0:T(8,128)(2,1)S(1)} collective-permute-done((bf16[112,768]{1,0:T(8,128)(2,1)S(1)}, bf16[112,768]{1,0:T(8,128)(2,1)S(1)}, u32[]{:S(2)}, u32[]{:S(2)}) %collective-permute-start.38) | collective-permute-done | bytes 172064 | tf_op jit(solution)/shard_map/ppermute | solution.py:396
  223.7 2.9 %collective-permute-done.39.refs_1_ = bf16[112,768]{1,0:T(8,128)(2,1)S(1)} collective-permute-done((bf16[112,768]{1,0:T(8,128)(2,1)S(1)}, bf16[112,768]{1,0:T(8,128)(2,1)S(1)}, u32[]{:S(2)}, u32[]{:S(2)}) %collective-permute-start.39) | collective-permute-done | bytes 172064 | tf_op jit(solution)/shard_map/ppermute | solution.py:396
  228.2 2.9 %collective-permute-done.41.refs_3_ = bf16[112,768]{1,0:T(8,128)(2,1)S(1)} collective-permute-done((bf16[112,768]{1,0:T(8,128)(2,1)S(1)}, bf16[112,768]{1,0:T(8,128)(2,1)S(1)}, u32[]{:S(2)}, u32[]{:S(2)}) %collective-permute-start.41) | collective-permute-done | bytes 172064 | tf_op jit(solution)/shard_map/ppermute | solution.py:396
  231.9 3.2 %collective-permute-start.23 = (bf16[128,768]{1,0:T(8,128)(2,1)S(1)}, bf16[128,768]{1,0:T(8,128)(2,1)S(1)}, u32[]{:S(2)}, u32[]{:S(2)}) collective-permute-start(bf16[128,768]{1,0:T(8,128)(2,1)S(1)} %copy-done.107), channel_id=1, source_target_pairs={{0,3},{1,0},{2,1},{3,2},{4,7},{5,4},{6,5},{7,6},{8,11},{9,8},{10,9... | collective-permute-start | bytes 589832 | tf_op jit(solution)/shard_map/ppermute | solution.py:384
  235.1 5.8 %collective-permute-done.31 = bf16[128,768]{1,0:T(8,128)(2,1)S(1)} collective-permute-done((bf16[128,768]{1,0:T(8,128)(2,1)S(1)}, bf16[128,768]{1,0:T(8,128)(2,1)S(1)}, u32[]{:S(2)}, u32[]{:S(2)}) %collective-permute-start.31) | collective-permute-done | bytes 196640 | tf_op jit(solution)/shard_map/ppermute | solution.py:384
  240.9 7.5 %collective-permute-done.27 = bf16[128,768]{1,0:T(8,128)(2,1)S(1)} collective-permute-done((bf16[128,768]{1,0:T(8,128)(2,1)S(1)}, bf16[128,768]{1,0:T(8,128)(2,1)S(1)}, u32[]{:S(2)}, u32[]{:S(2)}) %collective-permute-start.27) | collective-permute-done | bytes 196640 | tf_op jit(solution)/shard_map/ppermute | solution.py:384
  248.6 4.4 %collective-permute-start.32 = (bf16[128,768]{1,0:T(8,128)(2,1)S(1)}, bf16[128,768]{1,0:T(8,128)(2,1)S(1)}, u32[]{:S(2)}, u32[]{:S(2)}) collective-permute-start(bf16[128,768]{1,0:T(8,128)(2,1)S(1)} %add_convert_fusion.3.refs_0_), channel_id=1, source_target_pairs={{0,1},{1,2},{2,3},{3,0},{4,5},{5,6},{6,7},{7,4},{8,9},{9,10},{10,1... | collective-permute-start | bytes 589832 | tf_op jit(solution)/shard_map/ppermute | solution.py:384
  258.2 6.7 %collective-permute-done.33.refs_2_ = bf16[128,768]{1,0:T(8,128)(2,1)S(1)} collective-permute-done((bf16[128,768]{1,0:T(8,128)(2,1)S(1)}, bf16[128,768]{1,0:T(8,128)(2,1)S(1)}, u32[]{:S(2)}, u32[]{:S(2)}) %collective-permute-start.33) | collective-permute-done | bytes 196640 | tf_op jit(solution)/shard_map/ppermute | solution.py:384
  277.7 2.9 %ffn_grads_out.1 = (f32[768,768]{1,0:T(8,128)}, f32[768,768]{1,0:T(8,128)}, f32[16,768]{1,0:T(8,128)S(1)}) custom-call(s32[3]{0:T(128)S(1)} %copy-done.86, bf16[832,768]{1,0:T(8,128)(2,1)S(1)} %bitcast.67, bf16[832,768]{1,0:T(8,128)(2,1)S(1)} %collective-permute-done.50.other), custom_call_target="tpu_custom_call" | custom-call | bytes 8388608 | tf_op jit(solution)/shard_map/ffn_grads_out/pallas_call | solution.py:616
  (385 shorter events, 124.2 us)
Async XLA Ops:
  4.6 12.1 %collective-permute-start.4 = (bf16[512,384]{1,0:T(8,128)(2,1)S(1)}, bf16[512,384]{1,0:T(8,128)(2,1)S(1)}, u32[]{:S(2)}, u32[]{:S(2)}) collective-permute-start(bf16[512,384]{1,0:T(8,128)(2,1)S(1)} %get-tuple-element.114.refs_0_), channel_id=1, source_target_pairs={{0,8},{4,12},{8,0},{12,4},{1,9},{5,13},{9,1},{13,5},{2,10},{6,14},... | collective-permute-start | bytes 1179656 | tf_op jit(solution)/shard_map/ppermute | solution.py:387
  7.6 15.7 %collective-permute-start.3 = (bf16[512,384]{1,0:T(8,128)(2,1)S(1)}, bf16[512,384]{1,0:T(8,128)(2,1)S(1)}, u32[]{:S(2)}, u32[]{:S(2)}) collective-permute-start(bf16[512,384]{1,0:T(8,128)(2,1)S(1)} %get-tuple-element.114.refs_0_), channel_id=1, source_target_pairs={{0,4},{4,0},{8,12},{12,8},{1,5},{5,1},{9,13},{13,9},{2,6},{6,2},{1... | collective-permute-start | bytes 1179656 | tf_op jit(solution)/shard_map/ppermute | solution.py:387
  16.7 15.2 %collective-permute-start = (bf16[192,768]{1,0:T(8,128)(2,1)}, bf16[192,768]{1,0:T(8,128)(2,1)}, u32[]{:S(2)}, u32[]{:S(2)}) collective-permute-start(bf16[192,768]{1,0:T(8,128)(2,1)} %w_out.7), channel_id=1, source_target_pairs={{0,1},{1,2},{2,3},{3,0},{4,5},{5,6},{6,7},{7,4},{8,9},{9,10},{10,1... | collective-permute-start | bytes 884744 | tf_op jit(solution)/shard_map/ppermute | solution.py:384
  18.5 23.0 %collective-permute-start.1 = (bf16[192,768]{1,0:T(8,128)(2,1)}, bf16[192,768]{1,0:T(8,128)(2,1)}, u32[]{:S(2)}, u32[]{:S(2)}) collective-permute-start(bf16[192,768]{1,0:T(8,128)(2,1)} %w_out.7), channel_id=1, source_target_pairs={{0,2},{1,3},{2,0},{3,1},{4,6},{5,7},{6,4},{7,5},{8,10},{9,11},{10,... | collective-permute-start | bytes 884744 | tf_op jit(solution)/shard_map/ppermute | solution.py:384
  21.1 20.4 %collective-permute-start.2 = (bf16[192,768]{1,0:T(8,128)(2,1)}, bf16[192,768]{1,0:T(8,128)(2,1)}, u32[]{:S(2)}, u32[]{:S(2)}) collective-permute-start(bf16[192,768]{1,0:T(8,128)(2,1)} %w_out.7), channel_id=1, source_target_pairs={{0,3},{1,0},{2,1},{3,2},{4,7},{5,4},{6,5},{7,6},{8,11},{9,8},{10,9... | collective-permute-start | bytes 884744 | tf_op jit(solution)/shard_map/ppermute | solution.py:384
  30.9 14.8 %collective-permute-start.6 = (bf16[768,128]{1,0:T(8,128)(2,1)S(1)}, bf16[768,128]{1,0:T(8,128)(2,1)S(1)}, u32[]{:S(2)}, u32[]{:S(2)}) collective-permute-start(bf16[768,128]{1,0:T(8,128)(2,1)S(1)} %get-tuple-element.115.refs_0_.hp), channel_id=1, source_target_pairs={{0,1},{1,2},{2,3},{3,0},{4,5},{5,6},{6,7},{7,4},{8,9},{9,10},{10,1... | collective-permute-start | bytes 589832 | tf_op jit(solution)/shard_map/ppermute | solution.py:384
  31.6 28.6 %collective-permute-start.7 = (bf16[768,128]{1,0:T(8,128)(2,1)S(1)}, bf16[768,128]{1,0:T(8,128)(2,1)S(1)}, u32[]{:S(2)}, u32[]{:S(2)}) collective-permute-start(bf16[768,128]{1,0:T(8,128)(2,1)S(1)} %get-tuple-element.115.refs_0_.hp), channel_id=1, source_target_pairs={{0,2},{1,3},{2,0},{3,1},{4,6},{5,7},{6,4},{7,5},{8,10},{9,11},{10,... | collective-permute-start | bytes 589832 | tf_op jit(solution)/shard_map/ppermute | solution.py:384
  31.9 28.3 %collective-permute-start.8 = (bf16[768,128]{1,0:T(8,128)(2,1)S(1)}, bf16[768,128]{1,0:T(8,128)(2,1)S(1)}, u32[]{:S(2)}, u32[]{:S(2)}) collective-permute-start(bf16[768,128]{1,0:T(8,128)(2,1)S(1)} %get-tuple-element.115.refs_0_.hp), channel_id=1, source_target_pairs={{0,3},{1,0},{2,1},{3,2},{4,7},{5,4},{6,5},{7,6},{8,11},{9,8},{10,9... | collective-permute-start | bytes 589832 | tf_op jit(solution)/shard_map/ppermute | solution.py:384
  65.4 24.3 %collective-permute-start.11 = (bf16[128,768]{1,0:T(8,128)(2,1)}, bf16[128,768]{1,0:T(8,128)(2,1)}, u32[]{:S(2)}, u32[]{:S(2)}) collective-permute-start(bf16[128,768]{1,0:T(8,128)(2,1)} %get-tuple-element.121), channel_id=1, source_target_pairs={{0,1},{1,2},{2,3},{3,0},{4,5},{5,6},{6,7},{7,4},{8,9},{9,10},{10,1... | collective-permute-start | bytes 589832 | tf_op jit(solution)/shard_map/ppermute | solution.py:384
  74.6 15.1 %collective-permute-start.10 = (bf16[128,768]{1,0:T(8,128)(2,1)}, bf16[128,768]{1,0:T(8,128)(2,1)}, u32[]{:S(2)}, u32[]{:S(2)}) collective-permute-start(bf16[128,768]{1,0:T(8,128)(2,1)} %get-tuple-element.120), channel_id=1, source_target_pairs={{0,2},{1,3},{2,0},{3,1},{4,6},{5,7},{6,4},{7,5},{8,10},{9,11},{10,... | collective-permute-start | bytes 589832 | tf_op jit(solution)/shard_map/ppermute | solution.py:384
  93.1 25.1 %collective-permute-start.13 = (bf16[128,768]{1,0:T(8,128)(2,1)S(1)}, bf16[128,768]{1,0:T(8,128)(2,1)S(1)}, u32[]{:S(2)}, u32[]{:S(2)}) collective-permute-start(bf16[128,768]{1,0:T(8,128)(2,1)S(1)} %add_convert_fusion.5.ffn), channel_id=1, source_target_pairs={{0,2},{1,3},{2,0},{3,1},{4,6},{5,7},{6,4},{7,5},{8,10},{9,11},{10,... | collective-permute-start | bytes 589832 | tf_op jit(solution)/shard_map/ppermute | solution.py:384
  93.9 26.3 %collective-permute-start.12 = (bf16[128,768]{1,0:T(8,128)(2,1)S(1)}, bf16[128,768]{1,0:T(8,128)(2,1)S(1)}, u32[]{:S(2)}, u32[]{:S(2)}) collective-permute-start(bf16[128,768]{1,0:T(8,128)(2,1)S(1)} %add_convert_fusion.5.ffn), channel_id=1, source_target_pairs={{0,1},{1,2},{2,3},{3,0},{4,5},{5,6},{6,7},{7,4},{8,9},{9,10},{10,1... | collective-permute-start | bytes 589832 | tf_op jit(solution)/shard_map/ppermute | solution.py:384
  101.9 25.1 %collective-permute-start.17 = (bf16[128,768]{1,0:T(8,128)(2,1)S(1)}, bf16[128,768]{1,0:T(8,128)(2,1)S(1)}, u32[]{:S(2)}, u32[]{:S(2)}) collective-permute-start(bf16[128,768]{1,0:T(8,128)(2,1)S(1)} %get-tuple-element.135), channel_id=1, source_target_pairs={{0,1},{1,2},{2,3},{3,0},{4,5},{5,6},{6,7},{7,4},{8,9},{9,10},{10,1... | collective-permute-start | bytes 589832 | tf_op jit(solution)/shard_map/ppermute | solution.py:384
  131.3 16.3 %collective-permute-start.28 = (bf16[128,768]{1,0:T(8,128)(2,1)}, bf16[128,768]{1,0:T(8,128)(2,1)}, u32[]{:S(2)}, u32[]{:S(2)}) collective-permute-start(bf16[128,768]{1,0:T(8,128)(2,1)} %add_convert_fusion.4.dh), channel_id=1, source_target_pairs={{0,3},{1,0},{2,1},{3,2},{4,7},{5,4},{6,5},{7,6},{8,11},{9,8},{10,9... | collective-permute-start | bytes 589832 | tf_op jit(solution)/shard_map/ppermute | solution.py:384
  142.3 14.4 %collective-permute-start.18 = (bf16[2,384,128]{2,1,0:T(8,128)(2,1)}, bf16[2,384,128]{2,1,0:T(8,128)(2,1)}, u32[]{:S(2)}, u32[]{:S(2)}) collective-permute-start(bf16[2,384,128]{2,1,0:T(8,128)(2,1)} %get-tuple-element.141), channel_id=1, source_target_pairs={{0,4},{4,0},{8,12},{12,8},{1,5},{5,1},{9,13},{13,9},{2,6},{6,2},{1... | collective-permute-start | bytes 589832 | tf_op jit(solution)/shard_map/ppermute | solution.py:387
  147.1 26.9 %collective-permute-start.43 = (bf16[832,768]{1,0:T(8,128)(2,1)}, bf16[832,768]{1,0:T(8,128)(2,1)}, u32[]{:S(2)}, u32[]{:S(2)}) collective-permute-start(bf16[832,768]{1,0:T(8,128)(2,1)} %get-tuple-element.207), channel_id=1, source_target_pairs={{0,4},{4,0},{8,12},{12,8},{1,5},{5,1},{9,13},{13,9},{2,6},{6,2},{1... | collective-permute-start | bytes 3833864 | tf_op jit(solution)/shard_map/ppermute | solution.py:387
  147.1 14.7 %collective-permute-start.24 = (bf16[128,768]{1,0:T(8,128)(2,1)}, bf16[128,768]{1,0:T(8,128)(2,1)S(1)}, u32[]{:S(2)}, u32[]{:S(2)}) collective-permute-start(bf16[128,768]{1,0:T(8,128)(2,1)} %add_convert_fusion.4.dh), channel_id=1, source_target_pairs={{0,2},{1,3},{2,0},{3,1},{4,6},{5,7},{6,4},{7,5},{8,10},{9,11},{10,... | collective-permute-start | bytes 589832 | tf_op jit(solution)/shard_map/ppermute | solution.py:384
  147.1 17.9 %collective-permute-start.20 = (bf16[128,768]{1,0:T(8,128)(2,1)}, bf16[128,768]{1,0:T(8,128)(2,1)S(1)}, u32[]{:S(2)}, u32[]{:S(2)}) collective-permute-start(bf16[128,768]{1,0:T(8,128)(2,1)} %add_convert_fusion.4.dh), channel_id=1, source_target_pairs={{0,1},{1,2},{2,3},{3,0},{4,5},{5,6},{6,7},{7,4},{8,9},{9,10},{10,1... | collective-permute-start | bytes 589832 | tf_op jit(solution)/shard_map/ppermute | solution.py:384
  156.7 13.4 %collective-permute-start.29 = (bf16[2,384,128]{2,1,0:T(8,128)(2,1)S(1)}, bf16[2,384,128]{2,1,0:T(8,128)(2,1)S(1)}, u32[]{:S(2)}, u32[]{:S(2)}) collective-permute-start(bf16[2,384,128]{2,1,0:T(8,128)(2,1)S(1)} %get-tuple-element.160), channel_id=1, source_target_pairs={{0,4},{4,0},{8,12},{12,8},{1,5},{5,1},{9,13},{13,9},{2,6},{6,2},{1... | collective-permute-start | bytes 589832 | tf_op jit(solution)/shard_map/ppermute | solution.py:387
  172.3 13.2 %collective-permute-start.22 = (bf16[384,128]{1,0:T(8,128)(2,1)S(1)}, bf16[384,128]{1,0:T(8,128)(2,1)S(1)}, u32[]{:S(2)}, u32[]{:S(2)}) collective-permute-start(bf16[384,128]{1,0:T(8,128)(2,1)S(1)} %fusion.13), channel_id=1, source_target_pairs={{0,8},{4,12},{8,0},{12,4},{1,9},{5,13},{9,1},{13,5},{2,10},{6,14},... | collective-permute-start | bytes 294920 | tf_op jit(solution)/shard_map/ppermute | solution.py:387
  176.2 12.9 %collective-permute-start.46 = (bf16[208,768]{1,0:T(8,128)(2,1)}, bf16[208,768]{1,0:T(8,128)(2,1)S(1)}, u32[]{:S(2)}, u32[]{:S(2)}) collective-permute-start(bf16[208,768]{1,0:T(8,128)(2,1)} %get-tuple-element.236), channel_id=1, source_target_pairs={{0,24},{4,28},{8,16},{12,20},{16,8},{20,12},{24,0},{28,4},{1,25},{... | collective-permute-start | bytes 958472 | tf_op jit(solution)/shard_map/ppermute | solution.py:396
  177.6 14.5 %collective-permute-start.45 = (bf16[208,768]{1,0:T(8,128)(2,1)}, bf16[208,768]{1,0:T(8,128)(2,1)}, u32[]{:S(2)}, u32[]{:S(2)}) collective-permute-start(bf16[208,768]{1,0:T(8,128)(2,1)} %get-tuple-element.237), channel_id=1, source_target_pairs={{0,16},{4,20},{8,24},{12,28},{16,0},{20,4},{24,8},{28,12},{1,17},{... | collective-permute-start | bytes 958472 | tf_op jit(solution)/shard_map/ppermute | solution.py:396
  178.1 14.9 %collective-permute-start.44 = (bf16[208,768]{1,0:T(8,128)(2,1)}, bf16[208,768]{1,0:T(8,128)(2,1)}, u32[]{:S(2)}, u32[]{:S(2)}) collective-permute-start(bf16[208,768]{1,0:T(8,128)(2,1)} %get-tuple-element.235), channel_id=1, source_target_pairs={{0,8},{4,12},{8,0},{12,4},{16,24},{20,28},{24,16},{28,20},{1,9},{5... | collective-permute-start | bytes 958472 | tf_op jit(solution)/shard_map/ppermute | solution.py:396
  197.5 15.8 %collective-permute-start.49 = (bf16[208,768]{1,0:T(8,128)(2,1)S(1)}, bf16[208,768]{1,0:T(8,128)(2,1)S(1)}, u32[]{:S(2)}, u32[]{:S(2)}) collective-permute-start(bf16[208,768]{1,0:T(8,128)(2,1)S(1)} %fusion.2.refs_0_), channel_id=1, source_target_pairs={{0,24},{4,28},{8,16},{12,20},{16,8},{20,12},{24,0},{28,4},{1,25},{... | collective-permute-start | bytes 958472 | tf_op jit(solution)/shard_map/ppermute | solution.py:396
  198.1 18.8 %collective-permute-start.38 = (bf16[112,768]{1,0:T(8,128)(2,1)S(1)}, bf16[112,768]{1,0:T(8,128)(2,1)S(1)}, u32[]{:S(2)}, u32[]{:S(2)}) collective-permute-start(bf16[112,768]{1,0:T(8,128)(2,1)S(1)} %get-tuple-element.239), channel_id=1, source_target_pairs={{0,24},{4,28},{8,16},{12,20},{16,8},{20,12},{24,0},{28,4},{1,25},{... | collective-permute-start | bytes 516104 | tf_op jit(solution)/shard_map/ppermute | solution.py:396
  200.7 18.1 %collective-permute-start.37 = (bf16[112,768]{1,0:T(8,128)(2,1)S(1)}, bf16[112,768]{1,0:T(8,128)(2,1)S(1)}, u32[]{:S(2)}, u32[]{:S(2)}) collective-permute-start(bf16[112,768]{1,0:T(8,128)(2,1)S(1)} %get-tuple-element.240), channel_id=1, source_target_pairs={{0,16},{4,20},{8,24},{12,28},{16,0},{20,4},{24,8},{28,12},{1,17},{... | collective-permute-start | bytes 516104 | tf_op jit(solution)/shard_map/ppermute | solution.py:396
  204.0 15.1 %collective-permute-start.36 = (bf16[112,768]{1,0:T(8,128)(2,1)S(1)}, bf16[112,768]{1,0:T(8,128)(2,1)S(1)}, u32[]{:S(2)}, u32[]{:S(2)}) collective-permute-start(bf16[112,768]{1,0:T(8,128)(2,1)S(1)} %get-tuple-element.238), channel_id=1, source_target_pairs={{0,8},{4,12},{8,0},{12,4},{16,24},{20,28},{24,16},{28,20},{1,9},{5... | collective-permute-start | bytes 516104 | tf_op jit(solution)/shard_map/ppermute | solution.py:396
  213.5 64.2 %collective-permute-start.50 = (bf16[832,768]{1,0:T(8,128)(2,1)S(1)}, bf16[832,768]{1,0:T(8,128)(2,1)S(1)}, u32[]{:S(2)}, u32[]{:S(2)}) collective-permute-start(bf16[832,768]{1,0:T(8,128)(2,1)S(1)} %bitcast.66), channel_id=1, source_target_pairs={{0,4},{4,0},{8,12},{12,8},{1,5},{5,1},{9,13},{13,9},{2,6},{6,2},{1... | collective-permute-start | bytes 3833864 | tf_op jit(solution)/shard_map/ppermute | solution.py:387
  231.1 35.7 %collective-permute-start.42 = (bf16[448,768]{1,0:T(8,128)(2,1)S(1)}, bf16[448,768]{1,0:T(8,128)(2,1)S(1)}, u32[]{:S(2)}, u32[]{:S(2)}) collective-permute-start(bf16[448,768]{1,0:T(8,128)(2,1)S(1)} %bitcast.68), channel_id=1, source_target_pairs={{0,4},{4,0},{8,12},{12,8},{1,5},{5,1},{9,13},{13,9},{2,6},{6,2},{1... | collective-permute-start | bytes 2064392 | tf_op jit(solution)/shard_map/ppermute | solution.py:387
  231.3 17.1 %collective-permute-start.27 = (bf16[128,768]{1,0:T(8,128)(2,1)S(1)}, bf16[128,768]{1,0:T(8,128)(2,1)S(1)}, u32[]{:S(2)}, u32[]{:S(2)}) collective-permute-start(bf16[128,768]{1,0:T(8,128)(2,1)S(1)} %copy-done.101), channel_id=1, source_target_pairs={{0,2},{1,3},{2,0},{3,1},{4,6},{5,7},{6,4},{7,5},{8,10},{9,11},{10,... | collective-permute-start | bytes 589832 | tf_op jit(solution)/shard_map/ppermute | solution.py:384
  231.9 16.5 %collective-permute-start.23 = (bf16[128,768]{1,0:T(8,128)(2,1)S(1)}, bf16[128,768]{1,0:T(8,128)(2,1)S(1)}, u32[]{:S(2)}, u32[]{:S(2)}) collective-permute-start(bf16[128,768]{1,0:T(8,128)(2,1)S(1)} %copy-done.107), channel_id=1, source_target_pairs={{0,3},{1,0},{2,1},{3,2},{4,7},{5,4},{6,5},{7,6},{8,11},{9,8},{10,9... | collective-permute-start | bytes 589832 | tf_op jit(solution)/shard_map/ppermute | solution.py:384
  252.9 12.4 %collective-permute-start.34 = (bf16[128,768]{1,0:T(8,128)(2,1)S(1)}, bf16[128,768]{1,0:T(8,128)(2,1)S(1)}, u32[]{:S(2)}, u32[]{:S(2)}) collective-permute-start(bf16[128,768]{1,0:T(8,128)(2,1)S(1)} %add_convert_fusion.3.refs_0_), channel_id=1, source_target_pairs={{0,3},{1,0},{2,1},{3,2},{4,7},{5,4},{6,5},{7,6},{8,11},{9,8},{10,9... | collective-permute-start | bytes 589832 | tf_op jit(solution)/shard_map/ppermute | solution.py:384
  (145 other events, 1398.2 us)

commit v2 on v1

v2 whole, which is shorter than its diff:
```python
import functools

import jax
import jax.numpy as jnp
from jax import lax
from jax.experimental import pallas as pl
from jax.experimental.pallas import tpu as pltpu
from jax.sharding import PartitionSpec as P

HEAD_DIM = 64
BLOCK = 128
LANES = 128
SCALE = HEAD_DIM**-0.5
EPS = 1e-12
f32 = jnp.float32
bf16 = jnp.bfloat16
i32 = jnp.int32
MIB = 1 << 20


def nn(a, b):
    return lax.dot_general(a, b, (((1,), (0,)), ((), ())), preferred_element_type=f32)


def nt(a, b):
    return lax.dot_general(a, b, (((1,), (1,)), ((), ())), preferred_element_type=f32)


def tn(a, b):
    return lax.dot_general(a, b, (((0,), (0,)), ((), ())), preferred_element_type=f32)


def mean(v):
    return jnp.mean(v, axis=-1, keepdims=True)


def col_sum(v):
    return jnp.sum(v, axis=0, keepdims=True)


def rows8(*rows):
    width = rows[0].shape[1]
    pad = jnp.zeros((8 - len(rows), width), f32)
    return jnp.concatenate(rows + (pad,), axis=0)


def shape(dims, dtype):
    return jax.ShapeDtypeStruct(dims, dtype)


def near(dims, dtype):
    return pltpu.VMEM(dims, dtype)


SMEM = pl.BlockSpec(memory_space=pltpu.SMEM)
VMEM = pl.BlockSpec(memory_space=pltpu.VMEM)


def cost(flops, nbytes, trans=0):
    return pl.CostEstimate(flops=int(flops), bytes_accessed=int(nbytes), transcendentals=int(trans))


def call(kernel, outs, name, args, scalars=0, vmem=16, scratch=(), estimate=None):
    return pl.pallas_call(
        kernel,
        out_shape=outs,
        in_specs=[SMEM] * scalars + [VMEM] * (len(args) - scalars),
        out_specs=jax.tree.map(lambda _: VMEM, outs),
        scratch_shapes=list(scratch),
        compiler_params=pltpu.CompilerParams(vmem_limit_bytes=vmem * MIB),
        cost_estimate=estimate,
        name=name,
    )(*args)


def chunk_of(ref, c, rows):
    return ref[pl.ds(pl.multiple_of(c * rows, rows), rows), :]


def kv_kernel(tok, wk_t, wv_t, bv, kv, wkv_t):
    heads = wk_t.shape[0] // HEAD_DIM
    rows, bias = [], []
    for h in range(heads):
        part = slice(h * HEAD_DIM, (h + 1) * HEAD_DIM)
        rows += [wk_t[part, :], wv_t[part, :]]
        bias += [jnp.zeros((1, HEAD_DIM), f32), bv[:, part]]
    both = jnp.concatenate(rows, axis=0)
    wkv_t[...] = both
    kv[...] = (nt(tok[...], both) + jnp.concatenate(bias, axis=1)).astype(bf16)


def q_kernel(tok, wq_t, bq, q):
    heads = wq_t.shape[0] // HEAD_DIM
    full = (nt(tok[...], wq_t[...]) + bq[...]).astype(bf16) * jnp.asarray(SCALE, bf16)
    zero = jnp.zeros((full.shape[0], HEAD_DIM), bf16)
    cols = []
    for h in range(heads):
        cols += [full[:, h * HEAD_DIM : (h + 1) * HEAD_DIM], zero]
    q[...] = jnp.concatenate(cols, axis=1)


def attend_kernel(n_blk, at, bucket, lens, q, *refs):
    kvs, hp, probs = refs[:n_blk], refs[n_blk], refs[n_blk + 1]
    rows = bucket.shape[0]
    heads = q.shape[1] // LANES
    b = at[2]
    q_at = lax.broadcasted_iota(i32, (BLOCK, 1), 0)
    k_at = lax.broadcasted_iota(i32, (1, BLOCK), 1)
    for r in range(rows):
        bk = bucket[r]
        size = BLOCK << bk
        slot = b >> bk
        limit = lens[r, slot]
        q_in = jnp.where(q_at + (b * BLOCK - slot * size) < limit, 1, 0)
        k_in = []
        for j in range(n_blk):
            kb = b ^ j
            k_slot = kb >> bk
            inside = jnp.where(k_at + (kb * BLOCK - k_slot * size) < limit, 1, 0)
            k_in.append(jnp.where(k_slot == slot, inside, 2))
        allowed = q_in == jnp.concatenate(k_in, axis=1)
        here = slice(r * BLOCK, (r + 1) * BLOCK)
        outs = []
        for h in range(heads):
            lanes = slice(h * LANES, (h + 1) * LANES)
            kvh = jnp.concatenate([kv[here, lanes] for kv in kvs], axis=0)
            scores = jnp.where(allowed, nt(q[here, lanes], kvh), -1e30)
            weights = jnp.exp(scores - jnp.max(scores, axis=-1, keepdims=True))
            total = jnp.sum(weights, axis=-1, keepdims=True)
            p = (weights / total).astype(bf16)
            probs[(r * heads + h) * BLOCK : (r * heads + h + 1) * BLOCK, :] = p
            outs.append(nn(p, kvh)[:, HEAD_DIM:].astype(bf16))
        base = r * (BLOCK + HEAD_DIM)
        hp[base : base + BLOCK, :] = jnp.concatenate(outs[:2], axis=1)
        hp[base + BLOCK : base + BLOCK + HEAD_DIM, :] = jnp.concatenate(
            [outs[2][:HEAD_DIM], outs[2][HEAD_DIM:]], axis=1
        )


def unpack(h):
    odd = jnp.concatenate([h[BLOCK:, :HEAD_DIM], h[BLOCK:, HEAD_DIM:]], axis=0)
    return jnp.concatenate([h[:BLOCK, :], odd], axis=1)


def ffn_kernel(n, k, at, tok, b_out, g1, b1, w_in, b_in, w_outer, *refs):
    hps, wouts = refs[:n], refs[n : 2 * n]
    part, n1_out, s1_out, low_out, act_out, slope_out, held = refs[2 * n :]
    z = at[0]
    c = lax.rem(z - k + n, n)
    for i in range(n):
        held[lax.rem(z - i + n, n)] = nn(unpack(chunk_of(hps[i], c, BLOCK + HEAD_DIM)), wouts[i][...])
    attn = held[0]
    for j in range(1, n):
        attn = attn + held[j]
    resid = chunk_of(tok, c, BLOCK).astype(f32) + (attn + b_out[...])
    center = resid - mean(resid)
    s1 = lax.rsqrt(mean(center * center) + EPS)
    n1 = center * s1
    low = (n1 * g1[...] + b1[...]).astype(bf16)
    inner = nn(low, w_in[...]) + b_in[...]
    cdf = 0.5 * (1.0 + lax.erf(inner * (0.5**0.5)))
    act = (inner * cdf).astype(bf16)
    slope = cdf + inner * (0.3989422804014327 * jnp.exp(-0.5 * inner * inner))
    part[...] = nn(act, w_outer[...]).astype(bf16)
    n1_out[...] = n1
    s1_out[...] = jnp.broadcast_to(s1, s1_out.shape)
    low_out[...] = low
    act_out[...] = act
    slope_out[...] = slope.astype(bf16)


def ffn_back_kernel(
    n, k, at, cot, n1, slope, ffn, g1, b1, b_outer, g2, b2, w_in, w_outer,
    out, dres2_out, dffn_out, dinner_out, part, sums,
):
    hidden = n1[...] * g1[...] + b1[...]
    resid = hidden + (ffn[...].astype(f32) + b_outer[...])
    center = resid - mean(resid)
    s2 = lax.rsqrt(mean(center * center) + EPS)
    n2 = center * s2
    out[...] = (n2 * g2[...] + b2[...]).astype(bf16)
    ct = chunk_of(cot, lax.rem(at[0] - k + n, n), BLOCK).astype(f32)
    dn = ct * g2[...]
    dres2 = s2 * (dn - mean(dn) - n2 * mean(dn * n2))
    dffn = dres2.astype(bf16)
    dinner = (nt(dffn, w_outer[...]) * slope[...].astype(f32)).astype(bf16)
    part[...] = nt(dinner, w_in[...]).astype(bf16)
    dres2_out[...] = dres2
    dffn_out[...] = dffn
    dinner_out[...] = dinner
    sums[...] = rows8(
        col_sum(ct * n2), col_sum(ct), col_sum(dffn.astype(f32)), col_sum(dinner.astype(f32))
    )


def attend_back_kernel(n_blk, n, k, at, dh, dres2, n1, s1, g1, w_out, q, probs, *refs):
    kvs = refs[:n_blk]
    dres1_out, dattn_out, sums, dq_out, send, keep = refs[n_blk:]
    heads = q.shape[1] // LANES
    c = lax.rem(at[0] - k + n, n)
    here = pl.ds(pl.multiple_of(c * BLOCK, BLOCK), BLOCK)
    dhidden = dh[...].astype(f32) + dres2[...]
    norm = n1[...]
    dn = dhidden * g1[...]
    dres1 = s1[:, :1] * (dn - mean(dn) - norm * mean(dn * norm))
    dattn = dres1.astype(bf16)
    dres1_out[...] = dres1
    dattn_out[...] = dattn
    sums[...] = rows8(col_sum(dhidden * norm), col_sum(dhidden), col_sum(dattn.astype(f32)))
    zero = jnp.zeros((HEAD_DIM, w_out.shape[1]), bf16)
    spread = []
    for h in range(heads):
        spread += [zero, w_out[h * HEAD_DIM : (h + 1) * HEAD_DIM, :]]
    dheads = nt(dattn, jnp.concatenate(spread, axis=0)).astype(bf16)
    dqs = []
    for h in range(heads):
        lanes = slice(h * LANES, (h + 1) * LANES)
        kvh = jnp.concatenate([kv[here, lanes] for kv in kvs], axis=0)
        p = chunk_of(probs, c * heads + h, BLOCK)
        pf = p.astype(f32)
        dp = nt(dheads[:, lanes], kvh)
        delta = jnp.sum(pf * dp, axis=-1, keepdims=True)
        ds = (pf * (dp - delta)).astype(bf16)
        dqs.append((nn(ds, kvh) * SCALE)[:, :HEAD_DIM].astype(bf16))
        left = jnp.concatenate([q[here, lanes], dheads[:, lanes]], axis=0)
        dkv = tn(left, jnp.concatenate([ds, p], axis=0)).astype(bf16)
        for j in range(n_blk):
            target = keep if j % 2 == 0 else send
            target[j // 2, lanes, :] = dkv[:, j * BLOCK : (j + 1) * BLOCK]
    dq_out[...] = jnp.concatenate(dqs, axis=1)


def input_kernel(dq, keep, recv, far, wq_t, wkv_t, part, dkv_t, sums):
    total = keep[0].astype(f32) + recv[0].astype(f32) + far[...].astype(f32)
    low_t = total.astype(bf16)
    low = low_t.T
    part[...] = (nn(dq[...], wq_t[...]) + nn(low, wkv_t[...])).astype(bf16)
    dkv_t[...] = low_t
    width = sums.shape[1]
    first = col_sum(dq[...].astype(f32))
    second = col_sum(low.astype(f32))
    sums[...] = rows8(
        jnp.concatenate([first, jnp.zeros((1, width - first.shape[1]), f32)], axis=1),
        jnp.concatenate([second, jnp.zeros((1, width - second.shape[1]), f32)], axis=1),
    )


def ordered_sum(n, z, refs, held):
    for k in range(n):
        held[lax.rem(z - k + n, n)] = refs[k][...]
    total = held[0]
    for j in range(1, n):
        total = total + held[j]
    return total


def pick(first, one, other):
    return jnp.where(first, one, other)


def ffn_grad_kernel(n, at, *refs):
    low, dinner, act, dffn, sums = (refs[i * n : (i + 1) * n] for i in range(5))
    keep, send, held = refs[5 * n :]
    first = at[1] == 0
    tail = ordered_sum(n, at[0], sums, held).astype(bf16)
    a = jnp.concatenate([pick(first, x[...], y[...]) for x, y in zip(low, act)], axis=0)
    b = jnp.concatenate([pick(first, x[...], y[...]) for x, y in zip(dinner, dffn)], axis=0)
    c = jnp.concatenate([pick(first, y[...], x[...]) for x, y in zip(low, act)], axis=0)
    d = jnp.concatenate([pick(first, y[...], x[...]) for x, y in zip(dinner, dffn)], axis=0)
    rows = a.shape[1]
    rest = keep.shape[0] - rows
    tail = jnp.concatenate([tail, jnp.zeros((rest - 8, tail.shape[1]), bf16)], axis=0)
    send[:rows, :] = tn(c, d).astype(bf16)
    send[rows:, :] = tail
    keep[:rows, :] = tn(a, b).astype(bf16)
    keep[rows:, :] = tail


def attend_grad_kernel(n, at, tok, hp, *refs):
    dattn, dq, dkv_t, sums1, sums2 = (refs[i * n : (i + 1) * n] for i in range(5))
    keep, send, held1, held2 = refs[5 * n :]
    z = at[0]
    first = at[1] == 0
    total1 = ordered_sum(n, z, sums1, held1)
    total2 = ordered_sum(n, z, sums2, held2)
    tail = jnp.concatenate([total1, total2], axis=0).astype(bf16)
    toks, heads = [], []
    for k in range(n):
        c = lax.rem(z - k + n, n)
        toks.append(chunk_of(tok, c, BLOCK))
        heads.append(unpack(chunk_of(hp, c, BLOCK + HEAD_DIM)))
    toks = jnp.concatenate(toks, axis=0)
    g_out = tn(jnp.concatenate(heads, axis=0), jnp.concatenate([x[...] for x in dattn], axis=0))
    g_q = tn(jnp.concatenate([x[...] for x in dq], axis=0), toks)
    g_kv = nn(jnp.concatenate([x[...] for x in dkv_t], axis=1), toks)
    one = jnp.concatenate([g_out, g_q], axis=0).astype(bf16)
    two = g_kv.astype(bf16)
    rows = two.shape[0]
    rest = keep.shape[0] - rows
    tail = jnp.concatenate([tail, jnp.zeros((rest - 16, tail.shape[1]), bf16)], axis=0)
    send[:rows, :] = pick(first, two, one)
    send[rows:, :] = tail
    keep[:rows, :] = pick(first, one, two)
    keep[rows:, :] = tail


def gather_kernel(m, at, *refs):
    out = refs[m]
    for s in range(m):
        out[at[3] ^ s] = refs[s][...]


def ffn_final_kernel(at, mine, other, g_in, g_outer, gain, bias, b_outer, b_in):
    first = at[1] == 0
    rows = g_in.shape[0]
    a = mine[...]
    b = other[...]
    g_in[...] = pick(first, a[:rows], b[:rows]).astype(f32)
    g_outer[...] = pick(first, b[:rows], a[:rows]).astype(f32)
    tail = pick(first, a[rows : rows + 16], b[rows : rows + 16]).astype(f32)
    for i, ref in enumerate((gain, bias, b_outer, b_in)):
        ref[...] = tail[i : i + 1]


def attend_final_kernel(at, mine, other, g_out, g_q, g_k, g_v, gain, bias, b_out, b_q, b_v):
    first = at[1] == 0
    width = g_out.shape[0]
    a = mine[...]
    b = other[...]
    one = pick(first, a, b).astype(f32)
    two = pick(first, b, a).astype(f32)
    g_out[...] = one[:width]
    g_q[...] = one[width : 2 * width]
    tail = one[2 * width : 2 * width + 16]
    values = []
    for h in range(width // HEAD_DIM):
        part = slice(h * HEAD_DIM, (h + 1) * HEAD_DIM)
        g_k[part, :] = two[h * LANES : h * LANES + HEAD_DIM]
        g_v[part, :] = two[h * LANES + HEAD_DIM : (h + 1) * LANES]
        values.append(tail[9:10, h * LANES + HEAD_DIM : (h + 1) * LANES])
    for i, ref in enumerate((gain, bias, b_out)):
        ref[...] = tail[i : i + 1]
    b_q[...] = tail[8:9, :width]
    b_v[...] = jnp.concatenate(values, axis=1)


def output_kernel(n, at, *refs):
    out = refs[n]
    for k in range(n):
        out[lax.rem(at[0] - k + n, n)] = refs[k][...]


def solution(mesh):
    n_dp = mesh.shape["dp"]
    n_blk = mesh.shape["blk"]
    n = mesh.shape["tensor"]
    half_blk = n_blk // 2
    m = n_dp * half_blk

    def shift(v, k):
        return lax.ppermute(v, "tensor", [(i, (i + k) % n) for i in range(n)])

    def flip(v, bit):
        return lax.ppermute(v, "blk", [(i, i ^ bit) for i in range(n_blk)])

    def flip_member(v, s):
        perm = []
        for dp in range(n_dp):
            for blk in range(n_blk):
                i = (dp * half_blk + blk // 2) ^ s
                to = (i // half_blk) * n_blk + (i % half_blk) * 2 + blk % 2
                perm.append((dp * n_blk + blk, to))
        return lax.ppermute(v, ("dp", "blk"), perm)

    def scatter_grads(keep, send, member):
        recv = flip(send, 1)
        rows = keep.shape[0] // m
        width = keep.shape[1]
        keep3 = keep.reshape(m, rows, width)
        recv3 = recv.reshape(m, rows, width)

        def piece(s):
            mine = lax.dynamic_index_in_dim(keep3, member ^ s, 0, keepdims=False)
            theirs = lax.dynamic_index_in_dim(recv3, member ^ s, 0, keepdims=False)
            return mine.astype(f32) + theirs.astype(f32)

        got = [flip_member(piece(s).astype(bf16), s) for s in range(1, m)]
        total = piece(0)
        for part in got:
            total = total + part.astype(f32)
        return total.astype(bf16)

    def gather_grads(total, at, name):
        rows, width = total.shape
        every = [total] + [flip_member(total, s) for s in range(1, m)]
        mine = call(
            functools.partial(gather_kernel, m),
            shape((m, rows, width), bf16),
            name,
            (at, *every),
            scalars=1,
        )
        return mine.reshape(m * rows, width)

    def body(
        tokens, bucket_ids, seq_lengths, w_query, b_query, w_key, w_value, b_value, w_out, b_out,
        norm1_gain, norm1_bias, w_inner, b_inner, w_outer, b_outer, norm2_gain, norm2_bias,
        cotangent,
    ):
        row_count, block, width = tokens.shape
        count = row_count * block
        local = w_query.shape[1]
        heads = local // HEAD_DIM
        lanes = heads * LANES
        hidden_units = w_inner.shape[1]
        blk = lax.axis_index("blk").astype(i32)
        z = lax.axis_index("tensor").astype(i32)
        member = (lax.axis_index("dp") * half_blk + blk // 2).astype(i32)
        at = jnp.stack([z, blk % 2, blk, member])
        tok = tokens.reshape(count, width)
        cot = cotangent.reshape(count, width)
        row = lambda v: v.reshape(1, -1)
        wq_t, wk_t, wv_t = w_query.T, w_key.T, w_value.T

        wouts = [w_out] + [shift(w_out, k) for k in range(1, n)]
        kv, wkv_t = call(
            kv_kernel,
            (near((count, lanes), bf16), near((lanes, width), bf16)),
            "kv_rows",
            (tok, wk_t, wv_t, row(b_value)),
            estimate=cost(4 * count * width * local, 3 * MIB),
        )
        kv_far = flip(kv, 2)
        kv_core = flip(kv, 1)
        q = call(
            q_kernel,
            near((count, lanes), bf16),
            "query_rows",
            (tok, wq_t, row(b_query)),
            estimate=cost(2 * count * width * local, 2 * MIB),
        )
        kv_both = flip(kv_far, 1)
        kvs = [kv, kv_core, kv_far, kv_both]
        q, *wouts = lax.optimization_barrier((q, *wouts))
        hp, probs = call(
            functools.partial(attend_kernel, n_blk),
            (
                near((row_count * (BLOCK + HEAD_DIM), LANES), bf16),
                near((row_count * heads * BLOCK, n_blk * BLOCK), bf16),
            ),
            "attend",
            (at, bucket_ids, seq_lengths, q, *kvs),
            scalars=3,
            estimate=cost(2e9, 4 * MIB),
        )
        hps = [hp] + [shift(hp, k) for k in range(1, n)]

        chunk = lambda w, dt: near((BLOCK, w), dt)
        order = [k for k in range(1, n)] + [0]

        def ffn(k):
            return call(
                functools.partial(ffn_kernel, n, k),
                (
                    chunk(width, bf16), chunk(width, f32), chunk(LANES, f32), chunk(width, bf16),
                    chunk(hidden_units, bf16), chunk(hidden_units, bf16),
                ),
                "ffn",
                (
                    at, tok, row(b_out), row(norm1_gain), row(norm1_bias), w_inner, row(b_inner),
                    w_outer, *hps, *wouts,
                ),
                scalars=1,
                scratch=[pltpu.VMEM((n, BLOCK, width), f32)],
                estimate=cost(6 * BLOCK * width * width, 5 * MIB),
            )

        def scatter(parts, extra=None):
            total = parts[0].astype(f32)
            for k in range(1, n):
                total = total + shift(parts[k], -k).astype(f32)
            if extra is not None:
                total = total + extra
            return total.astype(bf16)

        def gather(total):
            return [total] + [shift(total, k) for k in range(1, n)]

        first = {k: ffn(k) for k in order}
        ffns = gather(scatter([first[k][0] for k in range(n)]))

        def ffn_back(k):
            _, n1, _, _, _, slope = first[k]
            return call(
                functools.partial(ffn_back_kernel, n, k),
                (
                    chunk(width, bf16), chunk(width, f32), chunk(width, bf16),
                    chunk(hidden_units, bf16), chunk(width, bf16), near((8, width), f32),
                ),
                "ffn_back",
                (
                    at, cot, n1, slope, ffns[k], row(norm1_gain), row(norm1_bias), row(b_outer),
                    row(norm2_gain), row(norm2_bias), w_inner, w_outer,
                ),
                scalars=1,
                estimate=cost(4 * BLOCK * width * width, 5 * MIB),
            )

        second = {k: ffn_back(k) for k in range(n)}
        dhs = gather(scatter([second[k][4] for k in range(n)]))

        half = width + 16 * m
        half += -half % (16 * m)
        keep1, send1 = call(
            functools.partial(ffn_grad_kernel, n),
            (near((half, width), bf16), near((half, width), bf16)),
            "ffn_grads",
            (
                at,
                *[first[k][3] for k in range(n)],
                *[second[k][3] for k in range(n)],
                *[first[k][4] for k in range(n)],
                *[second[k][2] for k in range(n)],
                *[second[k][5] for k in range(n)],
            ),
            scalars=1,
            scratch=[pltpu.VMEM((n, 8, width), f32)],
            estimate=cost(4 * count * width * width, 6 * MIB),
        )
        total1 = scatter_grads(keep1, send1, member)

        def attend_back(k, dh):
            _, n1, s1, _, _, _ = first[k]
            return call(
                functools.partial(attend_back_kernel, n_blk, n, k),
                (
                    chunk(width, f32), chunk(width, bf16), near((8, width), f32), chunk(local, bf16),
                    near((half_blk, lanes, BLOCK), bf16), near((half_blk, lanes, BLOCK), bf16),
                ),
                "attend_back",
                (at, dh, second[k][1], n1, s1, row(norm1_gain), w_out, q, probs, *kvs),
                scalars=1,
                estimate=cost(1e9, 4 * MIB),
            )

        third = {}
        for k in range(n):
            dh = dhs[k]
            if k == n - 1:
                dh, total1 = lax.optimization_barrier((dh, total1))
            third[k] = attend_back(k, dh)
        mine1 = gather_grads(total1, at, "gather_ffn_grads")

        def input_part(k):
            _, _, _, dq, send, keep = third[k]
            recv = flip(send, 1)
            out = (keep[1].astype(f32) + recv[1].astype(f32)).astype(bf16)
            far = flip(out, 2)
            return call(
                input_kernel,
                (chunk(width, bf16), near((lanes, BLOCK), bf16), near((8, width), f32)),
                "input_part",
                (dq, keep, recv, far, wq_t, wkv_t),
                estimate=cost(6 * BLOCK * width * local, 2 * MIB),
            )

        fourth = {k: input_part(k) for k in order}
        d_tok = scatter([fourth[k][0] for k in range(n)], third[0][0])

        rows2 = 2 * local + 16
        rows2 += -rows2 % (16 * m)
        hp, mine1 = lax.optimization_barrier((hp, mine1))
        keep2, send2 = call(
            functools.partial(attend_grad_kernel, n),
            (near((rows2, width), bf16), near((rows2, width), bf16)),
            "attend_grads",
            (
                at, tok, hp,
                *[third[k][1] for k in range(n)],
                *[third[k][3] for k in range(n)],
                *[fourth[k][1] for k in range(n)],
                *[third[k][2] for k in range(n)],
                *[fourth[k][2] for k in range(n)],
            ),
            scalars=1,
            scratch=[pltpu.VMEM((n, 8, width), f32)] * 2,
            estimate=cost(2 * count * width * 4 * local, 5 * MIB),
        )
        other1 = flip(mine1, 1)
        vector = shape((1, width), f32)
        short = shape((1, local), f32)
        g_w_inner, g_w_outer, g_gain2, g_bias2, g_b_outer, g_b_inner = call(
            ffn_final_kernel,
            (shape((width, hidden_units), f32), shape((hidden_units, width), f32)) + (vector,) * 4,
            "ffn_grads_out",
            (at, mine1, other1),
            scalars=1,
            estimate=cost(0, 8 * MIB),
        )
        total2 = scatter_grads(keep2, send2, member)
        total2, d_tok, g_b_outer = lax.optimization_barrier((total2, d_tok, g_b_outer))
        mine2 = gather_grads(total2, at, "gather_attend_grads")
        other2 = flip(mine2, 1)

        assemble = lambda parts, name: call(
            functools.partial(output_kernel, n),
            shape((row_count, block, width), bf16),
            name,
            (at, *parts),
            scalars=1,
            estimate=cost(0, 2 * MIB),
        )
        output = assemble([second[k][0] for k in range(n)], "output_rows")
        d_tokens = assemble(gather(d_tok), "input_grad_rows")
        wide = shape((local, width), f32)
        g_w_out, g_q, g_k, g_v, g_gain1, g_bias1, g_b_out, g_b_query, g_b_value = call(
            attend_final_kernel,
            (wide,) * 4 + (vector,) * 3 + (short,) * 2,
            "attend_grads_out",
            (at, mine2, other2),
            scalars=1,
            estimate=cost(0, 5 * MIB),
        )
        flat = lambda v: v.reshape(-1)
        return (
            output, d_tokens, g_q.T, flat(g_b_query), g_k.T, g_v.T, flat(g_b_value), g_w_out,
            flat(g_b_out), flat(g_gain1), flat(g_bias1), g_w_inner, flat(g_b_inner), g_w_outer,
            flat(g_b_outer), flat(g_gain2), flat(g_bias2),
        )

    spread, cols, vec, rows_ = P("dp", "blk", None), P(None, "tensor"), P("tensor"), P("tensor", None)
    return jax.shard_map(
        body,
        mesh=mesh,
        in_specs=(
            spread, P("dp"), P("dp", None), cols, vec, cols, cols, vec, rows_, P(), P(), P(),
            cols, vec, rows_, P(), P(), P(), spread,
        ),
        out_specs=(
            spread, spread, cols, vec, cols, cols, vec, rows_, P(), P(), P(), cols, vec, rows_,
            P(), P(), P(),
        ),
        check_vma=False,
    )
```

time: 284 us -> 275 us (0.968)
  local copies, waits for them, and re-layouts: 43 us -> 17.5 us
  waiting for transfers between devices: 98 us -> 113 us
    unnamed x258 -> x140, local copies, waits for them, and re-layouts: 40.4 us -> 17.5 us
    ppermute x24, waiting for transfers between devices: 57.2 us -> 72.4 us  [shift(): return lax.ppermute(v, 'tensor', [(i, (i + k) % n) for i in range(n)])]
    ppermute x12, waiting for transfers between devices: 27.4 us -> 18.2 us  [flip_member(): return lax.ppermute(v, ('dp', 'blk'), perm)]
    ppermute x15, waiting for transfers between devices: 13.4 us -> 22.5 us  [flip(): return lax.ppermute(v, 'blk', [(i, i ^ bit) for i in range(n_blk)])]
    pallas_call x0 -> x6, other arithmetic: none -> 3.63 us  [call(): pl.pallas_call(kernel, out_shape=outs, in_specs=[SMEM] * scalars + [VMEM]...]
    convert_element_type x7, other arithmetic: 6.94 us -> 4.04 us  [the longest x2 1.67 us: scatter_grads(): got = [flip_member(piece(s).astype(bf16), s) for s in range(1, m)]]
    pallas_call x28 -> x27, Pallas kernels: 52.5 us -> 51.7 us  [call(): pl.pallas_call(kernel, out_shape=outs, in_specs=[SMEM] * scalars + [VMEM]...]
  transfers between devices with their start and end apart: 51 -> 51, of which waited for: 25 -> 24; matrix products, arithmetic and copies ran while one was open for 5% -> 3% of each run, Pallas kernels for 17% -> 11%
where the time goes in v2:
time: 275 us; the launch traced here: 272 us
  waiting for transfers between devices  113 us (41%)
  starting transfers between devices  78.7 us (29%)
  Pallas kernels  51.7 us (19%)
  local copies, waits for them, and re-layouts  17.5 us (6%)
  other arithmetic  9.37 us (3%)
    ppermute x24, waiting for transfers between devices, shift(): return lax.ppermute(v, 'tensor', [(i, (i + k) % n) for i in range(n)])  72.4 us
    ppermute x24, starting transfers between devices, shift(): return lax.ppermute(v, 'tensor', [(i, (i + k) % n) for i in range(n)])  54.6 us
    pallas_call x27, Pallas kernels, call(): pl.pallas_call(kernel, out_shape=outs, in_specs=[SMEM] * scalars + [VMEM]...  51.7 us
    ppermute x15, waiting for transfers between devices, flip(): return lax.ppermute(v, 'blk', [(i, i ^ bit) for i in range(n_blk)])  22.5 us
    ppermute x12, waiting for transfers between devices, flip_member(): return lax.ppermute(v, ('dp', 'blk'), perm)  18.2 us
    unnamed x140, local copies, waits for them, and re-layouts  17.5 us
    ppermute x12, starting transfers between devices, flip_member(): return lax.ppermute(v, ('dp', 'blk'), perm)  17.1 us
    ppermute x15, starting transfers between devices, flip(): return lax.ppermute(v, 'blk', [(i, i ^ bit) for i in range(n_blk)])  7.03 us
  transfers between devices with their start and end apart: 51, of which 24 were waited for; matrix products, arithmetic and copies ran while one was open for 3% of the time, Pallas kernels for 11%

profile of v2, /device:TPU:0, one launch (start us, length us, event | category | flops | bytes accessed | tf_op | source)
XLA Modules:
  0.0 271.9 jit_solution(1686893405550337731)
XLA Ops:
  5.1 3.0 %collective-permute-start.4 = (bf16[512,384]{1,0:T(8,128)(2,1)S(1)}, bf16[512,384]{1,0:T(8,128)(2,1)S(1)}, u32[]{:S(2)}, u32[]{:S(2)}) collective-permute-start(bf16[512,384]{1,0:T(8,128)(2,1)S(1)} %get-tuple-element.134.refs_0_), channel_id=1, source_target_pairs={{0,8},{4,12},{8,0},{12,4},{1,9},{5,13},{9,1},{13,5},{2,10},{6,14},... | collective-permute-start | bytes 1179656 | tf_op jit(solution)/shard_map/ppermute | solution.py:364
  8.1 9.1 %collective-permute-done.4.refs_2_ = bf16[512,384]{1,0:T(8,128)(2,1)S(1)} collective-permute-done((bf16[512,384]{1,0:T(8,128)(2,1)S(1)}, bf16[512,384]{1,0:T(8,128)(2,1)S(1)}, u32[]{:S(2)}, u32[]{:S(2)}) %collective-permute-start.4) | collective-permute-done | bytes 393248 | tf_op jit(solution)/shard_map/ppermute | solution.py:364
  19.1 2.6 collective-permute-start.1
  23.6 5.6 %collective-permute-done.refs_5_ = bf16[192,768]{1,0:T(8,128)(2,1)} collective-permute-done((bf16[192,768]{1,0:T(8,128)(2,1)S(1)}, bf16[192,768]{1,0:T(8,128)(2,1)}, u32[]{:S(2)}, u32[]{:S(2)}) %collective-permute-start) | collective-permute-done | bytes 294944 | tf_op jit(solution)/shard_map/ppermute | solution.py:361
  29.2 12.4 %collective-permute-done.1.refs_6_ = bf16[192,768]{1,0:T(8,128)(2,1)} collective-permute-done((bf16[192,768]{1,0:T(8,128)(2,1)S(1)}, bf16[192,768]{1,0:T(8,128)(2,1)}, u32[]{:S(2)}, u32[]{:S(2)}) %collective-permute-start.1) | collective-permute-done | bytes 294944 | tf_op jit(solution)/shard_map/ppermute | solution.py:361
  43.6 5.5 %attend.1 = (bf16[768,128]{1,0:T(8,128)(2,1)S(1)}, bf16[1536,512]{1,0:T(8,128)(2,1)S(1)}) custom-call(s32[4]{0:T(128)S(1)} %pad_add_fusion.at, s32[4]{0:T(128)S(1)} %copy-done.62, s32[4,4]{1,0:T(4,128)S(1)} %copy-done.61, bf16[512,384]{1,0:T(8,128)(2,1)S(1)} %query_rows.1.q, bf16[512,384]{1,0:T(8,128)(2,1)S(1)} %copy-done.10, ...), custom_call_target="tpu_custom_call" | custom-call | flops 2000000000 | bytes 4194304 | tf_op jit(solution)/shard_map/attend/pallas_call | solution.py:64
  49.1 6.8 %collective-permute-start.6 = (bf16[768,128]{1,0:T(8,128)(2,1)S(1)}, bf16[768,128]{1,0:T(8,128)(2,1)S(1)}, u32[]{:S(2)}, u32[]{:S(2)}) collective-permute-start(bf16[768,128]{1,0:T(8,128)(2,1)S(1)} %get-tuple-element.183.refs_0_.hp), channel_id=1, source_target_pairs={{0,1},{1,2},{2,3},{3,0},{4,5},{5,6},{6,7},{7,4},{8,9},{9,10},{10,1... | collective-permute-start | bytes 589832 | tf_op jit(solution)/shard_map/ppermute | solution.py:361
  58.4 4.4 %collective-permute-done.6.refs_1_ = bf16[768,128]{1,0:T(8,128)(2,1)S(1)} collective-permute-done((bf16[768,128]{1,0:T(8,128)(2,1)S(1)}, bf16[768,128]{1,0:T(8,128)(2,1)S(1)}, u32[]{:S(2)}, u32[]{:S(2)}) %collective-permute-start.6) | collective-permute-done | bytes 196640 | tf_op jit(solution)/shard_map/ppermute | solution.py:361
  62.8 7.4 %collective-permute-done.7.refs_2_ = bf16[768,128]{1,0:T(8,128)(2,1)S(1)} collective-permute-done((bf16[768,128]{1,0:T(8,128)(2,1)S(1)}, bf16[768,128]{1,0:T(8,128)(2,1)S(1)}, u32[]{:S(2)}, u32[]{:S(2)}) %collective-permute-start.7) | collective-permute-done | bytes 196640 | tf_op jit(solution)/shard_map/ppermute | solution.py:361
  72.8 4.7 %collective-permute-start.11 = (bf16[128,768]{1,0:T(8,128)(2,1)S(1)}, bf16[128,768]{1,0:T(8,128)(2,1)S(1)}, u32[]{:S(2)}, u32[]{:S(2)}) collective-permute-start(bf16[128,768]{1,0:T(8,128)(2,1)S(1)} %get-tuple-element.145), channel_id=1, source_target_pairs={{0,1},{1,2},{2,3},{3,0},{4,5},{5,6},{6,7},{7,4},{8,9},{9,10},{10,1... | collective-permute-start | bytes 589832 | tf_op jit(solution)/shard_map/ppermute | solution.py:361
  87.8 4.0 %collective-permute-done.10 = bf16[128,768]{1,0:T(8,128)(2,1)S(1)} collective-permute-done((bf16[128,768]{1,0:T(8,128)(2,1)S(1)}, bf16[128,768]{1,0:T(8,128)(2,1)S(1)}, u32[]{:S(2)}, u32[]{:S(2)}) %collective-permute-start.10) | collective-permute-done | bytes 196640 | tf_op jit(solution)/shard_map/ppermute | solution.py:361
  91.8 2.5 collective-permute-done.9
  101.0 3.3 %collective-permute-done.12.ffn = bf16[128,768]{1,0:T(8,128)(2,1)S(1)} collective-permute-done((bf16[128,768]{1,0:T(8,128)(2,1)S(1)}, bf16[128,768]{1,0:T(8,128)(2,1)S(1)}, u32[]{:S(2)}, u32[]{:S(2)}) %collective-permute-start.12) | collective-permute-done | bytes 196640 | tf_op jit(solution)/shard_map/ppermute | solution.py:361
  106.1 4.6 %collective-permute-done.13.ffn = bf16[128,768]{1,0:T(8,128)(2,1)S(1)} collective-permute-done((bf16[128,768]{1,0:T(8,128)(2,1)S(1)}, bf16[128,768]{1,0:T(8,128)(2,1)S(1)}, u32[]{:S(2)}, u32[]{:S(2)}) %collective-permute-start.13) | collective-permute-done | bytes 196640 | tf_op jit(solution)/shard_map/ppermute | solution.py:361
  116.4 3.0 %ffn_grads.1 = (bf16[832,768]{1,0:T(8,128)(2,1)S(1)}, bf16[832,768]{1,0:T(8,128)(2,1)}) custom-call(s32[4]{0:T(128)S(1)} %pad_add_fusion.at, bf16[128,768]{1,0:T(8,128)(2,1)S(1)} %get-tuple-element.160.refs_0_, bf16[128,768]{1,0:T(8,128)(2,1)S(1)} %get-tuple-element.161.refs_1_, bf16[128,768]{1,0:T(8,128)(2,1)S(1)} %get-tuple-element.162.refs_2_, ...), custom_call_target="tpu_custom_call" | custom-call | flops 1207959552 | bytes 6291456 | tf_op jit(solution)/shard_map/ffn_grads/pallas_call | solution.py:64
  120.5 3.3 %collective-permute-start.17 = (bf16[128,768]{1,0:T(8,128)(2,1)S(1)}, bf16[128,768]{1,0:T(8,128)(2,1)S(1)}, u32[]{:S(2)}, u32[]{:S(2)}) collective-permute-start(bf16[128,768]{1,0:T(8,128)(2,1)S(1)} %get-tuple-element.159), channel_id=1, source_target_pairs={{0,1},{1,2},{2,3},{3,0},{4,5},{5,6},{6,7},{7,4},{8,9},{9,10},{10,1... | collective-permute-start | bytes 589832 | tf_op jit(solution)/shard_map/ppermute | solution.py:361
  123.7 3.4 %collective-permute-start.16 = (bf16[128,768]{1,0:T(8,128)(2,1)S(1)}, bf16[128,768]{1,0:T(8,128)(2,1)S(1)}, u32[]{:S(2)}, u32[]{:S(2)}) collective-permute-start(bf16[128,768]{1,0:T(8,128)(2,1)S(1)} %get-tuple-element.158), channel_id=1, source_target_pairs={{0,2},{1,3},{2,0},{3,1},{4,6},{5,7},{6,4},{7,5},{8,10},{9,11},{10,... | collective-permute-start | bytes 589832 | tf_op jit(solution)/shard_map/ppermute | solution.py:361
  127.1 5.3 %collective-permute-done.17 = bf16[128,768]{1,0:T(8,128)(2,1)S(1)} collective-permute-done((bf16[128,768]{1,0:T(8,128)(2,1)S(1)}, bf16[128,768]{1,0:T(8,128)(2,1)S(1)}, u32[]{:S(2)}, u32[]{:S(2)}) %collective-permute-start.17) | collective-permute-done | bytes 196640 | tf_op jit(solution)/shard_map/ppermute | solution.py:361
  132.4 8.2 %collective-permute-done.16 = bf16[128,768]{1,0:T(8,128)(2,1)S(1)} collective-permute-done((bf16[128,768]{1,0:T(8,128)(2,1)S(1)}, bf16[128,768]{1,0:T(8,128)(2,1)S(1)}, u32[]{:S(2)}, u32[]{:S(2)}) %collective-permute-start.16) | collective-permute-done | bytes 196640 | tf_op jit(solution)/shard_map/ppermute | solution.py:361
  141.4 4.7 %collective-permute-start.26 = (bf16[128,768]{1,0:T(8,128)(2,1)}, bf16[128,768]{1,0:T(8,128)(2,1)}, u32[]{:S(2)}, u32[]{:S(2)}) collective-permute-start(bf16[128,768]{1,0:T(8,128)(2,1)} %add_convert_fusion.4.dh), channel_id=1, source_target_pairs={{0,1},{1,2},{2,3},{3,0},{4,5},{5,6},{6,7},{7,4},{8,9},{9,10},{10,1... | collective-permute-start | bytes 589832 | tf_op jit(solution)/shard_map/ppermute | solution.py:361
  146.1 3.4 %attend_back.4 = (f32[128,768]{1,0:T(8,128)S(1)}, bf16[128,768]{1,0:T(8,128)(2,1)S(1)}, f32[8,768]{1,0:T(8,128)S(1)}, bf16[128,192]{1,0:T(8,128)(2,1)S(1)}, bf16...) custom-call(s32[4]{0:T(128)S(1)} %pad_add_fusion.at, bf16[128,768]{1,0:T(8,128)(2,1)} %add_convert_fusion.4.dh, ...), custom_call_target="tpu_custom_call" | custom-call | flops 1000000000 | bytes 4194304 | tf_op jit(solution)/shard_map/attend_back/pallas_call | solution.py:64
  159.3 3.2 %attend_back.5 = (f32[128,768]{1,0:T(8,128)}, bf16[128,768]{1,0:T(8,128)(2,1)S(1)}, f32[8,768]{1,0:T(8,128)S(1)}, bf16[128,192]{1,0:T(8,128)(2,1)S(1)}, bf16[2,3...) custom-call(s32[4]{0:T(128)S(1)} %pad_add_fusion.at, bf16[128,768]{1,0:T(8,128)(2,1)} %collective-permute-done.26.dh, ...), custom_call_target="tpu_custom_call" | custom-call | flops 1000000000 | bytes 4194304 | tf_op jit(solution)/shard_map/attend_back/pallas_call | solution.py:64
  169.9 2.7 %attend_back.6 = (f32[128,768]{1,0:T(8,128)}, bf16[128,768]{1,0:T(8,128)(2,1)S(1)}, f32[8,768]{1,0:T(8,128)S(1)}, bf16[128,192]{1,0:T(8,128)(2,1)S(1)}, bf16[2,3...) custom-call(s32[4]{0:T(128)S(1)} %pad_add_fusion.at, bf16[128,768]{1,0:T(8,128)(2,1)S(1)} %collective-permute-done.27.dh, ...), custom_call_target="tpu_custom_call" | custom-call | flops 1000000000 | bytes 4194304 | tf_op jit(solution)/shard_map/attend_back/pallas_call | solution.py:64
  173.2 3.1 %collective-permute-done.22 = bf16[208,768]{1,0:T(8,128)(2,1)S(1)} collective-permute-done((bf16[208,768]{1,0:T(8,128)(2,1)S(1)}, bf16[208,768]{1,0:T(8,128)(2,1)S(1)}, u32[]{:S(2)}, u32[]{:S(2)}) %collective-permute-start.22) | collective-permute-done | bytes 319520 | tf_op jit(solution)/shard_map/ppermute | solution.py:373
  176.4 6.5 %collective-permute-done.21 = bf16[208,768]{1,0:T(8,128)(2,1)S(1)} collective-permute-done((bf16[208,768]{1,0:T(8,128)(2,1)S(1)}, bf16[208,768]{1,0:T(8,128)(2,1)S(1)}, u32[]{:S(2)}, u32[]{:S(2)}) %collective-permute-start.21) | collective-permute-done | bytes 319520 | tf_op jit(solution)/shard_map/ppermute | solution.py:373
  184.7 2.8 %attend_back.7 = (f32[128,768]{1,0:T(8,128)}, bf16[128,768]{1,0:T(8,128)(2,1)S(1)}, f32[8,768]{1,0:T(8,128)S(1)}, bf16[128,192]{1,0:T(8,128)(2,1)S(1)}, bf16[2,3...) custom-call(s32[4]{0:T(128)S(1)} %pad_add_fusion.at, bf16[128,768]{1,0:T(8,128)(2,1)S(1)} %collective-permute-done.18.dh, ...), custom_call_target="tpu_custom_call" | custom-call | flops 1000000000 | bytes 4194304 | tf_op jit(solution)/shard_map/attend_back/pallas_call | solution.py:64
  195.3 13.3 %collective-permute-done.35.far = bf16[384,128]{1,0:T(8,128)(2,1)S(1)} collective-permute-done((bf16[384,128]{1,0:T(8,128)(2,1)S(1)}, bf16[384,128]{1,0:T(8,128)(2,1)S(1)}, u32[]{:S(2)}, u32[]{:S(2)}) %collective-permute-start.35) | collective-permute-done | bytes 98336 | tf_op jit(solution)/shard_map/ppermute | solution.py:364
  218.0 6.9 %collective-permute-done.41 = bf16[128,768]{1,0:T(8,128)(2,1)S(1)} collective-permute-done((bf16[128,768]{1,0:T(8,128)(2,1)S(1)}, bf16[128,768]{1,0:T(8,128)(2,1)S(1)}, u32[]{:S(2)}, u32[]{:S(2)}) %collective-permute-start.41) | collective-permute-done | bytes 196640 | tf_op jit(solution)/shard_map/ppermute | solution.py:361
  231.9 2.9 %ffn_grads_out.1 = (f32[768,768]{1,0:T(8,128)}, f32[768,768]{1,0:T(8,128)}, f32[1,768]{1,0:T(1,128)S(1)}, f32[1,768]{1,0:T(1,128)S(1)}, f32[1,768]{1,0:T(1,128)S(1)}, /*index=5*/f32[1,768]{1,0:T(1,128)S(1)}) custom-call(s32[4]{0:T(128)S(1)} %pad_add_fusion.at, bf16[832,768]{1,0:T(8,128)(2,1)S(1)} %bitcast.75, bf16[832,768]{1,0:T(8,128)(2,1)S(1)} %collective-permute-done.43.other), custom_call_target="tpu_custom_call" | custom-call | bytes 8388608 | tf_op jit(solution)/shard_map/ffn_grads_out/pallas_call | solution.py:64
  238.4 3.7 %collective-permute-done.47.refs_1_ = bf16[112,768]{1,0:T(8,128)(2,1)S(1)} collective-permute-done((bf16[112,768]{1,0:T(8,128)(2,1)S(1)}, bf16[112,768]{1,0:T(8,128)(2,1)S(1)}, u32[]{:S(2)}, u32[]{:S(2)}) %collective-permute-start.47) | collective-permute-done | bytes 172064 | tf_op jit(solution)/shard_map/ppermute | solution.py:373
  244.6 8.8 %collective-permute-start.44 = (bf16[128,768]{1,0:T(8,128)(2,1)S(1)}, bf16[128,768]{1,0:T(8,128)(2,1)S(1)}, u32[]{:S(2)}, u32[]{:S(2)}) collective-permute-start(bf16[128,768]{1,0:T(8,128)(2,1)S(1)} %add_convert_fusion.3.refs_0_), channel_id=1, source_target_pairs={{0,1},{1,2},{2,3},{3,0},{4,5},{5,6},{6,7},{7,4},{8,9},{9,10},{10,1... | collective-permute-start | bytes 589832 | tf_op jit(solution)/shard_map/ppermute | solution.py:361
  259.7 6.1 %collective-permute-done.45.refs_2_ = bf16[128,768]{1,0:T(8,128)(2,1)S(1)} collective-permute-done((bf16[128,768]{1,0:T(8,128)(2,1)S(1)}, bf16[128,768]{1,0:T(8,128)(2,1)S(1)}, u32[]{:S(2)}, u32[]{:S(2)}) %collective-permute-start.45) | collective-permute-done | bytes 196640 | tf_op jit(solution)/shard_map/ppermute | solution.py:361
  (263 shorter events, 103.1 us)
Async XLA Ops:
  8.1 33.5 %collective-permute-start.3 = (bf16[512,384]{1,0:T(8,128)(2,1)S(1)}, bf16[512,384]{1,0:T(8,128)(2,1)}, u32[]{:S(2)}, u32[]{:S(2)}) collective-permute-start(bf16[512,384]{1,0:T(8,128)(2,1)S(1)} %get-tuple-element.134.refs_0_), channel_id=1, source_target_pairs={{0,4},{4,0},{8,12},{12,8},{1,5},{5,1},{9,13},{13,9},{2,6},{6,2},{1... | collective-permute-start | bytes 1179656 | tf_op jit(solution)/shard_map/ppermute | solution.py:364
  17.2 24.4 %collective-permute-start.5 = (bf16[512,384]{1,0:T(8,128)(2,1)S(1)}, bf16[512,384]{1,0:T(8,128)(2,1)}, u32[]{:S(2)}, u32[]{:S(2)}) collective-permute-start(bf16[512,384]{1,0:T(8,128)(2,1)S(1)} %collective-permute-done.4.refs_2_), channel_id=1, source_target_pairs={{0,4},{4,0},{8,12},{12,8},{1,5},{5,1},{9,13},{13,9},{2,6},{6,2},{1... | collective-permute-start | bytes 1179656 | tf_op jit(solution)/shard_map/ppermute | solution.py:364
  19.1 22.5 %collective-permute-start.1 = (bf16[192,768]{1,0:T(8,128)(2,1)S(1)}, bf16[192,768]{1,0:T(8,128)(2,1)}, u32[]{:S(2)}, u32[]{:S(2)}) collective-permute-start(bf16[192,768]{1,0:T(8,128)(2,1)S(1)} %copy-done.4), channel_id=1, source_target_pairs={{0,2},{1,3},{2,0},{3,1},{4,6},{5,7},{6,4},{7,5},{8,10},{9,11},{10,... | collective-permute-start | bytes 884744 | tf_op jit(solution)/shard_map/ppermute | solution.py:361
  21.7 19.9 %collective-permute-start.2 = (bf16[192,768]{1,0:T(8,128)(2,1)S(1)}, bf16[192,768]{1,0:T(8,128)(2,1)}, u32[]{:S(2)}, u32[]{:S(2)}) collective-permute-start(bf16[192,768]{1,0:T(8,128)(2,1)S(1)} %copy-done.4), channel_id=1, source_target_pairs={{0,3},{1,0},{2,1},{3,2},{4,7},{5,4},{6,5},{7,6},{8,11},{9,8},{10,9... | collective-permute-start | bytes 884744 | tf_op jit(solution)/shard_map/ppermute | solution.py:361
  49.1 13.7 %collective-permute-start.6 = (bf16[768,128]{1,0:T(8,128)(2,1)S(1)}, bf16[768,128]{1,0:T(8,128)(2,1)S(1)}, u32[]{:S(2)}, u32[]{:S(2)}) collective-permute-start(bf16[768,128]{1,0:T(8,128)(2,1)S(1)} %get-tuple-element.183.refs_0_.hp), channel_id=1, source_target_pairs={{0,1},{1,2},{2,3},{3,0},{4,5},{5,6},{6,7},{7,4},{8,9},{9,10},{10,1... | collective-permute-start | bytes 589832 | tf_op jit(solution)/shard_map/ppermute | solution.py:361
  55.9 14.3 %collective-permute-start.7 = (bf16[768,128]{1,0:T(8,128)(2,1)S(1)}, bf16[768,128]{1,0:T(8,128)(2,1)S(1)}, u32[]{:S(2)}, u32[]{:S(2)}) collective-permute-start(bf16[768,128]{1,0:T(8,128)(2,1)S(1)} %get-tuple-element.183.refs_0_.hp), channel_id=1, source_target_pairs={{0,2},{1,3},{2,0},{3,1},{4,6},{5,7},{6,4},{7,5},{8,10},{9,11},{10,... | collective-permute-start | bytes 589832 | tf_op jit(solution)/shard_map/ppermute | solution.py:361
  57.5 12.7 %collective-permute-start.8 = (bf16[768,128]{1,0:T(8,128)(2,1)S(1)}, bf16[768,128]{1,0:T(8,128)(2,1)S(1)}, u32[]{:S(2)}, u32[]{:S(2)}) collective-permute-start(bf16[768,128]{1,0:T(8,128)(2,1)S(1)} %get-tuple-element.183.refs_0_.hp), channel_id=1, source_target_pairs={{0,3},{1,0},{2,1},{3,2},{4,7},{5,4},{6,5},{7,6},{8,11},{9,8},{10,9... | collective-permute-start | bytes 589832 | tf_op jit(solution)/shard_map/ppermute | solution.py:361
  72.8 15.0 %collective-permute-start.11 = (bf16[128,768]{1,0:T(8,128)(2,1)S(1)}, bf16[128,768]{1,0:T(8,128)(2,1)S(1)}, u32[]{:S(2)}, u32[]{:S(2)}) collective-permute-start(bf16[128,768]{1,0:T(8,128)(2,1)S(1)} %get-tuple-element.145), channel_id=1, source_target_pairs={{0,1},{1,2},{2,3},{3,0},{4,5},{5,6},{6,7},{7,4},{8,9},{9,10},{10,1... | collective-permute-start | bytes 589832 | tf_op jit(solution)/shard_map/ppermute | solution.py:361
  96.7 14.0 %collective-permute-start.13 = (bf16[128,768]{1,0:T(8,128)(2,1)S(1)}, bf16[128,768]{1,0:T(8,128)(2,1)S(1)}, u32[]{:S(2)}, u32[]{:S(2)}) collective-permute-start(bf16[128,768]{1,0:T(8,128)(2,1)S(1)} %add_convert_fusion.5.ffn), channel_id=1, source_target_pairs={{0,2},{1,3},{2,0},{3,1},{4,6},{5,7},{6,4},{7,5},{8,10},{9,11},{10,... | collective-permute-start | bytes 589832 | tf_op jit(solution)/shard_map/ppermute | solution.py:361
  98.3 14.9 %collective-permute-start.14 = (bf16[128,768]{1,0:T(8,128)(2,1)S(1)}, bf16[128,768]{1,0:T(8,128)(2,1)S(1)}, u32[]{:S(2)}, u32[]{:S(2)}) collective-permute-start(bf16[128,768]{1,0:T(8,128)(2,1)S(1)} %add_convert_fusion.5.ffn), channel_id=1, source_target_pairs={{0,3},{1,0},{2,1},{3,2},{4,7},{5,4},{6,5},{7,6},{8,11},{9,8},{10,9... | collective-permute-start | bytes 589832 | tf_op jit(solution)/shard_map/ppermute | solution.py:361
  120.4 43.0 %collective-permute-start.19 = (bf16[832,768]{1,0:T(8,128)(2,1)}, bf16[832,768]{1,0:T(8,128)(2,1)}, u32[]{:S(2)}, u32[]{:S(2)}) collective-permute-start(bf16[832,768]{1,0:T(8,128)(2,1)} %get-tuple-element.181), channel_id=1, source_target_pairs={{0,4},{4,0},{8,12},{12,8},{1,5},{5,1},{9,13},{13,9},{2,6},{6,2},{1... | collective-permute-start | bytes 3833864 | tf_op jit(solution)/shard_map/ppermute | solution.py:364
  123.7 16.9 %collective-permute-start.16 = (bf16[128,768]{1,0:T(8,128)(2,1)S(1)}, bf16[128,768]{1,0:T(8,128)(2,1)S(1)}, u32[]{:S(2)}, u32[]{:S(2)}) collective-permute-start(bf16[128,768]{1,0:T(8,128)(2,1)S(1)} %get-tuple-element.158), channel_id=1, source_target_pairs={{0,2},{1,3},{2,0},{3,1},{4,6},{5,7},{6,4},{7,5},{8,10},{9,11},{10,... | collective-permute-start | bytes 589832 | tf_op jit(solution)/shard_map/ppermute | solution.py:361
  127.1 13.5 %collective-permute-start.15 = (bf16[128,768]{1,0:T(8,128)(2,1)S(1)}, bf16[128,768]{1,0:T(8,128)(2,1)S(1)}, u32[]{:S(2)}, u32[]{:S(2)}) collective-permute-start(bf16[128,768]{1,0:T(8,128)(2,1)S(1)} %get-tuple-element.157), channel_id=1, source_target_pairs={{0,3},{1,0},{2,1},{3,2},{4,7},{5,4},{6,5},{7,6},{8,11},{9,8},{10,9... | collective-permute-start | bytes 589832 | tf_op jit(solution)/shard_map/ppermute | solution.py:361
  141.4 13.1 %collective-permute-start.26 = (bf16[128,768]{1,0:T(8,128)(2,1)}, bf16[128,768]{1,0:T(8,128)(2,1)}, u32[]{:S(2)}, u32[]{:S(2)}) collective-permute-start(bf16[128,768]{1,0:T(8,128)(2,1)} %add_convert_fusion.4.dh), channel_id=1, source_target_pairs={{0,1},{1,2},{2,3},{3,0},{4,5},{5,6},{6,7},{7,4},{8,9},{9,10},{10,1... | collective-permute-start | bytes 589832 | tf_op jit(solution)/shard_map/ppermute | solution.py:361
  152.9 31.7 %collective-permute-start.18 = (bf16[128,768]{1,0:T(8,128)(2,1)}, bf16[128,768]{1,0:T(8,128)(2,1)S(1)}, u32[]{:S(2)}, u32[]{:S(2)}) collective-permute-start(bf16[128,768]{1,0:T(8,128)(2,1)} %add_convert_fusion.4.dh), channel_id=1, source_target_pairs={{0,3},{1,0},{2,1},{3,2},{4,7},{5,4},{6,5},{7,6},{8,11},{9,8},{10,9... | collective-permute-start | bytes 589832 | tf_op jit(solution)/shard_map/ppermute | solution.py:361
  152.9 15.4 %collective-permute-start.27 = (bf16[128,768]{1,0:T(8,128)(2,1)}, bf16[128,768]{1,0:T(8,128)(2,1)S(1)}, u32[]{:S(2)}, u32[]{:S(2)}) collective-permute-start(bf16[128,768]{1,0:T(8,128)(2,1)} %add_convert_fusion.4.dh), channel_id=1, source_target_pairs={{0,2},{1,3},{2,0},{3,1},{4,6},{5,7},{6,4},{7,5},{8,10},{9,11},{10,... | collective-permute-start | bytes 589832 | tf_op jit(solution)/shard_map/ppermute | solution.py:361
  167.5 15.3 %collective-permute-start.21 = (bf16[208,768]{1,0:T(8,128)(2,1)S(1)}, bf16[208,768]{1,0:T(8,128)(2,1)S(1)}, u32[]{:S(2)}, u32[]{:S(2)}) collective-permute-start(bf16[208,768]{1,0:T(8,128)(2,1)S(1)} %get-tuple-element.251), channel_id=1, source_target_pairs={{0,16},{4,20},{8,24},{12,28},{16,0},{20,4},{24,8},{28,12},{1,17},{... | collective-permute-start | bytes 958472 | tf_op jit(solution)/shard_map/ppermute | solution.py:373
  168.3 15.1 %collective-permute-start.20 = (bf16[208,768]{1,0:T(8,128)(2,1)S(1)}, bf16[208,768]{1,0:T(8,128)(2,1)S(1)}, u32[]{:S(2)}, u32[]{:S(2)}) collective-permute-start(bf16[208,768]{1,0:T(8,128)(2,1)S(1)} %get-tuple-element.249), channel_id=1, source_target_pairs={{0,8},{4,12},{8,0},{12,4},{16,24},{20,28},{24,16},{28,20},{1,9},{5... | collective-permute-start | bytes 958472 | tf_op jit(solution)/shard_map/ppermute | solution.py:373
  172.6 17.0 %collective-permute-start.29 = (bf16[384,128]{1,0:T(8,128)(2,1)S(1)}, bf16[384,128]{1,0:T(8,128)(2,1)S(1)}, u32[]{:S(2)}, u32[]{:S(2)}) collective-permute-start(bf16[384,128]{1,0:T(8,128)(2,1)S(1)} %fusion.12), channel_id=1, source_target_pairs={{0,8},{4,12},{8,0},{12,4},{1,9},{5,13},{9,1},{13,5},{2,10},{6,14},... | collective-permute-start | bytes 294920 | tf_op jit(solution)/shard_map/ppermute | solution.py:364
  189.1 19.9 %collective-permute-start.23 = (bf16[208,768]{1,0:T(8,128)(2,1)S(1)}, bf16[208,768]{1,0:T(8,128)(2,1)S(1)}, u32[]{:S(2)}, u32[]{:S(2)}) collective-permute-start(bf16[208,768]{1,0:T(8,128)(2,1)S(1)} %fusion.2.refs_0_), channel_id=1, source_target_pairs={{0,8},{4,12},{8,0},{12,4},{16,24},{20,28},{24,16},{28,20},{1,9},{5... | collective-permute-start | bytes 958472 | tf_op jit(solution)/shard_map/ppermute | solution.py:373
  189.7 19.3 %collective-permute-start.24 = (bf16[208,768]{1,0:T(8,128)(2,1)S(1)}, bf16[208,768]{1,0:T(8,128)(2,1)S(1)}, u32[]{:S(2)}, u32[]{:S(2)}) collective-permute-start(bf16[208,768]{1,0:T(8,128)(2,1)S(1)} %fusion.2.refs_0_), channel_id=1, source_target_pairs={{0,16},{4,20},{8,24},{12,28},{16,0},{20,4},{24,8},{28,12},{1,17},{... | collective-permute-start | bytes 958472 | tf_op jit(solution)/shard_map/ppermute | solution.py:373
  191.1 17.9 %collective-permute-start.25 = (bf16[208,768]{1,0:T(8,128)(2,1)S(1)}, bf16[208,768]{1,0:T(8,128)(2,1)S(1)}, u32[]{:S(2)}, u32[]{:S(2)}) collective-permute-start(bf16[208,768]{1,0:T(8,128)(2,1)S(1)} %fusion.2.refs_0_), channel_id=1, source_target_pairs={{0,24},{4,28},{8,16},{12,20},{16,8},{20,12},{24,0},{28,4},{1,25},{... | collective-permute-start | bytes 958472 | tf_op jit(solution)/shard_map/ppermute | solution.py:373
  192.7 16.0 %collective-permute-start.35 = (bf16[384,128]{1,0:T(8,128)(2,1)S(1)}, bf16[384,128]{1,0:T(8,128)(2,1)S(1)}, u32[]{:S(2)}, u32[]{:S(2)}) collective-permute-start(bf16[384,128]{1,0:T(8,128)(2,1)S(1)} %fusion.15), channel_id=1, source_target_pairs={{0,8},{4,12},{8,0},{12,4},{1,9},{5,13},{9,1},{13,5},{2,10},{6,14},... | collective-permute-start | bytes 294920 | tf_op jit(solution)/shard_map/ppermute | solution.py:364
  211.4 20.4 %collective-permute-start.43 = (bf16[832,768]{1,0:T(8,128)(2,1)S(1)}, bf16[832,768]{1,0:T(8,128)(2,1)S(1)}, u32[]{:S(2)}, u32[]{:S(2)}) collective-permute-start(bf16[832,768]{1,0:T(8,128)(2,1)S(1)} %bitcast.74), channel_id=1, source_target_pairs={{0,4},{4,0},{8,12},{12,8},{1,5},{5,1},{9,13},{13,9},{2,6},{6,2},{1... | collective-permute-start | bytes 3833864 | tf_op jit(solution)/shard_map/ppermute | solution.py:364
  211.9 12.9 %collective-permute-start.41 = (bf16[128,768]{1,0:T(8,128)(2,1)S(1)}, bf16[128,768]{1,0:T(8,128)(2,1)S(1)}, u32[]{:S(2)}, u32[]{:S(2)}) collective-permute-start(bf16[128,768]{1,0:T(8,128)(2,1)S(1)} %get-tuple-element.227), channel_id=1, source_target_pairs={{0,2},{1,3},{2,0},{3,1},{4,6},{5,7},{6,4},{7,5},{8,10},{9,11},{10,... | collective-permute-start | bytes 589832 | tf_op jit(solution)/shard_map/ppermute | solution.py:361
  213.3 13.0 %collective-permute-start.40 = (bf16[128,768]{1,0:T(8,128)(2,1)S(1)}, bf16[128,768]{1,0:T(8,128)(2,1)S(1)}, u32[]{:S(2)}, u32[]{:S(2)}) collective-permute-start(bf16[128,768]{1,0:T(8,128)(2,1)S(1)} %get-tuple-element.226), channel_id=1, source_target_pairs={{0,3},{1,0},{2,1},{3,2},{4,7},{5,4},{6,5},{7,6},{8,11},{9,8},{10,9... | collective-permute-start | bytes 589832 | tf_op jit(solution)/shard_map/ppermute | solution.py:361
  214.8 13.7 %collective-permute-start.42 = (bf16[128,768]{1,0:T(8,128)(2,1)S(1)}, bf16[128,768]{1,0:T(8,128)(2,1)S(1)}, u32[]{:S(2)}, u32[]{:S(2)}) collective-permute-start(bf16[128,768]{1,0:T(8,128)(2,1)S(1)} %get-tuple-element.228), channel_id=1, source_target_pairs={{0,1},{1,2},{2,3},{3,0},{4,5},{5,6},{6,7},{7,4},{8,9},{9,10},{10,1... | collective-permute-start | bytes 589832 | tf_op jit(solution)/shard_map/ppermute | solution.py:361
  215.5 13.2 %collective-permute-start.39 = (bf16[112,768]{1,0:T(8,128)(2,1)S(1)}, bf16[112,768]{1,0:T(8,128)(2,1)S(1)}, u32[]{:S(2)}, u32[]{:S(2)}) collective-permute-start(bf16[112,768]{1,0:T(8,128)(2,1)S(1)} %get-tuple-element.253), channel_id=1, source_target_pairs={{0,24},{4,28},{8,16},{12,20},{16,8},{20,12},{24,0},{28,4},{1,25},{... | collective-permute-start | bytes 516104 | tf_op jit(solution)/shard_map/ppermute | solution.py:373
  244.5 23.6 %collective-permute-start.50 = (bf16[448,768]{1,0:T(8,128)(2,1)S(1)}, bf16[448,768]{1,0:T(8,128)(2,1)S(1)}, u32[]{:S(2)}, u32[]{:S(2)}) collective-permute-start(bf16[448,768]{1,0:T(8,128)(2,1)S(1)} %bitcast.76), channel_id=1, source_target_pairs={{0,4},{4,0},{8,12},{12,8},{1,5},{5,1},{9,13},{13,9},{2,6},{6,2},{1... | collective-permute-start | bytes 2064392 | tf_op jit(solution)/shard_map/ppermute | solution.py:364
  244.6 15.1 %collective-permute-start.44 = (bf16[128,768]{1,0:T(8,128)(2,1)S(1)}, bf16[128,768]{1,0:T(8,128)(2,1)S(1)}, u32[]{:S(2)}, u32[]{:S(2)}) collective-permute-start(bf16[128,768]{1,0:T(8,128)(2,1)S(1)} %add_convert_fusion.3.refs_0_), channel_id=1, source_target_pairs={{0,1},{1,2},{2,3},{3,0},{4,5},{5,6},{6,7},{7,4},{8,9},{9,10},{10,1... | collective-permute-start | bytes 589832 | tf_op jit(solution)/shard_map/ppermute | solution.py:361
  253.4 12.4 %collective-permute-start.45 = (bf16[128,768]{1,0:T(8,128)(2,1)S(1)}, bf16[128,768]{1,0:T(8,128)(2,1)S(1)}, u32[]{:S(2)}, u32[]{:S(2)}) collective-permute-start(bf16[128,768]{1,0:T(8,128)(2,1)S(1)} %add_convert_fusion.3.refs_0_), channel_id=1, source_target_pairs={{0,2},{1,3},{2,0},{3,1},{4,6},{5,7},{6,4},{7,5},{8,10},{9,11},{10,... | collective-permute-start | bytes 589832 | tf_op jit(solution)/shard_map/ppermute | solution.py:361
  253.4 13.2 %collective-permute-start.46 = (bf16[128,768]{1,0:T(8,128)(2,1)S(1)}, bf16[128,768]{1,0:T(8,128)(2,1)S(1)}, u32[]{:S(2)}, u32[]{:S(2)}) collective-permute-start(bf16[128,768]{1,0:T(8,128)(2,1)S(1)} %add_convert_fusion.3.refs_0_), channel_id=1, source_target_pairs={{0,3},{1,0},{2,1},{3,2},{4,7},{5,4},{6,5},{7,6},{8,11},{9,8},{10,9... | collective-permute-start | bytes 589832 | tf_op jit(solution)/shard_map/ppermute | solution.py:361
  (89 other events, 1055.7 us)

commit v3 on v2

v3 whole, which is shorter than its diff:
```python
import functools

import jax
import jax.numpy as jnp
from jax import lax
from jax.experimental import pallas as pl
from jax.experimental.pallas import tpu as pltpu
from jax.sharding import PartitionSpec as P

HEAD_DIM = 64
BLOCK = 128
LANES = 128
SCALE = HEAD_DIM**-0.5
EPS = 1e-12
f32 = jnp.float32
bf16 = jnp.bfloat16
i32 = jnp.int32
MIB = 1 << 20
PACKED = BLOCK + HEAD_DIM


def nn(a, b):
    return lax.dot_general(a, b, (((1,), (0,)), ((), ())), preferred_element_type=f32)


def nt(a, b):
    return lax.dot_general(a, b, (((1,), (1,)), ((), ())), preferred_element_type=f32)


def tn(a, b):
    return lax.dot_general(a, b, (((0,), (0,)), ((), ())), preferred_element_type=f32)


def mean(v):
    return jnp.mean(v, axis=-1, keepdims=True)


def col_sum(v):
    return jnp.sum(v, axis=0, keepdims=True)


def row_at(at, i):
    half = at[0] % 2
    return 2 * half + i if i < 2 else 2 * (1 - half) + (i - 2)


def rows8(*rows):
    width = rows[0].shape[1]
    pad = jnp.zeros((8 - len(rows), width), f32)
    return jnp.concatenate(rows + (pad,), axis=0)


def shape(dims, dtype):
    return jax.ShapeDtypeStruct(dims, dtype)


def near(dims, dtype):
    return pltpu.VMEM(dims, dtype)


SMEM = pl.BlockSpec(memory_space=pltpu.SMEM)
VMEM = pl.BlockSpec(memory_space=pltpu.VMEM)


def call(kernel, outs, name, args, scalars=0, vmem=16, scratch=()):
    return pl.pallas_call(
        kernel,
        out_shape=outs,
        in_specs=[SMEM] * scalars + [VMEM] * (len(args) - scalars),
        out_specs=jax.tree.map(lambda _: VMEM, outs),
        scratch_shapes=list(scratch),
        compiler_params=pltpu.CompilerParams(vmem_limit_bytes=vmem * MIB),
        cost_estimate=pl.CostEstimate(flops=1, bytes_accessed=1, transcendentals=0),
        name=name,
    )(*args)


def chunk_of(ref, c, rows):
    return ref[pl.ds(pl.multiple_of(c * rows, rows), rows), :]


def kv_kernel(tok, wk_t, wv_t, bv, kv, wkv_t):
    heads = wk_t.shape[0] // HEAD_DIM
    rows, bias = [], []
    for h in range(heads):
        part = slice(h * HEAD_DIM, (h + 1) * HEAD_DIM)
        rows += [wk_t[part, :], wv_t[part, :]]
        bias += [jnp.zeros((1, HEAD_DIM), f32), bv[:, part]]
    both = jnp.concatenate(rows, axis=0)
    wkv_t[...] = both
    kv[...] = (nt(tok[...], both) + jnp.concatenate(bias, axis=1)).astype(bf16)


def q_kernel(tok, wq_t, bq, q):
    heads = wq_t.shape[0] // HEAD_DIM
    full = (nt(tok[...], wq_t[...]) + bq[...]).astype(bf16) * jnp.asarray(SCALE, bf16)
    zero = jnp.zeros((full.shape[0], HEAD_DIM), bf16)
    cols = []
    for h in range(heads):
        cols += [full[:, h * HEAD_DIM : (h + 1) * HEAD_DIM], zero]
    q[...] = jnp.concatenate(cols, axis=1)


def weights_kernel(n, at, w_out, first_z, first_core, second_z, second_core, *refs):
    outs_z, outs_core = refs[: n - 2], refs[n - 2 : 2 * (n - 2)]
    w_out_all, w_in_far, w_outer_far = refs[2 * (n - 2) :]
    z = at[0]
    local = w_out.shape[0]
    part = local // 2
    half = second_z.shape[0]

    def put(ref, base, rows, value):
        ref[pl.ds(pl.multiple_of(base, rows), rows), :] = value

    w_out_all[pl.ds(pl.multiple_of(z * local, local), local), :] = w_out[...]
    for b, first, second, outs in (
        (at[1], first_z, second_z, outs_z),
        (1 - at[1], first_core, second_core, outs_core),
    ):
        put(w_in_far, b * half, half, first[:half, :])
        put(w_outer_far, b * half, half, second[...])
        put(w_out_all, ((z ^ 1) * 2 + b) * part, part, first[half:, :])
        for i, ref in enumerate(outs):
            put(w_out_all, ((z ^ (i + 2)) * 2 + b) * part, part, ref[...])


def attend_kernel(n_blk, ids, at, bucket, lens, q, *refs):
    kvs, hp, probs = refs[:n_blk], refs[n_blk], refs[n_blk + 1]
    heads = q.shape[1] // LANES
    b = at[2]
    q_at = lax.broadcasted_iota(i32, (BLOCK, 1), 0)
    k_at = lax.broadcasted_iota(i32, (1, BLOCK), 1)
    for i, row in enumerate(ids):
        r = row_at(at, row)
        bk = bucket[r]
        size = BLOCK << bk
        slot = b >> bk
        limit = lens[r, slot]
        q_in = jnp.where(q_at + (b * BLOCK - slot * size) < limit, 1, 0)
        k_in = []
        for j in range(n_blk):
            kb = b ^ j
            k_slot = kb >> bk
            inside = jnp.where(k_at + (kb * BLOCK - k_slot * size) < limit, 1, 0)
            k_in.append(jnp.where(k_slot == slot, inside, 2))
        allowed = q_in == jnp.concatenate(k_in, axis=1)
        here = pl.ds(pl.multiple_of(r * BLOCK, BLOCK), BLOCK)
        outs = []
        for h in range(heads):
            lanes = slice(h * LANES, (h + 1) * LANES)
            kvh = jnp.concatenate([kv[here, lanes] for kv in kvs], axis=0)
            scores = jnp.where(allowed, nt(q[here, lanes], kvh), -1e30)
            weights = jnp.exp(scores - jnp.max(scores, axis=-1, keepdims=True))
            total = jnp.sum(weights, axis=-1, keepdims=True)
            p = (weights / total).astype(bf16)
            probs[(i * heads + h) * BLOCK : (i * heads + h + 1) * BLOCK, :] = p
            outs.append(nn(p, kvh)[:, HEAD_DIM:].astype(bf16))
        base = i * PACKED
        hp[base : base + BLOCK, :] = jnp.concatenate(outs[:2], axis=1)
        hp[base + BLOCK : base + PACKED, :] = jnp.concatenate(
            [outs[2][:HEAD_DIM], outs[2][HEAD_DIM:]], axis=1
        )


def unpack(h):
    odd = jnp.concatenate([h[BLOCK:, :HEAD_DIM], h[BLOCK:, HEAD_DIM:]], axis=0)
    return jnp.concatenate([h[:BLOCK, :], odd], axis=1)


def pack(v):
    odd = jnp.concatenate([v[:HEAD_DIM, LANES:], v[HEAD_DIM:, LANES:]], axis=1)
    return jnp.concatenate([v[:, :LANES], odd], axis=0)


def gelu_and_slope(inner):
    cdf = 0.5 * (1.0 + lax.erf(inner * (0.5**0.5)))
    slope = cdf + inner * (0.3989422804014327 * jnp.exp(-0.5 * inner * inner))
    return (inner * cdf).astype(bf16), slope.astype(bf16)


def ffn_kernel(
    n, i, at, tok, w_out, b_out, g1, b1, w_in, w_in_far, b_in, b_in_far, w_outer, w_outer_far, *refs
):
    hps = refs[:n]
    part, n1_out, s1_out, share, act_out, slopes, held = refs[n:]
    z = at[0]
    local = w_out.shape[0] // n
    for s in range(n):
        j = z ^ s
        held[j] = nn(unpack(hps[s][i * PACKED : (i + 1) * PACKED, :]), chunk_of(w_out, j, local))
    attn = held[0]
    for j in range(1, n):
        attn = attn + held[j]
    resid = chunk_of(tok, row_at(at, i), BLOCK).astype(f32) + (attn + b_out[...])
    center = resid - mean(resid)
    s1 = lax.rsqrt(mean(center * center) + EPS)
    n1 = center * s1
    low = (n1 * g1[...] + b1[...]).astype(bf16)
    act, slope = gelu_and_slope(nn(low, w_in[...]) + b_in[...])
    act_far, slope_far = gelu_and_slope(nn(low, w_in_far[...]) + b_in_far[...])
    part[...] = (nn(act, w_outer[...]) + nn(act_far, w_outer_far[...])).astype(bf16)
    n1_out[...] = n1
    s1_out[...] = jnp.broadcast_to(s1, s1_out.shape)
    share[:BLOCK, :] = low
    share[BLOCK:, :] = act_far
    act_out[...] = act
    slopes[:BLOCK, :] = slope
    slopes[BLOCK:, :] = slope_far


def ffn_back_kernel(
    i, at, cot, n1, slopes, mine, theirs, g1, b1, b_outer, g2, b2, w_in, w_in_far, w_outer,
    w_outer_far, share, dinner_out, part, dres2_out
):
    hidden = n1[...] * g1[...] + b1[...]
    ffn = mine[...].astype(f32) + theirs[...].astype(f32)
    resid = hidden + (ffn + b_outer[...])
    center = resid - mean(resid)
    s2 = lax.rsqrt(mean(center * center) + EPS)
    n2 = center * s2
    ct = chunk_of(cot, row_at(at, i), BLOCK).astype(f32)
    dn = ct * g2[...]
    dres2 = s2 * (dn - mean(dn) - n2 * mean(dn * n2))
    dffn = dres2.astype(bf16)
    dinner = (nt(dffn, w_outer[...]) * slopes[:BLOCK, :].astype(f32)).astype(bf16)
    dinner_far = (nt(dffn, w_outer_far[...]) * slopes[BLOCK:, :].astype(f32)).astype(bf16)
    part[...] = (nt(dinner, w_in[...]) + nt(dinner_far, w_in_far[...])).astype(bf16)
    dres2_out[...] = dres2
    dinner_out[...] = dinner
    share[:BLOCK, :] = dffn
    share[BLOCK : 2 * BLOCK, :] = dinner_far
    share[2 * BLOCK : 3 * BLOCK, :] = (n2 * g2[...] + b2[...]).astype(bf16)
    sums = rows8(col_sum(ct * n2), col_sum(ct), col_sum(dffn.astype(f32)))
    share[3 * BLOCK :, :] = jnp.concatenate([sums, jnp.zeros_like(sums)], axis=0).astype(bf16)


def norm_back_kernel(n, at, mine, theirs, dres2, n1, s1, g1, w_out, dres1_out, dattn_out, dh, dh_far):
    dhidden = (mine[...].astype(f32) + theirs[...].astype(f32)) + dres2[...]
    norm = n1[...]
    dn = dhidden * g1[...]
    dres1 = s1[:, :1] * (dn - mean(dn) - norm * mean(dn * norm))
    dattn = dres1.astype(bf16)
    dres1_out[...] = dres1
    dattn_out[:BLOCK, :] = dattn
    sums = rows8(col_sum(dhidden * norm), col_sum(dhidden), col_sum(dattn.astype(f32)))
    dattn_out[BLOCK:, :] = jnp.concatenate([sums, jnp.zeros_like(sums)], axis=0).astype(bf16)
    local = w_out.shape[0] // n
    dh[...] = pack(nt(dattn, chunk_of(w_out, at[0], local)).astype(bf16))
    dh_far[...] = pack(nt(dattn, chunk_of(w_out, at[0] ^ 1, local)).astype(bf16))


def attend_back_kernel(n_blk, i, at, packed, q, probs, *refs):
    kvs = refs[:n_blk]
    dq_out, send, keep = refs[n_blk:]
    heads = q.shape[1] // LANES
    c = row_at(at, i)
    here = pl.ds(pl.multiple_of(c * BLOCK, BLOCK), BLOCK)
    flat = unpack(packed[...])
    zero = jnp.zeros((BLOCK, HEAD_DIM), bf16)
    dqs = []
    for h in range(heads):
        lanes = slice(h * LANES, (h + 1) * LANES)
        dhead = jnp.concatenate([zero, flat[:, h * HEAD_DIM : (h + 1) * HEAD_DIM]], axis=1)
        kvh = jnp.concatenate([kv[here, lanes] for kv in kvs], axis=0)
        at_p = (i % 2) * heads + h
        p = probs[at_p * BLOCK : (at_p + 1) * BLOCK, :]
        pf = p.astype(f32)
        dp = nt(dhead, kvh)
        delta = jnp.sum(pf * dp, axis=-1, keepdims=True)
        ds = (pf * (dp - delta)).astype(bf16)
        dqs.append((nn(ds, kvh) * SCALE)[:, :HEAD_DIM].astype(bf16))
        left = jnp.concatenate([q[here, lanes], dhead], axis=0)
        dkv = tn(left, jnp.concatenate([ds, p], axis=0)).astype(bf16)
        for j in range(n_blk):
            target = keep if j % 2 == 0 else send
            target[j // 2, lanes, :] = dkv[:, j * BLOCK : (j + 1) * BLOCK]
    dq_out[...] = jnp.concatenate(dqs, axis=1)


def input_kernel(dq, keep, recv, far, wq_t, wkv_t, *refs):
    theirs, (part, dkv_t, sums) = refs[:-3], refs[-3:]
    total = keep[0].astype(f32) + recv[0].astype(f32) + far[...].astype(f32)
    low_t = total.astype(bf16)
    low = low_t.T
    grad = nn(dq[...], wq_t[...]) + nn(low, wkv_t[...])
    if theirs:
        grad = grad + theirs[0][...].astype(f32)
    part[...] = grad.astype(bf16)
    dkv_t[...] = low_t
    width = sums.shape[1]
    first = col_sum(dq[...].astype(f32))
    second = col_sum(low.astype(f32))
    sums[...] = rows8(
        jnp.concatenate([first, jnp.zeros((1, width - first.shape[1]), f32)], axis=1),
        jnp.concatenate([second, jnp.zeros((1, width - second.shape[1]), f32)], axis=1),
    )


def pick(first, one, other):
    return jnp.where(first, one, other)


def join(values, axis=0):
    return jnp.concatenate(list(values), axis=axis)


def ordered_sum(at, parts, held):
    for i, part in enumerate(parts):
        held[row_at(at, i)] = part.astype(f32)
    total = held[0]
    for r in range(1, len(parts)):
        total = total + held[r]
    return total


def ffn_grad_kernel(at, *refs):
    share1, share2, act, dinner = refs[:4], refs[4:8], refs[8:10], refs[10:12]
    keep, send, held = refs[12:]
    first = at[1] == 0
    low = join(x[:BLOCK, :] for x in share1)
    acts = join([x[...] for x in act] + [x[BLOCK:, :] for x in share1[2:]])
    dffn = join(x[:BLOCK, :] for x in share2)
    dinners = join([x[...] for x in dinner] + [x[BLOCK : 2 * BLOCK, :] for x in share2[2:]])
    tail = ordered_sum(at, [x[3 * BLOCK : 3 * BLOCK + 8, :] for x in share2], held)
    bias = rows8(tail[0:1], tail[1:2], tail[2:3], col_sum(dinners.astype(f32)))
    rows = low.shape[1]
    rest = keep.shape[0] - rows
    bias = join([bias, jnp.zeros((rest - 8, bias.shape[1]), f32)]).astype(bf16)
    send[:rows, :] = tn(pick(first, acts, low), pick(first, dffn, dinners)).astype(bf16)
    send[rows:, :] = bias
    keep[:rows, :] = tn(pick(first, low, acts), pick(first, dinners, dffn)).astype(bf16)
    keep[rows:, :] = bias


def attend_grad_kernel(at, tok, hp_mine, hp_other, *refs):
    dattn, dq, dkv_t, sums2 = (refs[4 * i : 4 * i + 4] for i in range(4))
    keep, send, held = refs[16:]
    first = at[1] == 0
    total1 = ordered_sum(at, [x[BLOCK : BLOCK + 8, :] for x in dattn], held)
    total2 = sums2[0][...] + sums2[1][...] + sums2[2][...] + sums2[3][...]
    toks = join(chunk_of(tok, row_at(at, i), BLOCK) for i in range(4))
    heads = join(unpack(hp[i * PACKED : (i + 1) * PACKED, :]) for hp in (hp_mine, hp_other) for i in range(2))
    g_out = tn(heads, join(x[:BLOCK, :] for x in dattn))
    g_q = tn(join(x[...] for x in dq), toks)
    g_kv = nn(join((x[...] for x in dkv_t), axis=1), toks)
    one = join([g_out, g_q]).astype(bf16)
    two = g_kv.astype(bf16)
    rows = two.shape[0]
    rest = keep.shape[0] - rows
    tail = join([total1, total2, jnp.zeros((rest - 16, total1.shape[1]), f32)]).astype(bf16)
    send[:rows, :] = pick(first, two, one)
    send[rows:, :] = tail
    keep[:rows, :] = pick(first, one, two)
    keep[rows:, :] = tail


def gather_kernel(m, at, *refs):
    out = refs[m]
    for s in range(m):
        out[at[3] ^ s] = refs[s][...]


def ffn_final_kernel(at, mine, other, g_in, g_outer, gain, bias, b_outer, b_in):
    first = at[1] == 0
    rows = g_in.shape[0]
    a = mine[...]
    b = other[...]
    g_in[...] = pick(first, a[:rows], b[:rows]).astype(f32)
    g_outer[...] = pick(first, b[:rows], a[:rows]).astype(f32)
    tail = pick(first, a[rows : rows + 16], b[rows : rows + 16]).astype(f32)
    for i, ref in enumerate((gain, bias, b_outer, b_in)):
        ref[...] = tail[i]


def attend_final_kernel(at, mine, other, g_out, g_q, g_k, g_v, gain, bias, b_out, b_q, b_v):
    first = at[1] == 0
    width = g_out.shape[0]
    a = mine[...]
    b = other[...]
    one = pick(first, a, b).astype(f32)
    two = pick(first, b, a).astype(f32)
    g_out[...] = one[:width]
    g_q[...] = one[width : 2 * width]
    tail = one[2 * width : 2 * width + 16]
    values = []
    for h in range(width // HEAD_DIM):
        part = slice(h * HEAD_DIM, (h + 1) * HEAD_DIM)
        g_k[part, :] = two[h * LANES : h * LANES + HEAD_DIM]
        g_v[part, :] = two[h * LANES + HEAD_DIM : (h + 1) * LANES]
        values.append(tail[9:10, h * LANES + HEAD_DIM : (h + 1) * LANES])
    for i, ref in enumerate((gain, bias, b_out)):
        ref[...] = tail[i]
    b_q[...] = tail[8, :width]
    b_v[...] = jnp.concatenate(values, axis=1)[0]


def output_kernel(at, *refs):
    out = refs[4]
    for i in range(4):
        out[row_at(at, i)] = refs[i][2 * BLOCK : 3 * BLOCK, :]


def rows_kernel(at, *refs):
    out = refs[4]
    for i in range(4):
        out[row_at(at, i)] = refs[i][...]


def solution(mesh):
    n_dp = mesh.shape["dp"]
    n_blk = mesh.shape["blk"]
    n = mesh.shape["tensor"]
    half_blk = n_blk // 2
    m = n_dp * half_blk

    def swap(v, bit):
        return lax.ppermute(v, "tensor", [(i, i ^ bit) for i in range(n)])

    def flip(v, bit):
        return lax.ppermute(v, "blk", [(i, i ^ bit) for i in range(n_blk)])

    def flip_member(v, s):
        perm = []
        for dp in range(n_dp):
            for blk in range(n_blk):
                i = (dp * half_blk + blk // 2) ^ s
                to = (i // half_blk) * n_blk + (i % half_blk) * 2 + blk % 2
                perm.append((dp * n_blk + blk, to))
        return lax.ppermute(v, ("dp", "blk"), perm)

    def scatter_grads(keep, send, member):
        recv = flip(send, 1)
        rows = keep.shape[0] // m
        width = keep.shape[1]
        keep3 = keep.reshape(m, rows, width)
        recv3 = recv.reshape(m, rows, width)

        def piece(s):
            mine = lax.dynamic_index_in_dim(keep3, member ^ s, 0, keepdims=False)
            theirs = lax.dynamic_index_in_dim(recv3, member ^ s, 0, keepdims=False)
            return mine.astype(f32) + theirs.astype(f32)

        got = [flip_member(piece(s).astype(bf16), s) for s in range(1, m)]
        total = piece(0)
        for part in got:
            total = total + part.astype(f32)
        return total.astype(bf16)

    def gather_grads(total, at, name):
        rows, width = total.shape
        every = [total] + [flip_member(total, s) for s in range(1, m)]
        mine = call(
            functools.partial(gather_kernel, m),
            shape((m, rows, width), bf16),
            name,
            (at, *every),
            scalars=1,
        )
        return mine.reshape(m * rows, width)

    def body(
        tokens, bucket_ids, seq_lengths, w_query, b_query, w_key, w_value, b_value, w_out, b_out,
        norm1_gain, norm1_bias, w_inner, b_inner, w_outer, b_outer, norm2_gain, norm2_bias,
        cotangent,
    ):
        row_count, block, width = tokens.shape
        count = row_count * block
        local = w_query.shape[1]
        heads = local // HEAD_DIM
        lanes = heads * LANES
        units = w_inner.shape[1]
        blk = lax.axis_index("blk").astype(i32)
        z = lax.axis_index("tensor").astype(i32)
        core = blk % 2
        member = (lax.axis_index("dp") * half_blk + blk // 2).astype(i32)
        at = jnp.stack([z, core, blk, member])
        tok = tokens.reshape(count, width)
        cot = cotangent.reshape(count, width)
        row = lambda v: v.reshape(1, -1)
        wq_t, wk_t, wv_t = w_query.T, w_key.T, w_value.T
        fence = lax.optimization_barrier

        half_of = lambda w: lax.dynamic_slice_in_dim(w, core * (w.shape[0] // 2), w.shape[0] // 2, 0)
        out_half = half_of(w_out)
        first_half = jnp.concatenate([half_of(w_inner), out_half], axis=0)
        first_z = swap(first_half, 1)
        second_z = swap(half_of(w_outer), 1)
        outs_z = [swap(out_half, s) for s in range(2, n)]
        b_inner_far = swap(b_inner, 1)

        kv, wkv_t = call(
            kv_kernel,
            (near((count, lanes), bf16), near((lanes, width), bf16)),
            "kv_rows",
            (tok, wk_t, wv_t, row(b_value)),
        )
        kv_far = flip(kv, 2)
        kv_core = flip(kv, 1)
        q = call(q_kernel, near((count, lanes), bf16), "query_rows", (tok, wq_t, row(b_query)))
        kv_far, first_z = fence((kv_far, first_z))
        kv_both = flip(kv_far, 1)
        kvs = [kv, kv_core, kv_far, kv_both]
        first_core = flip(first_z, 1)

        def attend(ids, q):
            return call(
                functools.partial(attend_kernel, n_blk, ids),
                (near((2 * PACKED, LANES), bf16), near((2 * heads * BLOCK, n_blk * BLOCK), bf16)),
                "attend",
                (at, bucket_ids, seq_lengths, q, *kvs),
                scalars=3,
            )

        q, second_z = fence((q, second_z))
        hp_other, probs_other = attend((2, 3), q)
        hps = {1: swap(hp_other, 1), 3: swap(hp_other, 3)}
        q, *outs_z = fence((q, *outs_z))
        hp_mine, probs_mine = attend((0, 1), q)
        hps[0] = hp_mine
        hps[2] = swap(hp_mine, 2)
        second_core = flip(second_z, 1)
        outs_core = [flip(v, 1) for v in outs_z]
        w_out_all, w_inner_far, w_outer_far = call(
            functools.partial(weights_kernel, n),
            (near((n * local, width), bf16), near(w_inner.shape, bf16), near(w_outer.shape, bf16)),
            "far_weights",
            (at, w_out, first_z, first_core, second_z, second_core, *outs_z, *outs_core),
            scalars=1,
        )

        chunk = lambda rows, dt: near((rows, width), dt)
        gains1 = (row(norm1_gain), row(norm1_bias))

        def ffn(i):
            return call(
                functools.partial(ffn_kernel, n, i),
                (
                    chunk(BLOCK, bf16), chunk(BLOCK, f32), near((BLOCK, LANES), f32),
                    chunk(2 * BLOCK, bf16), near((BLOCK, units), bf16), near((2 * BLOCK, units), bf16),
                ),
                "ffn",
                (
                    at, tok, w_out_all, row(b_out), *gains1, w_inner, w_inner_far, row(b_inner),
                    row(b_inner_far), w_outer, w_outer_far, *[hps[s] for s in range(n)],
                ),
                scalars=1,
                scratch=[pltpu.VMEM((n, BLOCK, width), f32)],
            )

        parts, n1s, s1s, share1, acts, slopes = map(list, zip(*[ffn(i) for i in range(2)]))
        theirs = [swap(v, 2) for v in parts]

        def ffn_back(i):
            return call(
                functools.partial(ffn_back_kernel, i),
                (
                    chunk(3 * BLOCK + 16, bf16), near((BLOCK, units), bf16), chunk(BLOCK, bf16),
                    chunk(BLOCK, f32),
                ),
                "ffn_back",
                (
                    at, cot, n1s[i], slopes[i], parts[i], theirs[i], *gains1, row(b_outer),
                    row(norm2_gain), row(norm2_bias), w_inner, w_inner_far, w_outer, w_outer_far,
                ),
                scalars=1,
            )

        share2, dinners, parts2, dres2 = map(list, zip(*[ffn_back(i) for i in range(2)]))
        theirs2 = [swap(v, 2) for v in parts2]
        *share1, theirs[1] = fence((*share1, theirs[1]))
        share1 += [swap(v, 1) for v in share1]

        def norm_back(i):
            return call(
                functools.partial(norm_back_kernel, n),
                (
                    chunk(BLOCK, f32), chunk(BLOCK + 16, bf16), near((PACKED, LANES), bf16),
                    near((PACKED, LANES), bf16),
                ),
                "norm_back",
                (at, parts2[i], theirs2[i], dres2[i], n1s[i], s1s[i], gains1[0], w_out_all),
                scalars=1,
            )

        dres1, dattn, dheads, dheads_far = map(list, zip(*[norm_back(i) for i in range(2)]))
        dheads += [swap(v, 1) for v in dheads_far]
        share2 += [swap(v, 1) for v in share2]
        dattn += [swap(v, 1) for v in dattn]

        def attend_back(i):
            return call(
                functools.partial(attend_back_kernel, n_blk, i),
                (
                    near((BLOCK, local), bf16), near((half_blk, lanes, BLOCK), bf16),
                    near((half_blk, lanes, BLOCK), bf16),
                ),
                "attend_back",
                (at, dheads[i], q, probs_mine if i < 2 else probs_other, *kvs),
                scalars=1,
            )

        thirds = [attend_back(i) for i in range(4)]

        grad_rows = width + 16 * m
        grad_rows += -grad_rows % (16 * m)
        keep1, send1 = call(
            ffn_grad_kernel,
            (chunk(grad_rows, bf16), chunk(grad_rows, bf16)),
            "ffn_grads",
            (at, *share1, *share2, *acts, *dinners),
            scalars=1,
            scratch=[pltpu.VMEM((n, 8, width), f32)],
        )
        total1 = scatter_grads(keep1, send1, member)
        mine1 = gather_grads(total1, at, "gather_ffn_grads")
        output = call(
            output_kernel,
            shape((row_count, block, width), bf16),
            "output_rows",
            (at, *share2),
            scalars=1,
        )

        recvs = [flip(t[1], 1) for t in thirds]
        fars = [
            flip((t[2][1].astype(f32) + recv[1].astype(f32)).astype(bf16), 2)
            for t, recv in zip(thirds, recvs)
        ]

        def input_part(i, *theirs):
            dq, _, keep = thirds[i]
            return call(
                input_kernel,
                (chunk(BLOCK, bf16), near((lanes, BLOCK), bf16), chunk(8, f32)),
                "input_part",
                (dq, keep, recvs[i], fars[i], wq_t, wkv_t, *theirs),
            )

        fourth = {i: input_part(i) for i in (2, 3)}
        fourth |= {i: input_part(i, swap(fourth[i + 2][0], 1)) for i in (0, 1)}
        d_toks = []
        for i in range(2):
            pair = fourth[i][0]
            total = (pair.astype(f32) + swap(pair, 2).astype(f32)) + dres1[i]
            d_toks.append(total.astype(bf16))
        d_toks += [swap(v, 1) for v in d_toks]

        rows2 = 2 * local + 16
        rows2 += -rows2 % (16 * m)
        keep2, send2 = call(
            attend_grad_kernel,
            (chunk(rows2, bf16), chunk(rows2, bf16)),
            "attend_grads",
            (
                at, tok, hp_mine, hp_other, *dattn,
                *[thirds[i][0] for i in range(4)],
                *[fourth[i][1] for i in range(4)],
                *[fourth[i][2] for i in range(4)],
            ),
            scalars=1,
            scratch=[pltpu.VMEM((n, 8, width), f32)],
        )
        vector = shape((width,), f32)
        short = shape((local,), f32)
        total2 = scatter_grads(keep2, send2, member)
        mine2 = gather_grads(total2, at, "gather_attend_grads")
        other1 = flip(mine1, 1)
        other2 = flip(mine2, 1)
        g_w_inner, g_w_outer, g_gain2, g_bias2, g_b_outer, g_b_inner = call(
            ffn_final_kernel,
            (shape((width, units), f32), shape((units, width), f32)) + (vector,) * 4,
            "ffn_grads_out",
            (at, mine1, other1),
            scalars=1,
        )
        d_tokens = call(
            rows_kernel,
            shape((row_count, block, width), bf16),
            "input_grad_rows",
            (at, *d_toks),
            scalars=1,
        )
        wide = shape((local, width), f32)
        g_w_out, g_q, g_k, g_v, g_gain1, g_bias1, g_b_out, g_b_query, g_b_value = call(
            attend_final_kernel,
            (wide,) * 4 + (vector,) * 3 + (short,) * 2,
            "attend_grads_out",
            (at, mine2, other2),
            scalars=1,
        )
        return (
            output, d_tokens, g_q.T, g_b_query, g_k.T, g_v.T, g_b_value, g_w_out, g_b_out, g_gain1,
            g_bias1, g_w_inner, g_b_inner, g_w_outer, g_b_outer, g_gain2, g_bias2,
        )

    spread, cols, vec, rows_ = P("dp", "blk", None), P(None, "tensor"), P("tensor"), P("tensor", None)
    return jax.shard_map(
        body,
        mesh=mesh,
        in_specs=(
            spread, P("dp"), P("dp", None), cols, vec, cols, cols, vec, rows_, P(), P(), P(),
            cols, vec, rows_, P(), P(), P(), spread,
        ),
        out_specs=(
            spread, spread, cols, vec, cols, cols, vec, rows_, P(), P(), P(), cols, vec, rows_,
            P(), P(), P(),
        ),
        check_vma=False,
    )
```

time: 275 us -> 265 us (0.964)
  waiting for transfers between devices: 113 us -> 131 us
  starting transfers between devices: 78.7 us -> 61.6 us
  local copies, waits for them, and re-layouts: 17.5 us -> 12 us
    ppermute x24 -> x26, waiting for transfers between devices: 72.4 us -> 103 us  [swap(): return lax.ppermute(v, 'tensor', [(i, i ^ bit) for i in range(n)])]
    ppermute x24 -> x26, starting transfers between devices: 54.6 us -> 34.7 us  [swap(): return lax.ppermute(v, 'tensor', [(i, i ^ bit) for i in range(n)])]
    ppermute x15 -> x19, waiting for transfers between devices: 22.5 us -> 9.33 us  [flip(): return lax.ppermute(v, 'blk', [(i, i ^ bit) for i in range(n_blk)])]
    unnamed x140, local copies, waits for them, and re-layouts: 17.5 us -> 9.77 us
    pallas_call x6 -> x0, other arithmetic: 3.63 us -> none  [call(): pl.pallas_call(kernel, out_shape=outs, in_specs=[SMEM] * scalars + [VMEM]...]
    ppermute x15 -> x19, starting transfers between devices: 7.03 us -> 9.54 us  [flip(): return lax.ppermute(v, 'blk', [(i, i ^ bit) for i in range(n_blk)])]
  transfers between devices with their start and end apart: 51 -> 57, of which waited for: 24 -> 25; matrix products, arithmetic and copies ran while one was open for 3% -> 3% of each run, Pallas kernels for 11% -> 17%
where the time goes in v3:
time: 265 us
  waiting for transfers between devices  131 us (49%)
  starting transfers between devices  61.6 us (23%)
  Pallas kernels  49.6 us (19%)
  local copies, waits for them, and re-layouts  12 us (5%)
  other arithmetic  8.6 us (3%)
    ppermute x26, waiting for transfers between devices, swap(): return lax.ppermute(v, 'tensor', [(i, i ^ bit) for i in range(n)])  103 us
    pallas_call x27, Pallas kernels, call(): pl.pallas_call(kernel, out_shape=outs, in_specs=[SMEM] * scalars + [VMEM]...  49.6 us
    ppermute x26, starting transfers between devices, swap(): return lax.ppermute(v, 'tensor', [(i, i ^ bit) for i in range(n)])  34.7 us
    ppermute x12, waiting for transfers between devices, flip_member(): return lax.ppermute(v, ('dp', 'blk'), perm)  19.4 us
    ppermute x12, starting transfers between devices, flip_member(): return lax.ppermute(v, ('dp', 'blk'), perm)  17.4 us
    unnamed x140, local copies, waits for them, and re-layouts  9.77 us
    ppermute x19, starting transfers between devices, flip(): return lax.ppermute(v, 'blk', [(i, i ^ bit) for i in range(n_blk)])  9.54 us
    ppermute x19, waiting for transfers between devices, flip(): return lax.ppermute(v, 'blk', [(i, i ^ bit) for i in range(n_blk)])  9.33 us
  transfers between devices with their start and end apart: 57, of which 25 were waited for; matrix products, arithmetic and copies ran while one was open for 3% of the time, Pallas kernels for 17%

profile of v3, /device:TPU:0, one launch (start us, length us, event | category | flops | bytes accessed | tf_op | source)
XLA Modules:
  0.0 264.6 jit_solution(6147565584931541751)
XLA Ops:
  3.0 3.1 %collective-permute-start.1 = (bf16[480,768]{1,0:T(8,128)(2,1)S(1)}, bf16[480,768]{1,0:T(8,128)(2,1)}, u32[]{:S(2)}, u32[]{:S(2)}) collective-permute-start(bf16[480,768]{1,0:T(8,128)(2,1)S(1)} %pad_maximum_fusion), channel_id=1, source_target_pairs={{0,1},{1,0},{2,3},{3,2},{4,5},{5,4},{6,7},{7,6},{8,9},{9,8},{10,11... | collective-permute-start | bytes 2211848 | tf_op jit(solution)/shard_map/ppermute | solution.py:417
  8.9 8.7 %collective-permute-done.refs_2_ = bf16[512,384]{1,0:T(8,128)(2,1)S(1)} collective-permute-done((bf16[512,384]{1,0:T(8,128)(2,1)S(1)}, bf16[512,384]{1,0:T(8,128)(2,1)S(1)}, u32[]{:S(2)}, u32[]{:S(2)}) %collective-permute-start) | collective-permute-done | bytes 393248 | tf_op jit(solution)/shard_map/ppermute | solution.py:420
  17.6 5.9 %collective-permute-done.1.first_z = bf16[480,768]{1,0:T(8,128)(2,1)} collective-permute-done((bf16[480,768]{1,0:T(8,128)(2,1)S(1)}, bf16[480,768]{1,0:T(8,128)(2,1)}, u32[]{:S(2)}, u32[]{:S(2)}) %collective-permute-start.1) | collective-permute-done | bytes 737312 | tf_op jit(solution)/shard_map/ppermute | solution.py:417
  24.5 10.8 %collective-permute-done.3.second_z = bf16[384,768]{1,0:T(8,128)(2,1)} collective-permute-done((bf16[384,768]{1,0:T(8,128)(2,1)S(1)}, bf16[384,768]{1,0:T(8,128)(2,1)}, u32[]{:S(2)}, u32[]{:S(2)}) %collective-permute-start.3) | collective-permute-done | bytes 589856 | tf_op jit(solution)/shard_map/ppermute | solution.py:417
  35.3 2.8 %collective-permute-start.5 = (bf16[96,768]{1,0:T(8,128)(2,1)S(1)}, bf16[96,768]{1,0:T(8,128)(2,1)}, u32[]{:S(2)}, u32[]{:S(2)}) collective-permute-start(bf16[96,768]{1,0:T(8,128)(2,1)S(1)} %copy-done.62), channel_id=1, source_target_pairs={{0,2},{1,3},{2,0},{3,1},{4,6},{5,7},{6,4},{7,5},{8,10},{9,11},{10,... | collective-permute-start | bytes 442376 | tf_op jit(solution)/shard_map/ppermute | solution.py:417
  38.1 7.8 %collective-permute-done.5.refs_0_ = bf16[96,768]{1,0:T(8,128)(2,1)} collective-permute-done((bf16[96,768]{1,0:T(8,128)(2,1)S(1)}, bf16[96,768]{1,0:T(8,128)(2,1)}, u32[]{:S(2)}, u32[]{:S(2)}) %collective-permute-start.5) | collective-permute-done | bytes 147488 | tf_op jit(solution)/shard_map/ppermute | solution.py:417
  45.8 3.5 %collective-permute-start.6 = (bf16[96,768]{1,0:T(8,128)(2,1)S(1)}, bf16[96,768]{1,0:T(8,128)(2,1)}, u32[]{:S(2)}, u32[]{:S(2)}) collective-permute-start(bf16[96,768]{1,0:T(8,128)(2,1)S(1)} %copy-done.62), channel_id=1, source_target_pairs={{0,3},{1,2},{2,1},{3,0},{4,7},{5,6},{6,5},{7,4},{8,11},{9,10},{10,... | collective-permute-start | bytes 442376 | tf_op jit(solution)/shard_map/ppermute | solution.py:417
  49.4 4.3 %collective-permute-done.6.refs_1_ = bf16[96,768]{1,0:T(8,128)(2,1)} collective-permute-done((bf16[96,768]{1,0:T(8,128)(2,1)S(1)}, bf16[96,768]{1,0:T(8,128)(2,1)}, u32[]{:S(2)}, u32[]{:S(2)}) %collective-permute-start.6) | collective-permute-done | bytes 147488 | tf_op jit(solution)/shard_map/ppermute | solution.py:417
  56.2 3.3 %attend.3 = (bf16[384,128]{1,0:T(8,128)(2,1)S(1)}, bf16[768,512]{1,0:T(8,128)(2,1)S(1)}) custom-call(s32[4]{0:T(128)S(1)} %pad_add_fusion.at, s32[4]{0:T(128)S(1)} %copy-done.58, s32[4,4]{1,0:T(4,128)S(1)} %copy-done.57, bf16[512,384]{1,0:T(8,128)(2,1)S(1)} %query_rows.1.q, bf16[512,384]{1,0:T(8,128)(2,1)S(1)} %get-tuple-element.106.refs_0_, ...), custom_call_target="tpu_custom_call" | custom-call | flops 1 | bytes 1 | tf_op jit(solution)/shard_map/attend/pallas_call | solution.py:66
  59.5 3.3 %attend.2 = (bf16[384,128]{1,0:T(8,128)(2,1)S(1)}, bf16[768,512]{1,0:T(8,128)(2,1)S(1)}) custom-call(s32[4]{0:T(128)S(1)} %pad_add_fusion.at, s32[4]{0:T(128)S(1)} %copy-done.58, s32[4,4]{1,0:T(4,128)S(1)} %copy-done.57, bf16[512,384]{1,0:T(8,128)(2,1)S(1)} %query_rows.1.q, bf16[512,384]{1,0:T(8,128)(2,1)S(1)} %get-tuple-element.106.refs_0_, ...), custom_call_target="tpu_custom_call" | custom-call | flops 1 | bytes 1 | tf_op jit(solution)/shard_map/attend/pallas_call | solution.py:66
  69.6 3.7 %collective-permute-done.13.refs_2_ = bf16[384,128]{1,0:T(8,128)(2,1)S(1)} collective-permute-done((bf16[384,128]{1,0:T(8,128)(2,1)S(1)}, bf16[384,128]{1,0:T(8,128)(2,1)S(1)}, u32[]{:S(2)}, u32[]{:S(2)}) %collective-permute-start.13) | collective-permute-done | bytes 98336 | tf_op jit(solution)/shard_map/ppermute | solution.py:417
  73.3 2.3 ffn.2
  75.7 3.7 %collective-permute-start.15 = (bf16[128,768]{1,0:T(8,128)(2,1)S(1)}, bf16[128,768]{1,0:T(8,128)(2,1)S(1)}, u32[]{:S(2)}, u32[]{:S(2)}) collective-permute-start(bf16[128,768]{1,0:T(8,128)(2,1)S(1)} %get-tuple-element.121.mine), channel_id=1, source_target_pairs={{0,2},{1,3},{2,0},{3,1},{4,6},{5,7},{6,4},{7,5},{8,10},{9,11},{10,... | collective-permute-start | bytes 589832 | tf_op jit(solution)/shard_map/ppermute | solution.py:417
  79.4 2.3 ffn.3
  81.9 11.3 %collective-permute-done.15.theirs = bf16[128,768]{1,0:T(8,128)(2,1)S(1)} collective-permute-done((bf16[128,768]{1,0:T(8,128)(2,1)S(1)}, bf16[128,768]{1,0:T(8,128)(2,1)S(1)}, u32[]{:S(2)}, u32[]{:S(2)}) %collective-permute-start.15) | collective-permute-done | bytes 196640 | tf_op jit(solution)/shard_map/ppermute | solution.py:417
  93.1 2.7 %ffn_back.2 = (bf16[400,768]{1,0:T(8,128)(2,1)S(1)}, bf16[128,768]{1,0:T(8,128)(2,1)S(1)}, bf16[128,768]{1,0:T(8,128)(2,1)S(1)}, f32[128,768]{1,0:T(8,128)S(1)}) custom-call(s32[4]{0:T(128)S(1)} %pad_add_fusion.at, bf16[512,768]{1,0:T(8,128)(2,1)S(1)} %bitcast.68, f32[128,768]{1,0:T(8,128)S(1)} %get-tuple-element.119.n1, ...), custom_call_target="tpu_custom_call" | custom-call | flops 1 | bytes 1 | tf_op jit(solution)/shard_map/ffn_back/pallas_call | solution.py:66
  97.0 2.7 %ffn_back.3 = (bf16[400,768]{1,0:T(8,128)(2,1)S(1)}, bf16[128,768]{1,0:T(8,128)(2,1)S(1)}, bf16[128,768]{1,0:T(8,128)(2,1)S(1)}, f32[128,768]{1,0:T(8,128)S(1)}) custom-call(s32[4]{0:T(128)S(1)} %pad_add_fusion.at, bf16[512,768]{1,0:T(8,128)(2,1)S(1)} %bitcast.69, f32[128,768]{1,0:T(8,128)S(1)} %get-tuple-element.123.n1, ...), custom_call_target="tpu_custom_call" | custom-call | flops 1 | bytes 1 | tf_op jit(solution)/shard_map/ffn_back/pallas_call | solution.py:66
  103.9 34.7 %collective-permute-done.47.refs_2_ = bf16[256,768]{1,0:T(8,128)(2,1)S(1)} collective-permute-done((bf16[256,768]{1,0:T(8,128)(2,1)S(1)}, bf16[256,768]{1,0:T(8,128)(2,1)S(1)}, u32[]{:S(2)}, u32[]{:S(2)}) %collective-permute-start.47) | collective-permute-done | bytes 393248 | tf_op jit(solution)/shard_map/ppermute | solution.py:417
  138.5 6.9 %collective-permute-done.48.refs_3_ = bf16[256,768]{1,0:T(8,128)(2,1)S(1)} collective-permute-done((bf16[256,768]{1,0:T(8,128)(2,1)S(1)}, bf16[256,768]{1,0:T(8,128)(2,1)S(1)}, u32[]{:S(2)}, u32[]{:S(2)}) %collective-permute-start.48) | collective-permute-done | bytes 393248 | tf_op jit(solution)/shard_map/ppermute | solution.py:417
  145.4 3.2 %ffn_grads.1 = (bf16[832,768]{1,0:T(8,128)(2,1)S(1)}, bf16[832,768]{1,0:T(8,128)(2,1)}) custom-call(s32[4]{0:T(128)S(1)} %pad_add_fusion.at, bf16[256,768]{1,0:T(8,128)(2,1)S(1)} %get-tuple-element.181.refs_0_, bf16[256,768]{1,0:T(8,128)(2,1)S(1)} %get-tuple-element.182.refs_1_, bf16[256,768]{1,0:T(8,128)(2,1)S(1)} %collective-permute-done.47.refs_2_, ...), custom_call_target="tpu_custom_call" | custom-call | flops 1 | bytes 1 | tf_op jit(solution)/shard_map/ffn_grads/pallas_call | solution.py:66
  151.8 3.1 %collective-permute-done.22.packed = bf16[192,128]{1,0:T(8,128)(2,1)S(1)} collective-permute-done((bf16[192,128]{1,0:T(8,128)(2,1)S(1)}, bf16[192,128]{1,0:T(8,128)(2,1)S(1)}, u32[]{:S(2)}, u32[]{:S(2)}) %collective-permute-start.22) | collective-permute-done | bytes 49184 | tf_op jit(solution)/shard_map/ppermute | solution.py:417
  157.2 2.9 %collective-permute-done.27.theirs = bf16[128,768]{1,0:T(8,128)(2,1)S(1)} collective-permute-done((bf16[128,768]{1,0:T(8,128)(2,1)S(1)}, bf16[128,768]{1,0:T(8,128)(2,1)S(1)}, u32[]{:S(2)}, u32[]{:S(2)}) %collective-permute-start.27) | collective-permute-done | bytes 196640 | tf_op jit(solution)/shard_map/ppermute | solution.py:417
  165.7 2.9 %attend_back.6 = (bf16[128,192]{1,0:T(8,128)(2,1)S(1)}, bf16[2,384,128]{2,1,0:T(8,128)(2,1)}, bf16[2,384,128]{2,1,0:T(8,128)(2,1)S(1)}) custom-call(s32[4]{0:T(128)S(1)} %pad_add_fusion.at, bf16[192,128]{1,0:T(8,128)(2,1)S(1)} %get-tuple-element.147.packed, bf16[512,384]{1,0:T(8,128)(2,1)S(1)} %query_rows.1.q, ...), custom_call_target="tpu_custom_call" | custom-call | flops 1 | bytes 1 | tf_op jit(solution)/shard_map/attend_back/pallas_call | solution.py:66
  193.3 2.6 collective-permute-start.52
  205.5 3.2 %collective-permute-done.51 = bf16[208,768]{1,0:T(8,128)(2,1)} collective-permute-done((bf16[208,768]{1,0:T(8,128)(2,1)}, bf16[208,768]{1,0:T(8,128)(2,1)}, u32[]{:S(2)}, u32[]{:S(2)}) %collective-permute-start.51) | collective-permute-done | bytes 319520 | tf_op jit(solution)/shard_map/ppermute | solution.py:429
  215.4 2.5 collective-permute-start.42
  218.5 2.5 collective-permute-done.53.refs_1_
  222.8 6.8 %collective-permute-done.55.refs_3_ = bf16[208,768]{1,0:T(8,128)(2,1)S(1)} collective-permute-done((bf16[208,768]{1,0:T(8,128)(2,1)S(1)}, bf16[208,768]{1,0:T(8,128)(2,1)S(1)}, u32[]{:S(2)}, u32[]{:S(2)}) %collective-permute-start.55) | collective-permute-done | bytes 319520 | tf_op jit(solution)/shard_map/ppermute | solution.py:429
  238.9 3.8 %collective-permute-done.43.refs_1_ = bf16[112,768]{1,0:T(8,128)(2,1)S(1)} collective-permute-done((bf16[112,768]{1,0:T(8,128)(2,1)S(1)}, bf16[112,768]{1,0:T(8,128)(2,1)S(1)}, u32[]{:S(2)}, u32[]{:S(2)}) %collective-permute-start.43) | collective-permute-done | bytes 172064 | tf_op jit(solution)/shard_map/ppermute | solution.py:429
  247.2 4.2 %collective-permute-done.34 = bf16[128,768]{1,0:T(8,128)(2,1)S(1)} collective-permute-done((bf16[128,768]{1,0:T(8,128)(2,1)S(1)}, bf16[128,768]{1,0:T(8,128)(2,1)S(1)}, u32[]{:S(2)}, u32[]{:S(2)}) %collective-permute-start.34) | collective-permute-done | bytes 196640 | tf_op jit(solution)/shard_map/ppermute | solution.py:417
  254.4 3.8 %collective-permute-done.36.refs_3_ = bf16[128,768]{1,0:T(8,128)(2,1)S(1)} collective-permute-done((bf16[128,768]{1,0:T(8,128)(2,1)S(1)}, bf16[128,768]{1,0:T(8,128)(2,1)S(1)}, u32[]{:S(2)}, u32[]{:S(2)}) %collective-permute-start.36) | collective-permute-done | bytes 196640 | tf_op jit(solution)/shard_map/ppermute | solution.py:417
  261.7 3.0 %ffn_grads_out.1 = (f32[768,768]{1,0:T(8,128)}, f32[768,768]{1,0:T(8,128)}, f32[768]{0:T(1024)}, f32[768]{0:T(1024)}, f32[768]{0:T(1024)}, /*index=5*/f32[768]{0:T(1024)}) custom-call(s32[4]{0:T(128)S(1)} %pad_add_fusion.at, bf16[832,768]{1,0:T(8,128)(2,1)S(1)} %bitcast.67, bf16[832,768]{1,0:T(8,128)(2,1)S(1)} %collective-permute-done.56.other), custom_call_target="tpu_custom_call" | custom-call | flops 1 | bytes 1 | tf_op jit(solution)/shard_map/ffn_grads_out/pallas_call | solution.py:66
  (272 shorter events, 94.6 us)
Async XLA Ops:
  3.0 20.5 %collective-permute-start.1 = (bf16[480,768]{1,0:T(8,128)(2,1)S(1)}, bf16[480,768]{1,0:T(8,128)(2,1)}, u32[]{:S(2)}, u32[]{:S(2)}) collective-permute-start(bf16[480,768]{1,0:T(8,128)(2,1)S(1)} %pad_maximum_fusion), channel_id=1, source_target_pairs={{0,1},{1,0},{2,3},{3,2},{4,5},{5,4},{6,7},{7,6},{8,9},{9,8},{10,11... | collective-permute-start | bytes 2211848 | tf_op jit(solution)/shard_map/ppermute | solution.py:417
  6.1 29.2 %collective-permute-start.3 = (bf16[384,768]{1,0:T(8,128)(2,1)S(1)}, bf16[384,768]{1,0:T(8,128)(2,1)}, u32[]{:S(2)}, u32[]{:S(2)}) collective-permute-start(bf16[384,768]{1,0:T(8,128)(2,1)S(1)} %constant_dynamic-slice_fusion), channel_id=1, source_target_pairs={{0,1},{1,0},{2,3},{3,2},{4,5},{5,4},{6,7},{7,6},{8,9},{9,8},{10,11... | collective-permute-start | bytes 1769480 | tf_op jit(solution)/shard_map/ppermute | solution.py:417
  23.5 43.9 %collective-permute-start.2 = (bf16[480,768]{1,0:T(8,128)(2,1)}, bf16[480,768]{1,0:T(8,128)(2,1)}, u32[]{:S(2)}, u32[]{:S(2)}) collective-permute-start(bf16[480,768]{1,0:T(8,128)(2,1)} %collective-permute-done.1.first_z), channel_id=1, source_target_pairs={{0,4},{4,0},{8,12},{12,8},{1,5},{5,1},{9,13},{13,9},{2,6},{6,2},{1... | collective-permute-start | bytes 2211848 | tf_op jit(solution)/shard_map/ppermute | solution.py:420
  23.5 30.2 %collective-permute-start.10 = (bf16[512,384]{1,0:T(8,128)(2,1)S(1)}, bf16[512,384]{1,0:T(8,128)(2,1)S(1)}, u32[]{:S(2)}, u32[]{:S(2)}) collective-permute-start(bf16[512,384]{1,0:T(8,128)(2,1)S(1)} %get-tuple-element.106.refs_0_), channel_id=1, source_target_pairs={{0,4},{4,0},{8,12},{12,8},{1,5},{5,1},{9,13},{13,9},{2,6},{6,2},{1... | collective-permute-start | bytes 1179656 | tf_op jit(solution)/shard_map/ppermute | solution.py:420
  24.0 30.2 %collective-permute-start.11 = (bf16[512,384]{1,0:T(8,128)(2,1)S(1)}, bf16[512,384]{1,0:T(8,128)(2,1)}, u32[]{:S(2)}, u32[]{:S(2)}) collective-permute-start(bf16[512,384]{1,0:T(8,128)(2,1)S(1)} %collective-permute-done.refs_2_), channel_id=1, source_target_pairs={{0,4},{4,0},{8,12},{12,8},{1,5},{5,1},{9,13},{13,9},{2,6},{6,2},{1... | collective-permute-start | bytes 1179656 | tf_op jit(solution)/shard_map/ppermute | solution.py:420
  35.3 32.1 %collective-permute-start.4 = (bf16[384,768]{1,0:T(8,128)(2,1)}, bf16[384,768]{1,0:T(8,128)(2,1)}, u32[]{:S(2)}, u32[]{:S(2)}) collective-permute-start(bf16[384,768]{1,0:T(8,128)(2,1)} %collective-permute-done.3.second_z), channel_id=1, source_target_pairs={{0,4},{4,0},{8,12},{12,8},{1,5},{5,1},{9,13},{13,9},{2,6},{6,2},{1... | collective-permute-start | bytes 1769480 | tf_op jit(solution)/shard_map/ppermute | solution.py:420
  53.7 11.4 %collective-permute-start.8 = (bf16[96,768]{1,0:T(8,128)(2,1)}, bf16[96,768]{1,0:T(8,128)(2,1)}, u32[]{:S(2)}, u32[]{:S(2)}) collective-permute-start(bf16[96,768]{1,0:T(8,128)(2,1)} %collective-permute-done.6.refs_1_), channel_id=1, source_target_pairs={{0,4},{4,0},{8,12},{12,8},{1,5},{5,1},{9,13},{13,9},{2,6},{6,2},{1... | collective-permute-start | bytes 442376 | tf_op jit(solution)/shard_map/ppermute | solution.py:420
  75.7 17.4 %collective-permute-start.15 = (bf16[128,768]{1,0:T(8,128)(2,1)S(1)}, bf16[128,768]{1,0:T(8,128)(2,1)S(1)}, u32[]{:S(2)}, u32[]{:S(2)}) collective-permute-start(bf16[128,768]{1,0:T(8,128)(2,1)S(1)} %get-tuple-element.121.mine), channel_id=1, source_target_pairs={{0,2},{1,3},{2,0},{3,1},{4,6},{5,7},{6,4},{7,5},{8,10},{9,11},{10,... | collective-permute-start | bytes 589832 | tf_op jit(solution)/shard_map/ppermute | solution.py:417
  81.7 15.3 %collective-permute-start.16 = (bf16[128,768]{1,0:T(8,128)(2,1)S(1)}, bf16[128,768]{1,0:T(8,128)(2,1)S(1)}, u32[]{:S(2)}, u32[]{:S(2)}) collective-permute-start(bf16[128,768]{1,0:T(8,128)(2,1)S(1)} %get-tuple-element.125.mine), channel_id=1, source_target_pairs={{0,2},{1,3},{2,0},{3,1},{4,6},{5,7},{6,4},{7,5},{8,10},{9,11},{10,... | collective-permute-start | bytes 589832 | tf_op jit(solution)/shard_map/ppermute | solution.py:417
  95.9 49.5 %collective-permute-start.17 = (bf16[400,768]{1,0:T(8,128)(2,1)S(1)}, bf16[400,768]{1,0:T(8,128)(2,1)S(1)}, u32[]{:S(2)}, u32[]{:S(2)}) collective-permute-start(bf16[400,768]{1,0:T(8,128)(2,1)S(1)} %get-tuple-element.122.refs_0_.refs_4_), channel_id=1, source_target_pairs={{0,1},{1,0},{2,3},{3,2},{4,5},{5,4},{6,7},{7,6},{8,9},{9,8},{10,11... | collective-permute-start | bytes 1843208 | tf_op jit(solution)/shard_map/ppermute | solution.py:417
  99.8 45.6 %collective-permute-start.18 = (bf16[400,768]{1,0:T(8,128)(2,1)S(1)}, bf16[400,768]{1,0:T(8,128)(2,1)S(1)}, u32[]{:S(2)}, u32[]{:S(2)}) collective-permute-start(bf16[400,768]{1,0:T(8,128)(2,1)S(1)} %get-tuple-element.126.refs_1_.refs_5_), channel_id=1, source_target_pairs={{0,1},{1,0},{2,3},{3,2},{4,5},{5,4},{6,7},{7,6},{8,9},{9,8},{10,11... | collective-permute-start | bytes 1843208 | tf_op jit(solution)/shard_map/ppermute | solution.py:417
  100.8 37.8 %collective-permute-start.47 = (bf16[256,768]{1,0:T(8,128)(2,1)S(1)}, bf16[256,768]{1,0:T(8,128)(2,1)S(1)}, u32[]{:S(2)}, u32[]{:S(2)}) collective-permute-start(bf16[256,768]{1,0:T(8,128)(2,1)S(1)} %get-tuple-element.181.refs_0_), channel_id=1, source_target_pairs={{0,1},{1,0},{2,3},{3,2},{4,5},{5,4},{6,7},{7,6},{8,9},{9,8},{10,11... | collective-permute-start | bytes 1179656 | tf_op jit(solution)/shard_map/ppermute | solution.py:417
  101.8 43.5 %collective-permute-start.48 = (bf16[256,768]{1,0:T(8,128)(2,1)S(1)}, bf16[256,768]{1,0:T(8,128)(2,1)S(1)}, u32[]{:S(2)}, u32[]{:S(2)}) collective-permute-start(bf16[256,768]{1,0:T(8,128)(2,1)S(1)} %get-tuple-element.182.refs_1_), channel_id=1, source_target_pairs={{0,1},{1,0},{2,3},{3,2},{4,5},{5,4},{6,7},{7,6},{8,9},{9,8},{10,11... | collective-permute-start | bytes 1179656 | tf_op jit(solution)/shard_map/ppermute | solution.py:417
  102.8 46.0 %collective-permute-start.19 = (bf16[128,768]{1,0:T(8,128)(2,1)S(1)}, bf16[128,768]{1,0:T(8,128)(2,1)S(1)}, u32[]{:S(2)}, u32[]{:S(2)}) collective-permute-start(bf16[128,768]{1,0:T(8,128)(2,1)S(1)} %get-tuple-element.127.mine), channel_id=1, source_target_pairs={{0,2},{1,3},{2,0},{3,1},{4,6},{5,7},{6,4},{7,5},{8,10},{9,11},{10,... | collective-permute-start | bytes 589832 | tf_op jit(solution)/shard_map/ppermute | solution.py:417
  148.7 39.9 %collective-permute-start.49 = (bf16[832,768]{1,0:T(8,128)(2,1)}, bf16[832,768]{1,0:T(8,128)(2,1)}, u32[]{:S(2)}, u32[]{:S(2)}) collective-permute-start(bf16[832,768]{1,0:T(8,128)(2,1)} %get-tuple-element.188), channel_id=1, source_target_pairs={{0,4},{4,0},{8,12},{12,8},{1,5},{5,1},{9,13},{13,9},{2,6},{6,2},{1... | collective-permute-start | bytes 3833864 | tf_op jit(solution)/shard_map/ppermute | solution.py:420
  148.8 11.4 %collective-permute-start.27 = (bf16[128,768]{1,0:T(8,128)(2,1)S(1)}, bf16[128,768]{1,0:T(8,128)(2,1)S(1)}, u32[]{:S(2)}, u32[]{:S(2)}) collective-permute-start(bf16[128,768]{1,0:T(8,128)(2,1)S(1)} %get-tuple-element.144.mine), channel_id=1, source_target_pairs={{0,2},{1,3},{2,0},{3,1},{4,6},{5,7},{6,4},{7,5},{8,10},{9,11},{10,... | collective-permute-start | bytes 589832 | tf_op jit(solution)/shard_map/ppermute | solution.py:417
  157.2 14.8 %collective-permute-start.23 = (bf16[2,384,128]{2,1,0:T(8,128)(2,1)S(1)}, bf16[2,384,128]{2,1,0:T(8,128)(2,1)S(1)}, u32[]{:S(2)}, u32[]{:S(2)}) collective-permute-start(bf16[2,384,128]{2,1,0:T(8,128)(2,1)S(1)} %get-tuple-element.140), channel_id=1, source_target_pairs={{0,4},{4,0},{8,12},{12,8},{1,5},{5,1},{9,13},{13,9},{2,6},{6,2},{1... | collective-permute-start | bytes 589832 | tf_op jit(solution)/shard_map/ppermute | solution.py:420
  169.1 16.4 %collective-permute-start.28 = (bf16[2,384,128]{2,1,0:T(8,128)(2,1)}, bf16[2,384,128]{2,1,0:T(8,128)(2,1)}, u32[]{:S(2)}, u32[]{:S(2)}) collective-permute-start(bf16[2,384,128]{2,1,0:T(8,128)(2,1)} %get-tuple-element.150), channel_id=1, source_target_pairs={{0,4},{4,0},{8,12},{12,8},{1,5},{5,1},{9,13},{13,9},{2,6},{6,2},{1... | collective-permute-start | bytes 589832 | tf_op jit(solution)/shard_map/ppermute | solution.py:420
  176.2 11.1 %collective-permute-start.21 = (bf16[384,128]{1,0:T(8,128)(2,1)}, bf16[384,128]{1,0:T(8,128)(2,1)}, u32[]{:S(2)}, u32[]{:S(2)}) collective-permute-start(bf16[384,128]{1,0:T(8,128)(2,1)} %fusion.12), channel_id=1, source_target_pairs={{0,8},{4,12},{8,0},{12,4},{1,9},{5,13},{9,1},{13,5},{2,10},{6,14},... | collective-permute-start | bytes 294920 | tf_op jit(solution)/shard_map/ppermute | solution.py:420
  177.8 26.1 %collective-permute-start.37 = (bf16[144,768]{1,0:T(8,128)(2,1)}, bf16[144,768]{1,0:T(8,128)(2,1)S(1)}, u32[]{:S(2)}, u32[]{:S(2)}) collective-permute-start(bf16[144,768]{1,0:T(8,128)(2,1)} %copy-done.45), channel_id=1, source_target_pairs={{0,1},{1,0},{2,3},{3,2},{4,5},{5,4},{6,7},{7,6},{8,9},{9,8},{10,11... | collective-permute-start | bytes 663560 | tf_op jit(solution)/shard_map/ppermute | solution.py:417
  182.9 21.0 %collective-permute-start.38 = (bf16[144,768]{1,0:T(8,128)(2,1)}, bf16[144,768]{1,0:T(8,128)(2,1)S(1)}, u32[]{:S(2)}, u32[]{:S(2)}) collective-permute-start(bf16[144,768]{1,0:T(8,128)(2,1)} %copy-done.47), channel_id=1, source_target_pairs={{0,1},{1,0},{2,3},{3,2},{4,5},{5,4},{6,7},{7,6},{8,9},{9,8},{10,11... | collective-permute-start | bytes 663560 | tf_op jit(solution)/shard_map/ppermute | solution.py:417
  187.3 11.1 %collective-permute-start.33 = (bf16[128,768]{1,0:T(8,128)(2,1)S(1)}, bf16[128,768]{1,0:T(8,128)(2,1)S(1)}, u32[]{:S(2)}, u32[]{:S(2)}) collective-permute-start(bf16[128,768]{1,0:T(8,128)(2,1)S(1)} %get-tuple-element.155), channel_id=1, source_target_pairs={{0,1},{1,0},{2,3},{3,2},{4,5},{5,4},{6,7},{7,6},{8,9},{9,8},{10,11... | collective-permute-start | bytes 589832 | tf_op jit(solution)/shard_map/ppermute | solution.py:417
  193.3 12.2 %collective-permute-start.52 = (bf16[208,768]{1,0:T(8,128)(2,1)}, bf16[208,768]{1,0:T(8,128)(2,1)}, u32[]{:S(2)}, u32[]{:S(2)}) collective-permute-start(bf16[208,768]{1,0:T(8,128)(2,1)} %get-tuple-element.196), channel_id=1, source_target_pairs={{0,24},{4,28},{8,16},{12,20},{16,8},{20,12},{24,0},{28,4},{1,25},{... | collective-permute-start | bytes 958472 | tf_op jit(solution)/shard_map/ppermute | solution.py:429
  195.9 12.8 %collective-permute-start.51 = (bf16[208,768]{1,0:T(8,128)(2,1)}, bf16[208,768]{1,0:T(8,128)(2,1)}, u32[]{:S(2)}, u32[]{:S(2)}) collective-permute-start(bf16[208,768]{1,0:T(8,128)(2,1)} %get-tuple-element.197), channel_id=1, source_target_pairs={{0,16},{4,20},{8,24},{12,28},{16,0},{20,4},{24,8},{28,12},{1,17},{... | collective-permute-start | bytes 958472 | tf_op jit(solution)/shard_map/ppermute | solution.py:429
  198.3 10.9 %collective-permute-start.50 = (bf16[208,768]{1,0:T(8,128)(2,1)}, bf16[208,768]{1,0:T(8,128)(2,1)}, u32[]{:S(2)}, u32[]{:S(2)}) collective-permute-start(bf16[208,768]{1,0:T(8,128)(2,1)} %get-tuple-element.195), channel_id=1, source_target_pairs={{0,8},{4,12},{8,0},{12,4},{16,24},{20,28},{24,16},{28,20},{1,9},{5... | collective-permute-start | bytes 958472 | tf_op jit(solution)/shard_map/ppermute | solution.py:429
  213.7 15.8 %collective-permute-start.55 = (bf16[208,768]{1,0:T(8,128)(2,1)S(1)}, bf16[208,768]{1,0:T(8,128)(2,1)S(1)}, u32[]{:S(2)}, u32[]{:S(2)}) collective-permute-start(bf16[208,768]{1,0:T(8,128)(2,1)S(1)} %fusion.2.refs_0_), channel_id=1, source_target_pairs={{0,24},{4,28},{8,16},{12,20},{16,8},{20,12},{24,0},{28,4},{1,25},{... | collective-permute-start | bytes 958472 | tf_op jit(solution)/shard_map/ppermute | solution.py:429
  215.4 17.2 %collective-permute-start.42 = (bf16[112,768]{1,0:T(8,128)(2,1)S(1)}, bf16[112,768]{1,0:T(8,128)(2,1)S(1)}, u32[]{:S(2)}, u32[]{:S(2)}) collective-permute-start(bf16[112,768]{1,0:T(8,128)(2,1)S(1)} %get-tuple-element.199), channel_id=1, source_target_pairs={{0,24},{4,28},{8,16},{12,20},{16,8},{20,12},{24,0},{28,4},{1,25},{... | collective-permute-start | bytes 516104 | tf_op jit(solution)/shard_map/ppermute | solution.py:429
  217.9 16.4 %collective-permute-start.41 = (bf16[112,768]{1,0:T(8,128)(2,1)S(1)}, bf16[112,768]{1,0:T(8,128)(2,1)S(1)}, u32[]{:S(2)}, u32[]{:S(2)}) collective-permute-start(bf16[112,768]{1,0:T(8,128)(2,1)S(1)} %get-tuple-element.200), channel_id=1, source_target_pairs={{0,16},{4,20},{8,24},{12,28},{16,0},{20,4},{24,8},{28,12},{1,17},{... | collective-permute-start | bytes 516104 | tf_op jit(solution)/shard_map/ppermute | solution.py:429
  221.0 13.3 %collective-permute-start.40 = (bf16[112,768]{1,0:T(8,128)(2,1)S(1)}, bf16[112,768]{1,0:T(8,128)(2,1)S(1)}, u32[]{:S(2)}, u32[]{:S(2)}) collective-permute-start(bf16[112,768]{1,0:T(8,128)(2,1)S(1)} %get-tuple-element.198), channel_id=1, source_target_pairs={{0,8},{4,12},{8,0},{12,4},{16,24},{20,28},{24,16},{28,20},{1,9},{5... | collective-permute-start | bytes 516104 | tf_op jit(solution)/shard_map/ppermute | solution.py:429
  230.2 31.5 %collective-permute-start.56 = (bf16[832,768]{1,0:T(8,128)(2,1)S(1)}, bf16[832,768]{1,0:T(8,128)(2,1)S(1)}, u32[]{:S(2)}, u32[]{:S(2)}) collective-permute-start(bf16[832,768]{1,0:T(8,128)(2,1)S(1)} %bitcast.66), channel_id=1, source_target_pairs={{0,4},{4,0},{8,12},{12,8},{1,5},{5,1},{9,13},{13,9},{2,6},{6,2},{1... | collective-permute-start | bytes 3833864 | tf_op jit(solution)/shard_map/ppermute | solution.py:420
  230.3 15.5 %collective-permute-start.26 = (bf16[128,768]{1,0:T(8,128)(2,1)S(1)}, bf16[128,768]{1,0:T(8,128)(2,1)S(1)}, u32[]{:S(2)}, u32[]{:S(2)}) collective-permute-start(bf16[128,768]{1,0:T(8,128)(2,1)S(1)} %copy-done.52), channel_id=1, source_target_pairs={{0,2},{1,3},{2,0},{3,1},{4,6},{5,7},{6,4},{7,5},{8,10},{9,11},{10,... | collective-permute-start | bytes 589832 | tf_op jit(solution)/shard_map/ppermute | solution.py:417
  245.7 14.0 %collective-permute-start.46 = (bf16[448,768]{1,0:T(8,128)(2,1)S(1)}, bf16[448,768]{1,0:T(8,128)(2,1)S(1)}, u32[]{:S(2)}, u32[]{:S(2)}) collective-permute-start(bf16[448,768]{1,0:T(8,128)(2,1)S(1)} %bitcast.70), channel_id=1, source_target_pairs={{0,4},{4,0},{8,12},{12,8},{1,5},{5,1},{9,13},{13,9},{2,6},{6,2},{1... | collective-permute-start | bytes 2064392 | tf_op jit(solution)/shard_map/ppermute | solution.py:420
  (95 other events, 952.3 us)

commit v4 on v3

v4 whole, which is shorter than its diff:
```python
import functools

import jax
import jax.numpy as jnp
from jax import lax
from jax.experimental import pallas as pl
from jax.experimental.pallas import tpu as pltpu
from jax.sharding import PartitionSpec as P

HEAD_DIM = 64
BLOCK = 128
LANES = 128
SCALE = HEAD_DIM**-0.5
EPS = 1e-12
f32 = jnp.float32
bf16 = jnp.bfloat16
i32 = jnp.int32
MIB = 1 << 20
FLOPS_US = 1e9
ATTEND_US = 50.0
BACK_US = 50.0
PACKED = BLOCK + HEAD_DIM


def nn(a, b):
    return lax.dot_general(a, b, (((1,), (0,)), ((), ())), preferred_element_type=f32)


def nt(a, b):
    return lax.dot_general(a, b, (((1,), (1,)), ((), ())), preferred_element_type=f32)


def tn(a, b):
    return lax.dot_general(a, b, (((0,), (0,)), ((), ())), preferred_element_type=f32)


def mean(v):
    return jnp.mean(v, axis=-1, keepdims=True)


def col_sum(v):
    return jnp.sum(v, axis=0, keepdims=True)


def row_at(at, i):
    half = at[0] % 2
    return 2 * half + i if i < 2 else 2 * (1 - half) + (i - 2)


def rows8(*rows):
    width = rows[0].shape[1]
    pad = jnp.zeros((8 - len(rows), width), f32)
    return jnp.concatenate(rows + (pad,), axis=0)


def shape(dims, dtype):
    return jax.ShapeDtypeStruct(dims, dtype)


def near(dims, dtype):
    return pltpu.VMEM(dims, dtype)


SMEM = pl.BlockSpec(memory_space=pltpu.SMEM)
VMEM = pl.BlockSpec(memory_space=pltpu.VMEM)


def call(kernel, outs, name, args, scalars=0, us=1.0, vmem=16, scratch=()):
    return pl.pallas_call(
        kernel,
        out_shape=outs,
        in_specs=[SMEM] * scalars + [VMEM] * (len(args) - scalars),
        out_specs=jax.tree.map(lambda _: VMEM, outs),
        scratch_shapes=list(scratch),
        compiler_params=pltpu.CompilerParams(vmem_limit_bytes=vmem * MIB),
        cost_estimate=pl.CostEstimate(flops=int(us * FLOPS_US), bytes_accessed=1, transcendentals=0),
        name=name,
    )(*args)


def chunk_of(ref, c, rows):
    return ref[pl.ds(pl.multiple_of(c * rows, rows), rows), :]


def kv_kernel(tok, wk_t, wv_t, bv, kv, wkv_t):
    heads = wk_t.shape[0] // HEAD_DIM
    rows, bias = [], []
    for h in range(heads):
        part = slice(h * HEAD_DIM, (h + 1) * HEAD_DIM)
        rows += [wk_t[part, :], wv_t[part, :]]
        bias += [jnp.zeros((1, HEAD_DIM), f32), bv[:, part]]
    both = jnp.concatenate(rows, axis=0)
    wkv_t[...] = both
    kv[...] = (nt(tok[...], both) + jnp.concatenate(bias, axis=1)).astype(bf16)


def q_kernel(tok, wq_t, bq, q):
    heads = wq_t.shape[0] // HEAD_DIM
    full = (nt(tok[...], wq_t[...]) + bq[...]).astype(bf16) * jnp.asarray(SCALE, bf16)
    zero = jnp.zeros((full.shape[0], HEAD_DIM), bf16)
    cols = []
    for h in range(heads):
        cols += [full[:, h * HEAD_DIM : (h + 1) * HEAD_DIM], zero]
    q[...] = jnp.concatenate(cols, axis=1)


def piece_kernel(at, w_in, w_outer, w_out, piece, out_piece, sems):
    tail = out_piece.shape[0]
    half = (piece.shape[0] - tail) // 2

    def part(ref, index, size):
        return ref.at[pl.ds(pl.multiple_of(index * size, 16), size), :]

    copies = [
        pltpu.make_async_copy(part(w_in, at[4], half), piece.at[pl.ds(0, half), :], sems.at[0]),
        pltpu.make_async_copy(part(w_outer, at[4], half), piece.at[pl.ds(half, half), :], sems.at[1]),
        pltpu.make_async_copy(part(w_out, at[2], tail), out_piece, sems.at[2]),
    ]
    for copy in copies:
        copy.start()
    for copy in copies:
        copy.wait()
    piece[2 * half :, :] = out_piece[...]


def weights_kernel(n, at, w_out, *refs):
    pieces, (w_out_all, w_in_far, w_outer_far) = refs[:8], refs[8:]
    z = at[0]
    local = w_out.shape[0]
    part = local // 4
    rows = w_in_far.shape[0] // 8

    def put(ref, base, value):
        size = value.shape[0]
        ref[pl.ds(pl.multiple_of(base, 16), size), :] = value

    put(w_out_all, z * local, w_out[...])
    for j, piece in enumerate(pieces):
        put(w_in_far, (at[4] ^ j) * rows, piece[:rows, :])
        put(w_outer_far, (at[4] ^ j) * rows, piece[rows : 2 * rows, :])
        for s in range(1, n if j < 4 else 0):
            base = 2 * rows + (s - 1) * part
            put(w_out_all, (z ^ s) * local + (at[2] ^ j) * part, piece[base : base + part, :])


def attend_kernel(n_blk, ids, at, bucket, lens, q, *refs):
    kvs, outs_to = refs[:n_blk], refs[n_blk:]
    heads = q.shape[1] // LANES
    b = at[2]
    q_at = lax.broadcasted_iota(i32, (BLOCK, 1), 0)
    k_at = lax.broadcasted_iota(i32, (1, BLOCK), 1)
    for order, row in enumerate(ids):
        hp, probs = outs_to[2 * (order // 2)], outs_to[2 * (order // 2) + 1]
        i = order % 2
        r = row_at(at, row)
        bk = bucket[r]
        size = BLOCK << bk
        slot = b >> bk
        limit = lens[r, slot]
        q_in = jnp.where(q_at + (b * BLOCK - slot * size) < limit, 1, 0)
        k_in = []
        for j in range(n_blk):
            kb = b ^ j
            k_slot = kb >> bk
            inside = jnp.where(k_at + (kb * BLOCK - k_slot * size) < limit, 1, 0)
            k_in.append(jnp.where(k_slot == slot, inside, 2))
        allowed = q_in == jnp.concatenate(k_in, axis=1)
        here = pl.ds(pl.multiple_of(r * BLOCK, BLOCK), BLOCK)
        outs = []
        for h in range(heads):
            lanes = slice(h * LANES, (h + 1) * LANES)
            kvh = jnp.concatenate([kv[here, lanes] for kv in kvs], axis=0)
            scores = jnp.where(allowed, nt(q[here, lanes], kvh), -1e30)
            weights = jnp.exp(scores - jnp.max(scores, axis=-1, keepdims=True))
            total = jnp.sum(weights, axis=-1, keepdims=True)
            p = (weights / total).astype(bf16)
            probs[(i * heads + h) * BLOCK : (i * heads + h + 1) * BLOCK, :] = p
            outs.append(nn(p, kvh)[:, HEAD_DIM:].astype(bf16))
        base = i * PACKED
        hp[base : base + BLOCK, :] = jnp.concatenate(outs[:2], axis=1)
        hp[base + BLOCK : base + PACKED, :] = jnp.concatenate(
            [outs[2][:HEAD_DIM], outs[2][HEAD_DIM:]], axis=1
        )


def unpack(h):
    odd = jnp.concatenate([h[BLOCK:, :HEAD_DIM], h[BLOCK:, HEAD_DIM:]], axis=0)
    return jnp.concatenate([h[:BLOCK, :], odd], axis=1)


def pack(v):
    odd = jnp.concatenate([v[:HEAD_DIM, LANES:], v[HEAD_DIM:, LANES:]], axis=1)
    return jnp.concatenate([v[:, :LANES], odd], axis=0)


def gelu_and_slope(inner):
    cdf = 0.5 * (1.0 + lax.erf(inner * (0.5**0.5)))
    slope = cdf + inner * (0.3989422804014327 * jnp.exp(-0.5 * inner * inner))
    return (inner * cdf).astype(bf16), slope.astype(bf16)


def ffn_kernel(
    n, i, at, tok, w_out, b_out, g1, b1, w_in, w_in_far, b_in, b_in_far, w_outer, w_outer_far, *refs
):
    hps = refs[:n]
    part, n1_out, s1_out, low_out, act_out, act_far_out, slopes, held = refs[n:]
    z = at[0]
    local = w_out.shape[0] // n
    for s in range(n):
        j = z ^ s
        held[j] = nn(unpack(hps[s][i * PACKED : (i + 1) * PACKED, :]), chunk_of(w_out, j, local))
    attn = held[0]
    for j in range(1, n):
        attn = attn + held[j]
    resid = chunk_of(tok, row_at(at, i), BLOCK).astype(f32) + (attn + b_out[...])
    center = resid - mean(resid)
    s1 = lax.rsqrt(mean(center * center) + EPS)
    n1 = center * s1
    low = (n1 * g1[...] + b1[...]).astype(bf16)
    act, slope = gelu_and_slope(nn(low, w_in[...]) + b_in[...])
    act_far, slope_far = gelu_and_slope(nn(low, w_in_far[...]) + b_in_far[...])
    part[...] = (nn(act, w_outer[...]) + nn(act_far, w_outer_far[...])).astype(bf16)
    n1_out[...] = n1
    s1_out[...] = jnp.broadcast_to(s1, s1_out.shape)
    low_out[...] = low
    act_out[...] = act
    act_far_out[...] = act_far
    slopes[:BLOCK, :] = slope
    slopes[BLOCK:, :] = slope_far


def ffn_back_kernel(
    i, at, cot, n1, slopes, mine, theirs, g1, b1, b_outer, g2, b2, w_in, w_in_far, w_outer,
    w_outer_far, out, dffn_out, dinner_out, dinner_far_out, part, dres2_out, sums
):
    hidden = n1[...] * g1[...] + b1[...]
    ffn = mine[...].astype(f32) + theirs[...].astype(f32)
    resid = hidden + (ffn + b_outer[...])
    center = resid - mean(resid)
    s2 = lax.rsqrt(mean(center * center) + EPS)
    n2 = center * s2
    ct = chunk_of(cot, row_at(at, i), BLOCK).astype(f32)
    dn = ct * g2[...]
    dres2 = s2 * (dn - mean(dn) - n2 * mean(dn * n2))
    dffn = dres2.astype(bf16)
    dinner = (nt(dffn, w_outer[...]) * slopes[:BLOCK, :].astype(f32)).astype(bf16)
    dinner_far = (nt(dffn, w_outer_far[...]) * slopes[BLOCK:, :].astype(f32)).astype(bf16)
    part[...] = (nt(dinner, w_in[...]) + nt(dinner_far, w_in_far[...])).astype(bf16)
    dres2_out[...] = dres2
    dinner_out[...] = dinner
    out[...] = (n2 * g2[...] + b2[...]).astype(bf16)
    dffn_out[...] = dffn
    dinner_far_out[...] = dinner_far
    sums[...] = rows8(
        col_sum(ct * n2), col_sum(ct), col_sum(dffn.astype(f32)),
        col_sum(dinner.astype(f32)), col_sum(dinner_far.astype(f32)),
    )


def norm_back_kernel(n, at, mine, theirs, dres2, n1, s1, g1, w_out, dres1_out, dattn_out, sums, dh, dh_far):
    dhidden = (mine[...].astype(f32) + theirs[...].astype(f32)) + dres2[...]
    norm = n1[...]
    dn = dhidden * g1[...]
    dres1 = s1[:, :1] * (dn - mean(dn) - norm * mean(dn * norm))
    dattn = dres1.astype(bf16)
    dres1_out[...] = dres1
    dattn_out[...] = dattn
    sums[...] = rows8(col_sum(dhidden * norm), col_sum(dhidden), col_sum(dattn.astype(f32)))
    local = w_out.shape[0] // n
    dh[...] = pack(nt(dattn, chunk_of(w_out, at[0], local)).astype(bf16))
    dh_far[...] = pack(nt(dattn, chunk_of(w_out, at[0] ^ 1, local)).astype(bf16))


def attend_back_kernel(n_blk, ids, at, first, second, q, probs, *refs):
    kvs = refs[:n_blk]
    dq_out, send, keep = refs[n_blk:]
    heads = q.shape[1] // LANES
    zero = jnp.zeros((BLOCK, HEAD_DIM), bf16)
    for i, packed in enumerate((first, second)):
        c = row_at(at, ids[i])
        here = pl.ds(pl.multiple_of(c * BLOCK, BLOCK), BLOCK)
        flat = unpack(packed[...])
        dqs = []
        for h in range(heads):
            lanes = slice(h * LANES, (h + 1) * LANES)
            dhead = jnp.concatenate([zero, flat[:, h * HEAD_DIM : (h + 1) * HEAD_DIM]], axis=1)
            kvh = jnp.concatenate([kv[here, lanes] for kv in kvs], axis=0)
            at_p = (i * heads + h) * BLOCK
            p = probs[at_p : at_p + BLOCK, :]
            pf = p.astype(f32)
            dp = nt(dhead, kvh)
            delta = jnp.sum(pf * dp, axis=-1, keepdims=True)
            ds = (pf * (dp - delta)).astype(bf16)
            dqs.append((nn(ds, kvh) * SCALE)[:, :HEAD_DIM].astype(bf16))
            left = jnp.concatenate([q[here, lanes], dhead], axis=0)
            dkv = tn(left, jnp.concatenate([ds, p], axis=0)).astype(bf16)
            for j in range(n_blk):
                target = keep if j % 2 == 0 else send
                target[j // 2, i, lanes, :] = dkv[:, j * BLOCK : (j + 1) * BLOCK]
        dq_out[i * BLOCK : (i + 1) * BLOCK, :] = jnp.concatenate(dqs, axis=1)


def input_kernel(dq, keep, recv, far, wq_t, wkv_t, *refs):
    theirs, (part, dkv_t, sums) = refs[:-3], refs[-3:]
    total = keep[0].astype(f32) + recv[0].astype(f32) + far[...].astype(f32)
    lows = [total[i].astype(bf16) for i in range(2)]
    low = jnp.concatenate([v.T for v in lows], axis=0)
    grad = nn(dq[...], wq_t[...]) + nn(low, wkv_t[...])
    if theirs:
        grad = grad + theirs[0][...].astype(f32)
    part[...] = grad.astype(bf16)
    dkv_t[...] = jnp.concatenate(lows, axis=1)
    width = sums.shape[1]
    one = col_sum(dq[...].astype(f32))
    two = col_sum(low.astype(f32))
    sums[...] = rows8(
        jnp.concatenate([one, jnp.zeros((1, width - one.shape[1]), f32)], axis=1),
        jnp.concatenate([two, jnp.zeros((1, width - two.shape[1]), f32)], axis=1),
    )


def pick(first, one, other):
    return jnp.where(first, one, other)


def join(values, axis=0):
    return jnp.concatenate(list(values), axis=axis)


def ffn_grad_kernel(m, at, hp_mine, hp_near, *refs):
    low, act, act_far, dffn, dinner, dinner_far, dattn, sums2, sums1 = (
        refs[2 * i : 2 * i + 2] for i in range(9)
    )
    keep, send = refs[18:]
    first = at[1] == 0
    both = lambda pair: join(x[...] for x in pair)
    lows, dffns, dattns = both(low), both(dffn), both(dattn)
    tail2 = sums2[0][...] + sums2[1][...]
    tail1 = sums1[0][...] + sums1[1][...]
    rows = lows.shape[1] // m
    out_rows = keep.shape[2] - rows - 16
    for q, (acts, dinners, hp) in enumerate(
        ((both(act), both(dinner), hp_mine), (both(act_far), both(dinner_far), hp_near))
    ):
        heads = join(unpack(hp[i * PACKED : (i + 1) * PACKED, :]) for i in range(2))
        g_out = tn(heads, dattns).astype(bf16)
        cut = g_out.shape[0] // 2
        tail = join([tail2[:3], tail2[3 + q : 4 + q], tail1[:3], jnp.zeros((9, tail1.shape[1]), f32)])
        tail = tail.astype(bf16)
        for target, one in ((keep, first), (send, jnp.logical_not(first))):
            main = tn(pick(one, lows, acts), pick(one, dinners, dffns)).astype(bf16)
            outs = pick(one, g_out[:cut], g_out[cut:])
            for i in range(m):
                target[i, q, :rows, :] = main[i * rows : (i + 1) * rows]
                if i * out_rows < cut:
                    block = outs[i * out_rows : (i + 1) * out_rows]
                else:
                    block = jnp.zeros((out_rows, outs.shape[1]), bf16)
                target[i, q, rows : rows + out_rows, :] = block
                target[i, q, rows + out_rows :, :] = tail


def attend_grad_kernel(m, at, tok, *refs):
    dq, dkv_t, sums = (refs[2 * i : 2 * i + 2] for i in range(3))
    keep, send = refs[6:]
    first = at[1] == 0
    toks = join(chunk_of(tok, row_at(at, i), BLOCK) for i in range(4))
    g_q = tn(join(x[...] for x in dq), toks)
    g_kv = nn(join((x[...] for x in dkv_t), axis=1), toks)
    half = (g_q.shape[0] + g_kv.shape[0]) // 2
    cut = half - g_q.shape[0]
    one = join([g_q, g_kv[:cut]]).astype(bf16)
    two = g_kv[cut:].astype(bf16)
    total = sums[0][...] + sums[1][...]
    rest = keep.shape[0] - half
    tail = join([total, jnp.zeros((rest - 8, total.shape[1]), f32)]).astype(bf16)
    keep[:half, :] = pick(first, one, two)
    keep[half:, :] = tail
    send[:half, :] = pick(first, two, one)
    send[half:, :] = tail


def gather_kernel(m, at, *refs):
    out = refs[m]
    for s in range(m):
        out[at[3] ^ s] = refs[s][...]


def ffn_final_kernel(m, at, mine, other, g_in, g_outer, g_out, *vectors):
    first = at[1] == 0
    rows = g_in.shape[0] // m
    out_rows = mine.shape[1] - rows - 16
    cut = g_out.shape[0] // 2
    for i in range(m):
        a, b = mine[i], other[i]
        one = pick(first, a, b).astype(f32)
        two = pick(first, b, a).astype(f32)
        g_in[i * rows : (i + 1) * rows, :] = one[:rows]
        g_outer[i * rows : (i + 1) * rows, :] = two[:rows]
        if i * out_rows < cut:
            at_row = i * out_rows
            g_out[at_row : at_row + out_rows, :] = one[rows : rows + out_rows]
            g_out[cut + at_row : cut + at_row + out_rows, :] = two[rows : rows + out_rows]
        if i == 0:
            for k, ref in enumerate(vectors):
                ref[...] = one[rows + out_rows + k]


def attend_final_kernel(at, mine, other, g_q, g_k, g_v, b_q, b_v):
    first = at[1] == 0
    width = g_q.shape[0]
    half = 3 * width // 2
    a = mine[...]
    b = other[...]
    one = pick(first, a, b).astype(f32)
    two = pick(first, b, a).astype(f32)
    g_q[...] = one[:width]
    g_kv = join([one[width:half], two[:half]])
    tail = one[half : half + 8]
    values = []
    for h in range(width // HEAD_DIM):
        part = slice(h * HEAD_DIM, (h + 1) * HEAD_DIM)
        g_k[part, :] = g_kv[h * LANES : h * LANES + HEAD_DIM]
        g_v[part, :] = g_kv[h * LANES + HEAD_DIM : (h + 1) * LANES]
        values.append(tail[1:2, h * LANES + HEAD_DIM : (h + 1) * LANES])
    b_q[...] = tail[0, :width]
    b_v[...] = jnp.concatenate(values, axis=1)[0]


def rows_kernel(at, *refs):
    out = refs[-1]
    rows = [v[i * BLOCK : (i + 1) * BLOCK, :] for v in refs[:-1] for i in range(v.shape[0] // BLOCK)]
    for i, value in enumerate(rows):
        out[row_at(at, i)] = value


def solution(mesh):
    n_dp = mesh.shape["dp"]
    n_blk = mesh.shape["blk"]
    n = mesh.shape["tensor"]
    half_blk = n_blk // 2
    m = n_dp * half_blk

    def swap(v, bit):
        return lax.ppermute(v, "tensor", [(i, i ^ bit) for i in range(n)])

    def flip(v, bit):
        return lax.ppermute(v, "blk", [(i, i ^ bit) for i in range(n_blk)])

    def flip_member(v, s):
        perm = []
        for dp in range(n_dp):
            for blk in range(n_blk):
                i = (dp * half_blk + blk // 2) ^ s
                to = (i // half_blk) * n_blk + (i % half_blk) * 2 + blk % 2
                perm.append((dp * n_blk + blk, to))
        return lax.ppermute(v, ("dp", "blk"), perm)

    def share_pieces(keep, recv, member):
        def piece(s):
            mine = lax.dynamic_index_in_dim(keep, member ^ s, 0, keepdims=False)
            theirs = lax.dynamic_index_in_dim(recv, member ^ s, 0, keepdims=False)
            return (mine.astype(f32) + theirs.astype(f32)).astype(bf16)

        return [piece(s) for s in range(m)]

    def add(own, got):
        total = own.astype(f32)
        for part in got:
            total = total + part.astype(f32)
        return total.astype(bf16)

    def gather_grads(total, at, name):
        rows, width = total.shape
        every = [total] + [flip_member(total, s) for s in range(1, m)]
        mine = call(
            functools.partial(gather_kernel, m),
            near((m, rows, width), bf16),
            name,
            (at, *every),
            scalars=1,
        )
        return mine

    def body(
        tokens, bucket_ids, seq_lengths, w_query, b_query, w_key, w_value, b_value, w_out, b_out,
        norm1_gain, norm1_bias, w_inner, b_inner, w_outer, b_outer, norm2_gain, norm2_bias,
        cotangent,
    ):
        row_count, block, width = tokens.shape
        count = row_count * block
        local = w_query.shape[1]
        heads = local // HEAD_DIM
        lanes = heads * LANES
        units = w_inner.shape[1]
        blk = lax.axis_index("blk").astype(i32)
        z = lax.axis_index("tensor").astype(i32)
        core = blk % 2
        member = (lax.axis_index("dp") * half_blk + blk // 2).astype(i32)
        cut_at = (lax.axis_index("dp") % 2) * n_blk + blk
        at = jnp.stack([z, core, blk, member, cut_at]).astype(i32)
        tok = tokens.reshape(count, width)
        cot = cotangent.reshape(count, width)
        row = lambda v: v.reshape(1, -1)
        wq_t, wk_t, wv_t = w_query.T, w_key.T, w_value.T
        fence = lax.optimization_barrier

        part = local // 4
        piece_rows = (width + units) // 8
        piece, out_piece = pl.pallas_call(
            piece_kernel,
            out_shape=(near((piece_rows + part, width), bf16), near((part, width), bf16)),
            in_specs=[SMEM] + [pl.BlockSpec(memory_space=pl.ANY)] * 3,
            out_specs=(VMEM, VMEM),
            scratch_shapes=[pltpu.SemaphoreType.DMA((3,))],
            compiler_params=pltpu.CompilerParams(vmem_limit_bytes=8 * MIB),
            name="weight_piece",
        )(at, w_inner, w_outer, w_out)
        kv, wkv_t = call(
            kv_kernel,
            (near((count, lanes), bf16), near((lanes, width), bf16)),
            "kv_rows",
            (tok, wk_t, wv_t, row(b_value)),
        )
        kv, piece, out_piece, b_far = fence((kv, piece, out_piece, b_inner))
        kv_far = flip(kv, 2)
        kv_core = flip(kv, 1)
        pieces = [swap(piece, 1)] + [swap(out_piece, s) for s in range(2, n)]
        b_inner_far = swap(b_far, 1)
        kv_far, *pieces = fence((kv_far, *pieces))
        own_piece = jnp.concatenate(pieces, axis=0)
        ffn_piece = pieces[0][:piece_rows]

        def across(v, dp_bit, blk_bit):
            there = lambda i: ((i // n_blk) ^ dp_bit) * n_blk + ((i % n_blk) ^ blk_bit)
            return lax.ppermute(v, ("dp", "blk"), [(i, there(i)) for i in range(n_dp * n_blk)])

        arrived = {0: own_piece, 2: across(own_piece, 0, 2)}
        arrived |= {4: across(ffn_piece, 1, 0), 6: across(ffn_piece, 1, 2)}

        q = call(q_kernel, near((count, lanes), bf16), "query_rows", (tok, wq_t, row(b_query)), us=0.5)
        kv_both = flip(kv_far, 1)
        kvs = [kv, kv_core, kv_far, kv_both]

        pair = (near((2 * PACKED, LANES), bf16), near((2 * heads * BLOCK, n_blk * BLOCK), bf16))
        hp_other, probs_other, hp_mine, probs_mine = call(
            functools.partial(attend_kernel, n_blk, (2, 3, 0, 1)),
            pair + pair,
            "attend",
            (at, bucket_ids, seq_lengths, q, *kvs),
            us=ATTEND_US,
            scalars=3,
        )
        hps = {0: hp_mine, 1: swap(hp_other, 1), 2: swap(hp_mine, 2), 3: swap(hp_other, 3)}
        held = [arrived[2], arrived[4], arrived[6], b_inner_far]
        hps[1], *held = fence((hps[1], *held))
        arrived[2], arrived[4], arrived[6], b_inner_far = held
        arrived |= {j + 1: flip(v, 1) for j, v in arrived.items()}
        w_out_all, w_inner_far, w_outer_far = call(
            functools.partial(weights_kernel, n),
            (near((n * local, width), bf16), near(w_inner.shape, bf16), near(w_outer.shape, bf16)),
            "far_weights",
            (at, w_out, *[arrived[j] for j in range(8)]),
            us=2.2,
            scalars=1,
        )

        chunk = lambda rows, dt: near((rows, width), dt)
        gains1 = (row(norm1_gain), row(norm1_bias))

        def ffn(i):
            return call(
                functools.partial(ffn_kernel, n, i),
                (
                    chunk(BLOCK, bf16), chunk(BLOCK, f32), near((BLOCK, LANES), f32),
                    chunk(BLOCK, bf16), near((BLOCK, units), bf16), near((BLOCK, units), bf16),
                    near((2 * BLOCK, units), bf16),
                ),
                "ffn",
                (
                    at, tok, w_out_all, row(b_out), *gains1, w_inner, w_inner_far, row(b_inner),
                    row(b_inner_far), w_outer, w_outer_far, *[hps[s] for s in range(n)],
                ),
                us=2.4,
                scalars=1,
                scratch=[pltpu.VMEM((n, BLOCK, width), f32)],
            )

        parts, n1s, s1s, lows, acts, acts_far, slopes = map(list, zip(*[ffn(i) for i in range(2)]))
        theirs = [swap(v, 2) for v in parts]

        def ffn_back(i):
            return call(
                functools.partial(ffn_back_kernel, i),
                (
                    chunk(BLOCK, bf16), chunk(BLOCK, bf16), near((BLOCK, units), bf16),
                    near((BLOCK, units), bf16), chunk(BLOCK, bf16), chunk(BLOCK, f32), chunk(8, f32),
                ),
                "ffn_back",
                (
                    at, cot, n1s[i], slopes[i], parts[i], theirs[i], *gains1, row(b_outer),
                    row(norm2_gain), row(norm2_bias), w_inner, w_inner_far, w_outer, w_outer_far,
                ),
                us=2.7,
                scalars=1,
            )

        outs, dffns, dinners, dinners_far, parts2, dres2, sums2 = map(list, zip(*[ffn_back(i) for i in range(2)]))
        theirs2 = [swap(v, 2) for v in parts2]
        def norm_back(i):
            return call(
                functools.partial(norm_back_kernel, n),
                (
                    chunk(BLOCK, f32), chunk(BLOCK, bf16), chunk(8, f32), near((PACKED, LANES), bf16),
                    near((PACKED, LANES), bf16),
                ),
                "norm_back",
                (at, parts2[i], theirs2[i], dres2[i], n1s[i], s1s[i], gains1[0], w_out_all),
                us=1.2,
                scalars=1,
            )

        dres1, dattn, sums1, dheads, dheads_far = map(list, zip(*[norm_back(i) for i in range(2)]))
        dheads += [swap(v, 1) for v in dheads_far]
        outs += [swap(v, 1) for v in outs]

        def attend_back(ids, probs, *packed):
            return call(
                functools.partial(attend_back_kernel, n_blk, ids),
                (
                    near((2 * BLOCK, local), bf16), near((half_blk, 2, lanes, BLOCK), bf16),
                    near((half_blk, 2, lanes, BLOCK), bf16),
                ),
                "attend_back",
                (at, *packed, q, probs, *kvs),
                scalars=1,
                us=BACK_US,
            )

        own = attend_back((0, 1), probs_mine, dheads[0], dheads[1])
        after, dheads[2], dheads[3] = fence((own[1], dheads[2], dheads[3]))
        own = (own[0], after, own[2])
        other = attend_back((2, 3), probs_other, dheads[2], dheads[3])

        out_rows = local // 2 // m
        out_rows += -out_rows % 16
        grad_rows = width // m + out_rows + 16
        after, dattn[0] = fence((other[1], dattn[0]))
        other = (other[0], after, other[2])
        keep1, send1 = call(
            functools.partial(ffn_grad_kernel, m),
            (near((m, 2, grad_rows, width), bf16), near((m, 2, grad_rows, width), bf16)),
            "ffn_grads",
            (
                at, hp_mine, hps[1], *lows, *acts, *acts_far, *dffns, *dinners, *dinners_far, *dattn,
                *sums2, *sums1,
            ),
            us=4.0,
            vmem=24,
            scalars=1,
        )
        def exchange(third):
            _, send, keep = third
            recv = flip(send, 1)
            return recv, (keep[1].astype(f32) + recv[1].astype(f32)).astype(bf16)

        def input_part(third, recv, far, *theirs):
            dq, _, keep = third
            return call(
                input_kernel,
                (chunk(2 * BLOCK, bf16), near((lanes, 2 * BLOCK), bf16), chunk(8, f32)),
                "input_part",
                (dq, keep, recv, far, wq_t, wkv_t, *theirs),
                us=1.0,
            )

        recv_own, sum_own = exchange(own)
        recv_other, sum_other = exchange(other)
        send1, sum_own, sum_other = fence((send1, sum_own, sum_other))
        recv1 = flip(send1, 1)
        far_own, far_other = flip(sum_own, 2), flip(sum_other, 2)
        pieces1 = share_pieces(keep1, recv1, member)
        far_own, far_other, pieces1, *ends = fence((far_own, far_other, pieces1, *outs[2:]))
        outs[2:] = ends
        part, *late = input_part(other, recv_other, far_other)
        got1 = [flip_member(v, s) for s, v in enumerate(pieces1[1:], 1)]
        pair, dkv_own, sums_own = input_part(own, recv_own, far_own, swap(part, 1))
        d_tok = pair.astype(f32) + swap(pair, 2).astype(f32) + jnp.concatenate(dres1, axis=0)
        d_tok = d_tok.astype(bf16)

        rows2 = 3 * local // 2 + 16
        rows2 += -rows2 % (16 * m)
        keep2, send2 = call(
            functools.partial(attend_grad_kernel, m),
            (chunk(rows2, bf16), chunk(rows2, bf16)),
            "attend_grads",
            (at, tok, own[0], other[0], dkv_own, late[0], sums_own, late[1]),
            us=1.5,
            scalars=1,
        )
        by_member = lambda v: v.reshape(m, rows2 // m, width)
        pieces2 = share_pieces(by_member(keep2), by_member(flip(send2, 1)), member)
        pieces2, got1 = fence((pieces2, got1))
        got2 = [flip_member(v, s) for s, v in enumerate(pieces2[1:], 1)]
        total1 = fence(add(pieces1[0], got1))
        near1 = swap(total1[1], 1)
        d_tok, near1 = fence((d_tok, near1))
        d_toks = [d_tok, swap(d_tok, 1)]
        share1 = total1[0].astype(f32) + near1.astype(f32)
        share1, got2 = fence((share1.astype(bf16), got2))
        mine1 = gather_grads(share1, at, "gather_ffn_grads")
        other1 = flip(mine1, 1)
        total2 = add(pieces2[0], got2)
        total2, *d_toks = fence((total2, *d_toks))
        mine2 = gather_grads(total2, at, "gather_attend_grads").reshape(rows2, width)
        other2 = flip(mine2, 1)

        vector = shape((width,), f32)
        short = shape((local,), f32)
        square = shape((width, units), f32)
        wide = shape((local, width), f32)
        g_w_inner, g_w_outer, g_w_out, g_gain2, g_bias2, g_b_outer, g_b_inner, g_gain1, g_bias1, g_b_out = call(
            functools.partial(ffn_final_kernel, m),
            (square, square, wide) + (vector,) * 7,
            "ffn_grads_out",
            (at, mine1, other1),
            us=3.0,
            scalars=1,
        )
        assemble = lambda parts, name: call(
            rows_kernel,
            shape((row_count, block, width), bf16),
            name,
            (at, *parts),
            us=1.5,
            scalars=1,
        )
        output = assemble(outs, "output_rows")
        d_tokens = assemble(d_toks, "input_grad_rows")
        other2, g_b_out = fence((other2, g_b_out))
        g_q, g_k, g_v, g_b_query, g_b_value = call(
            attend_final_kernel,
            (wide,) * 3 + (short,) * 2,
            "attend_grads_out",
            (at, mine2, other2),
            us=2.0,
            scalars=1,
        )
        return (
            output, d_tokens, g_q.T, g_b_query, g_k.T, g_v.T, g_b_value, g_w_out, g_b_out, g_gain1,
            g_bias1, g_w_inner, g_b_inner, g_w_outer, g_b_outer, g_gain2, g_bias2,
        )

    spread, cols, vec, rows_ = P("dp", "blk", None), P(None, "tensor"), P("tensor"), P("tensor", None)
    return jax.shard_map(
        body,
        mesh=mesh,
        in_specs=(
            spread, P("dp"), P("dp", None), cols, vec, cols, cols, vec, rows_, P(), P(), P(),
            cols, vec, rows_, P(), P(), P(), spread,
        ),
        out_specs=(
            spread, spread, cols, vec, cols, cols, vec, rows_, P(), P(), P(), cols, vec, rows_,
            P(), P(), P(),
        ),
        check_vma=False,
    )
```

time: 265 us -> 221 us (0.83)
  starting transfers between devices: 61.6 us -> 43.1 us
  waiting for transfers between devices: 131 us -> 120 us
  local copies, waits for them, and re-layouts: 12 us -> 6.27 us
  Pallas kernels: 49.6 us -> 44 us
  other arithmetic: 8.6 us -> 5.03 us
    ppermute x26 -> x19, waiting for transfers between devices: 103 us -> 69.4 us  [swap(): return lax.ppermute(v, 'tensor', [(i, i ^ bit) for i in range(n)])]
    ppermute x12, waiting for transfers between devices: 19.4 us -> 38.6 us  [flip_member(): return lax.ppermute(v, ('dp', 'blk'), perm)]
    ppermute x26 -> x19, starting transfers between devices: 34.7 us -> 19.2 us  [swap(): return lax.ppermute(v, 'tensor', [(i, i ^ bit) for i in range(n)])]
    ppermute x0 -> x3, waiting for transfers between devices: none -> 7.99 us  [across(): lax.ppermute(v, ('dp', 'blk'), [(i, there(i)) for i in range(n_dp * n_blk)])]
    pallas_call x27 -> x22, Pallas kernels: 49.6 us -> 42.9 us  [call(): pl.pallas_call(kernel, out_shape=outs, in_specs=[SMEM] * scalars + [VMEM]...]
    ppermute x19 -> x15, waiting for transfers between devices: 9.33 us -> 4.46 us  [flip(): return lax.ppermute(v, 'blk', [(i, i ^ bit) for i in range(n_blk)])]
    unnamed x140 -> x82, local copies, waits for them, and re-layouts: 9.77 us -> 6.1 us
    ppermute x0 -> x3, starting transfers between devices: none -> 3.62 us  [across(): lax.ppermute(v, ('dp', 'blk'), [(i, there(i)) for i in range(n_dp * n_blk)])]
  transfers between devices with their start and end apart: 57 -> 49, of which waited for: 25 -> 29; matrix products, arithmetic and copies ran while one was open for 3% -> 2% of each run, Pallas kernels for 17% -> 15%
where the time goes in v4:
time: 221 us; the launch traced here: 220 us
  waiting for transfers between devices  120 us (54%)
  Pallas kernels  44 us (20%)
  starting transfers between devices  43.1 us (20%)
  local copies, waits for them, and re-layouts  6.27 us (3%)
  other arithmetic  5.03 us (2%)
    ppermute x19, waiting for transfers between devices, swap(): return lax.ppermute(v, 'tensor', [(i, i ^ bit) for i in range(n)])  69.4 us
    pallas_call x22, Pallas kernels, call(): pl.pallas_call(kernel, out_shape=outs, in_specs=[SMEM] * scalars + [VMEM]...  42.9 us
    ppermute x12, waiting for transfers between devices, flip_member(): return lax.ppermute(v, ('dp', 'blk'), perm)  38.6 us
    ppermute x19, starting transfers between devices, swap(): return lax.ppermute(v, 'tensor', [(i, i ^ bit) for i in range(n)])  19.2 us
    ppermute x12, starting transfers between devices, flip_member(): return lax.ppermute(v, ('dp', 'blk'), perm)  14 us
    ppermute x3, waiting for transfers between devices, across(): lax.ppermute(v, ('dp', 'blk'), [(i, there(i)) for i in range(n_dp * n_blk)])  7.99 us
    ppermute x15, starting transfers between devices, flip(): return lax.ppermute(v, 'blk', [(i, i ^ bit) for i in range(n_blk)])  6.26 us
    unnamed x82, local copies, waits for them, and re-layouts  6.1 us
  transfers between devices with their start and end apart: 49, of which 29 were waited for; matrix products, arithmetic and copies ran while one was open for 2% of the time, Pallas kernels for 15%

profile of v4, /device:TPU:0, one launch (start us, length us, event | category | flops | bytes accessed | tf_op | source)
XLA Modules:
  0.0 220.2 jit_solution(14532945489759324296)
XLA Ops:
  7.0 3.0 %collective-permute-start = (bf16[512,384]{1,0:T(8,128)(2,1)S(1)}, bf16[512,384]{1,0:T(8,128)(2,1)S(1)}, u32[]{:S(2)}, u32[]{:S(2)}) collective-permute-start(bf16[512,384]{1,0:T(8,128)(2,1)S(1)} %get-tuple-element.147.refs_0_), channel_id=1, source_target_pairs={{0,8},{4,12},{8,0},{12,4},{1,9},{5,13},{9,1},{13,5},{2,10},{6,14},... | collective-permute-start | bytes 1179656 | tf_op jit(solution)/shard_map/ppermute | solution.py:448
  11.5 2.6 %collective-permute-start.2 = (bf16[48,768]{1,0:T(8,128)(2,1)S(1)}, bf16[48,768]{1,0:T(8,128)(2,1)S(1)}, u32[]{:S(2)}, u32[]{:S(2)}) collective-permute-start(bf16[48,768]{1,0:T(8,128)(2,1)S(1)} %get-tuple-element.149), channel_id=1, source_target_pairs={{0,2},{1,3},{2,0},{3,1},{4,6},{5,7},{6,4},{7,5},{8,10},{9,11},{10,... | collective-permute-start | bytes 221192 | tf_op jit(solution)/shard_map/ppermute | solution.py:445
  14.3 7.1 %collective-permute-done.2 = bf16[48,768]{1,0:T(8,128)(2,1)S(1)} collective-permute-done((bf16[48,768]{1,0:T(8,128)(2,1)S(1)}, bf16[48,768]{1,0:T(8,128)(2,1)S(1)}, u32[]{:S(2)}, u32[]{:S(2)}) %collective-permute-start.2) | collective-permute-done | bytes 73760 | tf_op jit(solution)/shard_map/ppermute | solution.py:445
  21.5 3.7 %collective-permute-done.3 = bf16[48,768]{1,0:T(8,128)(2,1)S(1)} collective-permute-done((bf16[48,768]{1,0:T(8,128)(2,1)S(1)}, bf16[48,768]{1,0:T(8,128)(2,1)S(1)}, u32[]{:S(2)}, u32[]{:S(2)}) %collective-permute-start.3) | collective-permute-done | bytes 73760 | tf_op jit(solution)/shard_map/ppermute | solution.py:445
  29.5 4.9 %attend.1 = (bf16[384,128]{1,0:T(8,128)(2,1)S(1)}, bf16[768,512]{1,0:T(8,128)(2,1)S(1)}, bf16[384,128]{1,0:T(8,128)(2,1)S(1)}, bf16[768,512]{1,0:T(8,128)(2,1)S(1)}) custom-call(s32[5]{0:T(128)S(1)} %stack.23.at, s32[4]{0:T(128)S(1)} %copy-done.26, s32[4,4]{1,0:T(4,128)S(1)} %copy-done.23, bf16[512,384]{1,0:T(8,128)(2,1)S(1)} %query_rows.1.q, ...), custom_call_target="tpu_custom_call" | custom-call | flops 49999998976 | bytes 1 | tf_op jit(solution)/shard_map/attend/pallas_call | solution.py:69
  36.5 2.6 %collective-permute-done.11 = f32[768]{0:T(1024)S(1)} collective-permute-done((f32[768]{0:T(1024)S(1)}, f32[768]{0:T(1024)S(1)}, u32[]{:S(2)}, u32[]{:S(2)}) %collective-permute-start.11) | collective-permute-done | bytes 3104 | tf_op jit(solution)/shard_map/ppermute | solution.py:445
  39.2 2.3 %collective-permute-done.9.refs_4_ = bf16[192,768]{1,0:T(8,128)(2,1)S(1)} collective-permute-done((bf16[192,768]{1,0:T(8,128)(2,1)S(1)}, bf16[192,768]{1,0:T(8,128)(2,1)S(1)}, u32[]{:S(2)}, u32[]{:S(2)}) %collective-permute-start.9) | collective-permute-done | bytes 294944 | tf_op jit(solution)/shard_map/ppermute | solution.py:536
  41.5 5.7 %collective-permute-done.8.refs_2_ = bf16[336,768]{1,0:T(8,128)(2,1)S(1)} collective-permute-done((bf16[336,768]{1,0:T(8,128)(2,1)S(1)}, bf16[336,768]{1,0:T(8,128)(2,1)S(1)}, u32[]{:S(2)}, u32[]{:S(2)}) %collective-permute-start.8) | collective-permute-done | bytes 516128 | tf_op jit(solution)/shard_map/ppermute | solution.py:536
  50.7 8.4 %collective-permute-done.15.refs_2_ = bf16[384,128]{1,0:T(8,128)(2,1)S(1)} collective-permute-done((bf16[384,128]{1,0:T(8,128)(2,1)S(1)}, bf16[384,128]{1,0:T(8,128)(2,1)S(1)}, u32[]{:S(2)}, u32[]{:S(2)}) %collective-permute-start.15) | collective-permute-done | bytes 98336 | tf_op jit(solution)/shard_map/ppermute | solution.py:445
  59.1 2.3 %ffn.3 = (bf16[128,768]{1,0:T(8,128)(2,1)S(1)}, f32[128,768]{1,0:T(8,128)S(1)}, f32[128,128]{1,0:T(8,128)S(1)}, bf16[128,768]{1,0:T(8,128)(2,1)S(1)}, bf16[128,7...) custom-call(s32[5]{0:T(128)S(1)} %stack.23.at, bf16[512,768]{1,0:T(8,128)(2,1)S(1)} %bitcast.50, ...), custom_call_target="tpu_custom_call" | custom-call | flops 2400000000 | bytes 1 | tf_op jit(solution)/shard_map/ffn/pallas_call | solution.py:69
  61.5 2.3 %ffn.2 = (bf16[128,768]{1,0:T(8,128)(2,1)S(1)}, f32[128,768]{1,0:T(8,128)S(1)}, f32[128,128]{1,0:T(8,128)S(1)}, bf16[128,768]{1,0:T(8,128)(2,1)S(1)}, bf16[128,7...) custom-call(s32[5]{0:T(128)S(1)} %stack.23.at, bf16[512,768]{1,0:T(8,128)(2,1)S(1)} %bitcast.51, ...), custom_call_target="tpu_custom_call" | custom-call | flops 2400000000 | bytes 1 | tf_op jit(solution)/shard_map/ffn/pallas_call | solution.py:69
  63.9 3.0 %collective-permute-start.17 = (bf16[128,768]{1,0:T(8,128)(2,1)S(1)}, bf16[128,768]{1,0:T(8,128)(2,1)S(1)}, u32[]{:S(2)}, u32[]{:S(2)}) collective-permute-start(bf16[128,768]{1,0:T(8,128)(2,1)S(1)} %get-tuple-element.167.mine), channel_id=1, source_target_pairs={{0,2},{1,3},{2,0},{3,1},{4,6},{5,7},{6,4},{7,5},{8,10},{9,11},{10,... | collective-permute-start | bytes 589832 | tf_op jit(solution)/shard_map/ppermute | solution.py:445
  66.8 9.9 %collective-permute-done.18.theirs = bf16[128,768]{1,0:T(8,128)(2,1)S(1)} collective-permute-done((bf16[128,768]{1,0:T(8,128)(2,1)S(1)}, bf16[128,768]{1,0:T(8,128)(2,1)S(1)}, u32[]{:S(2)}, u32[]{:S(2)}) %collective-permute-start.18) | collective-permute-done | bytes 196640 | tf_op jit(solution)/shard_map/ppermute | solution.py:445
  76.7 2.7 %ffn_back.3 = (bf16[128,768]{1,0:T(8,128)(2,1)S(1)}, bf16[128,768]{1,0:T(8,128)(2,1)S(1)}, bf16[128,768]{1,0:T(8,128)(2,1)S(1)}, bf16[128,768]{1,0:T(8,128)(2,1)...) custom-call(s32[5]{0:T(128)S(1)} %stack.23.at, bf16[512,768]{1,0:T(8,128)(2,1)S(1)} %bitcast.46, ...), custom_call_target="tpu_custom_call" | custom-call | flops 2700000000 | bytes 1 | tf_op jit(solution)/shard_map/ffn_back/pallas_call | solution.py:69
  80.8 3.2 %ffn_back.2 = (bf16[128,768]{1,0:T(8,128)(2,1)}, bf16[128,768]{1,0:T(8,128)(2,1)S(1)}, bf16[128,768]{1,0:T(8,128)(2,1)S(1)}, bf16[128,768]{1,0:T(8,128)(2,1)S(1)...) custom-call(s32[5]{0:T(128)S(1)} %stack.23.at, bf16[512,768]{1,0:T(8,128)(2,1)S(1)} %bitcast.47, ...), custom_call_target="tpu_custom_call" | custom-call | flops 2700000000 | bytes 1 | tf_op jit(solution)/shard_map/ffn_back/pallas_call | solution.py:69
  85.6 9.6 %collective-permute-done.20.theirs = bf16[128,768]{1,0:T(8,128)(2,1)S(1)} collective-permute-done((bf16[128,768]{1,0:T(8,128)(2,1)S(1)}, bf16[128,768]{1,0:T(8,128)(2,1)S(1)}, u32[]{:S(2)}, u32[]{:S(2)}) %collective-permute-start.20) | collective-permute-done | bytes 196640 | tf_op jit(solution)/shard_map/ppermute | solution.py:445
  96.5 2.9 %collective-permute-done.19.theirs = bf16[128,768]{1,0:T(8,128)(2,1)S(1)} collective-permute-done((bf16[128,768]{1,0:T(8,128)(2,1)S(1)}, bf16[128,768]{1,0:T(8,128)(2,1)S(1)}, u32[]{:S(2)}, u32[]{:S(2)}) %collective-permute-start.19) | collective-permute-done | bytes 196640 | tf_op jit(solution)/shard_map/ppermute | solution.py:445
  101.4 2.8 %attend_back.2 = (bf16[256,192]{1,0:T(8,128)(2,1)S(1)}, bf16[2,2,384,128]{3,2,1,0:T(8,128)(2,1)S(1)}, bf16[2,2,384,128]{3,2,1,0:T(8,128)(2,1)S(1)}) custom-call(s32[5]{0:T(128)S(1)} %stack.23.at, bf16[192,128]{1,0:T(8,128)(2,1)S(1)} %get-tuple-element.188.first, bf16[192,128]{1,0:T(8,128)(2,1)S(1)} %get-tuple-element.192.second, ...), custom_call_target="tpu_custom_call" | custom-call | flops 49999998976 | bytes 1 | tf_op jit(solution)/shard_map/attend_back/pallas_call | solution.py:69
  105.4 2.7 %attend_back.3 = (bf16[256,192]{1,0:T(8,128)(2,1)S(1)}, bf16[2,2,384,128]{3,2,1,0:T(8,128)(2,1)S(1)}, bf16[2,2,384,128]{3,2,1,0:T(8,128)(2,1)S(1)}) custom-call(s32[5]{0:T(128)S(1)} %stack.23.at, bf16[192,128]{1,0:T(8,128)(2,1)S(1)} %collective-permute-done.21.first, bf16[192,128]{1,0:T(8,128)(2,1)S(1)} %collective-permute-done.22.second, ...), custom_call_target="tpu_custom_call" | custom-call | flops 49999998976 | bytes 1 | tf_op jit(solution)/shard_map/attend_back/pallas_call | solution.py:69
  109.3 3.7 %ffn_grads.1 = (bf16[4,2,240,768]{3,2,1,0:T(8,128)(2,1)S(1)}, bf16[4,2,240,768]{3,2,1,0:T(8,128)(2,1)}) custom-call(s32[5]{0:T(128)S(1)} %stack.23.at, bf16[384,128]{1,0:T(8,128)(2,1)S(1)} %get-tuple-element.163.refs_0_.hp_mine, bf16[384,128]{1,0:T(8,128)(2,1)S(1)} %collective-permute-done.7.refs_1_.hp_near, ...), custom_call_target="tpu_custom_call" | custom-call | flops 4000000000 | bytes 1 | tf_op jit(solution)/shard_map/ffn_grads/pallas_call | solution.py:69
  120.5 2.6 %fusion.4 = (bf16[2,240,768]{2,1,0:T(8,128)(2,1)S(1)}, bf16[2,240,768]{2,1,0:T(8,128)(2,1)S(1)}, bf16[2,240,768]{2,1,0:T(8,128)(2,1)S(1)}, bf16[2,240,768]{2,1,0:T(8,128)(2,1)S(1)}) fusion(bf16[4,2,240,768]{3,2,1,0:T(8,128)(2,1)} %collective-permute-done.27, s32[]{:T(128)S(6)} %select_n.47, bf16[4,2,240,768]{3,2,1,0:T(8,128)(2,1)S(1)} %get-tuple-element.215, ...), kind=kLoop, calls=%fused_computation.10 | loop fusion | flops 5898240 | bytes 8847376 | tf_op jit(solution)/shard_map/convert_element_type | solution.py:463
  123.1 3.3 %collective-permute-done.28.refs_2_ = bf16[128,768]{1,0:T(8,128)(2,1)} collective-permute-done((bf16[128,768]{1,0:T(8,128)(2,1)}, bf16[128,768]{1,0:T(8,128)(2,1)}, u32[]{:S(2)}, u32[]{:S(2)}) %collective-permute-start.28) | collective-permute-done | bytes 196640 | tf_op jit(solution)/shard_map/ppermute | solution.py:445
  134.0 5.7 %collective-permute-done.30.refs_0_ = bf16[256,768]{1,0:T(8,128)(2,1)S(1)} collective-permute-done((bf16[256,768]{1,0:T(8,128)(2,1)S(1)}, bf16[256,768]{1,0:T(8,128)(2,1)S(1)}, u32[]{:S(2)}, u32[]{:S(2)}) %collective-permute-start.30) | collective-permute-done | bytes 393248 | tf_op jit(solution)/shard_map/ppermute | solution.py:445
  144.6 4.5 %collective-permute-done.32 = bf16[2,240,768]{2,1,0:T(8,128)(2,1)S(1)} collective-permute-done((bf16[2,240,768]{2,1,0:T(8,128)(2,1)S(1)}, bf16[2,240,768]{2,1,0:T(8,128)(2,1)S(1)}, u32[]{:S(2)}, u32[]{:S(2)}) %collective-permute-start.32) | collective-permute-done | bytes 737312 | tf_op jit(solution)/shard_map/ppermute | solution.py:457
  150.5 14.2 %collective-permute-done.34 = bf16[2,240,768]{2,1,0:T(8,128)(2,1)S(1)} collective-permute-done((bf16[2,240,768]{2,1,0:T(8,128)(2,1)S(1)}, bf16[2,240,768]{2,1,0:T(8,128)(2,1)S(1)}, u32[]{:S(2)}, u32[]{:S(2)}) %collective-permute-start.34) | collective-permute-done | bytes 737312 | tf_op jit(solution)/shard_map/ppermute | solution.py:457
  170.0 3.1 %collective-permute-done.36 = bf16[240,768]{1,0:T(8,128)(2,1)S(1)} collective-permute-done((bf16[240,768]{1,0:T(8,128)(2,1)S(1)}, bf16[240,768]{1,0:T(8,128)(2,1)S(1)}, u32[]{:S(2)}, u32[]{:S(2)}) %collective-permute-start.36) | collective-permute-done | bytes 368672 | tf_op jit(solution)/shard_map/ppermute | solution.py:445
  178.3 7.8 %collective-permute-done.45.refs_1_ = bf16[240,768]{1,0:T(8,128)(2,1)S(1)} collective-permute-done((bf16[240,768]{1,0:T(8,128)(2,1)S(1)}, bf16[240,768]{1,0:T(8,128)(2,1)S(1)}, u32[]{:S(2)}, u32[]{:S(2)}) %collective-permute-start.45) | collective-permute-done | bytes 368672 | tf_op jit(solution)/shard_map/ppermute | solution.py:457
  186.2 3.9 %collective-permute-done.47.refs_3_ = bf16[240,768]{1,0:T(8,128)(2,1)S(1)} collective-permute-done((bf16[240,768]{1,0:T(8,128)(2,1)S(1)}, bf16[240,768]{1,0:T(8,128)(2,1)S(1)}, u32[]{:S(2)}, u32[]{:S(2)}) %collective-permute-start.47) | collective-permute-done | bytes 368672 | tf_op jit(solution)/shard_map/ppermute | solution.py:457
  191.9 10.5 %collective-permute-done.40.refs_1_ = bf16[256,768]{1,0:T(8,128)(2,1)S(1)} collective-permute-done((bf16[256,768]{1,0:T(8,128)(2,1)S(1)}, bf16[256,768]{1,0:T(8,128)(2,1)S(1)}, u32[]{:S(2)}, u32[]{:S(2)}) %collective-permute-start.40) | collective-permute-done | bytes 393248 | tf_op jit(solution)/shard_map/ppermute | solution.py:445
  207.7 2.1 collective-permute-done.42.refs_2_
  211.7 2.1 output_rows.1
  215.3 3.1 %ffn_grads_out.1 = (f32[768,768]{1,0:T(8,128)}, f32[768,768]{1,0:T(8,128)}, f32[192,768]{1,0:T(8,128)}, f32[768]{0:T(1024)}, f32[768]{0:T(1024)}, /*index=5*/f32...) custom-call(s32[5]{0:T(128)S(1)} %stack.23.at, bf16[4,240,768]{2,1,0:T(8,128)(2,1)S(1)} %gather_ffn_grads.1.mine, ...), custom_call_target="tpu_custom_call" | custom-call | flops 3000000000 | bytes 1 | tf_op jit(solution)/shard_map/ffn_grads_out/pallas_call | solution.py:69
  (191 shorter events, 70.4 us)
Async XLA Ops:
  7.0 18.2 %collective-permute-start = (bf16[512,384]{1,0:T(8,128)(2,1)S(1)}, bf16[512,384]{1,0:T(8,128)(2,1)S(1)}, u32[]{:S(2)}, u32[]{:S(2)}) collective-permute-start(bf16[512,384]{1,0:T(8,128)(2,1)S(1)} %get-tuple-element.147.refs_0_), channel_id=1, source_target_pairs={{0,8},{4,12},{8,0},{12,4},{1,9},{5,13},{9,1},{13,5},{2,10},{6,14},... | collective-permute-start | bytes 1179656 | tf_op jit(solution)/shard_map/ppermute | solution.py:448
  10.0 15.2 %collective-permute-start.1 = (bf16[240,768]{1,0:T(8,128)(2,1)S(1)}, bf16[240,768]{1,0:T(8,128)(2,1)S(1)}, u32[]{:S(2)}, u32[]{:S(2)}) collective-permute-start(bf16[240,768]{1,0:T(8,128)(2,1)S(1)} %get-tuple-element.148), channel_id=1, source_target_pairs={{0,1},{1,0},{2,3},{3,2},{4,5},{5,4},{6,7},{7,6},{8,9},{9,8},{10,11... | collective-permute-start | bytes 1105928 | tf_op jit(solution)/shard_map/ppermute | solution.py:445
  11.5 9.9 %collective-permute-start.2 = (bf16[48,768]{1,0:T(8,128)(2,1)S(1)}, bf16[48,768]{1,0:T(8,128)(2,1)S(1)}, u32[]{:S(2)}, u32[]{:S(2)}) collective-permute-start(bf16[48,768]{1,0:T(8,128)(2,1)S(1)} %get-tuple-element.149), channel_id=1, source_target_pairs={{0,2},{1,3},{2,0},{3,1},{4,6},{5,7},{6,4},{7,5},{8,10},{9,11},{10,... | collective-permute-start | bytes 221192 | tf_op jit(solution)/shard_map/ppermute | solution.py:445
  14.1 11.1 %collective-permute-start.3 = (bf16[48,768]{1,0:T(8,128)(2,1)S(1)}, bf16[48,768]{1,0:T(8,128)(2,1)S(1)}, u32[]{:S(2)}, u32[]{:S(2)}) collective-permute-start(bf16[48,768]{1,0:T(8,128)(2,1)S(1)} %get-tuple-element.149), channel_id=1, source_target_pairs={{0,3},{1,2},{2,1},{3,0},{4,7},{5,6},{6,5},{7,4},{8,11},{9,10},{10,... | collective-permute-start | bytes 221192 | tf_op jit(solution)/shard_map/ppermute | solution.py:445
  14.3 15.2 %collective-permute-start.5 = (bf16[512,384]{1,0:T(8,128)(2,1)S(1)}, bf16[512,384]{1,0:T(8,128)(2,1)S(1)}, u32[]{:S(2)}, u32[]{:S(2)}) collective-permute-start(bf16[512,384]{1,0:T(8,128)(2,1)S(1)} %get-tuple-element.147.refs_0_), channel_id=1, source_target_pairs={{0,4},{4,0},{8,12},{12,8},{1,5},{5,1},{9,13},{13,9},{2,6},{6,2},{1... | collective-permute-start | bytes 1179656 | tf_op jit(solution)/shard_map/ppermute | solution.py:448
  25.7 13.4 %collective-permute-start.10 = (bf16[192,768]{1,0:T(8,128)(2,1)S(1)}, bf16[192,768]{1,0:T(8,128)(2,1)S(1)}, u32[]{:S(2)}, u32[]{:S(2)}) collective-permute-start(bf16[192,768]{1,0:T(8,128)(2,1)S(1)} %slice.21), channel_id=1, source_target_pairs={{0,24},{4,28},{8,16},{12,20},{16,8},{20,12},{24,0},{28,4},{1,25},{... | collective-permute-start | bytes 884744 | tf_op jit(solution)/shard_map/ppermute | solution.py:536
  27.2 14.3 %collective-permute-start.9 = (bf16[192,768]{1,0:T(8,128)(2,1)S(1)}, bf16[192,768]{1,0:T(8,128)(2,1)S(1)}, u32[]{:S(2)}, u32[]{:S(2)}) collective-permute-start(bf16[192,768]{1,0:T(8,128)(2,1)S(1)} %slice.21), channel_id=1, source_target_pairs={{0,16},{4,20},{8,24},{12,28},{16,0},{20,4},{24,8},{28,12},{1,17},{... | collective-permute-start | bytes 884744 | tf_op jit(solution)/shard_map/ppermute | solution.py:536
  27.9 19.2 %collective-permute-start.8 = (bf16[336,768]{1,0:T(8,128)(2,1)S(1)}, bf16[336,768]{1,0:T(8,128)(2,1)S(1)}, u32[]{:S(2)}, u32[]{:S(2)}) collective-permute-start(bf16[336,768]{1,0:T(8,128)(2,1)S(1)} %constant_dynamic-update-slice_fusion.refs_0_), channel_id=1, source_target_pairs={{0,8},{4,12},{8,0},{12,4},{16,24},{20,28},{24,16},{28,20},{1,9},{5... | collective-permute-start | bytes 1548296 | tf_op jit(solution)/shard_map/ppermute | solution.py:536
  34.4 7.1 %collective-permute-start.7 = (bf16[384,128]{1,0:T(8,128)(2,1)S(1)}, bf16[384,128]{1,0:T(8,128)(2,1)S(1)}, u32[]{:S(2)}, u32[]{:S(2)}) collective-permute-start(bf16[384,128]{1,0:T(8,128)(2,1)S(1)} %get-tuple-element.154), channel_id=1, source_target_pairs={{0,1},{1,0},{2,3},{3,2},{4,5},{5,4},{6,7},{7,6},{8,9},{9,8},{10,11... | collective-permute-start | bytes 294920 | tf_op jit(solution)/shard_map/ppermute | solution.py:445
  39.1 10.3 %collective-permute-start.4 = (bf16[336,768]{1,0:T(8,128)(2,1)S(1)}, bf16[336,768]{1,0:T(8,128)(2,1)S(1)}, u32[]{:S(2)}, u32[]{:S(2)}) collective-permute-start(bf16[336,768]{1,0:T(8,128)(2,1)S(1)} %constant_dynamic-update-slice_fusion.refs_0_), channel_id=1, source_target_pairs={{0,4},{4,0},{8,12},{12,8},{1,5},{5,1},{9,13},{13,9},{2,6},{6,2},{1... | collective-permute-start | bytes 1548296 | tf_op jit(solution)/shard_map/ppermute | solution.py:448
  47.8 11.3 %collective-permute-start.16 = (bf16[384,128]{1,0:T(8,128)(2,1)S(1)}, bf16[384,128]{1,0:T(8,128)(2,1)S(1)}, u32[]{:S(2)}, u32[]{:S(2)}) collective-permute-start(bf16[384,128]{1,0:T(8,128)(2,1)S(1)} %get-tuple-element.154), channel_id=1, source_target_pairs={{0,3},{1,2},{2,1},{3,0},{4,7},{5,6},{6,5},{7,4},{8,11},{9,10},{10,... | collective-permute-start | bytes 294920 | tf_op jit(solution)/shard_map/ppermute | solution.py:445
  49.5 9.6 %collective-permute-start.15 = (bf16[384,128]{1,0:T(8,128)(2,1)S(1)}, bf16[384,128]{1,0:T(8,128)(2,1)S(1)}, u32[]{:S(2)}, u32[]{:S(2)}) collective-permute-start(bf16[384,128]{1,0:T(8,128)(2,1)S(1)} %get-tuple-element.163.refs_0_.hp_mine), channel_id=1, source_target_pairs={{0,2},{1,3},{2,0},{3,1},{4,6},{5,7},{6,4},{7,5},{8,10},{9,11},{10,... | collective-permute-start | bytes 294920 | tf_op jit(solution)/shard_map/ppermute | solution.py:445
  61.4 15.3 %collective-permute-start.18 = (bf16[128,768]{1,0:T(8,128)(2,1)S(1)}, bf16[128,768]{1,0:T(8,128)(2,1)S(1)}, u32[]{:S(2)}, u32[]{:S(2)}) collective-permute-start(bf16[128,768]{1,0:T(8,128)(2,1)S(1)} %get-tuple-element.171.mine), channel_id=1, source_target_pairs={{0,2},{1,3},{2,0},{3,1},{4,6},{5,7},{6,4},{7,5},{8,10},{9,11},{10,... | collective-permute-start | bytes 589832 | tf_op jit(solution)/shard_map/ppermute | solution.py:445
  63.9 17.0 %collective-permute-start.17 = (bf16[128,768]{1,0:T(8,128)(2,1)S(1)}, bf16[128,768]{1,0:T(8,128)(2,1)S(1)}, u32[]{:S(2)}, u32[]{:S(2)}) collective-permute-start(bf16[128,768]{1,0:T(8,128)(2,1)S(1)} %get-tuple-element.167.mine), channel_id=1, source_target_pairs={{0,2},{1,3},{2,0},{3,1},{4,6},{5,7},{6,4},{7,5},{8,10},{9,11},{10,... | collective-permute-start | bytes 589832 | tf_op jit(solution)/shard_map/ppermute | solution.py:445
  79.4 15.8 %collective-permute-start.20 = (bf16[128,768]{1,0:T(8,128)(2,1)S(1)}, bf16[128,768]{1,0:T(8,128)(2,1)S(1)}, u32[]{:S(2)}, u32[]{:S(2)}) collective-permute-start(bf16[128,768]{1,0:T(8,128)(2,1)S(1)} %get-tuple-element.189.mine), channel_id=1, source_target_pairs={{0,2},{1,3},{2,0},{3,1},{4,6},{5,7},{6,4},{7,5},{8,10},{9,11},{10,... | collective-permute-start | bytes 589832 | tf_op jit(solution)/shard_map/ppermute | solution.py:445
  84.1 15.4 %collective-permute-start.19 = (bf16[128,768]{1,0:T(8,128)(2,1)S(1)}, bf16[128,768]{1,0:T(8,128)(2,1)S(1)}, u32[]{:S(2)}, u32[]{:S(2)}) collective-permute-start(bf16[128,768]{1,0:T(8,128)(2,1)S(1)} %get-tuple-element.185.mine), channel_id=1, source_target_pairs={{0,2},{1,3},{2,0},{3,1},{4,6},{5,7},{6,4},{7,5},{8,10},{9,11},{10,... | collective-permute-start | bytes 589832 | tf_op jit(solution)/shard_map/ppermute | solution.py:445
  96.4 7.8 %collective-permute-start.22 = (bf16[192,128]{1,0:T(8,128)(2,1)S(1)}, bf16[192,128]{1,0:T(8,128)(2,1)S(1)}, u32[]{:S(2)}, u32[]{:S(2)}) collective-permute-start(bf16[192,128]{1,0:T(8,128)(2,1)S(1)} %get-tuple-element.196), channel_id=1, source_target_pairs={{0,1},{1,0},{2,3},{3,2},{4,5},{5,4},{6,7},{7,6},{8,9},{9,8},{10,11... | collective-permute-start | bytes 147464 | tf_op jit(solution)/shard_map/ppermute | solution.py:445
  114.7 8.3 %collective-permute-start.29 = (bf16[128,768]{1,0:T(8,128)(2,1)S(1)}, bf16[128,768]{1,0:T(8,128)(2,1)}, u32[]{:S(2)}, u32[]{:S(2)}) collective-permute-start(bf16[128,768]{1,0:T(8,128)(2,1)S(1)} %get-tuple-element.172.refs_1_), channel_id=1, source_target_pairs={{0,1},{1,0},{2,3},{3,2},{4,5},{5,4},{6,7},{7,6},{8,9},{9,8},{10,11... | collective-permute-start | bytes 589832 | tf_op jit(solution)/shard_map/ppermute | solution.py:445
  115.6 10.7 %collective-permute-start.28 = (bf16[128,768]{1,0:T(8,128)(2,1)}, bf16[128,768]{1,0:T(8,128)(2,1)}, u32[]{:S(2)}, u32[]{:S(2)}) collective-permute-start(bf16[128,768]{1,0:T(8,128)(2,1)} %get-tuple-element.168.refs_0_), channel_id=1, source_target_pairs={{0,1},{1,0},{2,3},{3,2},{4,5},{5,4},{6,7},{7,6},{8,9},{9,8},{10,11... | collective-permute-start | bytes 589832 | tf_op jit(solution)/shard_map/ppermute | solution.py:445
  116.8 9.5 %collective-permute-start.25 = (bf16[2,384,128]{2,1,0:T(8,128)(2,1)}, bf16[2,384,128]{2,1,0:T(8,128)(2,1)}, u32[]{:S(2)}, u32[]{:S(2)}) collective-permute-start(bf16[2,384,128]{2,1,0:T(8,128)(2,1)} %fusion.6), channel_id=1, source_target_pairs={{0,8},{4,12},{8,0},{12,4},{1,9},{5,13},{9,1},{13,5},{2,10},{6,14},... | collective-permute-start | bytes 589832 | tf_op jit(solution)/shard_map/ppermute | solution.py:448
  117.3 10.7 %collective-permute-start.26 = (bf16[2,384,128]{2,1,0:T(8,128)(2,1)}, bf16[2,384,128]{2,1,0:T(8,128)(2,1)}, u32[]{:S(2)}, u32[]{:S(2)}) collective-permute-start(bf16[2,384,128]{2,1,0:T(8,128)(2,1)} %fusion.7), channel_id=1, source_target_pairs={{0,8},{4,12},{8,0},{12,4},{1,9},{5,13},{9,1},{13,5},{2,10},{6,14},... | collective-permute-start | bytes 589832 | tf_op jit(solution)/shard_map/ppermute | solution.py:448
  129.6 10.1 %collective-permute-start.30 = (bf16[256,768]{1,0:T(8,128)(2,1)S(1)}, bf16[256,768]{1,0:T(8,128)(2,1)S(1)}, u32[]{:S(2)}, u32[]{:S(2)}) collective-permute-start(bf16[256,768]{1,0:T(8,128)(2,1)S(1)} %get-tuple-element.224), channel_id=1, source_target_pairs={{0,1},{1,0},{2,3},{3,2},{4,5},{5,4},{6,7},{7,6},{8,9},{9,8},{10,11... | collective-permute-start | bytes 1179656 | tf_op jit(solution)/shard_map/ppermute | solution.py:445
  130.5 18.5 %collective-permute-start.32 = (bf16[2,240,768]{2,1,0:T(8,128)(2,1)S(1)}, bf16[2,240,768]{2,1,0:T(8,128)(2,1)S(1)}, u32[]{:S(2)}, u32[]{:S(2)}) collective-permute-start(bf16[2,240,768]{2,1,0:T(8,128)(2,1)S(1)} %get-tuple-element.231), channel_id=1, source_target_pairs={{0,8},{4,12},{8,0},{12,4},{16,24},{20,28},{24,16},{28,20},{1,9},{5... | collective-permute-start | bytes 2211848 | tf_op jit(solution)/shard_map/ppermute | solution.py:457
  131.0 19.4 %collective-permute-start.33 = (bf16[2,240,768]{2,1,0:T(8,128)(2,1)S(1)}, bf16[2,240,768]{2,1,0:T(8,128)(2,1)S(1)}, u32[]{:S(2)}, u32[]{:S(2)}) collective-permute-start(bf16[2,240,768]{2,1,0:T(8,128)(2,1)S(1)} %get-tuple-element.232), channel_id=1, source_target_pairs={{0,16},{4,20},{8,24},{12,28},{16,0},{20,4},{24,8},{28,12},{1,17},{... | collective-permute-start | bytes 2211848 | tf_op jit(solution)/shard_map/ppermute | solution.py:457
  132.5 32.1 %collective-permute-start.34 = (bf16[2,240,768]{2,1,0:T(8,128)(2,1)S(1)}, bf16[2,240,768]{2,1,0:T(8,128)(2,1)S(1)}, u32[]{:S(2)}, u32[]{:S(2)}) collective-permute-start(bf16[2,240,768]{2,1,0:T(8,128)(2,1)S(1)} %get-tuple-element.233), channel_id=1, source_target_pairs={{0,24},{4,28},{8,16},{12,20},{16,8},{20,12},{24,0},{28,4},{1,25},{... | collective-permute-start | bytes 2211848 | tf_op jit(solution)/shard_map/ppermute | solution.py:457
  142.6 23.7 %collective-permute-start.35 = (bf16[256,768]{1,0:T(8,128)(2,1)S(1)}, bf16[256,768]{1,0:T(8,128)(2,1)S(1)}, u32[]{:S(2)}, u32[]{:S(2)}) collective-permute-start(bf16[256,768]{1,0:T(8,128)(2,1)S(1)} %get-tuple-element.239), channel_id=1, source_target_pairs={{0,2},{1,3},{2,0},{3,1},{4,6},{5,7},{6,4},{7,5},{8,10},{9,11},{10,... | collective-permute-start | bytes 1179656 | tf_op jit(solution)/shard_map/ppermute | solution.py:445
  165.1 8.1 %collective-permute-start.36 = (bf16[240,768]{1,0:T(8,128)(2,1)S(1)}, bf16[240,768]{1,0:T(8,128)(2,1)S(1)}, u32[]{:S(2)}, u32[]{:S(2)}) collective-permute-start(bf16[240,768]{1,0:T(8,128)(2,1)S(1)} %slice_bitcast_fusion), channel_id=1, source_target_pairs={{0,1},{1,0},{2,3},{3,2},{4,5},{5,4},{6,7},{7,6},{8,9},{9,8},{10,11... | collective-permute-start | bytes 1105928 | tf_op jit(solution)/shard_map/ppermute | solution.py:445
  174.8 11.3 %collective-permute-start.45 = (bf16[240,768]{1,0:T(8,128)(2,1)S(1)}, bf16[240,768]{1,0:T(8,128)(2,1)S(1)}, u32[]{:S(2)}, u32[]{:S(2)}) collective-permute-start(bf16[240,768]{1,0:T(8,128)(2,1)S(1)} %fusion.5.refs_0_), channel_id=1, source_target_pairs={{0,8},{4,12},{8,0},{12,4},{16,24},{20,28},{24,16},{28,20},{1,9},{5... | collective-permute-start | bytes 1105928 | tf_op jit(solution)/shard_map/ppermute | solution.py:457
  176.4 9.8 %collective-permute-start.46 = (bf16[240,768]{1,0:T(8,128)(2,1)S(1)}, bf16[240,768]{1,0:T(8,128)(2,1)S(1)}, u32[]{:S(2)}, u32[]{:S(2)}) collective-permute-start(bf16[240,768]{1,0:T(8,128)(2,1)S(1)} %fusion.5.refs_0_), channel_id=1, source_target_pairs={{0,16},{4,20},{8,24},{12,28},{16,0},{20,4},{24,8},{28,12},{1,17},{... | collective-permute-start | bytes 1105928 | tf_op jit(solution)/shard_map/ppermute | solution.py:457
  177.0 13.1 %collective-permute-start.47 = (bf16[240,768]{1,0:T(8,128)(2,1)S(1)}, bf16[240,768]{1,0:T(8,128)(2,1)S(1)}, u32[]{:S(2)}, u32[]{:S(2)}) collective-permute-start(bf16[240,768]{1,0:T(8,128)(2,1)S(1)} %fusion.5.refs_0_), channel_id=1, source_target_pairs={{0,24},{4,28},{8,16},{12,20},{16,8},{20,12},{24,0},{28,4},{1,25},{... | collective-permute-start | bytes 1105928 | tf_op jit(solution)/shard_map/ppermute | solution.py:457
  190.8 24.5 %collective-permute-start.48 = (bf16[4,240,768]{2,1,0:T(8,128)(2,1)S(1)}, bf16[4,240,768]{2,1,0:T(8,128)(2,1)S(1)}, u32[]{:S(2)}, u32[]{:S(2)}) collective-permute-start(bf16[4,240,768]{2,1,0:T(8,128)(2,1)S(1)} %gather_ffn_grads.1.mine), channel_id=1, source_target_pairs={{0,4},{4,0},{8,12},{12,8},{1,5},{5,1},{9,13},{13,9},{2,6},{6,2},{1... | collective-permute-start | bytes 4423688 | tf_op jit(solution)/shard_map/ppermute | solution.py:448
  190.8 11.5 %collective-permute-start.40 = (bf16[256,768]{1,0:T(8,128)(2,1)S(1)}, bf16[256,768]{1,0:T(8,128)(2,1)S(1)}, u32[]{:S(2)}, u32[]{:S(2)}) collective-permute-start(bf16[256,768]{1,0:T(8,128)(2,1)S(1)} %fusion.refs_0_), channel_id=1, source_target_pairs={{0,1},{1,0},{2,3},{3,2},{4,5},{5,4},{6,7},{7,6},{8,9},{9,8},{10,11... | collective-permute-start | bytes 1179656 | tf_op jit(solution)/shard_map/ppermute | solution.py:445
  (57 other events, 422.2 us)

commit v5 on v4

--- a/solution.py
+++ b/solution.py
@@ -19,6 +19,9 @@
 FLOPS_US = 1e9
 ATTEND_US = 50.0
 BACK_US = 50.0
+FILL_US = 50.0
+INPUT_US = 50.0
+GRADS_US = 1.0
 PACKED = BLOCK + HEAD_DIM
 
 
@@ -257,15 +260,16 @@
     )
 
 
-def norm_back_kernel(n, at, mine, theirs, dres2, n1, s1, g1, w_out, dres1_out, dattn_out, sums, dh, dh_far):
+def norm_back_kernel(n, at, mine, theirs, dres2, n1, s1, g1, w_out, dres1_out, share, dh, dh_far):
     dhidden = (mine[...].astype(f32) + theirs[...].astype(f32)) + dres2[...]
     norm = n1[...]
     dn = dhidden * g1[...]
     dres1 = s1[:, :1] * (dn - mean(dn) - norm * mean(dn * norm))
     dattn = dres1.astype(bf16)
     dres1_out[...] = dres1
-    dattn_out[...] = dattn
-    sums[...] = rows8(col_sum(dhidden * norm), col_sum(dhidden), col_sum(dattn.astype(f32)))
+    share[:BLOCK, :] = dattn
+    sums = rows8(col_sum(dhidden * norm), col_sum(dhidden), col_sum(dattn.astype(f32)))
+    share[BLOCK:, :] = jnp.concatenate([sums, jnp.zeros_like(sums)], axis=0).astype(bf16)
     local = w_out.shape[0] // n
     dh[...] = pack(nt(dattn, chunk_of(w_out, at[0], local)).astype(bf16))
     dh_far[...] = pack(nt(dattn, chunk_of(w_out, at[0] ^ 1, local)).astype(bf16))
@@ -300,14 +304,11 @@
         dq_out[i * BLOCK : (i + 1) * BLOCK, :] = jnp.concatenate(dqs, axis=1)
 
 
-def input_kernel(dq, keep, recv, far, wq_t, wkv_t, *refs):
-    theirs, (part, dkv_t, sums) = refs[:-3], refs[-3:]
+def input_kernel(dq, keep, recv, far, wq_t, wkv_t, part, dkv_t, sums):
     total = keep[0].astype(f32) + recv[0].astype(f32) + far[...].astype(f32)
     lows = [total[i].astype(bf16) for i in range(2)]
     low = jnp.concatenate([v.T for v in lows], axis=0)
     grad = nn(dq[...], wq_t[...]) + nn(low, wkv_t[...])
-    if theirs:
-        grad = grad + theirs[0][...].astype(f32)
     part[...] = grad.astype(bf16)
     dkv_t[...] = jnp.concatenate(lows, axis=1)
     width = sums.shape[1]
@@ -327,53 +328,49 @@
     return jnp.concatenate(list(values), axis=axis)
 
 
-def ffn_grad_kernel(m, at, hp_mine, hp_near, *refs):
-    low, act, act_far, dffn, dinner, dinner_far, dattn, sums2, sums1 = (
-        refs[2 * i : 2 * i + 2] for i in range(9)
-    )
-    keep, send = refs[18:]
+def ordered_sum(at, parts, held):
+    for i, part in enumerate(parts):
+        held[row_at(at, i)] = part.astype(f32)
+    total = held[0]
+    for r in range(1, len(parts)):
+        total = total + held[r]
+    return total
+
+
+def ffn_grad_kernel(m, at, *refs):
+    low, act, act_far, dffn, dinner, dinner_far, sums2 = (refs[2 * i : 2 * i + 2] for i in range(7))
+    keep, send = refs[14:]
     first = at[1] == 0
     both = lambda pair: join(x[...] for x in pair)
-    lows, dffns, dattns = both(low), both(dffn), both(dattn)
+    lows, dffns = both(low), both(dffn)
     tail2 = sums2[0][...] + sums2[1][...]
-    tail1 = sums1[0][...] + sums1[1][...]
     rows = lows.shape[1] // m
-    out_rows = keep.shape[2] - rows - 16
-    for q, (acts, dinners, hp) in enumerate(
-        ((both(act), both(dinner), hp_mine), (both(act_far), both(dinner_far), hp_near))
-    ):
-        heads = join(unpack(hp[i * PACKED : (i + 1) * PACKED, :]) for i in range(2))
-        g_out = tn(heads, dattns).astype(bf16)
-        cut = g_out.shape[0] // 2
-        tail = join([tail2[:3], tail2[3 + q : 4 + q], tail1[:3], jnp.zeros((9, tail1.shape[1]), f32)])
+    for q, (acts, dinners) in enumerate(((both(act), both(dinner)), (both(act_far), both(dinner_far)))):
+        tail = join([tail2[:3], tail2[3 + q : 4 + q], jnp.zeros((12, tail2.shape[1]), f32)])
         tail = tail.astype(bf16)
         for target, one in ((keep, first), (send, jnp.logical_not(first))):
             main = tn(pick(one, lows, acts), pick(one, dinners, dffns)).astype(bf16)
-            outs = pick(one, g_out[:cut], g_out[cut:])
             for i in range(m):
                 target[i, q, :rows, :] = main[i * rows : (i + 1) * rows]
-                if i * out_rows < cut:
-                    block = outs[i * out_rows : (i + 1) * out_rows]
-                else:
-                    block = jnp.zeros((out_rows, outs.shape[1]), bf16)
-                target[i, q, rows : rows + out_rows, :] = block
-                target[i, q, rows + out_rows :, :] = tail
-
-
-def attend_grad_kernel(m, at, tok, *refs):
-    dq, dkv_t, sums = (refs[2 * i : 2 * i + 2] for i in range(3))
-    keep, send = refs[6:]
+                target[i, q, rows:, :] = tail
+
+
+def attend_grad_kernel(m, at, tok, hp_mine, hp_other, *refs):
+    shares, (dq, dkv_t, sums) = refs[:4], (refs[4 + 2 * i : 6 + 2 * i] for i in range(3))
+    keep, send, held = refs[10:]
     first = at[1] == 0
     toks = join(chunk_of(tok, row_at(at, i), BLOCK) for i in range(4))
+    heads = join(unpack(hp[i * PACKED : (i + 1) * PACKED, :]) for hp in (hp_mine, hp_other) for i in range(2))
+    g_out = tn(heads, join(x[:BLOCK, :] for x in shares))
     g_q = tn(join(x[...] for x in dq), toks)
     g_kv = nn(join((x[...] for x in dkv_t), axis=1), toks)
-    half = (g_q.shape[0] + g_kv.shape[0]) // 2
-    cut = half - g_q.shape[0]
-    one = join([g_q, g_kv[:cut]]).astype(bf16)
-    two = g_kv[cut:].astype(bf16)
+    one = join([g_out, g_q]).astype(bf16)
+    two = g_kv.astype(bf16)
+    half = two.shape[0]
+    norm = ordered_sum(at, [x[BLOCK : BLOCK + 8, :] for x in shares], held)
     total = sums[0][...] + sums[1][...]
     rest = keep.shape[0] - half
-    tail = join([total, jnp.zeros((rest - 8, total.shape[1]), f32)]).astype(bf16)
+    tail = join([norm, total, jnp.zeros((rest - 16, total.shape[1]), f32)]).astype(bf16)
     keep[:half, :] = pick(first, one, two)
     keep[half:, :] = tail
     send[:half, :] = pick(first, two, one)
@@ -386,44 +383,37 @@
         out[at[3] ^ s] = refs[s][...]
 
 
-def ffn_final_kernel(m, at, mine, other, g_in, g_outer, g_out, *vectors):
+def ffn_final_kernel(m, at, mine, other, g_in, g_outer, *vectors):
     first = at[1] == 0
     rows = g_in.shape[0] // m
-    out_rows = mine.shape[1] - rows - 16
-    cut = g_out.shape[0] // 2
     for i in range(m):
         a, b = mine[i], other[i]
-        one = pick(first, a, b).astype(f32)
-        two = pick(first, b, a).astype(f32)
-        g_in[i * rows : (i + 1) * rows, :] = one[:rows]
-        g_outer[i * rows : (i + 1) * rows, :] = two[:rows]
-        if i * out_rows < cut:
-            at_row = i * out_rows
-            g_out[at_row : at_row + out_rows, :] = one[rows : rows + out_rows]
-            g_out[cut + at_row : cut + at_row + out_rows, :] = two[rows : rows + out_rows]
-        if i == 0:
-            for k, ref in enumerate(vectors):
-                ref[...] = one[rows + out_rows + k]
-
-
-def attend_final_kernel(at, mine, other, g_q, g_k, g_v, b_q, b_v):
+        g_in[i * rows : (i + 1) * rows, :] = pick(first, a[:rows], b[:rows]).astype(f32)
+        g_outer[i * rows : (i + 1) * rows, :] = pick(first, b[:rows], a[:rows]).astype(f32)
+    tail = mine[0, rows:, :].astype(f32)
+    for k, ref in enumerate(vectors):
+        ref[...] = tail[k]
+
+
+def attend_final_kernel(at, mine, other, g_out, g_q, g_k, g_v, gain, bias, b_out, b_q, b_v):
     first = at[1] == 0
     width = g_q.shape[0]
-    half = 3 * width // 2
     a = mine[...]
     b = other[...]
     one = pick(first, a, b).astype(f32)
     two = pick(first, b, a).astype(f32)
-    g_q[...] = one[:width]
-    g_kv = join([one[width:half], two[:half]])
-    tail = one[half : half + 8]
+    g_out[...] = one[:width]
+    g_q[...] = one[width : 2 * width]
+    tail = one[2 * width : 2 * width + 16]
     values = []
     for h in range(width // HEAD_DIM):
         part = slice(h * HEAD_DIM, (h + 1) * HEAD_DIM)
-        g_k[part, :] = g_kv[h * LANES : h * LANES + HEAD_DIM]
-        g_v[part, :] = g_kv[h * LANES + HEAD_DIM : (h + 1) * LANES]
-        values.append(tail[1:2, h * LANES + HEAD_DIM : (h + 1) * LANES])
-    b_q[...] = tail[0, :width]
+        g_k[part, :] = two[h * LANES : h * LANES + HEAD_DIM]
+        g_v[part, :] = two[h * LANES + HEAD_DIM : (h + 1) * LANES]
+        values.append(tail[9:10, h * LANES + HEAD_DIM : (h + 1) * LANES])
+    for i, ref in enumerate((gain, bias, b_out)):
+        ref[...] = tail[i]
+    b_q[...] = tail[8, :width]
     b_v[...] = jnp.concatenate(values, axis=1)[0]
 
 
@@ -470,9 +460,11 @@
             total = total + part.astype(f32)
         return total.astype(bf16)
 
-    def gather_grads(total, at, name):
+    def gather_grads(total, at, name, *extra):
         rows, width = total.shape
-        every = [total] + [flip_member(total, s) for s in range(1, m)]
+        got = [flip_member(total, s) for s in range(1, m)]
+        got, extra = lax.optimization_barrier((got, extra))
+        every = [total] + got
         mine = call(
             functools.partial(gather_kernel, m),
             near((m, rows, width), bf16),
@@ -480,7 +472,7 @@
             (at, *every),
             scalars=1,
         )
-        return mine
+        return mine, *extra
 
     def body(
         tokens, bucket_ids, seq_lengths, w_query, b_query, w_key, w_value, b_value, w_out, b_out,
@@ -527,7 +519,8 @@
         kv_core = flip(kv, 1)
         pieces = [swap(piece, 1)] + [swap(out_piece, s) for s in range(2, n)]
         b_inner_far = swap(b_far, 1)
-        kv_far, *pieces = fence((kv_far, *pieces))
+        kv_far, b_inner_far, *pieces = fence((kv_far, b_inner_far, *pieces))
+        kv_both = flip(kv_far, 1)
         own_piece = jnp.concatenate(pieces, axis=0)
         ffn_piece = pieces[0][:piece_rows]
 
@@ -539,7 +532,6 @@
         arrived |= {4: across(ffn_piece, 1, 0), 6: across(ffn_piece, 1, 2)}
 
         q = call(q_kernel, near((count, lanes), bf16), "query_rows", (tok, wq_t, row(b_query)), us=0.5)
-        kv_both = flip(kv_far, 1)
         kvs = [kv, kv_core, kv_far, kv_both]
 
         pair = (near((2 * PACKED, LANES), bf16), near((2 * heads * BLOCK, n_blk * BLOCK), bf16))
@@ -552,9 +544,9 @@
             scalars=3,
         )
         hps = {0: hp_mine, 1: swap(hp_other, 1), 2: swap(hp_mine, 2), 3: swap(hp_other, 3)}
-        held = [arrived[2], arrived[4], arrived[6], b_inner_far]
-        hps[1], *held = fence((hps[1], *held))
-        arrived[2], arrived[4], arrived[6], b_inner_far = held
+        held = [arrived[2], arrived[4], arrived[6]]
+        hps[1], hps[2], hps[3], *held = fence((hps[1], hps[2], hps[3], *held))
+        arrived[2], arrived[4], arrived[6] = held
         arrived |= {j + 1: flip(v, 1) for j, v in arrived.items()}
         w_out_all, w_inner_far, w_outer_far = call(
             functools.partial(weights_kernel, n),
@@ -607,11 +599,23 @@
 
         outs, dffns, dinners, dinners_far, parts2, dres2, sums2 = map(list, zip(*[ffn_back(i) for i in range(2)]))
         theirs2 = [swap(v, 2) for v in parts2]
+        keep1, send1 = call(
+            functools.partial(ffn_grad_kernel, m),
+            (near((m, 2, width // m + 16, width), bf16),) * 2,
+            "ffn_grads",
+            (at, *lows, *acts, *acts_far, *dffns, *dinners, *dinners_far, *sums2),
+            us=FILL_US,
+            vmem=24,
+            scalars=1,
+        )
+        recv1 = flip(send1, 1)
+        pieces1 = share_pieces(keep1, recv1, member)
+
         def norm_back(i):
             return call(
                 functools.partial(norm_back_kernel, n),
                 (
-                    chunk(BLOCK, f32), chunk(BLOCK, bf16), chunk(8, f32), near((PACKED, LANES), bf16),
+                    chunk(BLOCK, f32), chunk(BLOCK + 16, bf16), near((PACKED, LANES), bf16),
                     near((PACKED, LANES), bf16),
                 ),
                 "norm_back",
@@ -620,8 +624,9 @@
                 scalars=1,
             )
 
-        dres1, dattn, sums1, dheads, dheads_far = map(list, zip(*[norm_back(i) for i in range(2)]))
+        dres1, shares, dheads, dheads_far = map(list, zip(*[norm_back(i) for i in range(2)]))
         dheads += [swap(v, 1) for v in dheads_far]
+        shares += [swap(v, 1) for v in shares]
         outs += [swap(v, 1) for v in outs]
 
         def attend_back(ids, probs, *packed):
@@ -638,90 +643,76 @@
             )
 
         own = attend_back((0, 1), probs_mine, dheads[0], dheads[1])
-        after, dheads[2], dheads[3] = fence((own[1], dheads[2], dheads[3]))
+        after, dheads[2], dheads[3], pieces1 = fence((own[1], dheads[2], dheads[3], pieces1))
         own = (own[0], after, own[2])
         other = attend_back((2, 3), probs_other, dheads[2], dheads[3])
 
-        out_rows = local // 2 // m
-        out_rows += -out_rows % 16
-        grad_rows = width // m + out_rows + 16
-        after, dattn[0] = fence((other[1], dattn[0]))
-        other = (other[0], after, other[2])
-        keep1, send1 = call(
-            functools.partial(ffn_grad_kernel, m),
-            (near((m, 2, grad_rows, width), bf16), near((m, 2, grad_rows, width), bf16)),
-            "ffn_grads",
-            (
-                at, hp_mine, hps[1], *lows, *acts, *acts_far, *dffns, *dinners, *dinners_far, *dattn,
-                *sums2, *sums1,
-            ),
-            us=4.0,
-            vmem=24,
-            scalars=1,
-        )
         def exchange(third):
             _, send, keep = third
             recv = flip(send, 1)
             return recv, (keep[1].astype(f32) + recv[1].astype(f32)).astype(bf16)
 
-        def input_part(third, recv, far, *theirs):
+        def input_part(third, recv, far, us):
             dq, _, keep = third
             return call(
                 input_kernel,
                 (chunk(2 * BLOCK, bf16), near((lanes, 2 * BLOCK), bf16), chunk(8, f32)),
                 "input_part",
-                (dq, keep, recv, far, wq_t, wkv_t, *theirs),
-                us=1.0,
+                (dq, keep, recv, far, wq_t, wkv_t),
+                us=us,
             )
 
         recv_own, sum_own = exchange(own)
         recv_other, sum_other = exchange(other)
-        send1, sum_own, sum_other = fence((send1, sum_own, sum_other))
-        recv1 = flip(send1, 1)
         far_own, far_other = flip(sum_own, 2), flip(sum_other, 2)
-        pieces1 = share_pieces(keep1, recv1, member)
-        far_own, far_other, pieces1, *ends = fence((far_own, far_other, pieces1, *outs[2:]))
-        outs[2:] = ends
-        part, *late = input_part(other, recv_other, far_other)
+        far_own, far_other, pieces1 = fence((far_own, far_other, pieces1))
+        part, *late = input_part(other, recv_other, far_other, 1.0)
+        part, pieces1, *ends = fence((part, pieces1, *shares[2:]))
+        shares[2:] = ends
+        from_near = swap(part, 1)
         got1 = [flip_member(v, s) for s, v in enumerate(pieces1[1:], 1)]
-        pair, dkv_own, sums_own = input_part(own, recv_own, far_own, swap(part, 1))
-        d_tok = pair.astype(f32) + swap(pair, 2).astype(f32) + jnp.concatenate(dres1, axis=0)
-        d_tok = d_tok.astype(bf16)
-
-        rows2 = 3 * local // 2 + 16
+        part_own, dkv_own, sums_own = input_part(own, recv_own, far_own, INPUT_US)
+        pair = (part_own.astype(f32) + from_near.astype(f32)).astype(bf16)
+
+        rows2 = 2 * local + 16
         rows2 += -rows2 % (16 * m)
         keep2, send2 = call(
             functools.partial(attend_grad_kernel, m),
             (chunk(rows2, bf16), chunk(rows2, bf16)),
             "attend_grads",
-            (at, tok, own[0], other[0], dkv_own, late[0], sums_own, late[1]),
-            us=1.5,
+            (
+                at, tok, hp_mine, hp_other, *shares, own[0], other[0], dkv_own, late[0], sums_own,
+                late[1],
+            ),
+            us=GRADS_US,
             scalars=1,
+            scratch=[pltpu.VMEM((n, 8, width), f32)],
         )
         by_member = lambda v: v.reshape(m, rows2 // m, width)
         pieces2 = share_pieces(by_member(keep2), by_member(flip(send2, 1)), member)
-        pieces2, got1 = fence((pieces2, got1))
         got2 = [flip_member(v, s) for s, v in enumerate(pieces2[1:], 1)]
+        crossed, got1 = fence((swap(pair, 2), got1))
+        d_tok = pair.astype(f32) + crossed.astype(f32) + jnp.concatenate(dres1, axis=0)
+        d_tok = d_tok.astype(bf16)
         total1 = fence(add(pieces1[0], got1))
-        near1 = swap(total1[1], 1)
-        d_tok, near1 = fence((d_tok, near1))
-        d_toks = [d_tok, swap(d_tok, 1)]
-        share1 = total1[0].astype(f32) + near1.astype(f32)
-        share1, got2 = fence((share1.astype(bf16), got2))
-        mine1 = gather_grads(share1, at, "gather_ffn_grads")
+        near1, d_far, got2 = fence((swap(total1[1], 1), swap(d_tok, 1), got2))
+        d_toks = [d_tok, d_far]
+        share1 = (total1[0].astype(f32) + near1.astype(f32)).astype(bf16)
+        total2 = add(pieces2[0], got2)
+        mine1, *ends = gather_grads(share1, at, "gather_ffn_grads", *outs[2:])
+        outs[2:] = ends
         other1 = flip(mine1, 1)
-        total2 = add(pieces2[0], got2)
-        total2, *d_toks = fence((total2, *d_toks))
-        mine2 = gather_grads(total2, at, "gather_attend_grads").reshape(rows2, width)
+        (mine2,) = gather_grads(total2, at, "gather_attend_grads")
+        mine2 = mine2.reshape(rows2, width)
         other2 = flip(mine2, 1)
 
         vector = shape((width,), f32)
         short = shape((local,), f32)
         square = shape((width, units), f32)
         wide = shape((local, width), f32)
-        g_w_inner, g_w_outer, g_w_out, g_gain2, g_bias2, g_b_outer, g_b_inner, g_gain1, g_bias1, g_b_out = call(
+        g_w_inner, g_w_outer, g_gain2, g_bias2, g_b_outer, g_b_inner = call(
             functools.partial(ffn_final_kernel, m),
-            (square, square, wide) + (vector,) * 7,
+            (square, square) + (vector,) * 4,
             "ffn_grads_out",
             (at, mine1, other1),
             us=3.0,
@@ -737,10 +728,10 @@
         )
         output = assemble(outs, "output_rows")
         d_tokens = assemble(d_toks, "input_grad_rows")
-        other2, g_b_out = fence((other2, g_b_out))
-        g_q, g_k, g_v, g_b_query, g_b_value = call(
+        other2, g_b_outer = fence((other2, g_b_outer))
+        g_w_out, g_q, g_k, g_v, g_gain1, g_bias1, g_b_out, g_b_query, g_b_value = call(
             attend_final_kernel,
-            (wide,) * 3 + (short,) * 2,
+            (wide,) * 4 + (vector,) * 3 + (short,) * 2,
             "attend_grads_out",
             (at, mine2, other2),
             us=2.0,

time: 221 us -> 202 us (0.914)
  waiting for transfers between devices: 120 us -> 96.8 us
  starting transfers between devices: 43.1 us -> 48.5 us
  local copies, waits for them, and re-layouts: 6.27 us -> 10.5 us
  other arithmetic: 5.03 us -> 1.7 us
    ppermute x19 -> x21, waiting for transfers between devices: 69.4 us -> 52 us  [swap(): return lax.ppermute(v, 'tensor', [(i, i ^ bit) for i in range(n)])]
    ppermute x3, waiting for transfers between devices: 7.99 us -> 0.01 us  [across(): lax.ppermute(v, ('dp', 'blk'), [(i, there(i)) for i in range(n_dp * n_blk)])]
    ppermute x19 -> x21, starting transfers between devices: 19.2 us -> 25.3 us  [swap(): return lax.ppermute(v, 'tensor', [(i, i ^ bit) for i in range(n)])]
    ppermute x15, waiting for transfers between devices: 4.46 us -> 10.4 us  [flip(): return lax.ppermute(v, 'blk', [(i, i ^ bit) for i in range(n_blk)])]
    ppermute x12, waiting for transfers between devices: 38.6 us -> 34.3 us  [flip_member(): return lax.ppermute(v, ('dp', 'blk'), perm)]
    unnamed x82 -> x98, local copies, waits for them, and re-layouts: 6.1 us -> 10.3 us
  transfers between devices with their start and end apart: 49 -> 51, of which waited for: 29 -> 27; matrix products, arithmetic and copies ran while one was open for 2% -> 1% of each run, Pallas kernels for 15% -> 17%
where the time goes in v5:
time: 202 us
  waiting for transfers between devices  96.8 us (48%)
  starting transfers between devices  48.5 us (24%)
  Pallas kernels  42.9 us (21%)
  local copies, waits for them, and re-layouts  10.5 us (5%)
    ppermute x21, waiting for transfers between devices, swap(): return lax.ppermute(v, 'tensor', [(i, i ^ bit) for i in range(n)])  52 us
    pallas_call x22, Pallas kernels, call(): pl.pallas_call(kernel, out_shape=outs, in_specs=[SMEM] * scalars + [VMEM]...  41.8 us
    ppermute x12, waiting for transfers between devices, flip_member(): return lax.ppermute(v, ('dp', 'blk'), perm)  34.3 us
    ppermute x21, starting transfers between devices, swap(): return lax.ppermute(v, 'tensor', [(i, i ^ bit) for i in range(n)])  25.3 us
    ppermute x12, starting transfers between devices, flip_member(): return lax.ppermute(v, ('dp', 'blk'), perm)  14.1 us
    ppermute x15, waiting for transfers between devices, flip(): return lax.ppermute(v, 'blk', [(i, i ^ bit) for i in range(n_blk)])  10.4 us
    unnamed x98, local copies, waits for them, and re-layouts  10.3 us
    ppermute x15, starting transfers between devices, flip(): return lax.ppermute(v, 'blk', [(i, i ^ bit) for i in range(n_blk)])  5.48 us
  transfers between devices with their start and end apart: 51, of which 27 were waited for; matrix products, arithmetic and copies ran while one was open for 1% of the time, Pallas kernels for 17%

profile of v5, /device:TPU:0, one launch (start us, length us, event | category | flops | bytes accessed | tf_op | source)
XLA Modules:
  0.0 201.9 jit_solution(10315616182434794380)
XLA Ops:
  7.8 3.0 %collective-permute-start = (bf16[512,384]{1,0:T(8,128)(2,1)}, bf16[512,384]{1,0:T(8,128)(2,1)S(1)}, u32[]{:S(2)}, u32[]{:S(2)}) collective-permute-start(bf16[512,384]{1,0:T(8,128)(2,1)} %get-tuple-element.152.refs_0_), channel_id=1, source_target_pairs={{0,8},{4,12},{8,0},{12,4},{1,9},{5,13},{9,1},{13,5},{2,10},{6,14},... | collective-permute-start | bytes 1179656 | tf_op jit(solution)/shard_map/ppermute | solution.py:438
  12.4 2.6 %collective-permute-start.3 = (bf16[48,768]{1,0:T(8,128)(2,1)S(1)}, bf16[48,768]{1,0:T(8,128)(2,1)S(1)}, u32[]{:S(2)}, u32[]{:S(2)}) collective-permute-start(bf16[48,768]{1,0:T(8,128)(2,1)S(1)} %get-tuple-element.155), channel_id=1, source_target_pairs={{0,2},{1,3},{2,0},{3,1},{4,6},{5,7},{6,4},{7,5},{8,10},{9,11},{10,... | collective-permute-start | bytes 221192 | tf_op jit(solution)/shard_map/ppermute | solution.py:435
  15.9 7.3 %collective-permute-done.1 = f32[768]{0:T(1024)S(1)} collective-permute-done((f32[768]{0:T(1024)S(1)}, f32[768]{0:T(1024)S(1)}, u32[]{:S(2)}, u32[]{:S(2)}) %collective-permute-start.1) | collective-permute-done | bytes 3104 | tf_op jit(solution)/shard_map/ppermute | solution.py:435
  23.2 2.9 %collective-permute-done.4 = bf16[48,768]{1,0:T(8,128)(2,1)S(1)} collective-permute-done((bf16[48,768]{1,0:T(8,128)(2,1)S(1)}, bf16[48,768]{1,0:T(8,128)(2,1)S(1)}, u32[]{:S(2)}, u32[]{:S(2)}) %collective-permute-start.4) | collective-permute-done | bytes 73760 | tf_op jit(solution)/shard_map/ppermute | solution.py:435
  30.6 5.6 %attend.1 = (bf16[384,128]{1,0:T(8,128)(2,1)S(1)}, bf16[768,512]{1,0:T(8,128)(2,1)S(1)}, bf16[384,128]{1,0:T(8,128)(2,1)S(1)}, bf16[768,512]{1,0:T(8,128)(2,1)S(1)}) custom-call(s32[5]{0:T(128)S(1)} %stack.23.at, s32[4]{0:T(128)S(1)} %copy-done.32, s32[4,4]{1,0:T(4,128)S(1)} %copy-done.29, bf16[512,384]{1,0:T(8,128)(2,1)S(1)} %query_rows.1.q, ...), custom_call_target="tpu_custom_call" | custom-call | flops 49999998976 | bytes 1 | tf_op jit(solution)/shard_map/attend/pallas_call | solution.py:72
  38.0 2.6 %collective-permute-start.9 = (bf16[384,128]{1,0:T(8,128)(2,1)S(1)}, bf16[384,128]{1,0:T(8,128)(2,1)S(1)}, u32[]{:S(2)}, u32[]{:S(2)}) collective-permute-start(bf16[384,128]{1,0:T(8,128)(2,1)S(1)} %get-tuple-element.161.refs_0_.hp_mine), channel_id=1, source_target_pairs={{0,2},{1,3},{2,0},{3,1},{4,6},{5,7},{6,4},{7,5},{8,10},{9,11},{10,... | collective-permute-start | bytes 294920 | tf_op jit(solution)/shard_map/ppermute | solution.py:435
  44.2 4.4 %collective-permute-done.9.refs_2_ = bf16[384,128]{1,0:T(8,128)(2,1)S(1)} collective-permute-done((bf16[384,128]{1,0:T(8,128)(2,1)S(1)}, bf16[384,128]{1,0:T(8,128)(2,1)S(1)}, u32[]{:S(2)}, u32[]{:S(2)}) %collective-permute-start.9) | collective-permute-done | bytes 98336 | tf_op jit(solution)/shard_map/ppermute | solution.py:435
  54.9 2.3 %ffn.2 = (bf16[128,768]{1,0:T(8,128)(2,1)S(1)}, f32[128,768]{1,0:T(8,128)S(1)}, f32[128,128]{1,0:T(8,128)S(1)}, bf16[128,768]{1,0:T(8,128)(2,1)S(1)}, bf16[128,7...) custom-call(s32[5]{0:T(128)S(1)} %stack.23.at, bf16[512,768]{1,0:T(8,128)(2,1)S(1)} %bitcast.54, ...), custom_call_target="tpu_custom_call" | custom-call | flops 2400000000 | bytes 1 | tf_op jit(solution)/shard_map/ffn/pallas_call | solution.py:72
  58.6 2.3 %ffn.3 = (bf16[128,768]{1,0:T(8,128)(2,1)S(1)}, f32[128,768]{1,0:T(8,128)S(1)}, f32[128,128]{1,0:T(8,128)S(1)}, bf16[128,768]{1,0:T(8,128)(2,1)S(1)}, bf16[128,7...) custom-call(s32[5]{0:T(128)S(1)} %stack.23.at, bf16[512,768]{1,0:T(8,128)(2,1)S(1)} %bitcast.55, ...), custom_call_target="tpu_custom_call" | custom-call | flops 2400000000 | bytes 1 | tf_op jit(solution)/shard_map/ffn/pallas_call | solution.py:72
  62.6 11.4 %collective-permute-done.17.theirs = bf16[128,768]{1,0:T(8,128)(2,1)S(1)} collective-permute-done((bf16[128,768]{1,0:T(8,128)(2,1)S(1)}, bf16[128,768]{1,0:T(8,128)(2,1)S(1)}, u32[]{:S(2)}, u32[]{:S(2)}) %collective-permute-start.17) | collective-permute-done | bytes 196640 | tf_op jit(solution)/shard_map/ppermute | solution.py:435
  74.0 2.7 %ffn_back.2 = (bf16[128,768]{1,0:T(8,128)(2,1)S(1)}, bf16[128,768]{1,0:T(8,128)(2,1)S(1)}, bf16[128,768]{1,0:T(8,128)(2,1)S(1)}, bf16[128,768]{1,0:T(8,128)(2,1)...) custom-call(s32[5]{0:T(128)S(1)} %stack.23.at, bf16[512,768]{1,0:T(8,128)(2,1)S(1)} %bitcast.50, ...), custom_call_target="tpu_custom_call" | custom-call | flops 2700000000 | bytes 1 | tf_op jit(solution)/shard_map/ffn_back/pallas_call | solution.py:72
  77.8 2.7 %ffn_back.3 = (bf16[128,768]{1,0:T(8,128)(2,1)S(1)}, bf16[128,768]{1,0:T(8,128)(2,1)S(1)}, bf16[128,768]{1,0:T(8,128)(2,1)S(1)}, bf16[128,768]{1,0:T(8,128)(2,1)...) custom-call(s32[5]{0:T(128)S(1)} %stack.23.at, bf16[512,768]{1,0:T(8,128)(2,1)S(1)} %bitcast.51, ...), custom_call_target="tpu_custom_call" | custom-call | flops 2700000000 | bytes 1 | tf_op jit(solution)/shard_map/ffn_back/pallas_call | solution.py:72
  82.5 2.2 %ffn_grads.1 = (bf16[4,2,208,768]{3,2,1,0:T(8,128)(2,1)S(1)}, bf16[4,2,208,768]{3,2,1,0:T(8,128)(2,1)S(1)}) custom-call(s32[5]{0:T(128)S(1)} %stack.23.at, bf16[128,768]{1,0:T(8,128)(2,1)S(1)} %get-tuple-element.192.refs_0_, bf16[128,768]{1,0:T(8,128)(2,1)S(1)} %get-tuple-element.193.refs_1_, bf16[128,768]{1,0:T(8,128)(2,1)S(1)} %get-tuple-element.194.refs_2_, ...), custom_call_target="tpu_custom_call" | custom-call | flops 49999998976 | bytes 1 | tf_op jit(solution)/shard_map/ffn_grads/pallas_call | solution.py:72
  84.8 6.5 %collective-permute-done.19.theirs = bf16[128,768]{1,0:T(8,128)(2,1)S(1)} collective-permute-done((bf16[128,768]{1,0:T(8,128)(2,1)S(1)}, bf16[128,768]{1,0:T(8,128)(2,1)S(1)}, u32[]{:S(2)}, u32[]{:S(2)}) %collective-permute-start.19) | collective-permute-done | bytes 196640 | tf_op jit(solution)/shard_map/ppermute | solution.py:435
  92.6 2.9 %collective-permute-done.20.theirs = bf16[128,768]{1,0:T(8,128)(2,1)S(1)} collective-permute-done((bf16[128,768]{1,0:T(8,128)(2,1)S(1)}, bf16[128,768]{1,0:T(8,128)(2,1)S(1)}, u32[]{:S(2)}, u32[]{:S(2)}) %collective-permute-start.20) | collective-permute-done | bytes 196640 | tf_op jit(solution)/shard_map/ppermute | solution.py:435
  97.1 3.2 %attend_back.2 = (bf16[256,192]{1,0:T(8,128)(2,1)S(1)}, bf16[2,2,384,128]{3,2,1,0:T(8,128)(2,1)S(1)}, bf16[2,2,384,128]{3,2,1,0:T(8,128)(2,1)S(1)}) custom-call(s32[5]{0:T(128)S(1)} %stack.23.at, bf16[192,128]{1,0:T(8,128)(2,1)S(1)} %get-tuple-element.183.first, bf16[192,128]{1,0:T(8,128)(2,1)S(1)} %get-tuple-element.187.second, ...), custom_call_target="tpu_custom_call" | custom-call | flops 49999998976 | bytes 1 | tf_op jit(solution)/shard_map/attend_back/pallas_call | solution.py:72
  101.4 3.2 %attend_back.3 = (bf16[256,192]{1,0:T(8,128)(2,1)S(1)}, bf16[2,2,384,128]{3,2,1,0:T(8,128)(2,1)S(1)}, bf16[2,2,384,128]{3,2,1,0:T(8,128)(2,1)S(1)}) custom-call(s32[5]{0:T(128)S(1)} %stack.23.at, bf16[192,128]{1,0:T(8,128)(2,1)S(1)} %collective-permute-done.21.first, bf16[192,128]{1,0:T(8,128)(2,1)S(1)} %collective-permute-done.22.second, ...), custom_call_target="tpu_custom_call" | custom-call | flops 49999998976 | bytes 1 | tf_op jit(solution)/shard_map/attend_back/pallas_call | solution.py:72
  109.2 3.5 %collective-permute-done.26.far = bf16[2,384,128]{2,1,0:T(8,128)(2,1)S(1)} collective-permute-done((bf16[2,384,128]{2,1,0:T(8,128)(2,1)S(1)}, bf16[2,384,128]{2,1,0:T(8,128)(2,1)S(1)}, u32[]{:S(2)}, u32[]{:S(2)}) %collective-permute-start.26) | collective-permute-done | bytes 196640 | tf_op jit(solution)/shard_map/ppermute | solution.py:438
  112.8 3.6 %collective-permute-done.27.far = bf16[2,384,128]{2,1,0:T(8,128)(2,1)S(1)} collective-permute-done((bf16[2,384,128]{2,1,0:T(8,128)(2,1)S(1)}, bf16[2,384,128]{2,1,0:T(8,128)(2,1)S(1)}, u32[]{:S(2)}, u32[]{:S(2)}) %collective-permute-start.27) | collective-permute-done | bytes 196640 | tf_op jit(solution)/shard_map/ppermute | solution.py:438
  124.8 4.2 %collective-permute-done.30 = bf16[256,768]{1,0:T(8,128)(2,1)S(1)} collective-permute-done((bf16[256,768]{1,0:T(8,128)(2,1)S(1)}, bf16[256,768]{1,0:T(8,128)(2,1)S(1)}, u32[]{:S(2)}, u32[]{:S(2)}) %collective-permute-start.30) | collective-permute-done | bytes 393248 | tf_op jit(solution)/shard_map/ppermute | solution.py:435
  129.1 2.6 %collective-permute-start.31 = (bf16[256,768]{1,0:T(8,128)(2,1)S(1)}, bf16[256,768]{1,0:T(8,128)(2,1)S(1)}, u32[]{:S(2)}, u32[]{:S(2)}) collective-permute-start(bf16[256,768]{1,0:T(8,128)(2,1)S(1)} %add_convert_fusion.5), channel_id=1, source_target_pairs={{0,2},{1,3},{2,0},{3,1},{4,6},{5,7},{6,4},{7,5},{8,10},{9,11},{10,... | collective-permute-start | bytes 1179656 | tf_op jit(solution)/shard_map/ppermute | solution.py:435
  133.2 3.9 %collective-permute-done.32 = bf16[2,208,768]{2,1,0:T(8,128)(2,1)S(1)} collective-permute-done((bf16[2,208,768]{2,1,0:T(8,128)(2,1)S(1)}, bf16[2,208,768]{2,1,0:T(8,128)(2,1)S(1)}, u32[]{:S(2)}, u32[]{:S(2)}) %collective-permute-start.32) | collective-permute-done | bytes 639008 | tf_op jit(solution)/shard_map/ppermute | solution.py:447
  137.2 2.4 %collective-permute-done.33 = bf16[2,208,768]{2,1,0:T(8,128)(2,1)S(1)} collective-permute-done((bf16[2,208,768]{2,1,0:T(8,128)(2,1)S(1)}, bf16[2,208,768]{2,1,0:T(8,128)(2,1)S(1)}, u32[]{:S(2)}, u32[]{:S(2)}) %collective-permute-start.33) | collective-permute-done | bytes 639008 | tf_op jit(solution)/shard_map/ppermute | solution.py:447
  139.6 11.0 %collective-permute-done.34 = bf16[2,208,768]{2,1,0:T(8,128)(2,1)S(1)} collective-permute-done((bf16[2,208,768]{2,1,0:T(8,128)(2,1)S(1)}, bf16[2,208,768]{2,1,0:T(8,128)(2,1)S(1)}, u32[]{:S(2)}, u32[]{:S(2)}) %collective-permute-start.34) | collective-permute-done | bytes 639008 | tf_op jit(solution)/shard_map/ppermute | solution.py:447
  156.9 3.2 %collective-permute-done.38 = bf16[112,768]{1,0:T(8,128)(2,1)S(1)} collective-permute-done((bf16[112,768]{1,0:T(8,128)(2,1)S(1)}, bf16[112,768]{1,0:T(8,128)(2,1)S(1)}, u32[]{:S(2)}, u32[]{:S(2)}) %collective-permute-start.38) | collective-permute-done | bytes 172064 | tf_op jit(solution)/shard_map/ppermute | solution.py:447
  160.4 2.4 %collective-permute-done.40 = bf16[112,768]{1,0:T(8,128)(2,1)S(1)} collective-permute-done((bf16[112,768]{1,0:T(8,128)(2,1)S(1)}, bf16[112,768]{1,0:T(8,128)(2,1)S(1)}, u32[]{:S(2)}, u32[]{:S(2)}) %collective-permute-start.40) | collective-permute-done | bytes 172064 | tf_op jit(solution)/shard_map/ppermute | solution.py:447
  162.9 3.6 %collective-permute-done.35 = bf16[208,768]{1,0:T(8,128)(2,1)S(1)} collective-permute-done((bf16[208,768]{1,0:T(8,128)(2,1)S(1)}, bf16[208,768]{1,0:T(8,128)(2,1)S(1)}, u32[]{:S(2)}, u32[]{:S(2)}) %collective-permute-start.35) | collective-permute-done | bytes 319520 | tf_op jit(solution)/shard_map/ppermute | solution.py:435
  172.1 3.6 %collective-permute-done.44.refs_2_ = bf16[128,768]{1,0:T(8,128)(2,1)S(1)} collective-permute-done((bf16[128,768]{1,0:T(8,128)(2,1)S(1)}, bf16[128,768]{1,0:T(8,128)(2,1)S(1)}, u32[]{:S(2)}, u32[]{:S(2)}) %collective-permute-start.44) | collective-permute-done | bytes 196640 | tf_op jit(solution)/shard_map/ppermute | solution.py:435
  177.8 2.9 %collective-permute-done.43.refs_3_ = bf16[208,768]{1,0:T(8,128)(2,1)S(1)} collective-permute-done((bf16[208,768]{1,0:T(8,128)(2,1)S(1)}, bf16[208,768]{1,0:T(8,128)(2,1)S(1)}, u32[]{:S(2)}, u32[]{:S(2)}) %collective-permute-start.43) | collective-permute-done | bytes 319520 | tf_op jit(solution)/shard_map/ppermute | solution.py:447
  185.1 3.3 %collective-permute-done.46.refs_1_ = bf16[112,768]{1,0:T(8,128)(2,1)S(1)} collective-permute-done((bf16[112,768]{1,0:T(8,128)(2,1)S(1)}, bf16[112,768]{1,0:T(8,128)(2,1)S(1)}, u32[]{:S(2)}, u32[]{:S(2)}) %collective-permute-start.46) | collective-permute-done | bytes 172064 | tf_op jit(solution)/shard_map/ppermute | solution.py:447
  190.5 2.8 %collective-permute-done.48.refs_3_ = bf16[112,768]{1,0:T(8,128)(2,1)S(1)} collective-permute-done((bf16[112,768]{1,0:T(8,128)(2,1)S(1)}, bf16[112,768]{1,0:T(8,128)(2,1)S(1)}, u32[]{:S(2)}, u32[]{:S(2)}) %collective-permute-start.48) | collective-permute-done | bytes 172064 | tf_op jit(solution)/shard_map/ppermute | solution.py:447
  196.9 2.9 %ffn_grads_out.1 = (f32[768,768]{1,0:T(8,128)}, f32[768,768]{1,0:T(8,128)}, f32[768]{0:T(1024)}, f32[768]{0:T(1024)}, f32[768]{0:T(1024)}, /*index=5*/f32[768]{0:T(1024)}) custom-call(s32[5]{0:T(128)S(1)} %stack.23.at, bf16[4,208,768]{2,1,0:T(8,128)(2,1)S(1)} %gather_ffn_grads.1.mine, bf16[4,208,768]{2,1,0:T(8,128)(2,1)S(1)} %collective-permute-done.50.other), custom_call_target="tpu_custom_call" | custom-call | flops 3000000000 | bytes 1 | tf_op jit(solution)/shard_map/ffn_grads_out/pallas_call | solution.py:72
  (212 shorter events, 76.4 us)
Async XLA Ops:
  7.8 18.3 %collective-permute-start = (bf16[512,384]{1,0:T(8,128)(2,1)}, bf16[512,384]{1,0:T(8,128)(2,1)S(1)}, u32[]{:S(2)}, u32[]{:S(2)}) collective-permute-start(bf16[512,384]{1,0:T(8,128)(2,1)} %get-tuple-element.152.refs_0_), channel_id=1, source_target_pairs={{0,8},{4,12},{8,0},{12,4},{1,9},{5,13},{9,1},{13,5},{2,10},{6,14},... | collective-permute-start | bytes 1179656 | tf_op jit(solution)/shard_map/ppermute | solution.py:438
  10.8 15.3 %collective-permute-start.2 = (bf16[240,768]{1,0:T(8,128)(2,1)S(1)}, bf16[240,768]{1,0:T(8,128)(2,1)S(1)}, u32[]{:S(2)}, u32[]{:S(2)}) collective-permute-start(bf16[240,768]{1,0:T(8,128)(2,1)S(1)} %get-tuple-element.154), channel_id=1, source_target_pairs={{0,1},{1,0},{2,3},{3,2},{4,5},{5,4},{6,7},{7,6},{8,9},{9,8},{10,11... | collective-permute-start | bytes 1105928 | tf_op jit(solution)/shard_map/ppermute | solution.py:435
  12.4 10.8 %collective-permute-start.3 = (bf16[48,768]{1,0:T(8,128)(2,1)S(1)}, bf16[48,768]{1,0:T(8,128)(2,1)S(1)}, u32[]{:S(2)}, u32[]{:S(2)}) collective-permute-start(bf16[48,768]{1,0:T(8,128)(2,1)S(1)} %get-tuple-element.155), channel_id=1, source_target_pairs={{0,2},{1,3},{2,0},{3,1},{4,6},{5,7},{6,4},{7,5},{8,10},{9,11},{10,... | collective-permute-start | bytes 221192 | tf_op jit(solution)/shard_map/ppermute | solution.py:435
  15.0 11.1 %collective-permute-start.4 = (bf16[48,768]{1,0:T(8,128)(2,1)S(1)}, bf16[48,768]{1,0:T(8,128)(2,1)S(1)}, u32[]{:S(2)}, u32[]{:S(2)}) collective-permute-start(bf16[48,768]{1,0:T(8,128)(2,1)S(1)} %get-tuple-element.155), channel_id=1, source_target_pairs={{0,3},{1,2},{2,1},{3,0},{4,7},{5,6},{6,5},{7,4},{8,11},{9,10},{10,... | collective-permute-start | bytes 221192 | tf_op jit(solution)/shard_map/ppermute | solution.py:435
  15.2 8.0 %collective-permute-start.1 = (f32[768]{0:T(1024)S(1)}, f32[768]{0:T(1024)S(1)}, u32[]{:S(2)}, u32[]{:S(2)}) collective-permute-start(f32[768]{0:T(1024)S(1)} %copy-done.41), channel_id=1, source_target_pairs={{0,1},{1,0},{2,3},{3,2},{4,5},{5,4},{6,7},{7,6},{8,9},{9,8},{10,11... | collective-permute-start | bytes 9224 | tf_op jit(solution)/shard_map/ppermute | solution.py:435
  26.8 14.5 %collective-permute-start.12 = (bf16[192,768]{1,0:T(8,128)(2,1)S(1)}, bf16[192,768]{1,0:T(8,128)(2,1)S(1)}, u32[]{:S(2)}, u32[]{:S(2)}) collective-permute-start(bf16[192,768]{1,0:T(8,128)(2,1)S(1)} %slice.21), channel_id=1, source_target_pairs={{0,16},{4,20},{8,24},{12,28},{16,0},{20,4},{24,8},{28,12},{1,17},{... | collective-permute-start | bytes 884744 | tf_op jit(solution)/shard_map/ppermute | solution.py:529
  28.3 15.3 %collective-permute-start.13 = (bf16[192,768]{1,0:T(8,128)(2,1)S(1)}, bf16[192,768]{1,0:T(8,128)(2,1)}, u32[]{:S(2)}, u32[]{:S(2)}) collective-permute-start(bf16[192,768]{1,0:T(8,128)(2,1)S(1)} %slice.21), channel_id=1, source_target_pairs={{0,24},{4,28},{8,16},{12,20},{16,8},{20,12},{24,0},{28,4},{1,25},{... | collective-permute-start | bytes 884744 | tf_op jit(solution)/shard_map/ppermute | solution.py:529
  28.9 21.0 %collective-permute-start.11 = (bf16[336,768]{1,0:T(8,128)(2,1)S(1)}, bf16[336,768]{1,0:T(8,128)(2,1)}, u32[]{:S(2)}, u32[]{:S(2)}) collective-permute-start(bf16[336,768]{1,0:T(8,128)(2,1)S(1)} %constant_dynamic-update-slice_fusion.refs_0_), channel_id=1, source_target_pairs={{0,8},{4,12},{8,0},{12,4},{16,24},{20,28},{24,16},{28,20},{1,9},{5... | collective-permute-start | bytes 1548296 | tf_op jit(solution)/shard_map/ppermute | solution.py:529
  38.0 10.6 %collective-permute-start.9 = (bf16[384,128]{1,0:T(8,128)(2,1)S(1)}, bf16[384,128]{1,0:T(8,128)(2,1)S(1)}, u32[]{:S(2)}, u32[]{:S(2)}) collective-permute-start(bf16[384,128]{1,0:T(8,128)(2,1)S(1)} %get-tuple-element.161.refs_0_.hp_mine), channel_id=1, source_target_pairs={{0,2},{1,3},{2,0},{3,1},{4,6},{5,7},{6,4},{7,5},{8,10},{9,11},{10,... | collective-permute-start | bytes 294920 | tf_op jit(solution)/shard_map/ppermute | solution.py:435
  41.2 8.0 %collective-permute-start.10 = (bf16[384,128]{1,0:T(8,128)(2,1)S(1)}, bf16[384,128]{1,0:T(8,128)(2,1)S(1)}, u32[]{:S(2)}, u32[]{:S(2)}) collective-permute-start(bf16[384,128]{1,0:T(8,128)(2,1)S(1)} %get-tuple-element.160.hp_other), channel_id=1, source_target_pairs={{0,3},{1,2},{2,1},{3,0},{4,7},{5,6},{6,5},{7,4},{8,11},{9,10},{10,... | collective-permute-start | bytes 294920 | tf_op jit(solution)/shard_map/ppermute | solution.py:435
  57.2 16.8 %collective-permute-start.17 = (bf16[128,768]{1,0:T(8,128)(2,1)S(1)}, bf16[128,768]{1,0:T(8,128)(2,1)S(1)}, u32[]{:S(2)}, u32[]{:S(2)}) collective-permute-start(bf16[128,768]{1,0:T(8,128)(2,1)S(1)} %get-tuple-element.174.mine), channel_id=1, source_target_pairs={{0,2},{1,3},{2,0},{3,1},{4,6},{5,7},{6,4},{7,5},{8,10},{9,11},{10,... | collective-permute-start | bytes 589832 | tf_op jit(solution)/shard_map/ppermute | solution.py:435
  60.9 16.8 %collective-permute-start.18 = (bf16[128,768]{1,0:T(8,128)(2,1)S(1)}, bf16[128,768]{1,0:T(8,128)(2,1)S(1)}, u32[]{:S(2)}, u32[]{:S(2)}) collective-permute-start(bf16[128,768]{1,0:T(8,128)(2,1)S(1)} %get-tuple-element.178.mine), channel_id=1, source_target_pairs={{0,2},{1,3},{2,0},{3,1},{4,6},{5,7},{6,4},{7,5},{8,10},{9,11},{10,... | collective-permute-start | bytes 589832 | tf_op jit(solution)/shard_map/ppermute | solution.py:435
  76.8 14.6 %collective-permute-start.19 = (bf16[128,768]{1,0:T(8,128)(2,1)S(1)}, bf16[128,768]{1,0:T(8,128)(2,1)S(1)}, u32[]{:S(2)}, u32[]{:S(2)}) collective-permute-start(bf16[128,768]{1,0:T(8,128)(2,1)S(1)} %get-tuple-element.180.mine), channel_id=1, source_target_pairs={{0,2},{1,3},{2,0},{3,1},{4,6},{5,7},{6,4},{7,5},{8,10},{9,11},{10,... | collective-permute-start | bytes 589832 | tf_op jit(solution)/shard_map/ppermute | solution.py:435
  80.5 15.0 %collective-permute-start.20 = (bf16[128,768]{1,0:T(8,128)(2,1)S(1)}, bf16[128,768]{1,0:T(8,128)(2,1)S(1)}, u32[]{:S(2)}, u32[]{:S(2)}) collective-permute-start(bf16[128,768]{1,0:T(8,128)(2,1)S(1)} %get-tuple-element.184.mine), channel_id=1, source_target_pairs={{0,2},{1,3},{2,0},{3,1},{4,6},{5,7},{6,4},{7,5},{8,10},{9,11},{10,... | collective-permute-start | bytes 589832 | tf_op jit(solution)/shard_map/ppermute | solution.py:435
  84.7 15.5 %collective-permute-start.23 = (bf16[4,2,208,768]{3,2,1,0:T(8,128)(2,1)S(1)}, bf16[4,2,208,768]{3,2,1,0:T(8,128)(2,1)S(1)}, u32[]{:S(2)}, u32[]{:S(2)}) collective-permute-start(bf16[4,2,208,768]{3,2,1,0:T(8,128)(2,1)S(1)} %get-tuple-element.207), channel_id=1, source_target_pairs={{0,4},{4,0},{8,12},{12,8},{1,5},{5,1},{9,13},{13,9},{2,6},{6,2},{1... | collective-permute-start | bytes 7667720 | tf_op jit(solution)/shard_map/ppermute | solution.py:438
  92.5 8.5 %collective-permute-start.21 = (bf16[192,128]{1,0:T(8,128)(2,1)S(1)}, bf16[192,128]{1,0:T(8,128)(2,1)S(1)}, u32[]{:S(2)}, u32[]{:S(2)}) collective-permute-start(bf16[192,128]{1,0:T(8,128)(2,1)S(1)} %get-tuple-element.190), channel_id=1, source_target_pairs={{0,1},{1,0},{2,3},{3,2},{4,5},{5,4},{6,7},{7,6},{8,9},{9,8},{10,11... | collective-permute-start | bytes 147464 | tf_op jit(solution)/shard_map/ppermute | solution.py:435
  106.5 9.9 %collective-permute-start.27 = (bf16[2,384,128]{2,1,0:T(8,128)(2,1)S(1)}, bf16[2,384,128]{2,1,0:T(8,128)(2,1)S(1)}, u32[]{:S(2)}, u32[]{:S(2)}) collective-permute-start(bf16[2,384,128]{2,1,0:T(8,128)(2,1)S(1)} %fusion.10), channel_id=1, source_target_pairs={{0,8},{4,12},{8,0},{12,4},{1,9},{5,13},{9,1},{13,5},{2,10},{6,14},... | collective-permute-start | bytes 589832 | tf_op jit(solution)/shard_map/ppermute | solution.py:438
  107.2 9.8 %collective-permute-start.28 = (bf16[144,768]{1,0:T(8,128)(2,1)S(1)}, bf16[144,768]{1,0:T(8,128)(2,1)S(1)}, u32[]{:S(2)}, u32[]{:S(2)}) collective-permute-start(bf16[144,768]{1,0:T(8,128)(2,1)S(1)} %get-tuple-element.227.refs_0_), channel_id=1, source_target_pairs={{0,1},{1,0},{2,3},{3,2},{4,5},{5,4},{6,7},{7,6},{8,9},{9,8},{10,11... | collective-permute-start | bytes 663560 | tf_op jit(solution)/shard_map/ppermute | solution.py:435
  108.9 10.2 %collective-permute-start.29 = (bf16[144,768]{1,0:T(8,128)(2,1)S(1)}, bf16[144,768]{1,0:T(8,128)(2,1)S(1)}, u32[]{:S(2)}, u32[]{:S(2)}) collective-permute-start(bf16[144,768]{1,0:T(8,128)(2,1)S(1)} %get-tuple-element.228.refs_1_), channel_id=1, source_target_pairs={{0,1},{1,0},{2,3},{3,2},{4,5},{5,4},{6,7},{7,6},{8,9},{9,8},{10,11... | collective-permute-start | bytes 663560 | tf_op jit(solution)/shard_map/ppermute | solution.py:435
  119.1 10.0 %collective-permute-start.30 = (bf16[256,768]{1,0:T(8,128)(2,1)S(1)}, bf16[256,768]{1,0:T(8,128)(2,1)S(1)}, u32[]{:S(2)}, u32[]{:S(2)}) collective-permute-start(bf16[256,768]{1,0:T(8,128)(2,1)S(1)} %get-tuple-element.233), channel_id=1, source_target_pairs={{0,1},{1,0},{2,3},{3,2},{4,5},{5,4},{6,7},{7,6},{8,9},{9,8},{10,11... | collective-permute-start | bytes 1179656 | tf_op jit(solution)/shard_map/ppermute | solution.py:435
  120.8 16.4 %collective-permute-start.32 = (bf16[2,208,768]{2,1,0:T(8,128)(2,1)S(1)}, bf16[2,208,768]{2,1,0:T(8,128)(2,1)S(1)}, u32[]{:S(2)}, u32[]{:S(2)}) collective-permute-start(bf16[2,208,768]{2,1,0:T(8,128)(2,1)S(1)} %get-tuple-element.234), channel_id=1, source_target_pairs={{0,8},{4,12},{8,0},{12,4},{16,24},{20,28},{24,16},{28,20},{1,9},{5... | collective-permute-start | bytes 1916936 | tf_op jit(solution)/shard_map/ppermute | solution.py:447
  122.3 17.3 %collective-permute-start.33 = (bf16[2,208,768]{2,1,0:T(8,128)(2,1)S(1)}, bf16[2,208,768]{2,1,0:T(8,128)(2,1)S(1)}, u32[]{:S(2)}, u32[]{:S(2)}) collective-permute-start(bf16[2,208,768]{2,1,0:T(8,128)(2,1)S(1)} %get-tuple-element.235), channel_id=1, source_target_pairs={{0,16},{4,20},{8,24},{12,28},{16,0},{20,4},{24,8},{28,12},{1,17},{... | collective-permute-start | bytes 1916936 | tf_op jit(solution)/shard_map/ppermute | solution.py:447
  123.8 26.8 %collective-permute-start.34 = (bf16[2,208,768]{2,1,0:T(8,128)(2,1)S(1)}, bf16[2,208,768]{2,1,0:T(8,128)(2,1)S(1)}, u32[]{:S(2)}, u32[]{:S(2)}) collective-permute-start(bf16[2,208,768]{2,1,0:T(8,128)(2,1)S(1)} %get-tuple-element.236), channel_id=1, source_target_pairs={{0,24},{4,28},{8,16},{12,20},{16,8},{20,12},{24,0},{28,4},{1,25},{... | collective-permute-start | bytes 1916936 | tf_op jit(solution)/shard_map/ppermute | solution.py:447
  129.1 21.5 %collective-permute-start.31 = (bf16[256,768]{1,0:T(8,128)(2,1)S(1)}, bf16[256,768]{1,0:T(8,128)(2,1)S(1)}, u32[]{:S(2)}, u32[]{:S(2)}) collective-permute-start(bf16[256,768]{1,0:T(8,128)(2,1)S(1)} %add_convert_fusion.5), channel_id=1, source_target_pairs={{0,2},{1,3},{2,0},{3,1},{4,6},{5,7},{6,4},{7,5},{8,10},{9,11},{10,... | collective-permute-start | bytes 1179656 | tf_op jit(solution)/shard_map/ppermute | solution.py:435
  133.2 20.1 %collective-permute-start.37 = (bf16[448,768]{1,0:T(8,128)(2,1)S(1)}, bf16[448,768]{1,0:T(8,128)(2,1)S(1)}, u32[]{:S(2)}, u32[]{:S(2)}) collective-permute-start(bf16[448,768]{1,0:T(8,128)(2,1)S(1)} %get-tuple-element.250), channel_id=1, source_target_pairs={{0,4},{4,0},{8,12},{12,8},{1,5},{5,1},{9,13},{13,9},{2,6},{6,2},{1... | collective-permute-start | bytes 2064392 | tf_op jit(solution)/shard_map/ppermute | solution.py:438
  151.0 15.4 %collective-permute-start.36 = (bf16[256,768]{1,0:T(8,128)(2,1)S(1)}, bf16[256,768]{1,0:T(8,128)(2,1)S(1)}, u32[]{:S(2)}, u32[]{:S(2)}) collective-permute-start(bf16[256,768]{1,0:T(8,128)(2,1)S(1)} %fusion.refs_0_), channel_id=1, source_target_pairs={{0,1},{1,0},{2,3},{3,2},{4,5},{5,4},{6,7},{7,6},{8,9},{9,8},{10,11... | collective-permute-start | bytes 1179656 | tf_op jit(solution)/shard_map/ppermute | solution.py:435
  151.5 15.0 %collective-permute-start.35 = (bf16[208,768]{1,0:T(8,128)(2,1)S(1)}, bf16[208,768]{1,0:T(8,128)(2,1)S(1)}, u32[]{:S(2)}, u32[]{:S(2)}) collective-permute-start(bf16[208,768]{1,0:T(8,128)(2,1)S(1)} %slice_bitcast_fusion), channel_id=1, source_target_pairs={{0,1},{1,0},{2,3},{3,2},{4,5},{5,4},{6,7},{7,6},{8,9},{9,8},{10,11... | collective-permute-start | bytes 958472 | tf_op jit(solution)/shard_map/ppermute | solution.py:435
  166.5 11.3 %collective-permute-start.41 = (bf16[208,768]{1,0:T(8,128)(2,1)S(1)}, bf16[208,768]{1,0:T(8,128)(2,1)S(1)}, u32[]{:S(2)}, u32[]{:S(2)}) collective-permute-start(bf16[208,768]{1,0:T(8,128)(2,1)S(1)} %fusion.5.refs_0_), channel_id=1, source_target_pairs={{0,8},{4,12},{8,0},{12,4},{16,24},{20,28},{24,16},{28,20},{1,9},{5... | collective-permute-start | bytes 958472 | tf_op jit(solution)/shard_map/ppermute | solution.py:447
  168.3 9.6 %collective-permute-start.42 = (bf16[208,768]{1,0:T(8,128)(2,1)S(1)}, bf16[208,768]{1,0:T(8,128)(2,1)S(1)}, u32[]{:S(2)}, u32[]{:S(2)}) collective-permute-start(bf16[208,768]{1,0:T(8,128)(2,1)S(1)} %fusion.5.refs_0_), channel_id=1, source_target_pairs={{0,16},{4,20},{8,24},{12,28},{16,0},{20,4},{24,8},{28,12},{1,17},{... | collective-permute-start | bytes 958472 | tf_op jit(solution)/shard_map/ppermute | solution.py:447
  169.8 10.9 %collective-permute-start.43 = (bf16[208,768]{1,0:T(8,128)(2,1)S(1)}, bf16[208,768]{1,0:T(8,128)(2,1)S(1)}, u32[]{:S(2)}, u32[]{:S(2)}) collective-permute-start(bf16[208,768]{1,0:T(8,128)(2,1)S(1)} %fusion.5.refs_0_), channel_id=1, source_target_pairs={{0,24},{4,28},{8,16},{12,20},{16,8},{20,12},{24,0},{28,4},{1,25},{... | collective-permute-start | bytes 958472 | tf_op jit(solution)/shard_map/ppermute | solution.py:447
  181.4 15.6 %collective-permute-start.50 = (bf16[4,208,768]{2,1,0:T(8,128)(2,1)S(1)}, bf16[4,208,768]{2,1,0:T(8,128)(2,1)S(1)}, u32[]{:S(2)}, u32[]{:S(2)}) collective-permute-start(bf16[4,208,768]{2,1,0:T(8,128)(2,1)S(1)} %gather_ffn_grads.1.mine), channel_id=1, source_target_pairs={{0,4},{4,0},{8,12},{12,8},{1,5},{5,1},{9,13},{13,9},{2,6},{6,2},{1... | collective-permute-start | bytes 3833864 | tf_op jit(solution)/shard_map/ppermute | solution.py:438
  184.8 8.4 %collective-permute-start.48 = (bf16[112,768]{1,0:T(8,128)(2,1)S(1)}, bf16[112,768]{1,0:T(8,128)(2,1)S(1)}, u32[]{:S(2)}, u32[]{:S(2)}) collective-permute-start(bf16[112,768]{1,0:T(8,128)(2,1)S(1)} %fusion.8.refs_0_), channel_id=1, source_target_pairs={{0,24},{4,28},{8,16},{12,20},{16,8},{20,12},{24,0},{28,4},{1,25},{... | collective-permute-start | bytes 516104 | tf_op jit(solution)/shard_map/ppermute | solution.py:447
  (67 other events, 447.0 us)

commit v6 on v5

--- a/solution.py
+++ b/solution.py
@@ -66,6 +66,7 @@
 
 SMEM = pl.BlockSpec(memory_space=pltpu.SMEM)
 VMEM = pl.BlockSpec(memory_space=pltpu.VMEM)
+HBM = pl.BlockSpec(memory_space=pltpu.HBM)
 
 
 def call(kernel, outs, name, args, scalars=0, us=1.0, vmem=16, scratch=()):
@@ -85,16 +86,41 @@
     return ref[pl.ds(pl.multiple_of(c * rows, rows), rows), :]
 
 
-def kv_kernel(tok, wk_t, wv_t, bv, kv, wkv_t):
-    heads = wk_t.shape[0] // HEAD_DIM
-    rows, bias = [], []
-    for h in range(heads):
+def both_rows(wk_t, wv_t):
+    rows = []
+    for h in range(wk_t.shape[0] // HEAD_DIM):
         part = slice(h * HEAD_DIM, (h + 1) * HEAD_DIM)
         rows += [wk_t[part, :], wv_t[part, :]]
-        bias += [jnp.zeros((1, HEAD_DIM), f32), bv[:, part]]
-    both = jnp.concatenate(rows, axis=0)
-    wkv_t[...] = both
-    kv[...] = (nt(tok[...], both) + jnp.concatenate(bias, axis=1)).astype(bf16)
+    return jnp.concatenate(rows, axis=0)
+
+
+def front_kernel(at, tok, wk_t, wv_t, w_in, w_outer, w_out, bv, kv, piece, out_piece, tok_v, wk_v, wv_v, sems):
+    tail = out_piece.shape[0]
+    half = (piece.shape[0] - tail) // 2
+
+    def part(ref, index, size):
+        return ref.at[pl.ds(pl.multiple_of(index * size, 16), size), :]
+
+    moves = [
+        (tok, tok_v),
+        (wk_t, wk_v),
+        (wv_t, wv_v),
+        (part(w_in, at[4], half), piece.at[pl.ds(0, half), :]),
+        (part(w_outer, at[4], half), piece.at[pl.ds(half, half), :]),
+        (part(w_out, at[2], tail), out_piece),
+    ]
+    copies = [pltpu.make_async_copy(a, b, sems.at[i]) for i, (a, b) in enumerate(moves)]
+    for copy in copies:
+        copy.start()
+    for copy in copies[:3]:
+        copy.wait()
+    bias = []
+    for h in range(wk_v.shape[0] // HEAD_DIM):
+        bias += [jnp.zeros((1, HEAD_DIM), f32), bv[:, h * HEAD_DIM : (h + 1) * HEAD_DIM]]
+    kv[...] = (nt(tok_v[...], both_rows(wk_v, wv_v)) + jnp.concatenate(bias, axis=1)).astype(bf16)
+    for copy in copies[3:]:
+        copy.wait()
+    piece[2 * half :, :] = out_piece[...]
 
 
 def q_kernel(tok, wq_t, bq, q):
@@ -107,25 +133,6 @@
     q[...] = jnp.concatenate(cols, axis=1)
 
 
-def piece_kernel(at, w_in, w_outer, w_out, piece, out_piece, sems):
-    tail = out_piece.shape[0]
-    half = (piece.shape[0] - tail) // 2
-
-    def part(ref, index, size):
-        return ref.at[pl.ds(pl.multiple_of(index * size, 16), size), :]
-
-    copies = [
-        pltpu.make_async_copy(part(w_in, at[4], half), piece.at[pl.ds(0, half), :], sems.at[0]),
-        pltpu.make_async_copy(part(w_outer, at[4], half), piece.at[pl.ds(half, half), :], sems.at[1]),
-        pltpu.make_async_copy(part(w_out, at[2], tail), out_piece, sems.at[2]),
-    ]
-    for copy in copies:
-        copy.start()
-    for copy in copies:
-        copy.wait()
-    piece[2 * half :, :] = out_piece[...]
-
-
 def weights_kernel(n, at, w_out, *refs):
     pieces, (w_out_all, w_in_far, w_outer_far) = refs[:8], refs[8:]
     z = at[0]
@@ -147,13 +154,15 @@
 
 
 def attend_kernel(n_blk, ids, at, bucket, lens, q, *refs):
-    kvs, outs_to = refs[:n_blk], refs[n_blk:]
+    kvs = refs[:n_blk]
+    hp_first, hp_second, probs_first, probs_second, hp_late, held, sems = refs[n_blk:]
+    copies = []
     heads = q.shape[1] // LANES
     b = at[2]
     q_at = lax.broadcasted_iota(i32, (BLOCK, 1), 0)
     k_at = lax.broadcasted_iota(i32, (1, BLOCK), 1)
     for order, row in enumerate(ids):
-        hp, probs = outs_to[2 * (order // 2)], outs_to[2 * (order // 2) + 1]
+        hp, probs = ((hp_first, probs_first), (hp_second, probs_second))[order // 2]
         i = order % 2
         r = row_at(at, row)
         bk = bucket[r]
@@ -177,13 +186,26 @@
             weights = jnp.exp(scores - jnp.max(scores, axis=-1, keepdims=True))
             total = jnp.sum(weights, axis=-1, keepdims=True)
             p = (weights / total).astype(bf16)
-            probs[(i * heads + h) * BLOCK : (i * heads + h + 1) * BLOCK, :] = p
+            held[(order * heads + h) * BLOCK : (order * heads + h + 1) * BLOCK, :] = p
             outs.append(nn(p, kvh)[:, HEAD_DIM:].astype(bf16))
         base = i * PACKED
         hp[base : base + BLOCK, :] = jnp.concatenate(outs[:2], axis=1)
         hp[base + BLOCK : base + PACKED, :] = jnp.concatenate(
             [outs[2][:HEAD_DIM], outs[2][HEAD_DIM:]], axis=1
         )
+        size = heads * BLOCK
+        copies.append(
+            pltpu.make_async_copy(
+                held.at[pl.ds(order * size, size), :], probs.at[pl.ds(i * size, size), :], sems.at[order]
+            )
+        )
+        copies[-1].start()
+    for i, hp in enumerate((hp_first, hp_second)):
+        rows = hp.shape[0]
+        copies.append(pltpu.make_async_copy(hp, hp_late.at[pl.ds(i * rows, rows), :], sems.at[4 + i]))
+        copies[-1].start()
+    for copy in copies:
+        copy.wait()
 
 
 def unpack(h):
@@ -205,13 +227,16 @@
 def ffn_kernel(
     n, i, at, tok, w_out, b_out, g1, b1, w_in, w_in_far, b_in, b_in_far, w_outer, w_outer_far, *refs
 ):
-    hps = refs[:n]
-    part, n1_out, s1_out, low_out, act_out, act_far_out, slopes, held = refs[n:]
+    hps = refs[:n] if len(refs) > n + 7 + 1 else [refs[0].at[pl.ds(s * PACKED, PACKED), :] for s in range(n)]
+    refs = refs if len(refs) > n + 7 + 1 else refs[:1] * n + refs[1:]
+    part, n1_out, s1_out, low_out, act_out, act_far_out, slopes, *rest, held = refs[n:]
     z = at[0]
     local = w_out.shape[0] // n
     for s in range(n):
         j = z ^ s
-        held[j] = nn(unpack(hps[s][i * PACKED : (i + 1) * PACKED, :]), chunk_of(w_out, j, local))
+        held[j] = nn(unpack(hps[s][:PACKED, :]), chunk_of(w_out, j, local))
+        if rest:
+            rest[0][s * PACKED : (s + 1) * PACKED, :] = hps[s][PACKED:, :]
     attn = held[0]
     for j in range(1, n):
         attn = attn + held[j]
@@ -304,11 +329,11 @@
         dq_out[i * BLOCK : (i + 1) * BLOCK, :] = jnp.concatenate(dqs, axis=1)
 
 
-def input_kernel(dq, keep, recv, far, wq_t, wkv_t, part, dkv_t, sums):
+def input_kernel(dq, keep, recv, far, wq_t, wk_t, wv_t, part, dkv_t, sums):
     total = keep[0].astype(f32) + recv[0].astype(f32) + far[...].astype(f32)
     lows = [total[i].astype(bf16) for i in range(2)]
     low = jnp.concatenate([v.T for v in lows], axis=0)
-    grad = nn(dq[...], wq_t[...]) + nn(low, wkv_t[...])
+    grad = nn(dq[...], wq_t[...]) + nn(low, both_rows(wk_t, wv_t))
     part[...] = grad.astype(bf16)
     dkv_t[...] = jnp.concatenate(lows, axis=1)
     width = sums.shape[1]
@@ -355,12 +380,12 @@
                 target[i, q, rows:, :] = tail
 
 
-def attend_grad_kernel(m, at, tok, hp_mine, hp_other, *refs):
+def attend_grad_kernel(m, at, tok, hp_late, *refs):
     shares, (dq, dkv_t, sums) = refs[:4], (refs[4 + 2 * i : 6 + 2 * i] for i in range(3))
     keep, send, held = refs[10:]
     first = at[1] == 0
     toks = join(chunk_of(tok, row_at(at, i), BLOCK) for i in range(4))
-    heads = join(unpack(hp[i * PACKED : (i + 1) * PACKED, :]) for hp in (hp_mine, hp_other) for i in range(2))
+    heads = join(unpack(hp_late[i * PACKED : (i + 1) * PACKED, :]) for i in (2, 3, 0, 1))
     g_out = tn(heads, join(x[:BLOCK, :] for x in shares))
     g_q = tn(join(x[...] for x in dq), toks)
     g_kv = nn(join((x[...] for x in dkv_t), axis=1), toks)
@@ -460,19 +485,15 @@
             total = total + part.astype(f32)
         return total.astype(bf16)
 
-    def gather_grads(total, at, name, *extra):
-        rows, width = total.shape
-        got = [flip_member(total, s) for s in range(1, m)]
-        got, extra = lax.optimization_barrier((got, extra))
-        every = [total] + got
-        mine = call(
+    def gather_grads(every, at, name):
+        rows, width = every[0].shape
+        return call(
             functools.partial(gather_kernel, m),
             near((m, rows, width), bf16),
             name,
             (at, *every),
             scalars=1,
         )
-        return mine, *extra
 
     def body(
         tokens, bucket_ids, seq_lengths, w_query, b_query, w_key, w_value, b_value, w_out, b_out,
@@ -499,21 +520,21 @@
 
         part = local // 4
         piece_rows = (width + units) // 8
-        piece, out_piece = pl.pallas_call(
-            piece_kernel,
-            out_shape=(near((piece_rows + part, width), bf16), near((part, width), bf16)),
-            in_specs=[SMEM] + [pl.BlockSpec(memory_space=pl.ANY)] * 3,
-            out_specs=(VMEM, VMEM),
-            scratch_shapes=[pltpu.SemaphoreType.DMA((3,))],
-            compiler_params=pltpu.CompilerParams(vmem_limit_bytes=8 * MIB),
-            name="weight_piece",
-        )(at, w_inner, w_outer, w_out)
-        kv, wkv_t = call(
-            kv_kernel,
-            (near((count, lanes), bf16), near((lanes, width), bf16)),
-            "kv_rows",
-            (tok, wk_t, wv_t, row(b_value)),
-        )
+        kv, piece, out_piece = pl.pallas_call(
+            front_kernel,
+            out_shape=(
+                near((count, lanes), bf16), near((piece_rows + part, width), bf16),
+                near((part, width), bf16),
+            ),
+            in_specs=[SMEM] + [HBM] * 6 + [VMEM],
+            out_specs=(VMEM,) * 3,
+            scratch_shapes=[
+                pltpu.VMEM((count, width), bf16), pltpu.VMEM((local, width), bf16),
+                pltpu.VMEM((local, width), bf16), pltpu.SemaphoreType.DMA((6,)),
+            ],
+            compiler_params=pltpu.CompilerParams(vmem_limit_bytes=16 * MIB),
+            name="front",
+        )(at, *[pltpu.with_memory_space_constraint(v, pltpu.HBM) for v in (tok, wk_t, wv_t, w_inner, w_outer, w_out)], row(b_value))
         kv, piece, out_piece, b_far = fence((kv, piece, out_piece, b_inner))
         kv_far = flip(kv, 2)
         kv_core = flip(kv, 1)
@@ -534,15 +555,23 @@
         q = call(q_kernel, near((count, lanes), bf16), "query_rows", (tok, wq_t, row(b_query)), us=0.5)
         kvs = [kv, kv_core, kv_far, kv_both]
 
-        pair = (near((2 * PACKED, LANES), bf16), near((2 * heads * BLOCK, n_blk * BLOCK), bf16))
-        hp_other, probs_other, hp_mine, probs_mine = call(
+        prob_rows = 2 * heads * BLOCK
+        hp_other, hp_mine, probs_other, probs_mine, hp_late = pl.pallas_call(
             functools.partial(attend_kernel, n_blk, (2, 3, 0, 1)),
-            pair + pair,
-            "attend",
-            (at, bucket_ids, seq_lengths, q, *kvs),
-            us=ATTEND_US,
-            scalars=3,
-        )
+            out_shape=(near((2 * PACKED, LANES), bf16),) * 2
+            + (pltpu.HBM((prob_rows, n_blk * BLOCK), bf16),) * 2
+            + (pltpu.HBM((4 * PACKED, LANES), bf16),),
+            in_specs=[SMEM] * 3 + [VMEM] * (1 + n_blk),
+            out_specs=(VMEM,) * 2 + (HBM,) * 3,
+            scratch_shapes=[
+                pltpu.VMEM((2 * prob_rows, n_blk * BLOCK), bf16), pltpu.SemaphoreType.DMA((6,)),
+            ],
+            compiler_params=pltpu.CompilerParams(vmem_limit_bytes=16 * MIB),
+            cost_estimate=pl.CostEstimate(
+                flops=int(ATTEND_US * FLOPS_US), bytes_accessed=1, transcendentals=0
+            ),
+            name="attend",
+        )(at, bucket_ids, seq_lengths, q, *kvs)
         hps = {0: hp_mine, 1: swap(hp_other, 1), 2: swap(hp_mine, 2), 3: swap(hp_other, 3)}
         held = [arrived[2], arrived[4], arrived[6]]
         hps[1], hps[2], hps[3], *held = fence((hps[1], hps[2], hps[3], *held))
@@ -560,25 +589,27 @@
         chunk = lambda rows, dt: near((rows, width), dt)
         gains1 = (row(norm1_gain), row(norm1_bias))
 
-        def ffn(i):
+        def ffn(i, heads_in):
             return call(
                 functools.partial(ffn_kernel, n, i),
                 (
                     chunk(BLOCK, bf16), chunk(BLOCK, f32), near((BLOCK, LANES), f32),
                     chunk(BLOCK, bf16), near((BLOCK, units), bf16), near((BLOCK, units), bf16),
                     near((2 * BLOCK, units), bf16),
-                ),
+                )
+                + ((near((n * PACKED, LANES), bf16),) if i == 0 else ()),
                 "ffn",
                 (
                     at, tok, w_out_all, row(b_out), *gains1, w_inner, w_inner_far, row(b_inner),
-                    row(b_inner_far), w_outer, w_outer_far, *[hps[s] for s in range(n)],
+                    row(b_inner_far), w_outer, w_outer_far, *heads_in,
                 ),
                 us=2.4,
                 scalars=1,
                 scratch=[pltpu.VMEM((n, BLOCK, width), f32)],
             )
 
-        parts, n1s, s1s, lows, acts, acts_far, slopes = map(list, zip(*[ffn(i) for i in range(2)]))
+        *row0, second_heads = ffn(0, [hps[s] for s in range(n)])
+        parts, n1s, s1s, lows, acts, acts_far, slopes = map(list, zip(row0, ffn(1, [second_heads])))
         theirs = [swap(v, 2) for v in parts]
 
         def ffn_back(i):
@@ -658,7 +689,7 @@
                 input_kernel,
                 (chunk(2 * BLOCK, bf16), near((lanes, 2 * BLOCK), bf16), chunk(8, f32)),
                 "input_part",
-                (dq, keep, recv, far, wq_t, wkv_t),
+                (dq, keep, recv, far, wq_t, wk_t, wv_t),
                 us=us,
             )
 
@@ -681,7 +712,7 @@
             (chunk(rows2, bf16), chunk(rows2, bf16)),
             "attend_grads",
             (
-                at, tok, hp_mine, hp_other, *shares, own[0], other[0], dkv_own, late[0], sums_own,
+                at, tok, hp_late, *shares, own[0], other[0], dkv_own, late[0], sums_own,
                 late[1],
             ),
             us=GRADS_US,
@@ -691,19 +722,33 @@
         by_member = lambda v: v.reshape(m, rows2 // m, width)
         pieces2 = share_pieces(by_member(keep2), by_member(flip(send2, 1)), member)
         got2 = [flip_member(v, s) for s, v in enumerate(pieces2[1:], 1)]
-        crossed, got1 = fence((swap(pair, 2), got1))
+        got1, _, _ = fence((got1, keep2, pair))
+        total1 = fence(add(pieces1[0], got1))
+        near1 = swap(total1[1], 1)
+        crossed, near1, got2, *ends = fence((swap(pair, 2), near1, got2, *outs[2:]))
+        outs[2:] = ends
         d_tok = pair.astype(f32) + crossed.astype(f32) + jnp.concatenate(dres1, axis=0)
         d_tok = d_tok.astype(bf16)
-        total1 = fence(add(pieces1[0], got1))
-        near1, d_far, got2 = fence((swap(total1[1], 1), swap(d_tok, 1), got2))
-        d_toks = [d_tok, d_far]
         share1 = (total1[0].astype(f32) + near1.astype(f32)).astype(bf16)
         total2 = add(pieces2[0], got2)
-        mine1, *ends = gather_grads(share1, at, "gather_ffn_grads", *outs[2:])
-        outs[2:] = ends
+        shares1 = [flip_member(share1, k) for k in range(1, m)]
+        shares2 = [flip_member(total2, k) for k in range(1, m)]
+        shares1, shares2, d_far = fence((shares1, shares2, swap(d_tok, 1)))
+        d_toks = [d_tok, d_far]
+        assemble = lambda parts, name: call(
+            rows_kernel,
+            shape((row_count, block, width), bf16),
+            name,
+            (at, *parts),
+            us=1.5,
+            scalars=1,
+        )
+        output = assemble(outs, "output_rows")
+        d_tokens = assemble(d_toks, "input_grad_rows")
+        shares1, shares2, _, _ = fence((shares1, shares2, output, d_tokens))
+        mine1 = gather_grads([share1] + shares1, at, "gather_ffn_grads")
         other1 = flip(mine1, 1)
-        (mine2,) = gather_grads(total2, at, "gather_attend_grads")
-        mine2 = mine2.reshape(rows2, width)
+        mine2 = gather_grads([total2] + shares2, at, "gather_attend_grads").reshape(rows2, width)
         other2 = flip(mine2, 1)
 
         vector = shape((width,), f32)
@@ -718,16 +763,6 @@
             us=3.0,
             scalars=1,
         )
-        assemble = lambda parts, name: call(
-            rows_kernel,
-            shape((row_count, block, width), bf16),
-            name,
-            (at, *parts),
-            us=1.5,
-            scalars=1,
-        )
-        output = assemble(outs, "output_rows")
-        d_tokens = assemble(d_toks, "input_grad_rows")
         other2, g_b_outer = fence((other2, g_b_outer))
         g_w_out, g_q, g_k, g_v, g_gain1, g_bias1, g_b_out, g_b_query, g_b_value = call(
             attend_final_kernel,

time: 202 us -> 191 us (0.946)
  local copies, waits for them, and re-layouts: 10.5 us -> 4.62 us
  waiting for transfers between devices: 96.8 us -> 93.2 us
    pallas_call x22 -> x20, Pallas kernels: 41.8 us -> 33.5 us  [call(): pl.pallas_call(kernel, out_shape=outs, in_specs=[SMEM] * scalars + [VMEM]...]
    pallas_call x1 -> x2, Pallas kernels: 1.06 us -> 8.09 us  [the longest x1 5.61 us: body(): pl.pallas_call(functools.partial(attend_kernel, n_blk, (2, 3, 0, 1)), out...]
    ppermute x21, waiting for transfers between devices: 52 us -> 45.2 us  [swap(): return lax.ppermute(v, 'tensor', [(i, i ^ bit) for i in range(n)])]
    unnamed x98 -> x84, local copies, waits for them, and re-layouts: 10.3 us -> 4.45 us
    ppermute x12, waiting for transfers between devices: 34.3 us -> 37.1 us  [flip_member(): return lax.ppermute(v, ('dp', 'blk'), perm)]
    ppermute x21, starting transfers between devices: 25.3 us -> 22.8 us  [swap(): return lax.ppermute(v, 'tensor', [(i, i ^ bit) for i in range(n)])]
    ppermute x15, starting transfers between devices: 5.48 us -> 7.59 us  [flip(): return lax.ppermute(v, 'blk', [(i, i ^ bit) for i in range(n_blk)])]
  transfers between devices with their start and end apart: 51 -> 51, of which waited for: 27 -> 25; matrix products, arithmetic and copies ran while one was open for 1% -> 1% of each run, Pallas kernels for 17% -> 16%
where the time goes in v6:
time: 191 us
  waiting for transfers between devices  93.2 us (49%)
  starting transfers between devices  48.2 us (25%)
  Pallas kernels  41.6 us (22%)
  local copies, waits for them, and re-layouts  4.62 us (2%)
    ppermute x21, waiting for transfers between devices, swap(): return lax.ppermute(v, 'tensor', [(i, i ^ bit) for i in range(n)])  45.2 us
    ppermute x12, waiting for transfers between devices, flip_member(): return lax.ppermute(v, ('dp', 'blk'), perm)  37.1 us
    pallas_call x20, Pallas kernels, call(): pl.pallas_call(kernel, out_shape=outs, in_specs=[SMEM] * scalars + [VMEM]...  33.5 us
    ppermute x21, starting transfers between devices, swap(): return lax.ppermute(v, 'tensor', [(i, i ^ bit) for i in range(n)])  22.8 us
    ppermute x12, starting transfers between devices, flip_member(): return lax.ppermute(v, ('dp', 'blk'), perm)  14.2 us
    ppermute x15, waiting for transfers between devices, flip(): return lax.ppermute(v, 'blk', [(i, i ^ bit) for i in range(n_blk)])  8.89 us
    ppermute x15, starting transfers between devices, flip(): return lax.ppermute(v, 'blk', [(i, i ^ bit) for i in range(n_blk)])  7.59 us
    pallas_call x1, Pallas kernels, body(): pl.pallas_call(functools.partial(attend_kernel, n_blk, (2, 3, 0, 1)), out...  5.61 us
  transfers between devices with their start and end apart: 51, of which 25 were waited for; matrix products, arithmetic and copies ran while one was open for 1% of the time, Pallas kernels for 16%

profile of v6, /device:TPU:0, one launch (start us, length us, event | category | flops | bytes accessed | tf_op | source)
XLA Modules:
  0.0 190.8 jit_solution(8496900914715654619)
XLA Ops:
  1.5 2.5 %front.1 = (bf16[512,384]{1,0:T(8,128)(2,1)S(1)}, bf16[240,768]{1,0:T(8,128)(2,1)S(1)}, bf16[48,768]{1,0:T(8,128)(2,1)S(1)}) custom-call(s32[5]{0:T(128)S(1)} %stack.23.at, bf16[512,768]{1,0:T(8,128)(2,1)} %bitcast.48, bf16[192,768]{1,0:T(8,128)(2,1)} %bitcast.55, bf16[192,768]{1,0:T(8,128)(2,1)} %bitcast.58, bf16[768,768]{1,0:T(8,128)(2,1)} %w_in.9, ...), custom_call_target="tpu_custom_call" | custom-call | tf_op jit(solution)/shard_map/front/pallas_call | solution.py:523
  4.0 3.0 %collective-permute-start = (bf16[512,384]{1,0:T(8,128)(2,1)S(1)}, bf16[512,384]{1,0:T(8,128)(2,1)S(1)}, u32[]{:S(2)}, u32[]{:S(2)}) collective-permute-start(bf16[512,384]{1,0:T(8,128)(2,1)S(1)} %get-tuple-element.159.refs_0_), channel_id=1, source_target_pairs={{0,8},{4,12},{8,0},{12,4},{1,9},{5,13},{9,1},{13,5},{2,10},{6,14},... | collective-permute-start | bytes 1179656 | tf_op jit(solution)/shard_map/ppermute | solution.py:463
  8.6 2.6 %collective-permute-start.3 = (bf16[48,768]{1,0:T(8,128)(2,1)S(1)}, bf16[48,768]{1,0:T(8,128)(2,1)S(1)}, u32[]{:S(2)}, u32[]{:S(2)}) collective-permute-start(bf16[48,768]{1,0:T(8,128)(2,1)S(1)} %get-tuple-element.162), channel_id=1, source_target_pairs={{0,2},{1,3},{2,0},{3,1},{4,6},{5,7},{6,4},{7,5},{8,10},{9,11},{10,... | collective-permute-start | bytes 221192 | tf_op jit(solution)/shard_map/ppermute | solution.py:460
  12.1 7.3 %collective-permute-done.1 = f32[768]{0:T(1024)S(1)} collective-permute-done((f32[768]{0:T(1024)S(1)}, f32[768]{0:T(1024)S(1)}, u32[]{:S(2)}, u32[]{:S(2)}) %collective-permute-start.1) | collective-permute-done | bytes 3104 | tf_op jit(solution)/shard_map/ppermute | solution.py:460
  19.4 2.9 %collective-permute-done.4 = bf16[48,768]{1,0:T(8,128)(2,1)S(1)} collective-permute-done((bf16[48,768]{1,0:T(8,128)(2,1)S(1)}, bf16[48,768]{1,0:T(8,128)(2,1)S(1)}, u32[]{:S(2)}, u32[]{:S(2)}) %collective-permute-start.4) | collective-permute-done | bytes 73760 | tf_op jit(solution)/shard_map/ppermute | solution.py:460
  26.7 5.6 %attend.1 = (bf16[384,128]{1,0:T(8,128)(2,1)S(1)}, bf16[384,128]{1,0:T(8,128)(2,1)S(1)}, bf16[768,512]{1,0:T(8,128)(2,1)}, bf16[768,512]{1,0:T(8,128)(2,1)}, bf16[768,128]{1,0:T(8,128)(2,1)}) custom-call(s32[5]{0:T(128)S(1)} %stack.23.at, s32[4]{0:T(128)S(1)} %copy-done.28, s32[4,4]{1,0:T(4,128)S(1)} %copy-done.26, bf16[512,384]{1,0:T(8,128)(2,1)S(1)} %query_rows.1.q, ...), custom_call_target="tpu_custom_call" | custom-call | flops 49999998976 | bytes 1 | tf_op jit(solution)/shard_map/attend/pallas_call | solution.py:559
  32.5 2.6 %collective-permute-start.9 = (bf16[384,128]{1,0:T(8,128)(2,1)S(1)}, bf16[384,128]{1,0:T(8,128)(2,1)S(1)}, u32[]{:S(2)}, u32[]{:S(2)}) collective-permute-start(bf16[384,128]{1,0:T(8,128)(2,1)S(1)} %get-tuple-element.168.refs_0_), channel_id=1, source_target_pairs={{0,2},{1,3},{2,0},{3,1},{4,6},{5,7},{6,4},{7,5},{8,10},{9,11},{10,... | collective-permute-start | bytes 294920 | tf_op jit(solution)/shard_map/ppermute | solution.py:460
  39.5 3.7 %collective-permute-done.9.refs_2_ = bf16[384,128]{1,0:T(8,128)(2,1)S(1)} collective-permute-done((bf16[384,128]{1,0:T(8,128)(2,1)S(1)}, bf16[384,128]{1,0:T(8,128)(2,1)S(1)}, u32[]{:S(2)}, u32[]{:S(2)}) %collective-permute-start.9) | collective-permute-done | bytes 98336 | tf_op jit(solution)/shard_map/ppermute | solution.py:460
  45.8 1.7 collective-permute-done.15.refs_5_
  49.6 2.4 %ffn.2 = (bf16[128,768]{1,0:T(8,128)(2,1)S(1)}, f32[128,768]{1,0:T(8,128)S(1)}, f32[128,128]{1,0:T(8,128)S(1)}, bf16[128,768]{1,0:T(8,128)(2,1)S(1)}, bf16[128,7...) custom-call(s32[5]{0:T(128)S(1)} %stack.23.at, ...), custom_call_target="tpu_custom_call" | custom-call | flops 2400000000 | bytes 1 | tf_op jit(solution)/shard_map/ffn/pallas_call | solution.py:73
  52.8 2.3 %ffn.3 = (bf16[128,768]{1,0:T(8,128)(2,1)S(1)}, f32[128,768]{1,0:T(8,128)S(1)}, f32[128,128]{1,0:T(8,128)S(1)}, bf16[128,768]{1,0:T(8,128)(2,1)S(1)}, bf16[128,7...) custom-call(s32[5]{0:T(128)S(1)} %stack.23.at, bf16[512,768]{1,0:T(8,128)(2,1)S(1)} %bitcast.51, ...), custom_call_target="tpu_custom_call" | custom-call | flops 2400000000 | bytes 1 | tf_op jit(solution)/shard_map/ffn/pallas_call | solution.py:73
  55.1 2.3 %collective-permute-start.18 = (bf16[128,768]{1,0:T(8,128)(2,1)S(1)}, bf16[128,768]{1,0:T(8,128)(2,1)S(1)}, u32[]{:S(2)}, u32[]{:S(2)}) collective-permute-start(bf16[128,768]{1,0:T(8,128)(2,1)S(1)} %get-tuple-element.186.mine), channel_id=1, source_target_pairs={{0,2},{1,3},{2,0},{3,1},{4,6},{5,7},{6,4},{7,5},{8,10},{9,11},{10,... | collective-permute-start | bytes 589832 | tf_op jit(solution)/shard_map/ppermute | solution.py:460
  57.4 10.8 %collective-permute-done.17.theirs = bf16[128,768]{1,0:T(8,128)(2,1)S(1)} collective-permute-done((bf16[128,768]{1,0:T(8,128)(2,1)S(1)}, bf16[128,768]{1,0:T(8,128)(2,1)S(1)}, u32[]{:S(2)}, u32[]{:S(2)}) %collective-permute-start.17) | collective-permute-done | bytes 196640 | tf_op jit(solution)/shard_map/ppermute | solution.py:460
  68.2 2.7 %ffn_back.2 = (bf16[128,768]{1,0:T(8,128)(2,1)S(1)}, bf16[128,768]{1,0:T(8,128)(2,1)S(1)}, bf16[128,768]{1,0:T(8,128)(2,1)S(1)}, bf16[128,768]{1,0:T(8,128)(2,1)...) custom-call(s32[5]{0:T(128)S(1)} %stack.23.at, bf16[512,768]{1,0:T(8,128)(2,1)S(1)} %bitcast.62, ...), custom_call_target="tpu_custom_call" | custom-call | flops 2700000000 | bytes 1 | tf_op jit(solution)/shard_map/ffn_back/pallas_call | solution.py:73
  72.3 2.7 %ffn_back.3 = (bf16[128,768]{1,0:T(8,128)(2,1)S(1)}, bf16[128,768]{1,0:T(8,128)(2,1)S(1)}, bf16[128,768]{1,0:T(8,128)(2,1)S(1)}, bf16[128,768]{1,0:T(8,128)(2,1)...) custom-call(s32[5]{0:T(128)S(1)} %stack.23.at, bf16[512,768]{1,0:T(8,128)(2,1)S(1)} %bitcast.63, ...), custom_call_target="tpu_custom_call" | custom-call | flops 2700000000 | bytes 1 | tf_op jit(solution)/shard_map/ffn_back/pallas_call | solution.py:73
  76.7 2.2 %ffn_grads.1 = (bf16[4,2,208,768]{3,2,1,0:T(8,128)(2,1)S(1)}, bf16[4,2,208,768]{3,2,1,0:T(8,128)(2,1)S(1)}) custom-call(s32[5]{0:T(128)S(1)} %stack.23.at, bf16[128,768]{1,0:T(8,128)(2,1)S(1)} %get-tuple-element.202.refs_0_, bf16[128,768]{1,0:T(8,128)(2,1)S(1)} %get-tuple-element.203.refs_1_, bf16[128,768]{1,0:T(8,128)(2,1)S(1)} %get-tuple-element.204.refs_2_, ...), custom_call_target="tpu_custom_call" | custom-call | flops 49999998976 | bytes 1 | tf_op jit(solution)/shard_map/ffn_grads/pallas_call | solution.py:73
  79.0 7.4 %collective-permute-done.19.theirs = bf16[128,768]{1,0:T(8,128)(2,1)S(1)} collective-permute-done((bf16[128,768]{1,0:T(8,128)(2,1)S(1)}, bf16[128,768]{1,0:T(8,128)(2,1)S(1)}, u32[]{:S(2)}, u32[]{:S(2)}) %collective-permute-start.19) | collective-permute-done | bytes 196640 | tf_op jit(solution)/shard_map/ppermute | solution.py:460
  87.6 2.9 %collective-permute-done.20.theirs = bf16[128,768]{1,0:T(8,128)(2,1)S(1)} collective-permute-done((bf16[128,768]{1,0:T(8,128)(2,1)S(1)}, bf16[128,768]{1,0:T(8,128)(2,1)S(1)}, u32[]{:S(2)}, u32[]{:S(2)}) %collective-permute-start.20) | collective-permute-done | bytes 196640 | tf_op jit(solution)/shard_map/ppermute | solution.py:460
  92.2 2.7 %attend_back.2 = (bf16[256,192]{1,0:T(8,128)(2,1)S(1)}, bf16[2,2,384,128]{3,2,1,0:T(8,128)(2,1)S(1)}, bf16[2,2,384,128]{3,2,1,0:T(8,128)(2,1)S(1)}) custom-call(s32[5]{0:T(128)S(1)} %stack.23.at, bf16[192,128]{1,0:T(8,128)(2,1)S(1)} %get-tuple-element.191.first, bf16[192,128]{1,0:T(8,128)(2,1)S(1)} %get-tuple-element.195.second, ...), custom_call_target="tpu_custom_call" | custom-call | flops 49999998976 | bytes 1 | tf_op jit(solution)/shard_map/attend_back/pallas_call | solution.py:73
  96.1 2.7 %attend_back.3 = (bf16[256,192]{1,0:T(8,128)(2,1)S(1)}, bf16[2,2,384,128]{3,2,1,0:T(8,128)(2,1)S(1)}, bf16[2,2,384,128]{3,2,1,0:T(8,128)(2,1)S(1)}) custom-call(s32[5]{0:T(128)S(1)} %stack.23.at, bf16[192,128]{1,0:T(8,128)(2,1)S(1)} %collective-permute-done.21.first, bf16[192,128]{1,0:T(8,128)(2,1)S(1)} %collective-permute-done.22.second, ...), custom_call_target="tpu_custom_call" | custom-call | flops 49999998976 | bytes 1 | tf_op jit(solution)/shard_map/attend_back/pallas_call | solution.py:73
  107.0 3.5 %collective-permute-done.27.far = bf16[2,384,128]{2,1,0:T(8,128)(2,1)S(1)} collective-permute-done((bf16[2,384,128]{2,1,0:T(8,128)(2,1)S(1)}, bf16[2,384,128]{2,1,0:T(8,128)(2,1)S(1)}, u32[]{:S(2)}, u32[]{:S(2)}) %collective-permute-start.27) | collective-permute-done | bytes 196640 | tf_op jit(solution)/shard_map/ppermute | solution.py:463
  111.1 4.1 %collective-permute-done.29.refs_3_ = bf16[144,768]{1,0:T(8,128)(2,1)S(1)} collective-permute-done((bf16[144,768]{1,0:T(8,128)(2,1)S(1)}, bf16[144,768]{1,0:T(8,128)(2,1)S(1)}, u32[]{:S(2)}, u32[]{:S(2)}) %collective-permute-start.29) | collective-permute-done | bytes 221216 | tf_op jit(solution)/shard_map/ppermute | solution.py:460
  122.6 4.3 %collective-permute-done.30 = bf16[256,768]{1,0:T(8,128)(2,1)S(1)} collective-permute-done((bf16[256,768]{1,0:T(8,128)(2,1)S(1)}, bf16[256,768]{1,0:T(8,128)(2,1)S(1)}, u32[]{:S(2)}, u32[]{:S(2)}) %collective-permute-start.30) | collective-permute-done | bytes 393248 | tf_op jit(solution)/shard_map/ppermute | solution.py:460
  127.0 6.2 %collective-permute-done.32 = bf16[2,208,768]{2,1,0:T(8,128)(2,1)S(1)} collective-permute-done((bf16[2,208,768]{2,1,0:T(8,128)(2,1)S(1)}, bf16[2,208,768]{2,1,0:T(8,128)(2,1)S(1)}, u32[]{:S(2)}, u32[]{:S(2)}) %collective-permute-start.32) | collective-permute-done | bytes 639008 | tf_op jit(solution)/shard_map/ppermute | solution.py:472
  135.6 10.0 %collective-permute-done.34 = bf16[2,208,768]{2,1,0:T(8,128)(2,1)S(1)} collective-permute-done((bf16[2,208,768]{2,1,0:T(8,128)(2,1)S(1)}, bf16[2,208,768]{2,1,0:T(8,128)(2,1)S(1)}, u32[]{:S(2)}, u32[]{:S(2)}) %collective-permute-start.34) | collective-permute-done | bytes 639008 | tf_op jit(solution)/shard_map/ppermute | solution.py:472
  150.5 2.3 %collective-permute-done.37 = bf16[112,768]{1,0:T(8,128)(2,1)S(1)} collective-permute-done((bf16[112,768]{1,0:T(8,128)(2,1)S(1)}, bf16[112,768]{1,0:T(8,128)(2,1)S(1)}, u32[]{:S(2)}, u32[]{:S(2)}) %collective-permute-start.37) | collective-permute-done | bytes 172064 | tf_op jit(solution)/shard_map/ppermute | solution.py:472
  152.8 3.0 %collective-permute-done.39 = bf16[112,768]{1,0:T(8,128)(2,1)S(1)} collective-permute-done((bf16[112,768]{1,0:T(8,128)(2,1)S(1)}, bf16[112,768]{1,0:T(8,128)(2,1)S(1)}, u32[]{:S(2)}, u32[]{:S(2)}) %collective-permute-start.39) | collective-permute-done | bytes 172064 | tf_op jit(solution)/shard_map/ppermute | solution.py:472
  161.7 1.9 collective-permute-done.45.refs_1_
  167.9 12.7 %collective-permute-done.47.refs_3_ = bf16[112,768]{1,0:T(8,128)(2,1)S(1)} collective-permute-done((bf16[112,768]{1,0:T(8,128)(2,1)S(1)}, bf16[112,768]{1,0:T(8,128)(2,1)S(1)}, u32[]{:S(2)}, u32[]{:S(2)}) %collective-permute-start.47) | collective-permute-done | bytes 172064 | tf_op jit(solution)/shard_map/ppermute | solution.py:472
  184.0 1.8 collective-permute-done.50.other
  185.8 2.9 %ffn_grads_out.1 = (f32[768,768]{1,0:T(8,128)}, f32[768,768]{1,0:T(8,128)}, f32[768]{0:T(1024)}, f32[768]{0:T(1024)}, f32[768]{0:T(1024)}, /*index=5*/f32[768]{0:T(1024)}) custom-call(s32[5]{0:T(128)S(1)} %stack.23.at, bf16[4,208,768]{2,1,0:T(8,128)(2,1)S(1)} %gather_ffn_grads.1.mine, bf16[4,208,768]{2,1,0:T(8,128)(2,1)S(1)} %collective-permute-done.50.other), custom_call_target="tpu_custom_call" | custom-call | flops 3000000000 | bytes 1 | tf_op jit(solution)/shard_map/ffn_grads_out/pallas_call | solution.py:73
  188.8 2.0 %attend_grads_out.1 = (f32[192,768]{1,0:T(8,128)}, f32[192,768]{1,0:T(8,128)}, f32[192,768]{1,0:T(8,128)}, f32[192,768]{1,0:T(8,128)}, f32[768]{0:T(1024)}, /*in...) custom-call(s32[5]{0:T(128)S(1)} %stack.23.at, bf16[448,768]{1,0:T(8,128)(2,1)S(1)} %bitcast.65, ...), custom_call_target="tpu_custom_call" | custom-call | flops 2000000000 | bytes 1 | tf_op jit(solution)/shard_map/attend_grads_out/pallas_call | solution.py:73
  (197 shorter events, 61.7 us)
Async XLA Ops:
  4.0 18.3 %collective-permute-start = (bf16[512,384]{1,0:T(8,128)(2,1)S(1)}, bf16[512,384]{1,0:T(8,128)(2,1)S(1)}, u32[]{:S(2)}, u32[]{:S(2)}) collective-permute-start(bf16[512,384]{1,0:T(8,128)(2,1)S(1)} %get-tuple-element.159.refs_0_), channel_id=1, source_target_pairs={{0,8},{4,12},{8,0},{12,4},{1,9},{5,13},{9,1},{13,5},{2,10},{6,14},... | collective-permute-start | bytes 1179656 | tf_op jit(solution)/shard_map/ppermute | solution.py:463
  7.0 15.3 %collective-permute-start.2 = (bf16[240,768]{1,0:T(8,128)(2,1)S(1)}, bf16[240,768]{1,0:T(8,128)(2,1)S(1)}, u32[]{:S(2)}, u32[]{:S(2)}) collective-permute-start(bf16[240,768]{1,0:T(8,128)(2,1)S(1)} %get-tuple-element.161), channel_id=1, source_target_pairs={{0,1},{1,0},{2,3},{3,2},{4,5},{5,4},{6,7},{7,6},{8,9},{9,8},{10,11... | collective-permute-start | bytes 1105928 | tf_op jit(solution)/shard_map/ppermute | solution.py:460
  8.6 10.8 %collective-permute-start.3 = (bf16[48,768]{1,0:T(8,128)(2,1)S(1)}, bf16[48,768]{1,0:T(8,128)(2,1)S(1)}, u32[]{:S(2)}, u32[]{:S(2)}) collective-permute-start(bf16[48,768]{1,0:T(8,128)(2,1)S(1)} %get-tuple-element.162), channel_id=1, source_target_pairs={{0,2},{1,3},{2,0},{3,1},{4,6},{5,7},{6,4},{7,5},{8,10},{9,11},{10,... | collective-permute-start | bytes 221192 | tf_op jit(solution)/shard_map/ppermute | solution.py:460
  11.2 11.1 %collective-permute-start.4 = (bf16[48,768]{1,0:T(8,128)(2,1)S(1)}, bf16[48,768]{1,0:T(8,128)(2,1)S(1)}, u32[]{:S(2)}, u32[]{:S(2)}) collective-permute-start(bf16[48,768]{1,0:T(8,128)(2,1)S(1)} %get-tuple-element.162), channel_id=1, source_target_pairs={{0,3},{1,2},{2,1},{3,0},{4,7},{5,6},{6,5},{7,4},{8,11},{9,10},{10,... | collective-permute-start | bytes 221192 | tf_op jit(solution)/shard_map/ppermute | solution.py:460
  22.9 12.9 %collective-permute-start.12 = (bf16[192,768]{1,0:T(8,128)(2,1)S(1)}, bf16[192,768]{1,0:T(8,128)(2,1)S(1)}, u32[]{:S(2)}, u32[]{:S(2)}) collective-permute-start(bf16[192,768]{1,0:T(8,128)(2,1)S(1)} %slice.21), channel_id=1, source_target_pairs={{0,16},{4,20},{8,24},{12,28},{16,0},{20,4},{24,8},{28,12},{1,17},{... | collective-permute-start | bytes 884744 | tf_op jit(solution)/shard_map/ppermute | solution.py:550
  24.5 14.4 %collective-permute-start.13 = (bf16[192,768]{1,0:T(8,128)(2,1)S(1)}, bf16[192,768]{1,0:T(8,128)(2,1)}, u32[]{:S(2)}, u32[]{:S(2)}) collective-permute-start(bf16[192,768]{1,0:T(8,128)(2,1)S(1)} %slice.21), channel_id=1, source_target_pairs={{0,24},{4,28},{8,16},{12,20},{16,8},{20,12},{24,0},{28,4},{1,25},{... | collective-permute-start | bytes 884744 | tf_op jit(solution)/shard_map/ppermute | solution.py:550
  25.1 20.0 %collective-permute-start.11 = (bf16[336,768]{1,0:T(8,128)(2,1)S(1)}, bf16[336,768]{1,0:T(8,128)(2,1)S(1)}, u32[]{:S(2)}, u32[]{:S(2)}) collective-permute-start(bf16[336,768]{1,0:T(8,128)(2,1)S(1)} %constant_dynamic-update-slice_fusion.refs_0_), channel_id=1, source_target_pairs={{0,8},{4,12},{8,0},{12,4},{16,24},{20,28},{24,16},{28,20},{1,9},{5... | collective-permute-start | bytes 1548296 | tf_op jit(solution)/shard_map/ppermute | solution.py:550
  32.5 10.6 %collective-permute-start.9 = (bf16[384,128]{1,0:T(8,128)(2,1)S(1)}, bf16[384,128]{1,0:T(8,128)(2,1)S(1)}, u32[]{:S(2)}, u32[]{:S(2)}) collective-permute-start(bf16[384,128]{1,0:T(8,128)(2,1)S(1)} %get-tuple-element.168.refs_0_), channel_id=1, source_target_pairs={{0,2},{1,3},{2,0},{3,1},{4,6},{5,7},{6,4},{7,5},{8,10},{9,11},{10,... | collective-permute-start | bytes 294920 | tf_op jit(solution)/shard_map/ppermute | solution.py:460
  52.0 16.2 %collective-permute-start.17 = (bf16[128,768]{1,0:T(8,128)(2,1)S(1)}, bf16[128,768]{1,0:T(8,128)(2,1)S(1)}, u32[]{:S(2)}, u32[]{:S(2)}) collective-permute-start(bf16[128,768]{1,0:T(8,128)(2,1)S(1)} %get-tuple-element.181.mine), channel_id=1, source_target_pairs={{0,2},{1,3},{2,0},{3,1},{4,6},{5,7},{6,4},{7,5},{8,10},{9,11},{10,... | collective-permute-start | bytes 589832 | tf_op jit(solution)/shard_map/ppermute | solution.py:460
  55.1 17.2 %collective-permute-start.18 = (bf16[128,768]{1,0:T(8,128)(2,1)S(1)}, bf16[128,768]{1,0:T(8,128)(2,1)S(1)}, u32[]{:S(2)}, u32[]{:S(2)}) collective-permute-start(bf16[128,768]{1,0:T(8,128)(2,1)S(1)} %get-tuple-element.186.mine), channel_id=1, source_target_pairs={{0,2},{1,3},{2,0},{3,1},{4,6},{5,7},{6,4},{7,5},{8,10},{9,11},{10,... | collective-permute-start | bytes 589832 | tf_op jit(solution)/shard_map/ppermute | solution.py:460
  70.9 15.4 %collective-permute-start.19 = (bf16[128,768]{1,0:T(8,128)(2,1)S(1)}, bf16[128,768]{1,0:T(8,128)(2,1)S(1)}, u32[]{:S(2)}, u32[]{:S(2)}) collective-permute-start(bf16[128,768]{1,0:T(8,128)(2,1)S(1)} %get-tuple-element.188.mine), channel_id=1, source_target_pairs={{0,2},{1,3},{2,0},{3,1},{4,6},{5,7},{6,4},{7,5},{8,10},{9,11},{10,... | collective-permute-start | bytes 589832 | tf_op jit(solution)/shard_map/ppermute | solution.py:460
  75.0 15.5 %collective-permute-start.20 = (bf16[128,768]{1,0:T(8,128)(2,1)S(1)}, bf16[128,768]{1,0:T(8,128)(2,1)S(1)}, u32[]{:S(2)}, u32[]{:S(2)}) collective-permute-start(bf16[128,768]{1,0:T(8,128)(2,1)S(1)} %get-tuple-element.192.mine), channel_id=1, source_target_pairs={{0,2},{1,3},{2,0},{3,1},{4,6},{5,7},{6,4},{7,5},{8,10},{9,11},{10,... | collective-permute-start | bytes 589832 | tf_op jit(solution)/shard_map/ppermute | solution.py:460
  78.9 16.1 %collective-permute-start.23 = (bf16[4,2,208,768]{3,2,1,0:T(8,128)(2,1)S(1)}, bf16[4,2,208,768]{3,2,1,0:T(8,128)(2,1)S(1)}, u32[]{:S(2)}, u32[]{:S(2)}) collective-permute-start(bf16[4,2,208,768]{3,2,1,0:T(8,128)(2,1)S(1)} %get-tuple-element.217), channel_id=1, source_target_pairs={{0,4},{4,0},{8,12},{12,8},{1,5},{5,1},{9,13},{13,9},{2,6},{6,2},{1... | collective-permute-start | bytes 7667720 | tf_op jit(solution)/shard_map/ppermute | solution.py:463
  87.5 8.1 %collective-permute-start.21 = (bf16[192,128]{1,0:T(8,128)(2,1)S(1)}, bf16[192,128]{1,0:T(8,128)(2,1)S(1)}, u32[]{:S(2)}, u32[]{:S(2)}) collective-permute-start(bf16[192,128]{1,0:T(8,128)(2,1)S(1)} %get-tuple-element.200), channel_id=1, source_target_pairs={{0,1},{1,0},{2,3},{3,2},{4,5},{5,4},{6,7},{7,6},{8,9},{9,8},{10,11... | collective-permute-start | bytes 147464 | tf_op jit(solution)/shard_map/ppermute | solution.py:460
  100.8 9.7 %collective-permute-start.27 = (bf16[2,384,128]{2,1,0:T(8,128)(2,1)S(1)}, bf16[2,384,128]{2,1,0:T(8,128)(2,1)S(1)}, u32[]{:S(2)}, u32[]{:S(2)}) collective-permute-start(bf16[2,384,128]{2,1,0:T(8,128)(2,1)S(1)} %fusion.10), channel_id=1, source_target_pairs={{0,8},{4,12},{8,0},{12,4},{1,9},{5,13},{9,1},{13,5},{2,10},{6,14},... | collective-permute-start | bytes 589832 | tf_op jit(solution)/shard_map/ppermute | solution.py:463
  102.2 8.9 %collective-permute-start.28 = (bf16[144,768]{1,0:T(8,128)(2,1)S(1)}, bf16[144,768]{1,0:T(8,128)(2,1)S(1)}, u32[]{:S(2)}, u32[]{:S(2)}) collective-permute-start(bf16[144,768]{1,0:T(8,128)(2,1)S(1)} %get-tuple-element.237.refs_0_), channel_id=1, source_target_pairs={{0,1},{1,0},{2,3},{3,2},{4,5},{5,4},{6,7},{7,6},{8,9},{9,8},{10,11... | collective-permute-start | bytes 663560 | tf_op jit(solution)/shard_map/ppermute | solution.py:460
  103.8 11.4 %collective-permute-start.29 = (bf16[144,768]{1,0:T(8,128)(2,1)S(1)}, bf16[144,768]{1,0:T(8,128)(2,1)S(1)}, u32[]{:S(2)}, u32[]{:S(2)}) collective-permute-start(bf16[144,768]{1,0:T(8,128)(2,1)S(1)} %get-tuple-element.238.refs_1_), channel_id=1, source_target_pairs={{0,1},{1,0},{2,3},{3,2},{4,5},{5,4},{6,7},{7,6},{8,9},{9,8},{10,11... | collective-permute-start | bytes 663560 | tf_op jit(solution)/shard_map/ppermute | solution.py:460
  104.2 43.1 %collective-permute-start.40 = (bf16[128,768]{1,0:T(8,128)(2,1)S(1)}, bf16[128,768]{1,0:T(8,128)(2,1)S(1)}, u32[]{:S(2)}, u32[]{:S(2)}) collective-permute-start(bf16[128,768]{1,0:T(8,128)(2,1)S(1)} %get-tuple-element.182.refs_0_), channel_id=1, source_target_pairs={{0,1},{1,0},{2,3},{3,2},{4,5},{5,4},{6,7},{7,6},{8,9},{9,8},{10,11... | collective-permute-start | bytes 589832 | tf_op jit(solution)/shard_map/ppermute | solution.py:460
  115.2 11.7 %collective-permute-start.30 = (bf16[256,768]{1,0:T(8,128)(2,1)S(1)}, bf16[256,768]{1,0:T(8,128)(2,1)S(1)}, u32[]{:S(2)}, u32[]{:S(2)}) collective-permute-start(bf16[256,768]{1,0:T(8,128)(2,1)S(1)} %get-tuple-element.239), channel_id=1, source_target_pairs={{0,1},{1,0},{2,3},{3,2},{4,5},{5,4},{6,7},{7,6},{8,9},{9,8},{10,11... | collective-permute-start | bytes 1179656 | tf_op jit(solution)/shard_map/ppermute | solution.py:460
  116.8 16.4 %collective-permute-start.32 = (bf16[2,208,768]{2,1,0:T(8,128)(2,1)S(1)}, bf16[2,208,768]{2,1,0:T(8,128)(2,1)S(1)}, u32[]{:S(2)}, u32[]{:S(2)}) collective-permute-start(bf16[2,208,768]{2,1,0:T(8,128)(2,1)S(1)} %get-tuple-element.241), channel_id=1, source_target_pairs={{0,8},{4,12},{8,0},{12,4},{16,24},{20,28},{24,16},{28,20},{1,9},{5... | collective-permute-start | bytes 1916936 | tf_op jit(solution)/shard_map/ppermute | solution.py:472
  117.4 17.3 %collective-permute-start.33 = (bf16[2,208,768]{2,1,0:T(8,128)(2,1)S(1)}, bf16[2,208,768]{2,1,0:T(8,128)(2,1)S(1)}, u32[]{:S(2)}, u32[]{:S(2)}) collective-permute-start(bf16[2,208,768]{2,1,0:T(8,128)(2,1)S(1)} %get-tuple-element.242), channel_id=1, source_target_pairs={{0,16},{4,20},{8,24},{12,28},{16,0},{20,4},{24,8},{28,12},{1,17},{... | collective-permute-start | bytes 1916936 | tf_op jit(solution)/shard_map/ppermute | solution.py:472
  118.9 26.8 %collective-permute-start.34 = (bf16[2,208,768]{2,1,0:T(8,128)(2,1)S(1)}, bf16[2,208,768]{2,1,0:T(8,128)(2,1)S(1)}, u32[]{:S(2)}, u32[]{:S(2)}) collective-permute-start(bf16[2,208,768]{2,1,0:T(8,128)(2,1)S(1)} %get-tuple-element.243), channel_id=1, source_target_pairs={{0,24},{4,28},{8,16},{12,20},{16,8},{20,12},{24,0},{28,4},{1,25},{... | collective-permute-start | bytes 1916936 | tf_op jit(solution)/shard_map/ppermute | solution.py:472
  126.9 19.9 %collective-permute-start.36 = (bf16[448,768]{1,0:T(8,128)(2,1)S(1)}, bf16[448,768]{1,0:T(8,128)(2,1)S(1)}, u32[]{:S(2)}, u32[]{:S(2)}) collective-permute-start(bf16[448,768]{1,0:T(8,128)(2,1)S(1)} %get-tuple-element.255), channel_id=1, source_target_pairs={{0,4},{4,0},{8,12},{12,8},{1,5},{5,1},{9,13},{13,9},{2,6},{6,2},{1... | collective-permute-start | bytes 2064392 | tf_op jit(solution)/shard_map/ppermute | solution.py:463
  133.2 15.7 %collective-permute-start.41 = (bf16[128,768]{1,0:T(8,128)(2,1)S(1)}, bf16[128,768]{1,0:T(8,128)(2,1)S(1)}, u32[]{:S(2)}, u32[]{:S(2)}) collective-permute-start(bf16[128,768]{1,0:T(8,128)(2,1)S(1)} %get-tuple-element.187.refs_1_), channel_id=1, source_target_pairs={{0,1},{1,0},{2,3},{3,2},{4,5},{5,4},{6,7},{7,6},{8,9},{9,8},{10,11... | collective-permute-start | bytes 589832 | tf_op jit(solution)/shard_map/ppermute | solution.py:460
  134.8 15.7 %collective-permute-start.31 = (bf16[256,768]{1,0:T(8,128)(2,1)S(1)}, bf16[256,768]{1,0:T(8,128)(2,1)S(1)}, u32[]{:S(2)}, u32[]{:S(2)}) collective-permute-start(bf16[256,768]{1,0:T(8,128)(2,1)S(1)} %add_convert_fusion.5), channel_id=1, source_target_pairs={{0,2},{1,3},{2,0},{3,1},{4,6},{5,7},{6,4},{7,5},{8,10},{9,11},{10,... | collective-permute-start | bytes 1179656 | tf_op jit(solution)/shard_map/ppermute | solution.py:460
  146.1 10.0 %collective-permute-start.35 = (bf16[208,768]{1,0:T(8,128)(2,1)S(1)}, bf16[208,768]{1,0:T(8,128)(2,1)S(1)}, u32[]{:S(2)}, u32[]{:S(2)}) collective-permute-start(bf16[208,768]{1,0:T(8,128)(2,1)S(1)} %slice_bitcast_fusion.1), channel_id=1, source_target_pairs={{0,1},{1,0},{2,3},{3,2},{4,5},{5,4},{6,7},{7,6},{8,9},{9,8},{10,11... | collective-permute-start | bytes 958472 | tf_op jit(solution)/shard_map/ppermute | solution.py:460
  157.0 8.0 %collective-permute-start.46 = (bf16[112,768]{1,0:T(8,128)(2,1)S(1)}, bf16[112,768]{1,0:T(8,128)(2,1)S(1)}, u32[]{:S(2)}, u32[]{:S(2)}) collective-permute-start(bf16[112,768]{1,0:T(8,128)(2,1)S(1)} %fusion.8.refs_0_), channel_id=1, source_target_pairs={{0,16},{4,20},{8,24},{12,28},{16,0},{20,4},{24,8},{28,12},{1,17},{... | collective-permute-start | bytes 516104 | tf_op jit(solution)/shard_map/ppermute | solution.py:472
  158.4 22.2 %collective-permute-start.48 = (bf16[256,768]{1,0:T(8,128)(2,1)S(1)}, bf16[256,768]{1,0:T(8,128)(2,1)S(1)}, u32[]{:S(2)}, u32[]{:S(2)}) collective-permute-start(bf16[256,768]{1,0:T(8,128)(2,1)S(1)} %fusion.refs_0_), channel_id=1, source_target_pairs={{0,1},{1,0},{2,3},{3,2},{4,5},{5,4},{6,7},{7,6},{8,9},{9,8},{10,11... | collective-permute-start | bytes 1179656 | tf_op jit(solution)/shard_map/ppermute | solution.py:460
  159.6 21.0 %collective-permute-start.42 = (bf16[208,768]{1,0:T(8,128)(2,1)S(1)}, bf16[208,768]{1,0:T(8,128)(2,1)S(1)}, u32[]{:S(2)}, u32[]{:S(2)}) collective-permute-start(bf16[208,768]{1,0:T(8,128)(2,1)S(1)} %fusion.5.refs_0_), channel_id=1, source_target_pairs={{0,8},{4,12},{8,0},{12,4},{16,24},{20,28},{24,16},{28,20},{1,9},{5... | collective-permute-start | bytes 958472 | tf_op jit(solution)/shard_map/ppermute | solution.py:472
  161.1 19.5 %collective-permute-start.43 = (bf16[208,768]{1,0:T(8,128)(2,1)S(1)}, bf16[208,768]{1,0:T(8,128)(2,1)S(1)}, u32[]{:S(2)}, u32[]{:S(2)}) collective-permute-start(bf16[208,768]{1,0:T(8,128)(2,1)S(1)} %fusion.5.refs_0_), channel_id=1, source_target_pairs={{0,16},{4,20},{8,24},{12,28},{16,0},{20,4},{24,8},{28,12},{1,17},{... | collective-permute-start | bytes 958472 | tf_op jit(solution)/shard_map/ppermute | solution.py:472
  163.5 17.1 %collective-permute-start.44 = (bf16[208,768]{1,0:T(8,128)(2,1)S(1)}, bf16[208,768]{1,0:T(8,128)(2,1)S(1)}, u32[]{:S(2)}, u32[]{:S(2)}) collective-permute-start(bf16[208,768]{1,0:T(8,128)(2,1)S(1)} %fusion.5.refs_0_), channel_id=1, source_target_pairs={{0,24},{4,28},{8,16},{12,20},{16,8},{20,12},{24,0},{28,4},{1,25},{... | collective-permute-start | bytes 958472 | tf_op jit(solution)/shard_map/ppermute | solution.py:472
  165.0 15.6 %collective-permute-start.47 = (bf16[112,768]{1,0:T(8,128)(2,1)S(1)}, bf16[112,768]{1,0:T(8,128)(2,1)S(1)}, u32[]{:S(2)}, u32[]{:S(2)}) collective-permute-start(bf16[112,768]{1,0:T(8,128)(2,1)S(1)} %fusion.8.refs_0_), channel_id=1, source_target_pairs={{0,24},{4,28},{8,16},{12,20},{16,8},{20,12},{24,0},{28,4},{1,25},{... | collective-permute-start | bytes 516104 | tf_op jit(solution)/shard_map/ppermute | solution.py:472
  (60 other events, 471.3 us)

commit v7 on v6

--- a/solution.py
+++ b/solution.py
@@ -285,7 +285,7 @@
     )
 
 
-def norm_back_kernel(n, at, mine, theirs, dres2, n1, s1, g1, w_out, dres1_out, share, dh, dh_far):
+def norm_back_kernel(n, at, mine, theirs, dres2, n1, s1, g1, w_out, sums2, dres1_out, share, dh, dh_far):
     dhidden = (mine[...].astype(f32) + theirs[...].astype(f32)) + dres2[...]
     norm = n1[...]
     dn = dhidden * g1[...]
@@ -293,7 +293,9 @@
     dattn = dres1.astype(bf16)
     dres1_out[...] = dres1
     share[:BLOCK, :] = dattn
-    sums = rows8(col_sum(dhidden * norm), col_sum(dhidden), col_sum(dattn.astype(f32)))
+    sums = jnp.concatenate(
+        [col_sum(dhidden * norm), col_sum(dhidden), col_sum(dattn.astype(f32)), sums2[:5, :]], axis=0
+    )
     share[BLOCK:, :] = jnp.concatenate([sums, jnp.zeros_like(sums)], axis=0).astype(bf16)
     local = w_out.shape[0] // n
     dh[...] = pack(nt(dattn, chunk_of(w_out, at[0], local)).astype(bf16))
@@ -363,21 +365,17 @@
 
 
 def ffn_grad_kernel(m, at, *refs):
-    low, act, act_far, dffn, dinner, dinner_far, sums2 = (refs[2 * i : 2 * i + 2] for i in range(7))
-    keep, send = refs[14:]
+    low, act, act_far, dffn, dinner, dinner_far = (refs[2 * i : 2 * i + 2] for i in range(6))
+    keep, send = refs[12:]
     first = at[1] == 0
     both = lambda pair: join(x[...] for x in pair)
     lows, dffns = both(low), both(dffn)
-    tail2 = sums2[0][...] + sums2[1][...]
     rows = lows.shape[1] // m
     for q, (acts, dinners) in enumerate(((both(act), both(dinner)), (both(act_far), both(dinner_far)))):
-        tail = join([tail2[:3], tail2[3 + q : 4 + q], jnp.zeros((12, tail2.shape[1]), f32)])
-        tail = tail.astype(bf16)
         for target, one in ((keep, first), (send, jnp.logical_not(first))):
             main = tn(pick(one, lows, acts), pick(one, dinners, dffns)).astype(bf16)
             for i in range(m):
-                target[i, q, :rows, :] = main[i * rows : (i + 1) * rows]
-                target[i, q, rows:, :] = tail
+                target[i, q] = main[i * rows : (i + 1) * rows]
 
 
 def attend_grad_kernel(m, at, tok, hp_late, *refs):
@@ -394,6 +392,9 @@
     half = two.shape[0]
     norm = ordered_sum(at, [x[BLOCK : BLOCK + 8, :] for x in shares], held)
     total = sums[0][...] + sums[1][...]
+    row = lambda x, k: x[BLOCK + k : BLOCK + k + 1, :].astype(f32)
+    inner = row(shares[0], 6) + row(shares[1], 6) + row(shares[2], 7) + row(shares[3], 7)
+    norm = join([norm[:6], inner, jnp.zeros_like(inner)])
     rest = keep.shape[0] - half
     tail = join([norm, total, jnp.zeros((rest - 16, total.shape[1]), f32)]).astype(bf16)
     keep[:half, :] = pick(first, one, two)
@@ -408,23 +409,26 @@
         out[at[3] ^ s] = refs[s][...]
 
 
-def ffn_final_kernel(m, at, mine, other, g_in, g_outer, *vectors):
+def share_kernel(total1, near1, *refs):
+    parts, share = refs[:-1], refs[-1]
+    rows = near1.shape[0]
+    share[:rows, :] = (total1[0].astype(f32) + near1[...].astype(f32)).astype(bf16)
+    total = parts[0][...].astype(f32)
+    for part in parts[1:]:
+        total = total + part[...].astype(f32)
+    share[rows:, :] = total.astype(bf16)
+
+
+def final_kernel(m, at, mine, other, g_in, g_outer, g_out, g_q, g_k, g_v, *vectors):
     first = at[1] == 0
     rows = g_in.shape[0] // m
     for i in range(m):
-        a, b = mine[i], other[i]
-        g_in[i * rows : (i + 1) * rows, :] = pick(first, a[:rows], b[:rows]).astype(f32)
-        g_outer[i * rows : (i + 1) * rows, :] = pick(first, b[:rows], a[:rows]).astype(f32)
-    tail = mine[0, rows:, :].astype(f32)
-    for k, ref in enumerate(vectors):
-        ref[...] = tail[k]
-
-
-def attend_final_kernel(at, mine, other, g_out, g_q, g_k, g_v, gain, bias, b_out, b_q, b_v):
-    first = at[1] == 0
+        a, b = mine[i, :rows, :], other[i, :rows, :]
+        g_in[i * rows : (i + 1) * rows, :] = pick(first, a, b).astype(f32)
+        g_outer[i * rows : (i + 1) * rows, :] = pick(first, b, a).astype(f32)
     width = g_q.shape[0]
-    a = mine[...]
-    b = other[...]
+    a = join(mine[i, rows:, :] for i in range(m))
+    b = join(other[i, rows:, :] for i in range(m))
     one = pick(first, a, b).astype(f32)
     two = pick(first, b, a).astype(f32)
     g_out[...] = one[:width]
@@ -436,7 +440,8 @@
         g_k[part, :] = two[h * LANES : h * LANES + HEAD_DIM]
         g_v[part, :] = two[h * LANES + HEAD_DIM : (h + 1) * LANES]
         values.append(tail[9:10, h * LANES + HEAD_DIM : (h + 1) * LANES])
-    for i, ref in enumerate((gain, bias, b_out)):
+    b_q, b_v = vectors[7:]
+    for i, ref in enumerate(vectors[:7]):
         ref[...] = tail[i]
     b_q[...] = tail[8, :width]
     b_v[...] = jnp.concatenate(values, axis=1)[0]
@@ -632,9 +637,9 @@
         theirs2 = [swap(v, 2) for v in parts2]
         keep1, send1 = call(
             functools.partial(ffn_grad_kernel, m),
-            (near((m, 2, width // m + 16, width), bf16),) * 2,
+            (near((m, 2, width // m, width), bf16),) * 2,
             "ffn_grads",
-            (at, *lows, *acts, *acts_far, *dffns, *dinners, *dinners_far, *sums2),
+            (at, *lows, *acts, *acts_far, *dffns, *dinners, *dinners_far),
             us=FILL_US,
             vmem=24,
             scalars=1,
@@ -650,7 +655,7 @@
                     near((PACKED, LANES), bf16),
                 ),
                 "norm_back",
-                (at, parts2[i], theirs2[i], dres2[i], n1s[i], s1s[i], gains1[0], w_out_all),
+                (at, parts2[i], theirs2[i], dres2[i], n1s[i], s1s[i], gains1[0], w_out_all, sums2[i]),
                 us=1.2,
                 scalars=1,
             )
@@ -698,9 +703,9 @@
         far_own, far_other = flip(sum_own, 2), flip(sum_other, 2)
         far_own, far_other, pieces1 = fence((far_own, far_other, pieces1))
         part, *late = input_part(other, recv_other, far_other, 1.0)
-        part, pieces1, *ends = fence((part, pieces1, *shares[2:]))
+        part, pieces1 = fence((part, pieces1))
+        from_near, *ends = fence((swap(part, 1), *shares[2:]))
         shares[2:] = ends
-        from_near = swap(part, 1)
         got1 = [flip_member(v, s) for s, v in enumerate(pieces1[1:], 1)]
         part_own, dkv_own, sums_own = input_part(own, recv_own, far_own, INPUT_US)
         pair = (part_own.astype(f32) + from_near.astype(f32)).astype(bf16)
@@ -729,11 +734,15 @@
         outs[2:] = ends
         d_tok = pair.astype(f32) + crossed.astype(f32) + jnp.concatenate(dres1, axis=0)
         d_tok = d_tok.astype(bf16)
-        share1 = (total1[0].astype(f32) + near1.astype(f32)).astype(bf16)
-        total2 = add(pieces2[0], got2)
-        shares1 = [flip_member(share1, k) for k in range(1, m)]
-        shares2 = [flip_member(total2, k) for k in range(1, m)]
-        shares1, shares2, d_far = fence((shares1, shares2, swap(d_tok, 1)))
+        share = call(
+            share_kernel,
+            chunk(width // m + rows2 // m, bf16),
+            "grad_share",
+            (total1, near1, pieces2[0], *got2),
+            us=0.5,
+        )
+        shares_in = [flip_member(share, k) for k in range(1, m)]
+        shares_in, d_far = fence((shares_in, swap(d_tok, 1)))
         d_toks = [d_tok, d_far]
         assemble = lambda parts, name: call(
             rows_kernel,
@@ -745,31 +754,22 @@
         )
         output = assemble(outs, "output_rows")
         d_tokens = assemble(d_toks, "input_grad_rows")
-        shares1, shares2, _, _ = fence((shares1, shares2, output, d_tokens))
-        mine1 = gather_grads([share1] + shares1, at, "gather_ffn_grads")
-        other1 = flip(mine1, 1)
-        mine2 = gather_grads([total2] + shares2, at, "gather_attend_grads").reshape(rows2, width)
-        other2 = flip(mine2, 1)
-
+        mine = gather_grads([share] + shares_in, at, "gather_grads")
+        other, _, _ = fence((flip(mine, 1), output, d_tokens))
         vector = shape((width,), f32)
         short = shape((local,), f32)
         square = shape((width, units), f32)
         wide = shape((local, width), f32)
-        g_w_inner, g_w_outer, g_gain2, g_bias2, g_b_outer, g_b_inner = call(
-            functools.partial(ffn_final_kernel, m),
-            (square, square) + (vector,) * 4,
-            "ffn_grads_out",
-            (at, mine1, other1),
-            us=3.0,
-            scalars=1,
-        )
-        other2, g_b_outer = fence((other2, g_b_outer))
-        g_w_out, g_q, g_k, g_v, g_gain1, g_bias1, g_b_out, g_b_query, g_b_value = call(
-            attend_final_kernel,
-            (wide,) * 4 + (vector,) * 3 + (short,) * 2,
-            "attend_grads_out",
-            (at, mine2, other2),
-            us=2.0,
+        (
+            g_w_inner, g_w_outer, g_w_out, g_q, g_k, g_v, g_gain1, g_bias1, g_b_out, g_gain2, g_bias2,
+            g_b_outer, g_b_inner, g_b_query, g_b_value,
+        ) = call(
+            functools.partial(final_kernel, m),
+            (square,) * 2 + (wide,) * 4 + (vector,) * 7 + (short,) * 2,
+            "grads_out",
+            (at, mine, other),
+            us=4.0,
+            vmem=24,
             scalars=1,
         )
         return (

time: 191 us -> 186 us (0.974)
  starting transfers between devices: 48.2 us -> 41.3 us
  waiting for transfers between devices: 93.2 us -> 97.3 us
    ppermute x21, waiting for transfers between devices: 45.2 us -> 60.9 us  [swap(): return lax.ppermute(v, 'tensor', [(i, i ^ bit) for i in range(n)])]
    ppermute x12 -> x9, waiting for transfers between devices: 37.1 us -> 24.9 us  [flip_member(): return lax.ppermute(v, ('dp', 'blk'), perm)]
    ppermute x12 -> x9, starting transfers between devices: 14.2 us -> 10.6 us  [flip_member(): return lax.ppermute(v, ('dp', 'blk'), perm)]
    ppermute x21, starting transfers between devices: 22.8 us -> 20 us  [swap(): return lax.ppermute(v, 'tensor', [(i, i ^ bit) for i in range(n)])]
    pallas_call x20 -> x19, Pallas kernels: 33.5 us -> 31.9 us  [call(): pl.pallas_call(kernel, out_shape=outs, in_specs=[SMEM] * scalars + [VMEM]...]
    ppermute x15 -> x14, waiting for transfers between devices: 8.89 us -> 9.53 us  [flip(): return lax.ppermute(v, 'blk', [(i, i ^ bit) for i in range(n_blk)])]
    ppermute x15 -> x14, starting transfers between devices: 7.59 us -> 7.08 us  [flip(): return lax.ppermute(v, 'blk', [(i, i ^ bit) for i in range(n_blk)])]
  transfers between devices with their start and end apart: 51 -> 47, of which waited for: 25 -> 24; matrix products, arithmetic and copies ran while one was open for 1% -> 1% of each run, Pallas kernels for 16% -> 16%
where the time goes in v7:
time: 186 us
  waiting for transfers between devices  97.3 us (52%)
  starting transfers between devices  41.3 us (22%)
  Pallas kernels  40 us (22%)
  local copies, waits for them, and re-layouts  4.25 us (2%)
    ppermute x21, waiting for transfers between devices, swap(): return lax.ppermute(v, 'tensor', [(i, i ^ bit) for i in range(n)])  60.9 us
    pallas_call x19, Pallas kernels, call(): pl.pallas_call(kernel, out_shape=outs, in_specs=[SMEM] * scalars + [VMEM]...  31.9 us
    ppermute x9, waiting for transfers between devices, flip_member(): return lax.ppermute(v, ('dp', 'blk'), perm)  24.9 us
    ppermute x21, starting transfers between devices, swap(): return lax.ppermute(v, 'tensor', [(i, i ^ bit) for i in range(n)])  20 us
    ppermute x9, starting transfers between devices, flip_member(): return lax.ppermute(v, ('dp', 'blk'), perm)  10.6 us
    ppermute x14, waiting for transfers between devices, flip(): return lax.ppermute(v, 'blk', [(i, i ^ bit) for i in range(n_blk)])  9.53 us
    ppermute x14, starting transfers between devices, flip(): return lax.ppermute(v, 'blk', [(i, i ^ bit) for i in range(n_blk)])  7.08 us
    pallas_call x1, Pallas kernels, body(): pl.pallas_call(functools.partial(attend_kernel, n_blk, (2, 3, 0, 1)), out...  5.61 us
  transfers between devices with their start and end apart: 47, of which 24 were waited for; matrix products, arithmetic and copies ran while one was open for 1% of the time, Pallas kernels for 16%

profile of v7, /device:TPU:0, one launch (start us, length us, event | category | flops | bytes accessed | tf_op | source)
XLA Modules:
  0.0 185.9 jit_solution(4924044111985865796)
XLA Ops:
  1.5 2.5 %front.1 = (bf16[512,384]{1,0:T(8,128)(2,1)S(1)}, bf16[240,768]{1,0:T(8,128)(2,1)S(1)}, bf16[48,768]{1,0:T(8,128)(2,1)S(1)}) custom-call(s32[5]{0:T(128)S(1)} %stack.23.at, bf16[512,768]{1,0:T(8,128)(2,1)} %bitcast.39, bf16[192,768]{1,0:T(8,128)(2,1)} %bitcast.45, bf16[192,768]{1,0:T(8,128)(2,1)} %bitcast.48, bf16[768,768]{1,0:T(8,128)(2,1)} %w_in.9, ...), custom_call_target="tpu_custom_call" | custom-call | tf_op jit(solution)/shard_map/front/pallas_call | solution.py:528
  4.0 3.0 %collective-permute-start = (bf16[512,384]{1,0:T(8,128)(2,1)S(1)}, bf16[512,384]{1,0:T(8,128)(2,1)S(1)}, u32[]{:S(2)}, u32[]{:S(2)}) collective-permute-start(bf16[512,384]{1,0:T(8,128)(2,1)S(1)} %get-tuple-element.150.refs_0_), channel_id=1, source_target_pairs={{0,8},{4,12},{8,0},{12,4},{1,9},{5,13},{9,1},{13,5},{2,10},{6,14},... | collective-permute-start | bytes 1179656 | tf_op jit(solution)/shard_map/ppermute | solution.py:468
  8.6 2.6 %collective-permute-start.3 = (bf16[48,768]{1,0:T(8,128)(2,1)S(1)}, bf16[48,768]{1,0:T(8,128)(2,1)S(1)}, u32[]{:S(2)}, u32[]{:S(2)}) collective-permute-start(bf16[48,768]{1,0:T(8,128)(2,1)S(1)} %get-tuple-element.153), channel_id=1, source_target_pairs={{0,2},{1,3},{2,0},{3,1},{4,6},{5,7},{6,4},{7,5},{8,10},{9,11},{10,... | collective-permute-start | bytes 221192 | tf_op jit(solution)/shard_map/ppermute | solution.py:465
  12.1 7.3 %collective-permute-done.1 = f32[768]{0:T(1024)S(1)} collective-permute-done((f32[768]{0:T(1024)S(1)}, f32[768]{0:T(1024)S(1)}, u32[]{:S(2)}, u32[]{:S(2)}) %collective-permute-start.1) | collective-permute-done | bytes 3104 | tf_op jit(solution)/shard_map/ppermute | solution.py:465
  19.4 2.9 %collective-permute-done.4 = bf16[48,768]{1,0:T(8,128)(2,1)S(1)} collective-permute-done((bf16[48,768]{1,0:T(8,128)(2,1)S(1)}, bf16[48,768]{1,0:T(8,128)(2,1)S(1)}, u32[]{:S(2)}, u32[]{:S(2)}) %collective-permute-start.4) | collective-permute-done | bytes 73760 | tf_op jit(solution)/shard_map/ppermute | solution.py:465
  26.7 5.6 %attend.1 = (bf16[384,128]{1,0:T(8,128)(2,1)S(1)}, bf16[384,128]{1,0:T(8,128)(2,1)S(1)}, bf16[768,512]{1,0:T(8,128)(2,1)}, bf16[768,512]{1,0:T(8,128)(2,1)}, bf16[768,128]{1,0:T(8,128)(2,1)}) custom-call(s32[5]{0:T(128)S(1)} %stack.23.at, s32[4]{0:T(128)S(1)} %copy-done.28, s32[4,4]{1,0:T(4,128)S(1)} %copy-done.26, bf16[512,384]{1,0:T(8,128)(2,1)S(1)} %query_rows.1.q, ...), custom_call_target="tpu_custom_call" | custom-call | flops 49999998976 | bytes 1 | tf_op jit(solution)/shard_map/attend/pallas_call | solution.py:564
  32.5 2.6 %collective-permute-start.9 = (bf16[384,128]{1,0:T(8,128)(2,1)S(1)}, bf16[384,128]{1,0:T(8,128)(2,1)S(1)}, u32[]{:S(2)}, u32[]{:S(2)}) collective-permute-start(bf16[384,128]{1,0:T(8,128)(2,1)S(1)} %get-tuple-element.159.refs_0_), channel_id=1, source_target_pairs={{0,2},{1,3},{2,0},{3,1},{4,6},{5,7},{6,4},{7,5},{8,10},{9,11},{10,... | collective-permute-start | bytes 294920 | tf_op jit(solution)/shard_map/ppermute | solution.py:465
  35.8 1.7 collective-permute-start.10
  39.5 3.7 %collective-permute-done.9.refs_2_ = bf16[384,128]{1,0:T(8,128)(2,1)S(1)} collective-permute-done((bf16[384,128]{1,0:T(8,128)(2,1)S(1)}, bf16[384,128]{1,0:T(8,128)(2,1)S(1)}, u32[]{:S(2)}, u32[]{:S(2)}) %collective-permute-start.9) | collective-permute-done | bytes 98336 | tf_op jit(solution)/shard_map/ppermute | solution.py:465
  45.8 1.7 collective-permute-done.15.refs_5_
  49.6 2.3 %ffn.2 = (bf16[128,768]{1,0:T(8,128)(2,1)S(1)}, f32[128,768]{1,0:T(8,128)S(1)}, f32[128,128]{1,0:T(8,128)S(1)}, bf16[128,768]{1,0:T(8,128)(2,1)S(1)}, bf16[128,7...) custom-call(s32[5]{0:T(128)S(1)} %stack.23.at, ...), custom_call_target="tpu_custom_call" | custom-call | flops 2400000000 | bytes 1 | tf_op jit(solution)/shard_map/ffn/pallas_call | solution.py:73
  52.7 2.3 %ffn.3 = (bf16[128,768]{1,0:T(8,128)(2,1)S(1)}, f32[128,768]{1,0:T(8,128)S(1)}, f32[128,128]{1,0:T(8,128)S(1)}, bf16[128,768]{1,0:T(8,128)(2,1)S(1)}, bf16[128,7...) custom-call(s32[5]{0:T(128)S(1)} %stack.23.at, bf16[512,768]{1,0:T(8,128)(2,1)S(1)} %bitcast.42, ...), custom_call_target="tpu_custom_call" | custom-call | flops 2400000000 | bytes 1 | tf_op jit(solution)/shard_map/ffn/pallas_call | solution.py:73
  55.0 2.3 %collective-permute-start.18 = (bf16[128,768]{1,0:T(8,128)(2,1)S(1)}, bf16[128,768]{1,0:T(8,128)(2,1)S(1)}, u32[]{:S(2)}, u32[]{:S(2)}) collective-permute-start(bf16[128,768]{1,0:T(8,128)(2,1)S(1)} %get-tuple-element.177.mine), channel_id=1, source_target_pairs={{0,2},{1,3},{2,0},{3,1},{4,6},{5,7},{6,4},{7,5},{8,10},{9,11},{10,... | collective-permute-start | bytes 589832 | tf_op jit(solution)/shard_map/ppermute | solution.py:465
  57.3 10.8 %collective-permute-done.17.theirs = bf16[128,768]{1,0:T(8,128)(2,1)S(1)} collective-permute-done((bf16[128,768]{1,0:T(8,128)(2,1)S(1)}, bf16[128,768]{1,0:T(8,128)(2,1)S(1)}, u32[]{:S(2)}, u32[]{:S(2)}) %collective-permute-start.17) | collective-permute-done | bytes 196640 | tf_op jit(solution)/shard_map/ppermute | solution.py:465
  68.1 2.7 %ffn_back.2 = (bf16[128,768]{1,0:T(8,128)(2,1)S(1)}, bf16[128,768]{1,0:T(8,128)(2,1)S(1)}, bf16[128,768]{1,0:T(8,128)(2,1)S(1)}, bf16[128,768]{1,0:T(8,128)(2,1)...) custom-call(s32[5]{0:T(128)S(1)} %stack.23.at, bf16[512,768]{1,0:T(8,128)(2,1)S(1)} %bitcast.52, ...), custom_call_target="tpu_custom_call" | custom-call | flops 2700000000 | bytes 1 | tf_op jit(solution)/shard_map/ffn_back/pallas_call | solution.py:73
  72.3 2.7 %ffn_back.3 = (bf16[128,768]{1,0:T(8,128)(2,1)S(1)}, bf16[128,768]{1,0:T(8,128)(2,1)S(1)}, bf16[128,768]{1,0:T(8,128)(2,1)S(1)}, bf16[128,768]{1,0:T(8,128)(2,1)...) custom-call(s32[5]{0:T(128)S(1)} %stack.23.at, bf16[512,768]{1,0:T(8,128)(2,1)S(1)} %bitcast.53, ...), custom_call_target="tpu_custom_call" | custom-call | flops 2700000000 | bytes 1 | tf_op jit(solution)/shard_map/ffn_back/pallas_call | solution.py:73
  76.6 2.2 %ffn_grads.1 = (bf16[4,2,192,768]{3,2,1,0:T(8,128)(2,1)S(1)}, bf16[4,2,192,768]{3,2,1,0:T(8,128)(2,1)S(1)}) custom-call(s32[5]{0:T(128)S(1)} %stack.23.at, bf16[128,768]{1,0:T(8,128)(2,1)S(1)} %get-tuple-element.195.refs_0_, bf16[128,768]{1,0:T(8,128)(2,1)S(1)} %get-tuple-element.196.refs_1_, bf16[128,768]{1,0:T(8,128)(2,1)S(1)} %get-tuple-element.197.refs_2_, ...), custom_call_target="tpu_custom_call" | custom-call | flops 49999998976 | bytes 1 | tf_op jit(solution)/shard_map/ffn_grads/pallas_call | solution.py:73
  78.9 7.4 %collective-permute-done.19.theirs = bf16[128,768]{1,0:T(8,128)(2,1)S(1)} collective-permute-done((bf16[128,768]{1,0:T(8,128)(2,1)S(1)}, bf16[128,768]{1,0:T(8,128)(2,1)S(1)}, u32[]{:S(2)}, u32[]{:S(2)}) %collective-permute-start.19) | collective-permute-done | bytes 196640 | tf_op jit(solution)/shard_map/ppermute | solution.py:465
  87.6 2.9 %collective-permute-done.20.theirs = bf16[128,768]{1,0:T(8,128)(2,1)S(1)} collective-permute-done((bf16[128,768]{1,0:T(8,128)(2,1)S(1)}, bf16[128,768]{1,0:T(8,128)(2,1)S(1)}, u32[]{:S(2)}, u32[]{:S(2)}) %collective-permute-start.20) | collective-permute-done | bytes 196640 | tf_op jit(solution)/shard_map/ppermute | solution.py:465
  92.2 2.7 %attend_back.2 = (bf16[256,192]{1,0:T(8,128)(2,1)S(1)}, bf16[2,2,384,128]{3,2,1,0:T(8,128)(2,1)S(1)}, bf16[2,2,384,128]{3,2,1,0:T(8,128)(2,1)S(1)}) custom-call(s32[5]{0:T(128)S(1)} %stack.23.at, bf16[192,128]{1,0:T(8,128)(2,1)S(1)} %get-tuple-element.183.first, bf16[192,128]{1,0:T(8,128)(2,1)S(1)} %get-tuple-element.188.second, ...), custom_call_target="tpu_custom_call" | custom-call | flops 49999998976 | bytes 1 | tf_op jit(solution)/shard_map/attend_back/pallas_call | solution.py:73
  96.0 2.7 %attend_back.3 = (bf16[256,192]{1,0:T(8,128)(2,1)S(1)}, bf16[2,2,384,128]{3,2,1,0:T(8,128)(2,1)S(1)}, bf16[2,2,384,128]{3,2,1,0:T(8,128)(2,1)S(1)}) custom-call(s32[5]{0:T(128)S(1)} %stack.23.at, bf16[192,128]{1,0:T(8,128)(2,1)S(1)} %collective-permute-done.21.first, bf16[192,128]{1,0:T(8,128)(2,1)S(1)} %collective-permute-done.22.second, ...), custom_call_target="tpu_custom_call" | custom-call | flops 49999998976 | bytes 1 | tf_op jit(solution)/shard_map/attend_back/pallas_call | solution.py:73
  104.2 2.8 %collective-permute-done.25.far = bf16[2,384,128]{2,1,0:T(8,128)(2,1)S(1)} collective-permute-done((bf16[2,384,128]{2,1,0:T(8,128)(2,1)S(1)}, bf16[2,384,128]{2,1,0:T(8,128)(2,1)S(1)}, u32[]{:S(2)}, u32[]{:S(2)}) %collective-permute-start.25) | collective-permute-done | bytes 196640 | tf_op jit(solution)/shard_map/ppermute | solution.py:468
  107.0 3.5 %collective-permute-done.27.far = bf16[2,384,128]{2,1,0:T(8,128)(2,1)S(1)} collective-permute-done((bf16[2,384,128]{2,1,0:T(8,128)(2,1)S(1)}, bf16[2,384,128]{2,1,0:T(8,128)(2,1)S(1)}, u32[]{:S(2)}, u32[]{:S(2)}) %collective-permute-start.27) | collective-permute-done | bytes 196640 | tf_op jit(solution)/shard_map/ppermute | solution.py:468
  117.3 6.3 %collective-permute-done.28 = bf16[256,768]{1,0:T(8,128)(2,1)S(1)} collective-permute-done((bf16[256,768]{1,0:T(8,128)(2,1)S(1)}, bf16[256,768]{1,0:T(8,128)(2,1)S(1)}, u32[]{:S(2)}, u32[]{:S(2)}) %collective-permute-start.28) | collective-permute-done | bytes 393248 | tf_op jit(solution)/shard_map/ppermute | solution.py:465
  125.2 2.9 %collective-permute-done.32 = bf16[2,192,768]{2,1,0:T(8,128)(2,1)S(1)} collective-permute-done((bf16[2,192,768]{2,1,0:T(8,128)(2,1)S(1)}, bf16[2,192,768]{2,1,0:T(8,128)(2,1)S(1)}, u32[]{:S(2)}, u32[]{:S(2)}) %collective-permute-start.32) | collective-permute-done | bytes 589856 | tf_op jit(solution)/shard_map/ppermute | solution.py:477
  128.5 1.9 %collective-permute-done.33 = bf16[2,192,768]{2,1,0:T(8,128)(2,1)S(1)} collective-permute-done((bf16[2,192,768]{2,1,0:T(8,128)(2,1)S(1)}, bf16[2,192,768]{2,1,0:T(8,128)(2,1)S(1)}, u32[]{:S(2)}, u32[]{:S(2)}) %collective-permute-start.33) | collective-permute-done | bytes 589856 | tf_op jit(solution)/shard_map/ppermute | solution.py:477
  130.9 10.1 %collective-permute-done.34 = bf16[2,192,768]{2,1,0:T(8,128)(2,1)S(1)} collective-permute-done((bf16[2,192,768]{2,1,0:T(8,128)(2,1)S(1)}, bf16[2,192,768]{2,1,0:T(8,128)(2,1)S(1)}, u32[]{:S(2)}, u32[]{:S(2)}) %collective-permute-start.34) | collective-permute-done | bytes 589856 | tf_op jit(solution)/shard_map/ppermute | solution.py:477
  145.6 1.7 collective-permute-done.31
  147.3 6.2 %collective-permute-done.35.near1 = bf16[192,768]{1,0:T(8,128)(2,1)S(1)} collective-permute-done((bf16[192,768]{1,0:T(8,128)(2,1)S(1)}, bf16[192,768]{1,0:T(8,128)(2,1)S(1)}, u32[]{:S(2)}, u32[]{:S(2)}) %collective-permute-start.35) | collective-permute-done | bytes 294944 | tf_op jit(solution)/shard_map/ppermute | solution.py:465
  157.4 10.1 %collective-permute-done.45.refs_1_ = bf16[256,768]{1,0:T(8,128)(2,1)S(1)} collective-permute-done((bf16[256,768]{1,0:T(8,128)(2,1)S(1)}, bf16[256,768]{1,0:T(8,128)(2,1)S(1)}, u32[]{:S(2)}, u32[]{:S(2)}) %collective-permute-start.45) | collective-permute-done | bytes 393248 | tf_op jit(solution)/shard_map/ppermute | solution.py:465
  168.7 8.8 %collective-permute-done.44.refs_3_ = bf16[304,768]{1,0:T(8,128)(2,1)S(1)} collective-permute-done((bf16[304,768]{1,0:T(8,128)(2,1)S(1)}, bf16[304,768]{1,0:T(8,128)(2,1)S(1)}, u32[]{:S(2)}, u32[]{:S(2)}) %collective-permute-start.44) | collective-permute-done | bytes 466976 | tf_op jit(solution)/shard_map/ppermute | solution.py:477
  182.1 3.7 %grads_out.1 = (f32[768,768]{1,0:T(8,128)}, f32[768,768]{1,0:T(8,128)}, f32[192,768]{1,0:T(8,128)}, f32[192,768]{1,0:T(8,128)}, f32[192,768]{1,0:T(8,128)}, /*in...) custom-call(s32[5]{0:T(128)S(1)} %stack.23.at, ...), custom_call_target="tpu_custom_call" | custom-call | flops 4000000000 | bytes 1 | tf_op jit(solution)/shard_map/grads_out/pallas_call | solution.py:73
  (186 shorter events, 51.4 us)
Async XLA Ops:
  4.0 18.3 %collective-permute-start = (bf16[512,384]{1,0:T(8,128)(2,1)S(1)}, bf16[512,384]{1,0:T(8,128)(2,1)S(1)}, u32[]{:S(2)}, u32[]{:S(2)}) collective-permute-start(bf16[512,384]{1,0:T(8,128)(2,1)S(1)} %get-tuple-element.150.refs_0_), channel_id=1, source_target_pairs={{0,8},{4,12},{8,0},{12,4},{1,9},{5,13},{9,1},{13,5},{2,10},{6,14},... | collective-permute-start | bytes 1179656 | tf_op jit(solution)/shard_map/ppermute | solution.py:468
  7.0 15.3 %collective-permute-start.2 = (bf16[240,768]{1,0:T(8,128)(2,1)S(1)}, bf16[240,768]{1,0:T(8,128)(2,1)S(1)}, u32[]{:S(2)}, u32[]{:S(2)}) collective-permute-start(bf16[240,768]{1,0:T(8,128)(2,1)S(1)} %get-tuple-element.152), channel_id=1, source_target_pairs={{0,1},{1,0},{2,3},{3,2},{4,5},{5,4},{6,7},{7,6},{8,9},{9,8},{10,11... | collective-permute-start | bytes 1105928 | tf_op jit(solution)/shard_map/ppermute | solution.py:465
  8.6 10.8 %collective-permute-start.3 = (bf16[48,768]{1,0:T(8,128)(2,1)S(1)}, bf16[48,768]{1,0:T(8,128)(2,1)S(1)}, u32[]{:S(2)}, u32[]{:S(2)}) collective-permute-start(bf16[48,768]{1,0:T(8,128)(2,1)S(1)} %get-tuple-element.153), channel_id=1, source_target_pairs={{0,2},{1,3},{2,0},{3,1},{4,6},{5,7},{6,4},{7,5},{8,10},{9,11},{10,... | collective-permute-start | bytes 221192 | tf_op jit(solution)/shard_map/ppermute | solution.py:465
  11.2 11.1 %collective-permute-start.4 = (bf16[48,768]{1,0:T(8,128)(2,1)S(1)}, bf16[48,768]{1,0:T(8,128)(2,1)S(1)}, u32[]{:S(2)}, u32[]{:S(2)}) collective-permute-start(bf16[48,768]{1,0:T(8,128)(2,1)S(1)} %get-tuple-element.153), channel_id=1, source_target_pairs={{0,3},{1,2},{2,1},{3,0},{4,7},{5,6},{6,5},{7,4},{8,11},{9,10},{10,... | collective-permute-start | bytes 221192 | tf_op jit(solution)/shard_map/ppermute | solution.py:465
  22.9 12.9 %collective-permute-start.12 = (bf16[192,768]{1,0:T(8,128)(2,1)S(1)}, bf16[192,768]{1,0:T(8,128)(2,1)S(1)}, u32[]{:S(2)}, u32[]{:S(2)}) collective-permute-start(bf16[192,768]{1,0:T(8,128)(2,1)S(1)} %slice.18), channel_id=1, source_target_pairs={{0,16},{4,20},{8,24},{12,28},{16,0},{20,4},{24,8},{28,12},{1,17},{... | collective-permute-start | bytes 884744 | tf_op jit(solution)/shard_map/ppermute | solution.py:555
  24.5 14.4 %collective-permute-start.13 = (bf16[192,768]{1,0:T(8,128)(2,1)S(1)}, bf16[192,768]{1,0:T(8,128)(2,1)}, u32[]{:S(2)}, u32[]{:S(2)}) collective-permute-start(bf16[192,768]{1,0:T(8,128)(2,1)S(1)} %slice.18), channel_id=1, source_target_pairs={{0,24},{4,28},{8,16},{12,20},{16,8},{20,12},{24,0},{28,4},{1,25},{... | collective-permute-start | bytes 884744 | tf_op jit(solution)/shard_map/ppermute | solution.py:555
  25.1 20.0 %collective-permute-start.11 = (bf16[336,768]{1,0:T(8,128)(2,1)S(1)}, bf16[336,768]{1,0:T(8,128)(2,1)S(1)}, u32[]{:S(2)}, u32[]{:S(2)}) collective-permute-start(bf16[336,768]{1,0:T(8,128)(2,1)S(1)} %constant_dynamic-update-slice_fusion.refs_0_), channel_id=1, source_target_pairs={{0,8},{4,12},{8,0},{12,4},{16,24},{20,28},{24,16},{28,20},{1,9},{5... | collective-permute-start | bytes 1548296 | tf_op jit(solution)/shard_map/ppermute | solution.py:555
  32.5 10.6 %collective-permute-start.9 = (bf16[384,128]{1,0:T(8,128)(2,1)S(1)}, bf16[384,128]{1,0:T(8,128)(2,1)S(1)}, u32[]{:S(2)}, u32[]{:S(2)}) collective-permute-start(bf16[384,128]{1,0:T(8,128)(2,1)S(1)} %get-tuple-element.159.refs_0_), channel_id=1, source_target_pairs={{0,2},{1,3},{2,0},{3,1},{4,6},{5,7},{6,4},{7,5},{8,10},{9,11},{10,... | collective-permute-start | bytes 294920 | tf_op jit(solution)/shard_map/ppermute | solution.py:465
  51.9 16.2 %collective-permute-start.17 = (bf16[128,768]{1,0:T(8,128)(2,1)S(1)}, bf16[128,768]{1,0:T(8,128)(2,1)S(1)}, u32[]{:S(2)}, u32[]{:S(2)}) collective-permute-start(bf16[128,768]{1,0:T(8,128)(2,1)S(1)} %get-tuple-element.172.mine), channel_id=1, source_target_pairs={{0,2},{1,3},{2,0},{3,1},{4,6},{5,7},{6,4},{7,5},{8,10},{9,11},{10,... | collective-permute-start | bytes 589832 | tf_op jit(solution)/shard_map/ppermute | solution.py:465
  55.0 17.2 %collective-permute-start.18 = (bf16[128,768]{1,0:T(8,128)(2,1)S(1)}, bf16[128,768]{1,0:T(8,128)(2,1)S(1)}, u32[]{:S(2)}, u32[]{:S(2)}) collective-permute-start(bf16[128,768]{1,0:T(8,128)(2,1)S(1)} %get-tuple-element.177.mine), channel_id=1, source_target_pairs={{0,2},{1,3},{2,0},{3,1},{4,6},{5,7},{6,4},{7,5},{8,10},{9,11},{10,... | collective-permute-start | bytes 589832 | tf_op jit(solution)/shard_map/ppermute | solution.py:465
  70.9 15.4 %collective-permute-start.19 = (bf16[128,768]{1,0:T(8,128)(2,1)S(1)}, bf16[128,768]{1,0:T(8,128)(2,1)S(1)}, u32[]{:S(2)}, u32[]{:S(2)}) collective-permute-start(bf16[128,768]{1,0:T(8,128)(2,1)S(1)} %get-tuple-element.179.mine), channel_id=1, source_target_pairs={{0,2},{1,3},{2,0},{3,1},{4,6},{5,7},{6,4},{7,5},{8,10},{9,11},{10,... | collective-permute-start | bytes 589832 | tf_op jit(solution)/shard_map/ppermute | solution.py:465
  75.0 15.5 %collective-permute-start.20 = (bf16[128,768]{1,0:T(8,128)(2,1)S(1)}, bf16[128,768]{1,0:T(8,128)(2,1)S(1)}, u32[]{:S(2)}, u32[]{:S(2)}) collective-permute-start(bf16[128,768]{1,0:T(8,128)(2,1)S(1)} %get-tuple-element.184.mine), channel_id=1, source_target_pairs={{0,2},{1,3},{2,0},{3,1},{4,6},{5,7},{6,4},{7,5},{8,10},{9,11},{10,... | collective-permute-start | bytes 589832 | tf_op jit(solution)/shard_map/ppermute | solution.py:465
  78.9 16.0 %collective-permute-start.23 = (bf16[4,2,192,768]{3,2,1,0:T(8,128)(2,1)S(1)}, bf16[4,2,192,768]{3,2,1,0:T(8,128)(2,1)S(1)}, u32[]{:S(2)}, u32[]{:S(2)}) collective-permute-start(bf16[4,2,192,768]{3,2,1,0:T(8,128)(2,1)S(1)} %get-tuple-element.208), channel_id=1, source_target_pairs={{0,4},{4,0},{8,12},{12,8},{1,5},{5,1},{9,13},{13,9},{2,6},{6,2},{1... | collective-permute-start | bytes 7077896 | tf_op jit(solution)/shard_map/ppermute | solution.py:468
  100.8 9.7 %collective-permute-start.27 = (bf16[2,384,128]{2,1,0:T(8,128)(2,1)S(1)}, bf16[2,384,128]{2,1,0:T(8,128)(2,1)S(1)}, u32[]{:S(2)}, u32[]{:S(2)}) collective-permute-start(bf16[2,384,128]{2,1,0:T(8,128)(2,1)S(1)} %fusion.6), channel_id=1, source_target_pairs={{0,8},{4,12},{8,0},{12,4},{1,9},{5,13},{9,1},{13,5},{2,10},{6,14},... | collective-permute-start | bytes 589832 | tf_op jit(solution)/shard_map/ppermute | solution.py:468
  102.2 13.5 %collective-permute-start.29 = (bf16[144,768]{1,0:T(8,128)(2,1)S(1)}, bf16[144,768]{1,0:T(8,128)(2,1)S(1)}, u32[]{:S(2)}, u32[]{:S(2)}) collective-permute-start(bf16[144,768]{1,0:T(8,128)(2,1)S(1)} %get-tuple-element.229.refs_0_), channel_id=1, source_target_pairs={{0,1},{1,0},{2,3},{3,2},{4,5},{5,4},{6,7},{7,6},{8,9},{9,8},{10,11... | collective-permute-start | bytes 663560 | tf_op jit(solution)/shard_map/ppermute | solution.py:465
  103.8 13.0 %collective-permute-start.30 = (bf16[144,768]{1,0:T(8,128)(2,1)S(1)}, bf16[144,768]{1,0:T(8,128)(2,1)S(1)}, u32[]{:S(2)}, u32[]{:S(2)}) collective-permute-start(bf16[144,768]{1,0:T(8,128)(2,1)S(1)} %get-tuple-element.230.refs_1_), channel_id=1, source_target_pairs={{0,1},{1,0},{2,3},{3,2},{4,5},{5,4},{6,7},{7,6},{8,9},{9,8},{10,11... | collective-permute-start | bytes 663560 | tf_op jit(solution)/shard_map/ppermute | solution.py:465
  111.1 12.5 %collective-permute-start.28 = (bf16[256,768]{1,0:T(8,128)(2,1)S(1)}, bf16[256,768]{1,0:T(8,128)(2,1)S(1)}, u32[]{:S(2)}, u32[]{:S(2)}) collective-permute-start(bf16[256,768]{1,0:T(8,128)(2,1)S(1)} %get-tuple-element.228), channel_id=1, source_target_pairs={{0,1},{1,0},{2,3},{3,2},{4,5},{5,4},{6,7},{7,6},{8,9},{9,8},{10,11... | collective-permute-start | bytes 1179656 | tf_op jit(solution)/shard_map/ppermute | solution.py:465
  112.7 15.4 %collective-permute-start.32 = (bf16[2,192,768]{2,1,0:T(8,128)(2,1)S(1)}, bf16[2,192,768]{2,1,0:T(8,128)(2,1)S(1)}, u32[]{:S(2)}, u32[]{:S(2)}) collective-permute-start(bf16[2,192,768]{2,1,0:T(8,128)(2,1)S(1)} %get-tuple-element.233), channel_id=1, source_target_pairs={{0,8},{4,12},{8,0},{12,4},{16,24},{20,28},{24,16},{28,20},{1,9},{5... | collective-permute-start | bytes 1769480 | tf_op jit(solution)/shard_map/ppermute | solution.py:477
  114.2 16.3 %collective-permute-start.33 = (bf16[2,192,768]{2,1,0:T(8,128)(2,1)S(1)}, bf16[2,192,768]{2,1,0:T(8,128)(2,1)S(1)}, u32[]{:S(2)}, u32[]{:S(2)}) collective-permute-start(bf16[2,192,768]{2,1,0:T(8,128)(2,1)S(1)} %get-tuple-element.234), channel_id=1, source_target_pairs={{0,16},{4,20},{8,24},{12,28},{16,0},{20,4},{24,8},{28,12},{1,17},{... | collective-permute-start | bytes 1769480 | tf_op jit(solution)/shard_map/ppermute | solution.py:477
  115.7 25.4 %collective-permute-start.34 = (bf16[2,192,768]{2,1,0:T(8,128)(2,1)S(1)}, bf16[2,192,768]{2,1,0:T(8,128)(2,1)S(1)}, u32[]{:S(2)}, u32[]{:S(2)}) collective-permute-start(bf16[2,192,768]{2,1,0:T(8,128)(2,1)S(1)} %get-tuple-element.235), channel_id=1, source_target_pairs={{0,24},{4,28},{8,16},{12,20},{16,8},{20,12},{24,0},{28,4},{1,25},{... | collective-permute-start | bytes 1769480 | tf_op jit(solution)/shard_map/ppermute | solution.py:477
  116.8 26.8 %collective-permute-start.40 = (bf16[128,768]{1,0:T(8,128)(2,1)S(1)}, bf16[128,768]{1,0:T(8,128)(2,1)S(1)}, u32[]{:S(2)}, u32[]{:S(2)}) collective-permute-start(bf16[128,768]{1,0:T(8,128)(2,1)S(1)} %get-tuple-element.173.refs_0_), channel_id=1, source_target_pairs={{0,1},{1,0},{2,3},{3,2},{4,5},{5,4},{6,7},{7,6},{8,9},{9,8},{10,11... | collective-permute-start | bytes 589832 | tf_op jit(solution)/shard_map/ppermute | solution.py:465
  125.0 16.8 %collective-permute-start.36 = (bf16[448,768]{1,0:T(8,128)(2,1)S(1)}, bf16[448,768]{1,0:T(8,128)(2,1)S(1)}, u32[]{:S(2)}, u32[]{:S(2)}) collective-permute-start(bf16[448,768]{1,0:T(8,128)(2,1)S(1)} %get-tuple-element.247), channel_id=1, source_target_pairs={{0,4},{4,0},{8,12},{12,8},{1,5},{5,1},{9,13},{13,9},{2,6},{6,2},{1... | collective-permute-start | bytes 2064392 | tf_op jit(solution)/shard_map/ppermute | solution.py:468
  128.1 16.9 %collective-permute-start.41 = (bf16[128,768]{1,0:T(8,128)(2,1)S(1)}, bf16[128,768]{1,0:T(8,128)(2,1)S(1)}, u32[]{:S(2)}, u32[]{:S(2)}) collective-permute-start(bf16[128,768]{1,0:T(8,128)(2,1)S(1)} %get-tuple-element.178.refs_1_), channel_id=1, source_target_pairs={{0,1},{1,0},{2,3},{3,2},{4,5},{5,4},{6,7},{7,6},{8,9},{9,8},{10,11... | collective-permute-start | bytes 589832 | tf_op jit(solution)/shard_map/ppermute | solution.py:465
  130.5 16.8 %collective-permute-start.31 = (bf16[256,768]{1,0:T(8,128)(2,1)S(1)}, bf16[256,768]{1,0:T(8,128)(2,1)S(1)}, u32[]{:S(2)}, u32[]{:S(2)}) collective-permute-start(bf16[256,768]{1,0:T(8,128)(2,1)S(1)} %add_convert_fusion.5), channel_id=1, source_target_pairs={{0,2},{1,3},{2,0},{3,1},{4,6},{5,7},{6,4},{7,5},{8,10},{9,11},{10,... | collective-permute-start | bytes 1179656 | tf_op jit(solution)/shard_map/ppermute | solution.py:465
  141.4 12.1 %collective-permute-start.35 = (bf16[192,768]{1,0:T(8,128)(2,1)S(1)}, bf16[192,768]{1,0:T(8,128)(2,1)S(1)}, u32[]{:S(2)}, u32[]{:S(2)}) collective-permute-start(bf16[192,768]{1,0:T(8,128)(2,1)S(1)} %slice_bitcast_fusion), channel_id=1, source_target_pairs={{0,1},{1,0},{2,3},{3,2},{4,5},{5,4},{6,7},{7,6},{8,9},{9,8},{10,11... | collective-permute-start | bytes 884744 | tf_op jit(solution)/shard_map/ppermute | solution.py:465
  142.0 11.5 %collective-permute-start.37 = (bf16[112,768]{1,0:T(8,128)(2,1)S(1)}, bf16[112,768]{1,0:T(8,128)(2,1)S(1)}, u32[]{:S(2)}, u32[]{:S(2)}) collective-permute-start(bf16[112,768]{1,0:T(8,128)(2,1)S(1)} %get-tuple-element.284), channel_id=1, source_target_pairs={{0,8},{4,12},{8,0},{12,4},{16,24},{20,28},{24,16},{28,20},{1,9},{5... | collective-permute-start | bytes 516104 | tf_op jit(solution)/shard_map/ppermute | solution.py:477
  143.5 9.9 %collective-permute-start.38 = (bf16[112,768]{1,0:T(8,128)(2,1)S(1)}, bf16[112,768]{1,0:T(8,128)(2,1)S(1)}, u32[]{:S(2)}, u32[]{:S(2)}) collective-permute-start(bf16[112,768]{1,0:T(8,128)(2,1)S(1)} %get-tuple-element.283), channel_id=1, source_target_pairs={{0,16},{4,20},{8,24},{12,28},{16,0},{20,4},{24,8},{28,12},{1,17},{... | collective-permute-start | bytes 516104 | tf_op jit(solution)/shard_map/ppermute | solution.py:477
  145.0 8.5 %collective-permute-start.39 = (bf16[112,768]{1,0:T(8,128)(2,1)S(1)}, bf16[112,768]{1,0:T(8,128)(2,1)S(1)}, u32[]{:S(2)}, u32[]{:S(2)}) collective-permute-start(bf16[112,768]{1,0:T(8,128)(2,1)S(1)} %get-tuple-element.282), channel_id=1, source_target_pairs={{0,24},{4,28},{8,16},{12,20},{16,8},{20,12},{24,0},{28,4},{1,25},{... | collective-permute-start | bytes 516104 | tf_op jit(solution)/shard_map/ppermute | solution.py:477
  153.6 13.9 %collective-permute-start.42 = (bf16[304,768]{1,0:T(8,128)(2,1)S(1)}, bf16[304,768]{1,0:T(8,128)(2,1)S(1)}, u32[]{:S(2)}, u32[]{:S(2)}) collective-permute-start(bf16[304,768]{1,0:T(8,128)(2,1)S(1)} %grad_share.1.refs_0_), channel_id=1, source_target_pairs={{0,8},{4,12},{8,0},{12,4},{16,24},{20,28},{24,16},{28,20},{1,9},{5... | collective-permute-start | bytes 1400840 | tf_op jit(solution)/shard_map/ppermute | solution.py:477
  155.1 13.6 %collective-permute-start.43 = (bf16[304,768]{1,0:T(8,128)(2,1)S(1)}, bf16[304,768]{1,0:T(8,128)(2,1)S(1)}, u32[]{:S(2)}, u32[]{:S(2)}) collective-permute-start(bf16[304,768]{1,0:T(8,128)(2,1)S(1)} %grad_share.1.refs_0_), channel_id=1, source_target_pairs={{0,16},{4,20},{8,24},{12,28},{16,0},{20,4},{24,8},{28,12},{1,17},{... | collective-permute-start | bytes 1400840 | tf_op jit(solution)/shard_map/ppermute | solution.py:477
  156.5 20.9 %collective-permute-start.44 = (bf16[304,768]{1,0:T(8,128)(2,1)S(1)}, bf16[304,768]{1,0:T(8,128)(2,1)S(1)}, u32[]{:S(2)}, u32[]{:S(2)}) collective-permute-start(bf16[304,768]{1,0:T(8,128)(2,1)S(1)} %grad_share.1.refs_0_), channel_id=1, source_target_pairs={{0,24},{4,28},{8,16},{12,20},{16,8},{20,12},{24,0},{28,4},{1,25},{... | collective-permute-start | bytes 1400840 | tf_op jit(solution)/shard_map/ppermute | solution.py:477
  157.3 10.2 %collective-permute-start.45 = (bf16[256,768]{1,0:T(8,128)(2,1)S(1)}, bf16[256,768]{1,0:T(8,128)(2,1)S(1)}, u32[]{:S(2)}, u32[]{:S(2)}) collective-permute-start(bf16[256,768]{1,0:T(8,128)(2,1)S(1)} %fusion.refs_0_), channel_id=1, source_target_pairs={{0,1},{1,0},{2,3},{3,2},{4,5},{5,4},{6,7},{7,6},{8,9},{9,8},{10,11... | collective-permute-start | bytes 1179656 | tf_op jit(solution)/shard_map/ppermute | solution.py:465
  (56 other events, 447.1 us)

commit v8 on v7

--- a/solution.py
+++ b/solution.py
@@ -403,12 +403,6 @@
     send[half:, :] = tail
 
 
-def gather_kernel(m, at, *refs):
-    out = refs[m]
-    for s in range(m):
-        out[at[3] ^ s] = refs[s][...]
-
-
 def share_kernel(total1, near1, *refs):
     parts, share = refs[:-1], refs[-1]
     rows = near1.shape[0]
@@ -419,18 +413,22 @@
     share[rows:, :] = total.astype(bf16)
 
 
-def final_kernel(m, at, mine, other, g_in, g_outer, g_out, g_q, g_k, g_v, *vectors):
+def final_kernel(m, at, *refs):
+    mine, other = refs[:m], refs[m : 2 * m]
+    g_in, g_outer, g_out, g_q, g_k, g_v, *vectors, packed = refs[2 * m :]
     first = at[1] == 0
     rows = g_in.shape[0] // m
-    for i in range(m):
-        a, b = mine[i, :rows, :], other[i, :rows, :]
-        g_in[i * rows : (i + 1) * rows, :] = pick(first, a, b).astype(f32)
-        g_outer[i * rows : (i + 1) * rows, :] = pick(first, b, a).astype(f32)
+    for s in range(m):
+        i = at[3] ^ s
+        a, b = mine[s], other[s]
+        here = pl.ds(pl.multiple_of(i * rows, rows), rows)
+        g_in[here, :] = pick(first, a[:rows, :], b[:rows, :]).astype(f32)
+        g_outer[here, :] = pick(first, b[:rows, :], a[:rows, :]).astype(f32)
+        packed[0, i] = pick(first, a[rows:, :], b[rows:, :])
+        packed[1, i] = pick(first, b[rows:, :], a[rows:, :])
     width = g_q.shape[0]
-    a = join(mine[i, rows:, :] for i in range(m))
-    b = join(other[i, rows:, :] for i in range(m))
-    one = pick(first, a, b).astype(f32)
-    two = pick(first, b, a).astype(f32)
+    one = join(packed[0, i] for i in range(m)).astype(f32)
+    two = join(packed[1, i] for i in range(m)).astype(f32)
     g_out[...] = one[:width]
     g_q[...] = one[width : 2 * width]
     tail = one[2 * width : 2 * width + 16]
@@ -489,16 +487,6 @@
         for part in got:
             total = total + part.astype(f32)
         return total.astype(bf16)
-
-    def gather_grads(every, at, name):
-        rows, width = every[0].shape
-        return call(
-            functools.partial(gather_kernel, m),
-            near((m, rows, width), bf16),
-            name,
-            (at, *every),
-            scalars=1,
-        )
 
     def body(
         tokens, bucket_ids, seq_lengths, w_query, b_query, w_key, w_value, b_value, w_out, b_out,
@@ -712,6 +700,7 @@
 
         rows2 = 2 * local + 16
         rows2 += -rows2 % (16 * m)
+        hp_late, _ = fence((hp_late, pair))
         keep2, send2 = call(
             functools.partial(attend_grad_kernel, m),
             (chunk(rows2, bf16), chunk(rows2, bf16)),
@@ -742,7 +731,7 @@
             us=0.5,
         )
         shares_in = [flip_member(share, k) for k in range(1, m)]
-        shares_in, d_far = fence((shares_in, swap(d_tok, 1)))
+        shares_in[0], d_far = fence((shares_in[0], swap(d_tok, 1)))
         d_toks = [d_tok, d_far]
         assemble = lambda parts, name: call(
             rows_kernel,
@@ -754,8 +743,9 @@
         )
         output = assemble(outs, "output_rows")
         d_tokens = assemble(d_toks, "input_grad_rows")
-        mine = gather_grads([share] + shares_in, at, "gather_grads")
-        other, _, _ = fence((flip(mine, 1), output, d_tokens))
+        mine = [share] + shares_in
+        held, _, _ = fence((shares_in[0], output, d_tokens))
+        others = [flip(v, 1) for v in [share, held] + shares_in[1:]]
         vector = shape((width,), f32)
         short = shape((local,), f32)
         square = shape((width, units), f32)
@@ -767,10 +757,11 @@
             functools.partial(final_kernel, m),
             (square,) * 2 + (wide,) * 4 + (vector,) * 7 + (short,) * 2,
             "grads_out",
-            (at, mine, other),
+            (at, *mine, *others),
             us=4.0,
             vmem=24,
             scalars=1,
+            scratch=[pltpu.VMEM((2, m, rows2 // m, width), bf16)],
         )
         return (
             output, d_tokens, g_q.T, g_b_query, g_k.T, g_v.T, g_b_value, g_w_out, g_b_out, g_gain1,

time: 186 us -> 182 us (0.978)
  waiting for transfers between devices: 97.3 us -> 90.8 us
  starting transfers between devices: 41.3 us -> 43.9 us
    ppermute x21, waiting for transfers between devices: 60.9 us -> 51 us  [swap(): return lax.ppermute(v, 'tensor', [(i, i ^ bit) for i in range(n)])]
    ppermute x21, starting transfers between devices: 20 us -> 22.8 us  [swap(): return lax.ppermute(v, 'tensor', [(i, i ^ bit) for i in range(n)])]
    ppermute x9, waiting for transfers between devices: 24.9 us -> 27.3 us  [flip_member(): return lax.ppermute(v, ('dp', 'blk'), perm)]
    ppermute x14 -> x17, waiting for transfers between devices: 9.53 us -> 10.5 us  [flip(): return lax.ppermute(v, 'blk', [(i, i ^ bit) for i in range(n_blk)])]
    pallas_call x19 -> x18, Pallas kernels: 31.9 us -> 31.3 us  [call(): pl.pallas_call(kernel, out_shape=outs, in_specs=[SMEM] * scalars + [VMEM]...]
    ppermute x14 -> x17, starting transfers between devices: 7.08 us -> 7.01 us  [flip(): return lax.ppermute(v, 'blk', [(i, i ^ bit) for i in range(n_blk)])]
  transfers between devices with their start and end apart: 47 -> 50, of which waited for: 24 -> 26; matrix products, arithmetic and copies ran while one was open for 1% -> 1% of each run, Pallas kernels for 16% -> 16%
where the time goes in v8:
time: 182 us
  waiting for transfers between devices  90.8 us (50%)
  starting transfers between devices  43.9 us (24%)
  Pallas kernels  39.4 us (22%)
  local copies, waits for them, and re-layouts  4.26 us (2%)
    ppermute x21, waiting for transfers between devices, swap(): return lax.ppermute(v, 'tensor', [(i, i ^ bit) for i in range(n)])  51 us
    pallas_call x18, Pallas kernels, call(): pl.pallas_call(kernel, out_shape=outs, in_specs=[SMEM] * scalars + [VMEM]...  31.3 us
    ppermute x9, waiting for transfers between devices, flip_member(): return lax.ppermute(v, ('dp', 'blk'), perm)  27.3 us
    ppermute x21, starting transfers between devices, swap(): return lax.ppermute(v, 'tensor', [(i, i ^ bit) for i in range(n)])  22.8 us
    ppermute x9, starting transfers between devices, flip_member(): return lax.ppermute(v, ('dp', 'blk'), perm)  10.5 us
    ppermute x17, waiting for transfers between devices, flip(): return lax.ppermute(v, 'blk', [(i, i ^ bit) for i in range(n_blk)])  10.5 us
    ppermute x17, starting transfers between devices, flip(): return lax.ppermute(v, 'blk', [(i, i ^ bit) for i in range(n_blk)])  7.01 us
    pallas_call x1, Pallas kernels, body(): pl.pallas_call(functools.partial(attend_kernel, n_blk, (2, 3, 0, 1)), out...  5.61 us
  transfers between devices with their start and end apart: 50, of which 26 were waited for; matrix products, arithmetic and copies ran while one was open for 1% of the time, Pallas kernels for 16%

profile of v8, /device:TPU:0, one launch (start us, length us, event | category | flops | bytes accessed | tf_op | source)
XLA Modules:
  0.0 181.5 jit_solution(401167572373442909)
XLA Ops:
  1.5 2.5 %front.1 = (bf16[512,384]{1,0:T(8,128)(2,1)S(1)}, bf16[240,768]{1,0:T(8,128)(2,1)S(1)}, bf16[48,768]{1,0:T(8,128)(2,1)S(1)}) custom-call(s32[5]{0:T(128)S(1)} %stack.23.at, bf16[512,768]{1,0:T(8,128)(2,1)} %bitcast.39, bf16[192,768]{1,0:T(8,128)(2,1)} %bitcast.45, bf16[192,768]{1,0:T(8,128)(2,1)} %bitcast.48, bf16[768,768]{1,0:T(8,128)(2,1)} %w_in.9, ...), custom_call_target="tpu_custom_call" | custom-call | tf_op jit(solution)/shard_map/front/pallas_call | solution.py:516
  4.0 3.0 %collective-permute-start = (bf16[512,384]{1,0:T(8,128)(2,1)S(1)}, bf16[512,384]{1,0:T(8,128)(2,1)S(1)}, u32[]{:S(2)}, u32[]{:S(2)}) collective-permute-start(bf16[512,384]{1,0:T(8,128)(2,1)S(1)} %get-tuple-element.149.refs_0_), channel_id=1, source_target_pairs={{0,8},{4,12},{8,0},{12,4},{1,9},{5,13},{9,1},{13,5},{2,10},{6,14},... | collective-permute-start | bytes 1179656 | tf_op jit(solution)/shard_map/ppermute | solution.py:466
  8.6 2.6 %collective-permute-start.3 = (bf16[48,768]{1,0:T(8,128)(2,1)S(1)}, bf16[48,768]{1,0:T(8,128)(2,1)S(1)}, u32[]{:S(2)}, u32[]{:S(2)}) collective-permute-start(bf16[48,768]{1,0:T(8,128)(2,1)S(1)} %get-tuple-element.152), channel_id=1, source_target_pairs={{0,2},{1,3},{2,0},{3,1},{4,6},{5,7},{6,4},{7,5},{8,10},{9,11},{10,... | collective-permute-start | bytes 221192 | tf_op jit(solution)/shard_map/ppermute | solution.py:463
  12.1 7.3 %collective-permute-done.1 = f32[768]{0:T(1024)S(1)} collective-permute-done((f32[768]{0:T(1024)S(1)}, f32[768]{0:T(1024)S(1)}, u32[]{:S(2)}, u32[]{:S(2)}) %collective-permute-start.1) | collective-permute-done | bytes 3104 | tf_op jit(solution)/shard_map/ppermute | solution.py:463
  19.4 2.9 %collective-permute-done.4 = bf16[48,768]{1,0:T(8,128)(2,1)S(1)} collective-permute-done((bf16[48,768]{1,0:T(8,128)(2,1)S(1)}, bf16[48,768]{1,0:T(8,128)(2,1)S(1)}, u32[]{:S(2)}, u32[]{:S(2)}) %collective-permute-start.4) | collective-permute-done | bytes 73760 | tf_op jit(solution)/shard_map/ppermute | solution.py:463
  26.7 5.6 %attend.1 = (bf16[384,128]{1,0:T(8,128)(2,1)S(1)}, bf16[384,128]{1,0:T(8,128)(2,1)S(1)}, bf16[768,512]{1,0:T(8,128)(2,1)}, bf16[768,512]{1,0:T(8,128)(2,1)}, bf16[768,128]{1,0:T(8,128)(2,1)}) custom-call(s32[5]{0:T(128)S(1)} %stack.23.at, s32[4]{0:T(128)S(1)} %copy-done.28, s32[4,4]{1,0:T(4,128)S(1)} %copy-done.26, bf16[512,384]{1,0:T(8,128)(2,1)S(1)} %query_rows.1.q, ...), custom_call_target="tpu_custom_call" | custom-call | flops 49999998976 | bytes 1 | tf_op jit(solution)/shard_map/attend/pallas_call | solution.py:552
  32.5 2.6 %collective-permute-start.9 = (bf16[384,128]{1,0:T(8,128)(2,1)S(1)}, bf16[384,128]{1,0:T(8,128)(2,1)S(1)}, u32[]{:S(2)}, u32[]{:S(2)}) collective-permute-start(bf16[384,128]{1,0:T(8,128)(2,1)S(1)} %get-tuple-element.158.refs_0_), channel_id=1, source_target_pairs={{0,2},{1,3},{2,0},{3,1},{4,6},{5,7},{6,4},{7,5},{8,10},{9,11},{10,... | collective-permute-start | bytes 294920 | tf_op jit(solution)/shard_map/ppermute | solution.py:463
  39.5 3.6 %collective-permute-done.9.refs_2_ = bf16[384,128]{1,0:T(8,128)(2,1)S(1)} collective-permute-done((bf16[384,128]{1,0:T(8,128)(2,1)S(1)}, bf16[384,128]{1,0:T(8,128)(2,1)S(1)}, u32[]{:S(2)}, u32[]{:S(2)}) %collective-permute-start.9) | collective-permute-done | bytes 98336 | tf_op jit(solution)/shard_map/ppermute | solution.py:463
  49.6 2.4 %ffn.2 = (bf16[128,768]{1,0:T(8,128)(2,1)S(1)}, f32[128,768]{1,0:T(8,128)S(1)}, f32[128,128]{1,0:T(8,128)S(1)}, bf16[128,768]{1,0:T(8,128)(2,1)S(1)}, bf16[128,7...) custom-call(s32[5]{0:T(128)S(1)} %stack.23.at, ...), custom_call_target="tpu_custom_call" | custom-call | flops 2400000000 | bytes 1 | tf_op jit(solution)/shard_map/ffn/pallas_call | solution.py:73
  52.8 2.3 %ffn.3 = (bf16[128,768]{1,0:T(8,128)(2,1)S(1)}, f32[128,768]{1,0:T(8,128)S(1)}, f32[128,128]{1,0:T(8,128)S(1)}, bf16[128,768]{1,0:T(8,128)(2,1)S(1)}, bf16[128,7...) custom-call(s32[5]{0:T(128)S(1)} %stack.23.at, bf16[512,768]{1,0:T(8,128)(2,1)S(1)} %bitcast.42, ...), custom_call_target="tpu_custom_call" | custom-call | flops 2400000000 | bytes 1 | tf_op jit(solution)/shard_map/ffn/pallas_call | solution.py:73
  55.1 2.3 %collective-permute-start.18 = (bf16[128,768]{1,0:T(8,128)(2,1)S(1)}, bf16[128,768]{1,0:T(8,128)(2,1)S(1)}, u32[]{:S(2)}, u32[]{:S(2)}) collective-permute-start(bf16[128,768]{1,0:T(8,128)(2,1)S(1)} %get-tuple-element.176.mine), channel_id=1, source_target_pairs={{0,2},{1,3},{2,0},{3,1},{4,6},{5,7},{6,4},{7,5},{8,10},{9,11},{10,... | collective-permute-start | bytes 589832 | tf_op jit(solution)/shard_map/ppermute | solution.py:463
  57.4 10.8 %collective-permute-done.17.theirs = bf16[128,768]{1,0:T(8,128)(2,1)S(1)} collective-permute-done((bf16[128,768]{1,0:T(8,128)(2,1)S(1)}, bf16[128,768]{1,0:T(8,128)(2,1)S(1)}, u32[]{:S(2)}, u32[]{:S(2)}) %collective-permute-start.17) | collective-permute-done | bytes 196640 | tf_op jit(solution)/shard_map/ppermute | solution.py:463
  68.2 2.7 %ffn_back.2 = (bf16[128,768]{1,0:T(8,128)(2,1)S(1)}, bf16[128,768]{1,0:T(8,128)(2,1)S(1)}, bf16[128,768]{1,0:T(8,128)(2,1)S(1)}, bf16[128,768]{1,0:T(8,128)(2,1)...) custom-call(s32[5]{0:T(128)S(1)} %stack.23.at, bf16[512,768]{1,0:T(8,128)(2,1)S(1)} %bitcast.52, ...), custom_call_target="tpu_custom_call" | custom-call | flops 2700000000 | bytes 1 | tf_op jit(solution)/shard_map/ffn_back/pallas_call | solution.py:73
  72.3 2.7 %ffn_back.3 = (bf16[128,768]{1,0:T(8,128)(2,1)S(1)}, bf16[128,768]{1,0:T(8,128)(2,1)S(1)}, bf16[128,768]{1,0:T(8,128)(2,1)S(1)}, bf16[128,768]{1,0:T(8,128)(2,1)...) custom-call(s32[5]{0:T(128)S(1)} %stack.23.at, bf16[512,768]{1,0:T(8,128)(2,1)S(1)} %bitcast.53, ...), custom_call_target="tpu_custom_call" | custom-call | flops 2700000000 | bytes 1 | tf_op jit(solution)/shard_map/ffn_back/pallas_call | solution.py:73
  76.7 2.2 %ffn_grads.1 = (bf16[4,2,192,768]{3,2,1,0:T(8,128)(2,1)S(1)}, bf16[4,2,192,768]{3,2,1,0:T(8,128)(2,1)S(1)}) custom-call(s32[5]{0:T(128)S(1)} %stack.23.at, bf16[128,768]{1,0:T(8,128)(2,1)S(1)} %get-tuple-element.194.refs_0_, bf16[128,768]{1,0:T(8,128)(2,1)S(1)} %get-tuple-element.195.refs_1_, bf16[128,768]{1,0:T(8,128)(2,1)S(1)} %get-tuple-element.196.refs_2_, ...), custom_call_target="tpu_custom_call" | custom-call | flops 49999998976 | bytes 1 | tf_op jit(solution)/shard_map/ffn_grads/pallas_call | solution.py:73
  79.0 7.4 %collective-permute-done.19.theirs = bf16[128,768]{1,0:T(8,128)(2,1)S(1)} collective-permute-done((bf16[128,768]{1,0:T(8,128)(2,1)S(1)}, bf16[128,768]{1,0:T(8,128)(2,1)S(1)}, u32[]{:S(2)}, u32[]{:S(2)}) %collective-permute-start.19) | collective-permute-done | bytes 196640 | tf_op jit(solution)/shard_map/ppermute | solution.py:463
  87.6 2.9 %collective-permute-done.20.theirs = bf16[128,768]{1,0:T(8,128)(2,1)S(1)} collective-permute-done((bf16[128,768]{1,0:T(8,128)(2,1)S(1)}, bf16[128,768]{1,0:T(8,128)(2,1)S(1)}, u32[]{:S(2)}, u32[]{:S(2)}) %collective-permute-start.20) | collective-permute-done | bytes 196640 | tf_op jit(solution)/shard_map/ppermute | solution.py:463
  92.2 2.7 %attend_back.2 = (bf16[256,192]{1,0:T(8,128)(2,1)S(1)}, bf16[2,2,384,128]{3,2,1,0:T(8,128)(2,1)S(1)}, bf16[2,2,384,128]{3,2,1,0:T(8,128)(2,1)S(1)}) custom-call(s32[5]{0:T(128)S(1)} %stack.23.at, bf16[192,128]{1,0:T(8,128)(2,1)S(1)} %get-tuple-element.182.first, bf16[192,128]{1,0:T(8,128)(2,1)S(1)} %get-tuple-element.187.second, ...), custom_call_target="tpu_custom_call" | custom-call | flops 49999998976 | bytes 1 | tf_op jit(solution)/shard_map/attend_back/pallas_call | solution.py:73
  96.1 2.7 %attend_back.3 = (bf16[256,192]{1,0:T(8,128)(2,1)S(1)}, bf16[2,2,384,128]{3,2,1,0:T(8,128)(2,1)S(1)}, bf16[2,2,384,128]{3,2,1,0:T(8,128)(2,1)S(1)}) custom-call(s32[5]{0:T(128)S(1)} %stack.23.at, bf16[192,128]{1,0:T(8,128)(2,1)S(1)} %collective-permute-done.21.first, bf16[192,128]{1,0:T(8,128)(2,1)S(1)} %collective-permute-done.22.second, ...), custom_call_target="tpu_custom_call" | custom-call | flops 49999998976 | bytes 1 | tf_op jit(solution)/shard_map/attend_back/pallas_call | solution.py:73
  104.2 2.8 %collective-permute-done.25.far = bf16[2,384,128]{2,1,0:T(8,128)(2,1)S(1)} collective-permute-done((bf16[2,384,128]{2,1,0:T(8,128)(2,1)S(1)}, bf16[2,384,128]{2,1,0:T(8,128)(2,1)S(1)}, u32[]{:S(2)}, u32[]{:S(2)}) %collective-permute-start.25) | collective-permute-done | bytes 196640 | tf_op jit(solution)/shard_map/ppermute | solution.py:466
  107.0 3.5 %collective-permute-done.27.far = bf16[2,384,128]{2,1,0:T(8,128)(2,1)S(1)} collective-permute-done((bf16[2,384,128]{2,1,0:T(8,128)(2,1)S(1)}, bf16[2,384,128]{2,1,0:T(8,128)(2,1)S(1)}, u32[]{:S(2)}, u32[]{:S(2)}) %collective-permute-start.27) | collective-permute-done | bytes 196640 | tf_op jit(solution)/shard_map/ppermute | solution.py:466
  116.8 5.9 %collective-permute-done.28 = bf16[256,768]{1,0:T(8,128)(2,1)S(1)} collective-permute-done((bf16[256,768]{1,0:T(8,128)(2,1)S(1)}, bf16[256,768]{1,0:T(8,128)(2,1)S(1)}, u32[]{:S(2)}, u32[]{:S(2)}) %collective-permute-start.28) | collective-permute-done | bytes 393248 | tf_op jit(solution)/shard_map/ppermute | solution.py:463
  125.8 2.3 %collective-permute-done.32 = bf16[2,192,768]{2,1,0:T(8,128)(2,1)S(1)} collective-permute-done((bf16[2,192,768]{2,1,0:T(8,128)(2,1)S(1)}, bf16[2,192,768]{2,1,0:T(8,128)(2,1)S(1)}, u32[]{:S(2)}, u32[]{:S(2)}) %collective-permute-start.32) | collective-permute-done | bytes 589856 | tf_op jit(solution)/shard_map/ppermute | solution.py:475
  128.6 1.9 %collective-permute-done.33 = bf16[2,192,768]{2,1,0:T(8,128)(2,1)S(1)} collective-permute-done((bf16[2,192,768]{2,1,0:T(8,128)(2,1)S(1)}, bf16[2,192,768]{2,1,0:T(8,128)(2,1)S(1)}, u32[]{:S(2)}, u32[]{:S(2)}) %collective-permute-start.33) | collective-permute-done | bytes 589856 | tf_op jit(solution)/shard_map/ppermute | solution.py:475
  130.9 10.1 %collective-permute-done.34 = bf16[2,192,768]{2,1,0:T(8,128)(2,1)S(1)} collective-permute-done((bf16[2,192,768]{2,1,0:T(8,128)(2,1)S(1)}, bf16[2,192,768]{2,1,0:T(8,128)(2,1)S(1)}, u32[]{:S(2)}, u32[]{:S(2)}) %collective-permute-start.34) | collective-permute-done | bytes 589856 | tf_op jit(solution)/shard_map/ppermute | solution.py:475
  145.6 2.2 %collective-permute-done.31 = bf16[256,768]{1,0:T(8,128)(2,1)S(1)} collective-permute-done((bf16[256,768]{1,0:T(8,128)(2,1)S(1)}, bf16[256,768]{1,0:T(8,128)(2,1)S(1)}, u32[]{:S(2)}, u32[]{:S(2)}) %collective-permute-start.31) | collective-permute-done | bytes 393248 | tf_op jit(solution)/shard_map/ppermute | solution.py:463
  147.7 3.1 %collective-permute-done.35.near1 = bf16[192,768]{1,0:T(8,128)(2,1)S(1)} collective-permute-done((bf16[192,768]{1,0:T(8,128)(2,1)S(1)}, bf16[192,768]{1,0:T(8,128)(2,1)S(1)}, u32[]{:S(2)}, u32[]{:S(2)}) %collective-permute-start.35) | collective-permute-done | bytes 294944 | tf_op jit(solution)/shard_map/ppermute | solution.py:463
  158.4 3.4 %collective-permute-done.43.refs_1_ = bf16[256,768]{1,0:T(8,128)(2,1)S(1)} collective-permute-done((bf16[256,768]{1,0:T(8,128)(2,1)S(1)}, bf16[256,768]{1,0:T(8,128)(2,1)S(1)}, u32[]{:S(2)}, u32[]{:S(2)}) %collective-permute-start.43) | collective-permute-done | bytes 393248 | tf_op jit(solution)/shard_map/ppermute | solution.py:463
  163.6 4.6 %collective-permute-done.44.refs_2_ = bf16[304,768]{1,0:T(8,128)(2,1)S(1)} collective-permute-done((bf16[304,768]{1,0:T(8,128)(2,1)S(1)}, bf16[304,768]{1,0:T(8,128)(2,1)S(1)}, u32[]{:S(2)}, u32[]{:S(2)}) %collective-permute-start.44) | collective-permute-done | bytes 466976 | tf_op jit(solution)/shard_map/ppermute | solution.py:475
  168.2 7.5 %collective-permute-done.45.refs_3_ = bf16[304,768]{1,0:T(8,128)(2,1)S(1)} collective-permute-done((bf16[304,768]{1,0:T(8,128)(2,1)S(1)}, bf16[304,768]{1,0:T(8,128)(2,1)S(1)}, u32[]{:S(2)}, u32[]{:S(2)}) %collective-permute-start.45) | collective-permute-done | bytes 466976 | tf_op jit(solution)/shard_map/ppermute | solution.py:475
  175.7 1.8 collective-permute-done.49.refs_7_
  177.5 3.8 %grads_out.1 = (f32[768,768]{1,0:T(8,128)}, f32[768,768]{1,0:T(8,128)}, f32[192,768]{1,0:T(8,128)}, f32[192,768]{1,0:T(8,128)}, f32[192,768]{1,0:T(8,128)}, /*in...) custom-call(s32[5]{0:T(128)S(1)} %stack.23.at, ...), custom_call_target="tpu_custom_call" | custom-call | flops 4000000000 | bytes 1 | tf_op jit(solution)/shard_map/grads_out/pallas_call | solution.py:73
  (191 shorter events, 55.7 us)
Async XLA Ops:
  4.0 18.3 %collective-permute-start = (bf16[512,384]{1,0:T(8,128)(2,1)S(1)}, bf16[512,384]{1,0:T(8,128)(2,1)S(1)}, u32[]{:S(2)}, u32[]{:S(2)}) collective-permute-start(bf16[512,384]{1,0:T(8,128)(2,1)S(1)} %get-tuple-element.149.refs_0_), channel_id=1, source_target_pairs={{0,8},{4,12},{8,0},{12,4},{1,9},{5,13},{9,1},{13,5},{2,10},{6,14},... | collective-permute-start | bytes 1179656 | tf_op jit(solution)/shard_map/ppermute | solution.py:466
  7.0 15.3 %collective-permute-start.2 = (bf16[240,768]{1,0:T(8,128)(2,1)S(1)}, bf16[240,768]{1,0:T(8,128)(2,1)S(1)}, u32[]{:S(2)}, u32[]{:S(2)}) collective-permute-start(bf16[240,768]{1,0:T(8,128)(2,1)S(1)} %get-tuple-element.151), channel_id=1, source_target_pairs={{0,1},{1,0},{2,3},{3,2},{4,5},{5,4},{6,7},{7,6},{8,9},{9,8},{10,11... | collective-permute-start | bytes 1105928 | tf_op jit(solution)/shard_map/ppermute | solution.py:463
  8.6 10.8 %collective-permute-start.3 = (bf16[48,768]{1,0:T(8,128)(2,1)S(1)}, bf16[48,768]{1,0:T(8,128)(2,1)S(1)}, u32[]{:S(2)}, u32[]{:S(2)}) collective-permute-start(bf16[48,768]{1,0:T(8,128)(2,1)S(1)} %get-tuple-element.152), channel_id=1, source_target_pairs={{0,2},{1,3},{2,0},{3,1},{4,6},{5,7},{6,4},{7,5},{8,10},{9,11},{10,... | collective-permute-start | bytes 221192 | tf_op jit(solution)/shard_map/ppermute | solution.py:463
  11.2 11.1 %collective-permute-start.4 = (bf16[48,768]{1,0:T(8,128)(2,1)S(1)}, bf16[48,768]{1,0:T(8,128)(2,1)S(1)}, u32[]{:S(2)}, u32[]{:S(2)}) collective-permute-start(bf16[48,768]{1,0:T(8,128)(2,1)S(1)} %get-tuple-element.152), channel_id=1, source_target_pairs={{0,3},{1,2},{2,1},{3,0},{4,7},{5,6},{6,5},{7,4},{8,11},{9,10},{10,... | collective-permute-start | bytes 221192 | tf_op jit(solution)/shard_map/ppermute | solution.py:463
  22.9 12.9 %collective-permute-start.12 = (bf16[192,768]{1,0:T(8,128)(2,1)S(1)}, bf16[192,768]{1,0:T(8,128)(2,1)S(1)}, u32[]{:S(2)}, u32[]{:S(2)}) collective-permute-start(bf16[192,768]{1,0:T(8,128)(2,1)S(1)} %slice.18), channel_id=1, source_target_pairs={{0,16},{4,20},{8,24},{12,28},{16,0},{20,4},{24,8},{28,12},{1,17},{... | collective-permute-start | bytes 884744 | tf_op jit(solution)/shard_map/ppermute | solution.py:543
  24.5 14.4 %collective-permute-start.13 = (bf16[192,768]{1,0:T(8,128)(2,1)S(1)}, bf16[192,768]{1,0:T(8,128)(2,1)}, u32[]{:S(2)}, u32[]{:S(2)}) collective-permute-start(bf16[192,768]{1,0:T(8,128)(2,1)S(1)} %slice.18), channel_id=1, source_target_pairs={{0,24},{4,28},{8,16},{12,20},{16,8},{20,12},{24,0},{28,4},{1,25},{... | collective-permute-start | bytes 884744 | tf_op jit(solution)/shard_map/ppermute | solution.py:543
  25.1 20.0 %collective-permute-start.11 = (bf16[336,768]{1,0:T(8,128)(2,1)S(1)}, bf16[336,768]{1,0:T(8,128)(2,1)S(1)}, u32[]{:S(2)}, u32[]{:S(2)}) collective-permute-start(bf16[336,768]{1,0:T(8,128)(2,1)S(1)} %constant_dynamic-update-slice_fusion.refs_0_), channel_id=1, source_target_pairs={{0,8},{4,12},{8,0},{12,4},{16,24},{20,28},{24,16},{28,20},{1,9},{5... | collective-permute-start | bytes 1548296 | tf_op jit(solution)/shard_map/ppermute | solution.py:543
  32.5 10.6 %collective-permute-start.9 = (bf16[384,128]{1,0:T(8,128)(2,1)S(1)}, bf16[384,128]{1,0:T(8,128)(2,1)S(1)}, u32[]{:S(2)}, u32[]{:S(2)}) collective-permute-start(bf16[384,128]{1,0:T(8,128)(2,1)S(1)} %get-tuple-element.158.refs_0_), channel_id=1, source_target_pairs={{0,2},{1,3},{2,0},{3,1},{4,6},{5,7},{6,4},{7,5},{8,10},{9,11},{10,... | collective-permute-start | bytes 294920 | tf_op jit(solution)/shard_map/ppermute | solution.py:463
  52.0 16.2 %collective-permute-start.17 = (bf16[128,768]{1,0:T(8,128)(2,1)S(1)}, bf16[128,768]{1,0:T(8,128)(2,1)S(1)}, u32[]{:S(2)}, u32[]{:S(2)}) collective-permute-start(bf16[128,768]{1,0:T(8,128)(2,1)S(1)} %get-tuple-element.171.mine), channel_id=1, source_target_pairs={{0,2},{1,3},{2,0},{3,1},{4,6},{5,7},{6,4},{7,5},{8,10},{9,11},{10,... | collective-permute-start | bytes 589832 | tf_op jit(solution)/shard_map/ppermute | solution.py:463
  55.1 17.2 %collective-permute-start.18 = (bf16[128,768]{1,0:T(8,128)(2,1)S(1)}, bf16[128,768]{1,0:T(8,128)(2,1)S(1)}, u32[]{:S(2)}, u32[]{:S(2)}) collective-permute-start(bf16[128,768]{1,0:T(8,128)(2,1)S(1)} %get-tuple-element.176.mine), channel_id=1, source_target_pairs={{0,2},{1,3},{2,0},{3,1},{4,6},{5,7},{6,4},{7,5},{8,10},{9,11},{10,... | collective-permute-start | bytes 589832 | tf_op jit(solution)/shard_map/ppermute | solution.py:463
  70.9 15.5 %collective-permute-start.19 = (bf16[128,768]{1,0:T(8,128)(2,1)S(1)}, bf16[128,768]{1,0:T(8,128)(2,1)S(1)}, u32[]{:S(2)}, u32[]{:S(2)}) collective-permute-start(bf16[128,768]{1,0:T(8,128)(2,1)S(1)} %get-tuple-element.178.mine), channel_id=1, source_target_pairs={{0,2},{1,3},{2,0},{3,1},{4,6},{5,7},{6,4},{7,5},{8,10},{9,11},{10,... | collective-permute-start | bytes 589832 | tf_op jit(solution)/shard_map/ppermute | solution.py:463
  75.0 15.5 %collective-permute-start.20 = (bf16[128,768]{1,0:T(8,128)(2,1)S(1)}, bf16[128,768]{1,0:T(8,128)(2,1)S(1)}, u32[]{:S(2)}, u32[]{:S(2)}) collective-permute-start(bf16[128,768]{1,0:T(8,128)(2,1)S(1)} %get-tuple-element.183.mine), channel_id=1, source_target_pairs={{0,2},{1,3},{2,0},{3,1},{4,6},{5,7},{6,4},{7,5},{8,10},{9,11},{10,... | collective-permute-start | bytes 589832 | tf_op jit(solution)/shard_map/ppermute | solution.py:463
  78.9 16.1 %collective-permute-start.23 = (bf16[4,2,192,768]{3,2,1,0:T(8,128)(2,1)S(1)}, bf16[4,2,192,768]{3,2,1,0:T(8,128)(2,1)S(1)}, u32[]{:S(2)}, u32[]{:S(2)}) collective-permute-start(bf16[4,2,192,768]{3,2,1,0:T(8,128)(2,1)S(1)} %get-tuple-element.207), channel_id=1, source_target_pairs={{0,4},{4,0},{8,12},{12,8},{1,5},{5,1},{9,13},{13,9},{2,6},{6,2},{1... | collective-permute-start | bytes 7077896 | tf_op jit(solution)/shard_map/ppermute | solution.py:466
  100.8 9.7 %collective-permute-start.27 = (bf16[2,384,128]{2,1,0:T(8,128)(2,1)S(1)}, bf16[2,384,128]{2,1,0:T(8,128)(2,1)S(1)}, u32[]{:S(2)}, u32[]{:S(2)}) collective-permute-start(bf16[2,384,128]{2,1,0:T(8,128)(2,1)S(1)} %fusion.6), channel_id=1, source_target_pairs={{0,8},{4,12},{8,0},{12,4},{1,9},{5,13},{9,1},{13,5},{2,10},{6,14},... | collective-permute-start | bytes 589832 | tf_op jit(solution)/shard_map/ppermute | solution.py:466
  102.2 13.5 %collective-permute-start.29 = (bf16[144,768]{1,0:T(8,128)(2,1)S(1)}, bf16[144,768]{1,0:T(8,128)(2,1)S(1)}, u32[]{:S(2)}, u32[]{:S(2)}) collective-permute-start(bf16[144,768]{1,0:T(8,128)(2,1)S(1)} %get-tuple-element.228.refs_0_), channel_id=1, source_target_pairs={{0,1},{1,0},{2,3},{3,2},{4,5},{5,4},{6,7},{7,6},{8,9},{9,8},{10,11... | collective-permute-start | bytes 663560 | tf_op jit(solution)/shard_map/ppermute | solution.py:463
  103.8 13.0 %collective-permute-start.30 = (bf16[144,768]{1,0:T(8,128)(2,1)S(1)}, bf16[144,768]{1,0:T(8,128)(2,1)S(1)}, u32[]{:S(2)}, u32[]{:S(2)}) collective-permute-start(bf16[144,768]{1,0:T(8,128)(2,1)S(1)} %get-tuple-element.229.refs_1_), channel_id=1, source_target_pairs={{0,1},{1,0},{2,3},{3,2},{4,5},{5,4},{6,7},{7,6},{8,9},{9,8},{10,11... | collective-permute-start | bytes 663560 | tf_op jit(solution)/shard_map/ppermute | solution.py:463
  111.1 11.6 %collective-permute-start.28 = (bf16[256,768]{1,0:T(8,128)(2,1)S(1)}, bf16[256,768]{1,0:T(8,128)(2,1)S(1)}, u32[]{:S(2)}, u32[]{:S(2)}) collective-permute-start(bf16[256,768]{1,0:T(8,128)(2,1)S(1)} %get-tuple-element.227), channel_id=1, source_target_pairs={{0,1},{1,0},{2,3},{3,2},{4,5},{5,4},{6,7},{7,6},{8,9},{9,8},{10,11... | collective-permute-start | bytes 1179656 | tf_op jit(solution)/shard_map/ppermute | solution.py:463
  112.8 15.4 %collective-permute-start.32 = (bf16[2,192,768]{2,1,0:T(8,128)(2,1)S(1)}, bf16[2,192,768]{2,1,0:T(8,128)(2,1)S(1)}, u32[]{:S(2)}, u32[]{:S(2)}) collective-permute-start(bf16[2,192,768]{2,1,0:T(8,128)(2,1)S(1)} %get-tuple-element.232), channel_id=1, source_target_pairs={{0,8},{4,12},{8,0},{12,4},{16,24},{20,28},{24,16},{28,20},{1,9},{5... | collective-permute-start | bytes 1769480 | tf_op jit(solution)/shard_map/ppermute | solution.py:475
  114.2 16.3 %collective-permute-start.33 = (bf16[2,192,768]{2,1,0:T(8,128)(2,1)S(1)}, bf16[2,192,768]{2,1,0:T(8,128)(2,1)S(1)}, u32[]{:S(2)}, u32[]{:S(2)}) collective-permute-start(bf16[2,192,768]{2,1,0:T(8,128)(2,1)S(1)} %get-tuple-element.233), channel_id=1, source_target_pairs={{0,16},{4,20},{8,24},{12,28},{16,0},{20,4},{24,8},{28,12},{1,17},{... | collective-permute-start | bytes 1769480 | tf_op jit(solution)/shard_map/ppermute | solution.py:475
  115.7 25.4 %collective-permute-start.34 = (bf16[2,192,768]{2,1,0:T(8,128)(2,1)S(1)}, bf16[2,192,768]{2,1,0:T(8,128)(2,1)S(1)}, u32[]{:S(2)}, u32[]{:S(2)}) collective-permute-start(bf16[2,192,768]{2,1,0:T(8,128)(2,1)S(1)} %get-tuple-element.234), channel_id=1, source_target_pairs={{0,24},{4,28},{8,16},{12,20},{16,8},{20,12},{24,0},{28,4},{1,25},{... | collective-permute-start | bytes 1769480 | tf_op jit(solution)/shard_map/ppermute | solution.py:475
  124.2 17.6 %collective-permute-start.36 = (bf16[448,768]{1,0:T(8,128)(2,1)S(1)}, bf16[448,768]{1,0:T(8,128)(2,1)S(1)}, u32[]{:S(2)}, u32[]{:S(2)}) collective-permute-start(bf16[448,768]{1,0:T(8,128)(2,1)S(1)} %get-tuple-element.247), channel_id=1, source_target_pairs={{0,4},{4,0},{8,12},{12,8},{1,5},{5,1},{9,13},{13,9},{2,6},{6,2},{1... | collective-permute-start | bytes 2064392 | tf_op jit(solution)/shard_map/ppermute | solution.py:466
  124.3 19.2 %collective-permute-start.40 = (bf16[128,768]{1,0:T(8,128)(2,1)S(1)}, bf16[128,768]{1,0:T(8,128)(2,1)S(1)}, u32[]{:S(2)}, u32[]{:S(2)}) collective-permute-start(bf16[128,768]{1,0:T(8,128)(2,1)S(1)} %get-tuple-element.172.refs_0_), channel_id=1, source_target_pairs={{0,1},{1,0},{2,3},{3,2},{4,5},{5,4},{6,7},{7,6},{8,9},{9,8},{10,11... | collective-permute-start | bytes 589832 | tf_op jit(solution)/shard_map/ppermute | solution.py:463
  128.1 16.9 %collective-permute-start.41 = (bf16[128,768]{1,0:T(8,128)(2,1)S(1)}, bf16[128,768]{1,0:T(8,128)(2,1)S(1)}, u32[]{:S(2)}, u32[]{:S(2)}) collective-permute-start(bf16[128,768]{1,0:T(8,128)(2,1)S(1)} %get-tuple-element.177.refs_1_), channel_id=1, source_target_pairs={{0,1},{1,0},{2,3},{3,2},{4,5},{5,4},{6,7},{7,6},{8,9},{9,8},{10,11... | collective-permute-start | bytes 589832 | tf_op jit(solution)/shard_map/ppermute | solution.py:463
  130.5 17.3 %collective-permute-start.31 = (bf16[256,768]{1,0:T(8,128)(2,1)S(1)}, bf16[256,768]{1,0:T(8,128)(2,1)S(1)}, u32[]{:S(2)}, u32[]{:S(2)}) collective-permute-start(bf16[256,768]{1,0:T(8,128)(2,1)S(1)} %add_convert_fusion.5), channel_id=1, source_target_pairs={{0,2},{1,3},{2,0},{3,1},{4,6},{5,7},{6,4},{7,5},{8,10},{9,11},{10,... | collective-permute-start | bytes 1179656 | tf_op jit(solution)/shard_map/ppermute | solution.py:463
  141.4 9.4 %collective-permute-start.35 = (bf16[192,768]{1,0:T(8,128)(2,1)S(1)}, bf16[192,768]{1,0:T(8,128)(2,1)S(1)}, u32[]{:S(2)}, u32[]{:S(2)}) collective-permute-start(bf16[192,768]{1,0:T(8,128)(2,1)S(1)} %slice_bitcast_fusion), channel_id=1, source_target_pairs={{0,1},{1,0},{2,3},{3,2},{4,5},{5,4},{6,7},{7,6},{8,9},{9,8},{10,11... | collective-permute-start | bytes 884744 | tf_op jit(solution)/shard_map/ppermute | solution.py:463
  142.0 8.8 %collective-permute-start.37 = (bf16[112,768]{1,0:T(8,128)(2,1)S(1)}, bf16[112,768]{1,0:T(8,128)(2,1)S(1)}, u32[]{:S(2)}, u32[]{:S(2)}) collective-permute-start(bf16[112,768]{1,0:T(8,128)(2,1)S(1)} %get-tuple-element.282), channel_id=1, source_target_pairs={{0,8},{4,12},{8,0},{12,4},{16,24},{20,28},{24,16},{28,20},{1,9},{5... | collective-permute-start | bytes 516104 | tf_op jit(solution)/shard_map/ppermute | solution.py:475
  151.5 10.6 %collective-permute-start.42 = (bf16[304,768]{1,0:T(8,128)(2,1)S(1)}, bf16[304,768]{1,0:T(8,128)(2,1)S(1)}, u32[]{:S(2)}, u32[]{:S(2)}) collective-permute-start(bf16[304,768]{1,0:T(8,128)(2,1)S(1)} %grad_share.1.refs_0_), channel_id=1, source_target_pairs={{0,8},{4,12},{8,0},{12,4},{16,24},{20,28},{24,16},{28,20},{1,9},{5... | collective-permute-start | bytes 1400840 | tf_op jit(solution)/shard_map/ppermute | solution.py:475
  152.8 9.0 %collective-permute-start.43 = (bf16[256,768]{1,0:T(8,128)(2,1)S(1)}, bf16[256,768]{1,0:T(8,128)(2,1)S(1)}, u32[]{:S(2)}, u32[]{:S(2)}) collective-permute-start(bf16[256,768]{1,0:T(8,128)(2,1)S(1)} %fusion.refs_0_), channel_id=1, source_target_pairs={{0,1},{1,0},{2,3},{3,2},{4,5},{5,4},{6,7},{7,6},{8,9},{9,8},{10,11... | collective-permute-start | bytes 1179656 | tf_op jit(solution)/shard_map/ppermute | solution.py:463
  154.6 13.6 %collective-permute-start.44 = (bf16[304,768]{1,0:T(8,128)(2,1)S(1)}, bf16[304,768]{1,0:T(8,128)(2,1)S(1)}, u32[]{:S(2)}, u32[]{:S(2)}) collective-permute-start(bf16[304,768]{1,0:T(8,128)(2,1)S(1)} %grad_share.1.refs_0_), channel_id=1, source_target_pairs={{0,16},{4,20},{8,24},{12,28},{16,0},{20,4},{24,8},{28,12},{1,17},{... | collective-permute-start | bytes 1400840 | tf_op jit(solution)/shard_map/ppermute | solution.py:475
  156.1 19.6 %collective-permute-start.45 = (bf16[304,768]{1,0:T(8,128)(2,1)S(1)}, bf16[304,768]{1,0:T(8,128)(2,1)S(1)}, u32[]{:S(2)}, u32[]{:S(2)}) collective-permute-start(bf16[304,768]{1,0:T(8,128)(2,1)S(1)} %grad_share.1.refs_0_), channel_id=1, source_target_pairs={{0,24},{4,28},{8,16},{12,20},{16,8},{20,12},{24,0},{28,4},{1,25},{... | collective-permute-start | bytes 1400840 | tf_op jit(solution)/shard_map/ppermute | solution.py:475
  156.9 18.8 %collective-permute-start.46 = (bf16[304,768]{1,0:T(8,128)(2,1)S(1)}, bf16[304,768]{1,0:T(8,128)(2,1)S(1)}, u32[]{:S(2)}, u32[]{:S(2)}) collective-permute-start(bf16[304,768]{1,0:T(8,128)(2,1)S(1)} %grad_share.1.refs_0_), channel_id=1, source_target_pairs={{0,4},{4,0},{8,12},{12,8},{1,5},{5,1},{9,13},{13,9},{2,6},{6,2},{1... | collective-permute-start | bytes 1400840 | tf_op jit(solution)/shard_map/ppermute | solution.py:466
  163.6 12.1 %collective-permute-start.47 = (bf16[304,768]{1,0:T(8,128)(2,1)S(1)}, bf16[304,768]{1,0:T(8,128)(2,1)S(1)}, u32[]{:S(2)}, u32[]{:S(2)}) collective-permute-start(bf16[304,768]{1,0:T(8,128)(2,1)S(1)} %collective-permute-done.42.refs_1_), channel_id=1, source_target_pairs={{0,4},{4,0},{8,12},{12,8},{1,5},{5,1},{9,13},{13,9},{2,6},{6,2},{1... | collective-permute-start | bytes 1400840 | tf_op jit(solution)/shard_map/ppermute | solution.py:466
  (59 other events, 464.7 us)

commit v9 on v8

--- a/solution.py
+++ b/solution.py
@@ -390,10 +390,10 @@
     one = join([g_out, g_q]).astype(bf16)
     two = g_kv.astype(bf16)
     half = two.shape[0]
-    norm = ordered_sum(at, [x[BLOCK : BLOCK + 8, :] for x in shares], held)
+    tails = [x[BLOCK : BLOCK + 16, :].astype(f32) for x in shares]
+    norm = ordered_sum(at, [x[:8] for x in tails], held)
     total = sums[0][...] + sums[1][...]
-    row = lambda x, k: x[BLOCK + k : BLOCK + k + 1, :].astype(f32)
-    inner = row(shares[0], 6) + row(shares[1], 6) + row(shares[2], 7) + row(shares[3], 7)
+    inner = tails[0][6:7] + tails[1][6:7] + tails[2][7:8] + tails[3][7:8]
     norm = join([norm[:6], inner, jnp.zeros_like(inner)])
     rest = keep.shape[0] - half
     tail = join([norm, total, jnp.zeros((rest - 16, total.shape[1]), f32)]).astype(bf16)
@@ -542,8 +542,8 @@
             there = lambda i: ((i // n_blk) ^ dp_bit) * n_blk + ((i % n_blk) ^ blk_bit)
             return lax.ppermute(v, ("dp", "blk"), [(i, there(i)) for i in range(n_dp * n_blk)])
 
-        arrived = {0: own_piece, 2: across(own_piece, 0, 2)}
-        arrived |= {4: across(ffn_piece, 1, 0), 6: across(ffn_piece, 1, 2)}
+        arrived = {4: across(ffn_piece, 1, 0), 6: across(ffn_piece, 1, 2)}
+        arrived |= {0: own_piece, 2: across(own_piece, 0, 2)}
 
         q = call(q_kernel, near((count, lanes), bf16), "query_rows", (tok, wq_t, row(b_query)), us=0.5)
         kvs = [kv, kv_core, kv_far, kv_both]

time: 182 us -> 182 us (level)
  no operation moved by 1% of the time
where the time goes in v9:
time: 182 us
  waiting for transfers between devices  90.8 us (50%)
  starting transfers between devices  43.9 us (24%)
  Pallas kernels  39.4 us (22%)
  local copies, waits for them, and re-layouts  4.26 us (2%)
    ppermute x21, waiting for transfers between devices, swap(): return lax.ppermute(v, 'tensor', [(i, i ^ bit) for i in range(n)])  51 us
    pallas_call x18, Pallas kernels, call(): pl.pallas_call(kernel, out_shape=outs, in_specs=[SMEM] * scalars + [VMEM]...  31.3 us
    ppermute x9, waiting for transfers between devices, flip_member(): return lax.ppermute(v, ('dp', 'blk'), perm)  27.3 us
    ppermute x21, starting transfers between devices, swap(): return lax.ppermute(v, 'tensor', [(i, i ^ bit) for i in range(n)])  22.8 us
    ppermute x9, starting transfers between devices, flip_member(): return lax.ppermute(v, ('dp', 'blk'), perm)  10.5 us
    ppermute x17, waiting for transfers between devices, flip(): return lax.ppermute(v, 'blk', [(i, i ^ bit) for i in range(n_blk)])  10.5 us
    ppermute x17, starting transfers between devices, flip(): return lax.ppermute(v, 'blk', [(i, i ^ bit) for i in range(n_blk)])  7.01 us
    pallas_call x1, Pallas kernels, body(): pl.pallas_call(functools.partial(attend_kernel, n_blk, (2, 3, 0, 1)), out...  5.61 us
  transfers between devices with their start and end apart: 50, of which 26 were waited for; matrix products, arithmetic and copies ran while one was open for 1% of the time, Pallas kernels for 16%

profile of v9, /device:TPU:0, one launch (start us, length us, event | category | flops | bytes accessed | tf_op | source)
XLA Modules:
  0.0 181.5 jit_solution(9543936808587882143)
XLA Ops:
  1.5 2.5 %front.1 = (bf16[512,384]{1,0:T(8,128)(2,1)S(1)}, bf16[240,768]{1,0:T(8,128)(2,1)S(1)}, bf16[48,768]{1,0:T(8,128)(2,1)S(1)}) custom-call(s32[5]{0:T(128)S(1)} %stack.23.at, bf16[512,768]{1,0:T(8,128)(2,1)} %bitcast.39, bf16[192,768]{1,0:T(8,128)(2,1)} %bitcast.45, bf16[192,768]{1,0:T(8,128)(2,1)} %bitcast.48, bf16[768,768]{1,0:T(8,128)(2,1)} %w_in.9, ...), custom_call_target="tpu_custom_call" | custom-call | tf_op jit(solution)/shard_map/front/pallas_call | solution.py:516
  4.0 3.0 %collective-permute-start = (bf16[512,384]{1,0:T(8,128)(2,1)S(1)}, bf16[512,384]{1,0:T(8,128)(2,1)S(1)}, u32[]{:S(2)}, u32[]{:S(2)}) collective-permute-start(bf16[512,384]{1,0:T(8,128)(2,1)S(1)} %get-tuple-element.149.refs_0_), channel_id=1, source_target_pairs={{0,8},{4,12},{8,0},{12,4},{1,9},{5,13},{9,1},{13,5},{2,10},{6,14},... | collective-permute-start | bytes 1179656 | tf_op jit(solution)/shard_map/ppermute | solution.py:466
  8.6 2.6 %collective-permute-start.3 = (bf16[48,768]{1,0:T(8,128)(2,1)S(1)}, bf16[48,768]{1,0:T(8,128)(2,1)S(1)}, u32[]{:S(2)}, u32[]{:S(2)}) collective-permute-start(bf16[48,768]{1,0:T(8,128)(2,1)S(1)} %get-tuple-element.152), channel_id=1, source_target_pairs={{0,2},{1,3},{2,0},{3,1},{4,6},{5,7},{6,4},{7,5},{8,10},{9,11},{10,... | collective-permute-start | bytes 221192 | tf_op jit(solution)/shard_map/ppermute | solution.py:463
  12.1 7.3 %collective-permute-done.1 = f32[768]{0:T(1024)S(1)} collective-permute-done((f32[768]{0:T(1024)S(1)}, f32[768]{0:T(1024)S(1)}, u32[]{:S(2)}, u32[]{:S(2)}) %collective-permute-start.1) | collective-permute-done | bytes 3104 | tf_op jit(solution)/shard_map/ppermute | solution.py:463
  19.4 2.9 %collective-permute-done.4 = bf16[48,768]{1,0:T(8,128)(2,1)S(1)} collective-permute-done((bf16[48,768]{1,0:T(8,128)(2,1)S(1)}, bf16[48,768]{1,0:T(8,128)(2,1)S(1)}, u32[]{:S(2)}, u32[]{:S(2)}) %collective-permute-start.4) | collective-permute-done | bytes 73760 | tf_op jit(solution)/shard_map/ppermute | solution.py:463
  26.7 5.6 %attend.1 = (bf16[384,128]{1,0:T(8,128)(2,1)S(1)}, bf16[384,128]{1,0:T(8,128)(2,1)S(1)}, bf16[768,512]{1,0:T(8,128)(2,1)}, bf16[768,512]{1,0:T(8,128)(2,1)}, bf16[768,128]{1,0:T(8,128)(2,1)}) custom-call(s32[5]{0:T(128)S(1)} %stack.23.at, s32[4]{0:T(128)S(1)} %copy-done.28, s32[4,4]{1,0:T(4,128)S(1)} %copy-done.26, bf16[512,384]{1,0:T(8,128)(2,1)S(1)} %query_rows.1.q, ...), custom_call_target="tpu_custom_call" | custom-call | flops 49999998976 | bytes 1 | tf_op jit(solution)/shard_map/attend/pallas_call | solution.py:552
  32.5 2.6 %collective-permute-start.9 = (bf16[384,128]{1,0:T(8,128)(2,1)S(1)}, bf16[384,128]{1,0:T(8,128)(2,1)S(1)}, u32[]{:S(2)}, u32[]{:S(2)}) collective-permute-start(bf16[384,128]{1,0:T(8,128)(2,1)S(1)} %get-tuple-element.158.refs_0_), channel_id=1, source_target_pairs={{0,2},{1,3},{2,0},{3,1},{4,6},{5,7},{6,4},{7,5},{8,10},{9,11},{10,... | collective-permute-start | bytes 294920 | tf_op jit(solution)/shard_map/ppermute | solution.py:463
  39.5 3.6 %collective-permute-done.9.refs_2_ = bf16[384,128]{1,0:T(8,128)(2,1)S(1)} collective-permute-done((bf16[384,128]{1,0:T(8,128)(2,1)S(1)}, bf16[384,128]{1,0:T(8,128)(2,1)S(1)}, u32[]{:S(2)}, u32[]{:S(2)}) %collective-permute-start.9) | collective-permute-done | bytes 98336 | tf_op jit(solution)/shard_map/ppermute | solution.py:463
  49.6 2.4 %ffn.2 = (bf16[128,768]{1,0:T(8,128)(2,1)S(1)}, f32[128,768]{1,0:T(8,128)S(1)}, f32[128,128]{1,0:T(8,128)S(1)}, bf16[128,768]{1,0:T(8,128)(2,1)S(1)}, bf16[128,7...) custom-call(s32[5]{0:T(128)S(1)} %stack.23.at, ...), custom_call_target="tpu_custom_call" | custom-call | flops 2400000000 | bytes 1 | tf_op jit(solution)/shard_map/ffn/pallas_call | solution.py:73
  52.8 2.3 %ffn.3 = (bf16[128,768]{1,0:T(8,128)(2,1)S(1)}, f32[128,768]{1,0:T(8,128)S(1)}, f32[128,128]{1,0:T(8,128)S(1)}, bf16[128,768]{1,0:T(8,128)(2,1)S(1)}, bf16[128,7...) custom-call(s32[5]{0:T(128)S(1)} %stack.23.at, bf16[512,768]{1,0:T(8,128)(2,1)S(1)} %bitcast.42, ...), custom_call_target="tpu_custom_call" | custom-call | flops 2400000000 | bytes 1 | tf_op jit(solution)/shard_map/ffn/pallas_call | solution.py:73
  55.1 2.3 %collective-permute-start.18 = (bf16[128,768]{1,0:T(8,128)(2,1)S(1)}, bf16[128,768]{1,0:T(8,128)(2,1)S(1)}, u32[]{:S(2)}, u32[]{:S(2)}) collective-permute-start(bf16[128,768]{1,0:T(8,128)(2,1)S(1)} %get-tuple-element.176.mine), channel_id=1, source_target_pairs={{0,2},{1,3},{2,0},{3,1},{4,6},{5,7},{6,4},{7,5},{8,10},{9,11},{10,... | collective-permute-start | bytes 589832 | tf_op jit(solution)/shard_map/ppermute | solution.py:463
  57.4 10.8 %collective-permute-done.17.theirs = bf16[128,768]{1,0:T(8,128)(2,1)S(1)} collective-permute-done((bf16[128,768]{1,0:T(8,128)(2,1)S(1)}, bf16[128,768]{1,0:T(8,128)(2,1)S(1)}, u32[]{:S(2)}, u32[]{:S(2)}) %collective-permute-start.17) | collective-permute-done | bytes 196640 | tf_op jit(solution)/shard_map/ppermute | solution.py:463
  68.2 2.7 %ffn_back.2 = (bf16[128,768]{1,0:T(8,128)(2,1)S(1)}, bf16[128,768]{1,0:T(8,128)(2,1)S(1)}, bf16[128,768]{1,0:T(8,128)(2,1)S(1)}, bf16[128,768]{1,0:T(8,128)(2,1)...) custom-call(s32[5]{0:T(128)S(1)} %stack.23.at, bf16[512,768]{1,0:T(8,128)(2,1)S(1)} %bitcast.52, ...), custom_call_target="tpu_custom_call" | custom-call | flops 2700000000 | bytes 1 | tf_op jit(solution)/shard_map/ffn_back/pallas_call | solution.py:73
  72.3 2.7 %ffn_back.3 = (bf16[128,768]{1,0:T(8,128)(2,1)S(1)}, bf16[128,768]{1,0:T(8,128)(2,1)S(1)}, bf16[128,768]{1,0:T(8,128)(2,1)S(1)}, bf16[128,768]{1,0:T(8,128)(2,1)...) custom-call(s32[5]{0:T(128)S(1)} %stack.23.at, bf16[512,768]{1,0:T(8,128)(2,1)S(1)} %bitcast.53, ...), custom_call_target="tpu_custom_call" | custom-call | flops 2700000000 | bytes 1 | tf_op jit(solution)/shard_map/ffn_back/pallas_call | solution.py:73
  76.7 2.2 %ffn_grads.1 = (bf16[4,2,192,768]{3,2,1,0:T(8,128)(2,1)S(1)}, bf16[4,2,192,768]{3,2,1,0:T(8,128)(2,1)S(1)}) custom-call(s32[5]{0:T(128)S(1)} %stack.23.at, bf16[128,768]{1,0:T(8,128)(2,1)S(1)} %get-tuple-element.194.refs_0_, bf16[128,768]{1,0:T(8,128)(2,1)S(1)} %get-tuple-element.195.refs_1_, bf16[128,768]{1,0:T(8,128)(2,1)S(1)} %get-tuple-element.196.refs_2_, ...), custom_call_target="tpu_custom_call" | custom-call | flops 49999998976 | bytes 1 | tf_op jit(solution)/shard_map/ffn_grads/pallas_call | solution.py:73
  79.0 7.4 %collective-permute-done.19.theirs = bf16[128,768]{1,0:T(8,128)(2,1)S(1)} collective-permute-done((bf16[128,768]{1,0:T(8,128)(2,1)S(1)}, bf16[128,768]{1,0:T(8,128)(2,1)S(1)}, u32[]{:S(2)}, u32[]{:S(2)}) %collective-permute-start.19) | collective-permute-done | bytes 196640 | tf_op jit(solution)/shard_map/ppermute | solution.py:463
  87.6 2.9 %collective-permute-done.20.theirs = bf16[128,768]{1,0:T(8,128)(2,1)S(1)} collective-permute-done((bf16[128,768]{1,0:T(8,128)(2,1)S(1)}, bf16[128,768]{1,0:T(8,128)(2,1)S(1)}, u32[]{:S(2)}, u32[]{:S(2)}) %collective-permute-start.20) | collective-permute-done | bytes 196640 | tf_op jit(solution)/shard_map/ppermute | solution.py:463
  92.2 2.7 %attend_back.2 = (bf16[256,192]{1,0:T(8,128)(2,1)S(1)}, bf16[2,2,384,128]{3,2,1,0:T(8,128)(2,1)S(1)}, bf16[2,2,384,128]{3,2,1,0:T(8,128)(2,1)S(1)}) custom-call(s32[5]{0:T(128)S(1)} %stack.23.at, bf16[192,128]{1,0:T(8,128)(2,1)S(1)} %get-tuple-element.182.first, bf16[192,128]{1,0:T(8,128)(2,1)S(1)} %get-tuple-element.187.second, ...), custom_call_target="tpu_custom_call" | custom-call | flops 49999998976 | bytes 1 | tf_op jit(solution)/shard_map/attend_back/pallas_call | solution.py:73
  96.1 2.7 %attend_back.3 = (bf16[256,192]{1,0:T(8,128)(2,1)S(1)}, bf16[2,2,384,128]{3,2,1,0:T(8,128)(2,1)S(1)}, bf16[2,2,384,128]{3,2,1,0:T(8,128)(2,1)S(1)}) custom-call(s32[5]{0:T(128)S(1)} %stack.23.at, bf16[192,128]{1,0:T(8,128)(2,1)S(1)} %collective-permute-done.21.first, bf16[192,128]{1,0:T(8,128)(2,1)S(1)} %collective-permute-done.22.second, ...), custom_call_target="tpu_custom_call" | custom-call | flops 49999998976 | bytes 1 | tf_op jit(solution)/shard_map/attend_back/pallas_call | solution.py:73
  104.2 2.8 %collective-permute-done.25.far = bf16[2,384,128]{2,1,0:T(8,128)(2,1)S(1)} collective-permute-done((bf16[2,384,128]{2,1,0:T(8,128)(2,1)S(1)}, bf16[2,384,128]{2,1,0:T(8,128)(2,1)S(1)}, u32[]{:S(2)}, u32[]{:S(2)}) %collective-permute-start.25) | collective-permute-done | bytes 196640 | tf_op jit(solution)/shard_map/ppermute | solution.py:466
  107.0 3.5 %collective-permute-done.27.far = bf16[2,384,128]{2,1,0:T(8,128)(2,1)S(1)} collective-permute-done((bf16[2,384,128]{2,1,0:T(8,128)(2,1)S(1)}, bf16[2,384,128]{2,1,0:T(8,128)(2,1)S(1)}, u32[]{:S(2)}, u32[]{:S(2)}) %collective-permute-start.27) | collective-permute-done | bytes 196640 | tf_op jit(solution)/shard_map/ppermute | solution.py:466
  116.8 5.9 %collective-permute-done.28 = bf16[256,768]{1,0:T(8,128)(2,1)S(1)} collective-permute-done((bf16[256,768]{1,0:T(8,128)(2,1)S(1)}, bf16[256,768]{1,0:T(8,128)(2,1)S(1)}, u32[]{:S(2)}, u32[]{:S(2)}) %collective-permute-start.28) | collective-permute-done | bytes 393248 | tf_op jit(solution)/shard_map/ppermute | solution.py:463
  125.8 2.3 %collective-permute-done.32 = bf16[2,192,768]{2,1,0:T(8,128)(2,1)S(1)} collective-permute-done((bf16[2,192,768]{2,1,0:T(8,128)(2,1)S(1)}, bf16[2,192,768]{2,1,0:T(8,128)(2,1)S(1)}, u32[]{:S(2)}, u32[]{:S(2)}) %collective-permute-start.32) | collective-permute-done | bytes 589856 | tf_op jit(solution)/shard_map/ppermute | solution.py:475
  128.6 1.9 %collective-permute-done.33 = bf16[2,192,768]{2,1,0:T(8,128)(2,1)S(1)} collective-permute-done((bf16[2,192,768]{2,1,0:T(8,128)(2,1)S(1)}, bf16[2,192,768]{2,1,0:T(8,128)(2,1)S(1)}, u32[]{:S(2)}, u32[]{:S(2)}) %collective-permute-start.33) | collective-permute-done | bytes 589856 | tf_op jit(solution)/shard_map/ppermute | solution.py:475
  130.9 10.1 %collective-permute-done.34 = bf16[2,192,768]{2,1,0:T(8,128)(2,1)S(1)} collective-permute-done((bf16[2,192,768]{2,1,0:T(8,128)(2,1)S(1)}, bf16[2,192,768]{2,1,0:T(8,128)(2,1)S(1)}, u32[]{:S(2)}, u32[]{:S(2)}) %collective-permute-start.34) | collective-permute-done | bytes 589856 | tf_op jit(solution)/shard_map/ppermute | solution.py:475
  145.6 2.1 %collective-permute-done.31 = bf16[256,768]{1,0:T(8,128)(2,1)S(1)} collective-permute-done((bf16[256,768]{1,0:T(8,128)(2,1)S(1)}, bf16[256,768]{1,0:T(8,128)(2,1)S(1)}, u32[]{:S(2)}, u32[]{:S(2)}) %collective-permute-start.31) | collective-permute-done | bytes 393248 | tf_op jit(solution)/shard_map/ppermute | solution.py:463
  147.7 3.1 %collective-permute-done.35.near1 = bf16[192,768]{1,0:T(8,128)(2,1)S(1)} collective-permute-done((bf16[192,768]{1,0:T(8,128)(2,1)S(1)}, bf16[192,768]{1,0:T(8,128)(2,1)S(1)}, u32[]{:S(2)}, u32[]{:S(2)}) %collective-permute-start.35) | collective-permute-done | bytes 294944 | tf_op jit(solution)/shard_map/ppermute | solution.py:463
  158.4 3.4 %collective-permute-done.43.refs_1_ = bf16[256,768]{1,0:T(8,128)(2,1)S(1)} collective-permute-done((bf16[256,768]{1,0:T(8,128)(2,1)S(1)}, bf16[256,768]{1,0:T(8,128)(2,1)S(1)}, u32[]{:S(2)}, u32[]{:S(2)}) %collective-permute-start.43) | collective-permute-done | bytes 393248 | tf_op jit(solution)/shard_map/ppermute | solution.py:463
  163.6 4.6 %collective-permute-done.44.refs_2_ = bf16[304,768]{1,0:T(8,128)(2,1)S(1)} collective-permute-done((bf16[304,768]{1,0:T(8,128)(2,1)S(1)}, bf16[304,768]{1,0:T(8,128)(2,1)S(1)}, u32[]{:S(2)}, u32[]{:S(2)}) %collective-permute-start.44) | collective-permute-done | bytes 466976 | tf_op jit(solution)/shard_map/ppermute | solution.py:475
  168.2 7.5 %collective-permute-done.45.refs_3_ = bf16[304,768]{1,0:T(8,128)(2,1)S(1)} collective-permute-done((bf16[304,768]{1,0:T(8,128)(2,1)S(1)}, bf16[304,768]{1,0:T(8,128)(2,1)S(1)}, u32[]{:S(2)}, u32[]{:S(2)}) %collective-permute-start.45) | collective-permute-done | bytes 466976 | tf_op jit(solution)/shard_map/ppermute | solution.py:475
  175.7 1.8 collective-permute-done.49.refs_7_
  177.5 3.8 %grads_out.1 = (f32[768,768]{1,0:T(8,128)}, f32[768,768]{1,0:T(8,128)}, f32[192,768]{1,0:T(8,128)}, f32[192,768]{1,0:T(8,128)}, f32[192,768]{1,0:T(8,128)}, /*in...) custom-call(s32[5]{0:T(128)S(1)} %stack.23.at, ...), custom_call_target="tpu_custom_call" | custom-call | flops 4000000000 | bytes 1 | tf_op jit(solution)/shard_map/grads_out/pallas_call | solution.py:73
  (191 shorter events, 55.7 us)
Async XLA Ops:
  4.0 18.3 %collective-permute-start = (bf16[512,384]{1,0:T(8,128)(2,1)S(1)}, bf16[512,384]{1,0:T(8,128)(2,1)S(1)}, u32[]{:S(2)}, u32[]{:S(2)}) collective-permute-start(bf16[512,384]{1,0:T(8,128)(2,1)S(1)} %get-tuple-element.149.refs_0_), channel_id=1, source_target_pairs={{0,8},{4,12},{8,0},{12,4},{1,9},{5,13},{9,1},{13,5},{2,10},{6,14},... | collective-permute-start | bytes 1179656 | tf_op jit(solution)/shard_map/ppermute | solution.py:466
  7.0 15.3 %collective-permute-start.2 = (bf16[240,768]{1,0:T(8,128)(2,1)S(1)}, bf16[240,768]{1,0:T(8,128)(2,1)S(1)}, u32[]{:S(2)}, u32[]{:S(2)}) collective-permute-start(bf16[240,768]{1,0:T(8,128)(2,1)S(1)} %get-tuple-element.151), channel_id=1, source_target_pairs={{0,1},{1,0},{2,3},{3,2},{4,5},{5,4},{6,7},{7,6},{8,9},{9,8},{10,11... | collective-permute-start | bytes 1105928 | tf_op jit(solution)/shard_map/ppermute | solution.py:463
  8.6 10.8 %collective-permute-start.3 = (bf16[48,768]{1,0:T(8,128)(2,1)S(1)}, bf16[48,768]{1,0:T(8,128)(2,1)S(1)}, u32[]{:S(2)}, u32[]{:S(2)}) collective-permute-start(bf16[48,768]{1,0:T(8,128)(2,1)S(1)} %get-tuple-element.152), channel_id=1, source_target_pairs={{0,2},{1,3},{2,0},{3,1},{4,6},{5,7},{6,4},{7,5},{8,10},{9,11},{10,... | collective-permute-start | bytes 221192 | tf_op jit(solution)/shard_map/ppermute | solution.py:463
  11.2 11.1 %collective-permute-start.4 = (bf16[48,768]{1,0:T(8,128)(2,1)S(1)}, bf16[48,768]{1,0:T(8,128)(2,1)S(1)}, u32[]{:S(2)}, u32[]{:S(2)}) collective-permute-start(bf16[48,768]{1,0:T(8,128)(2,1)S(1)} %get-tuple-element.152), channel_id=1, source_target_pairs={{0,3},{1,2},{2,1},{3,0},{4,7},{5,6},{6,5},{7,4},{8,11},{9,10},{10,... | collective-permute-start | bytes 221192 | tf_op jit(solution)/shard_map/ppermute | solution.py:463
  22.9 12.9 %collective-permute-start.12 = (bf16[192,768]{1,0:T(8,128)(2,1)S(1)}, bf16[192,768]{1,0:T(8,128)(2,1)S(1)}, u32[]{:S(2)}, u32[]{:S(2)}) collective-permute-start(bf16[192,768]{1,0:T(8,128)(2,1)S(1)} %slice.18), channel_id=1, source_target_pairs={{0,16},{4,20},{8,24},{12,28},{16,0},{20,4},{24,8},{28,12},{1,17},{... | collective-permute-start | bytes 884744 | tf_op jit(solution)/shard_map/ppermute | solution.py:543
  24.5 14.4 %collective-permute-start.13 = (bf16[192,768]{1,0:T(8,128)(2,1)S(1)}, bf16[192,768]{1,0:T(8,128)(2,1)}, u32[]{:S(2)}, u32[]{:S(2)}) collective-permute-start(bf16[192,768]{1,0:T(8,128)(2,1)S(1)} %slice.18), channel_id=1, source_target_pairs={{0,24},{4,28},{8,16},{12,20},{16,8},{20,12},{24,0},{28,4},{1,25},{... | collective-permute-start | bytes 884744 | tf_op jit(solution)/shard_map/ppermute | solution.py:543
  25.1 20.0 %collective-permute-start.11 = (bf16[336,768]{1,0:T(8,128)(2,1)S(1)}, bf16[336,768]{1,0:T(8,128)(2,1)S(1)}, u32[]{:S(2)}, u32[]{:S(2)}) collective-permute-start(bf16[336,768]{1,0:T(8,128)(2,1)S(1)} %constant_dynamic-update-slice_fusion.refs_0_), channel_id=1, source_target_pairs={{0,8},{4,12},{8,0},{12,4},{16,24},{20,28},{24,16},{28,20},{1,9},{5... | collective-permute-start | bytes 1548296 | tf_op jit(solution)/shard_map/ppermute | solution.py:543
  32.5 10.6 %collective-permute-start.9 = (bf16[384,128]{1,0:T(8,128)(2,1)S(1)}, bf16[384,128]{1,0:T(8,128)(2,1)S(1)}, u32[]{:S(2)}, u32[]{:S(2)}) collective-permute-start(bf16[384,128]{1,0:T(8,128)(2,1)S(1)} %get-tuple-element.158.refs_0_), channel_id=1, source_target_pairs={{0,2},{1,3},{2,0},{3,1},{4,6},{5,7},{6,4},{7,5},{8,10},{9,11},{10,... | collective-permute-start | bytes 294920 | tf_op jit(solution)/shard_map/ppermute | solution.py:463
  52.0 16.2 %collective-permute-start.17 = (bf16[128,768]{1,0:T(8,128)(2,1)S(1)}, bf16[128,768]{1,0:T(8,128)(2,1)S(1)}, u32[]{:S(2)}, u32[]{:S(2)}) collective-permute-start(bf16[128,768]{1,0:T(8,128)(2,1)S(1)} %get-tuple-element.171.mine), channel_id=1, source_target_pairs={{0,2},{1,3},{2,0},{3,1},{4,6},{5,7},{6,4},{7,5},{8,10},{9,11},{10,... | collective-permute-start | bytes 589832 | tf_op jit(solution)/shard_map/ppermute | solution.py:463
  55.1 17.2 %collective-permute-start.18 = (bf16[128,768]{1,0:T(8,128)(2,1)S(1)}, bf16[128,768]{1,0:T(8,128)(2,1)S(1)}, u32[]{:S(2)}, u32[]{:S(2)}) collective-permute-start(bf16[128,768]{1,0:T(8,128)(2,1)S(1)} %get-tuple-element.176.mine), channel_id=1, source_target_pairs={{0,2},{1,3},{2,0},{3,1},{4,6},{5,7},{6,4},{7,5},{8,10},{9,11},{10,... | collective-permute-start | bytes 589832 | tf_op jit(solution)/shard_map/ppermute | solution.py:463
  70.9 15.5 %collective-permute-start.19 = (bf16[128,768]{1,0:T(8,128)(2,1)S(1)}, bf16[128,768]{1,0:T(8,128)(2,1)S(1)}, u32[]{:S(2)}, u32[]{:S(2)}) collective-permute-start(bf16[128,768]{1,0:T(8,128)(2,1)S(1)} %get-tuple-element.178.mine), channel_id=1, source_target_pairs={{0,2},{1,3},{2,0},{3,1},{4,6},{5,7},{6,4},{7,5},{8,10},{9,11},{10,... | collective-permute-start | bytes 589832 | tf_op jit(solution)/shard_map/ppermute | solution.py:463
  75.0 15.5 %collective-permute-start.20 = (bf16[128,768]{1,0:T(8,128)(2,1)S(1)}, bf16[128,768]{1,0:T(8,128)(2,1)S(1)}, u32[]{:S(2)}, u32[]{:S(2)}) collective-permute-start(bf16[128,768]{1,0:T(8,128)(2,1)S(1)} %get-tuple-element.183.mine), channel_id=1, source_target_pairs={{0,2},{1,3},{2,0},{3,1},{4,6},{5,7},{6,4},{7,5},{8,10},{9,11},{10,... | collective-permute-start | bytes 589832 | tf_op jit(solution)/shard_map/ppermute | solution.py:463
  78.9 16.1 %collective-permute-start.23 = (bf16[4,2,192,768]{3,2,1,0:T(8,128)(2,1)S(1)}, bf16[4,2,192,768]{3,2,1,0:T(8,128)(2,1)S(1)}, u32[]{:S(2)}, u32[]{:S(2)}) collective-permute-start(bf16[4,2,192,768]{3,2,1,0:T(8,128)(2,1)S(1)} %get-tuple-element.207), channel_id=1, source_target_pairs={{0,4},{4,0},{8,12},{12,8},{1,5},{5,1},{9,13},{13,9},{2,6},{6,2},{1... | collective-permute-start | bytes 7077896 | tf_op jit(solution)/shard_map/ppermute | solution.py:466
  100.8 9.7 %collective-permute-start.27 = (bf16[2,384,128]{2,1,0:T(8,128)(2,1)S(1)}, bf16[2,384,128]{2,1,0:T(8,128)(2,1)S(1)}, u32[]{:S(2)}, u32[]{:S(2)}) collective-permute-start(bf16[2,384,128]{2,1,0:T(8,128)(2,1)S(1)} %fusion.6), channel_id=1, source_target_pairs={{0,8},{4,12},{8,0},{12,4},{1,9},{5,13},{9,1},{13,5},{2,10},{6,14},... | collective-permute-start | bytes 589832 | tf_op jit(solution)/shard_map/ppermute | solution.py:466
  102.2 13.5 %collective-permute-start.29 = (bf16[144,768]{1,0:T(8,128)(2,1)S(1)}, bf16[144,768]{1,0:T(8,128)(2,1)S(1)}, u32[]{:S(2)}, u32[]{:S(2)}) collective-permute-start(bf16[144,768]{1,0:T(8,128)(2,1)S(1)} %get-tuple-element.228.refs_0_), channel_id=1, source_target_pairs={{0,1},{1,0},{2,3},{3,2},{4,5},{5,4},{6,7},{7,6},{8,9},{9,8},{10,11... | collective-permute-start | bytes 663560 | tf_op jit(solution)/shard_map/ppermute | solution.py:463
  103.8 13.0 %collective-permute-start.30 = (bf16[144,768]{1,0:T(8,128)(2,1)S(1)}, bf16[144,768]{1,0:T(8,128)(2,1)S(1)}, u32[]{:S(2)}, u32[]{:S(2)}) collective-permute-start(bf16[144,768]{1,0:T(8,128)(2,1)S(1)} %get-tuple-element.229.refs_1_), channel_id=1, source_target_pairs={{0,1},{1,0},{2,3},{3,2},{4,5},{5,4},{6,7},{7,6},{8,9},{9,8},{10,11... | collective-permute-start | bytes 663560 | tf_op jit(solution)/shard_map/ppermute | solution.py:463
  111.1 11.6 %collective-permute-start.28 = (bf16[256,768]{1,0:T(8,128)(2,1)S(1)}, bf16[256,768]{1,0:T(8,128)(2,1)S(1)}, u32[]{:S(2)}, u32[]{:S(2)}) collective-permute-start(bf16[256,768]{1,0:T(8,128)(2,1)S(1)} %get-tuple-element.227), channel_id=1, source_target_pairs={{0,1},{1,0},{2,3},{3,2},{4,5},{5,4},{6,7},{7,6},{8,9},{9,8},{10,11... | collective-permute-start | bytes 1179656 | tf_op jit(solution)/shard_map/ppermute | solution.py:463
  112.8 15.4 %collective-permute-start.32 = (bf16[2,192,768]{2,1,0:T(8,128)(2,1)S(1)}, bf16[2,192,768]{2,1,0:T(8,128)(2,1)S(1)}, u32[]{:S(2)}, u32[]{:S(2)}) collective-permute-start(bf16[2,192,768]{2,1,0:T(8,128)(2,1)S(1)} %get-tuple-element.232), channel_id=1, source_target_pairs={{0,8},{4,12},{8,0},{12,4},{16,24},{20,28},{24,16},{28,20},{1,9},{5... | collective-permute-start | bytes 1769480 | tf_op jit(solution)/shard_map/ppermute | solution.py:475
  114.2 16.3 %collective-permute-start.33 = (bf16[2,192,768]{2,1,0:T(8,128)(2,1)S(1)}, bf16[2,192,768]{2,1,0:T(8,128)(2,1)S(1)}, u32[]{:S(2)}, u32[]{:S(2)}) collective-permute-start(bf16[2,192,768]{2,1,0:T(8,128)(2,1)S(1)} %get-tuple-element.233), channel_id=1, source_target_pairs={{0,16},{4,20},{8,24},{12,28},{16,0},{20,4},{24,8},{28,12},{1,17},{... | collective-permute-start | bytes 1769480 | tf_op jit(solution)/shard_map/ppermute | solution.py:475
  115.7 25.4 %collective-permute-start.34 = (bf16[2,192,768]{2,1,0:T(8,128)(2,1)S(1)}, bf16[2,192,768]{2,1,0:T(8,128)(2,1)S(1)}, u32[]{:S(2)}, u32[]{:S(2)}) collective-permute-start(bf16[2,192,768]{2,1,0:T(8,128)(2,1)S(1)} %get-tuple-element.234), channel_id=1, source_target_pairs={{0,24},{4,28},{8,16},{12,20},{16,8},{20,12},{24,0},{28,4},{1,25},{... | collective-permute-start | bytes 1769480 | tf_op jit(solution)/shard_map/ppermute | solution.py:475
  124.2 17.6 %collective-permute-start.36 = (bf16[448,768]{1,0:T(8,128)(2,1)S(1)}, bf16[448,768]{1,0:T(8,128)(2,1)S(1)}, u32[]{:S(2)}, u32[]{:S(2)}) collective-permute-start(bf16[448,768]{1,0:T(8,128)(2,1)S(1)} %get-tuple-element.247), channel_id=1, source_target_pairs={{0,4},{4,0},{8,12},{12,8},{1,5},{5,1},{9,13},{13,9},{2,6},{6,2},{1... | collective-permute-start | bytes 2064392 | tf_op jit(solution)/shard_map/ppermute | solution.py:466
  124.3 19.2 %collective-permute-start.40 = (bf16[128,768]{1,0:T(8,128)(2,1)S(1)}, bf16[128,768]{1,0:T(8,128)(2,1)S(1)}, u32[]{:S(2)}, u32[]{:S(2)}) collective-permute-start(bf16[128,768]{1,0:T(8,128)(2,1)S(1)} %get-tuple-element.172.refs_0_), channel_id=1, source_target_pairs={{0,1},{1,0},{2,3},{3,2},{4,5},{5,4},{6,7},{7,6},{8,9},{9,8},{10,11... | collective-permute-start | bytes 589832 | tf_op jit(solution)/shard_map/ppermute | solution.py:463
  128.1 16.9 %collective-permute-start.41 = (bf16[128,768]{1,0:T(8,128)(2,1)S(1)}, bf16[128,768]{1,0:T(8,128)(2,1)S(1)}, u32[]{:S(2)}, u32[]{:S(2)}) collective-permute-start(bf16[128,768]{1,0:T(8,128)(2,1)S(1)} %get-tuple-element.177.refs_1_), channel_id=1, source_target_pairs={{0,1},{1,0},{2,3},{3,2},{4,5},{5,4},{6,7},{7,6},{8,9},{9,8},{10,11... | collective-permute-start | bytes 589832 | tf_op jit(solution)/shard_map/ppermute | solution.py:463
  130.5 17.3 %collective-permute-start.31 = (bf16[256,768]{1,0:T(8,128)(2,1)S(1)}, bf16[256,768]{1,0:T(8,128)(2,1)S(1)}, u32[]{:S(2)}, u32[]{:S(2)}) collective-permute-start(bf16[256,768]{1,0:T(8,128)(2,1)S(1)} %add_convert_fusion.5), channel_id=1, source_target_pairs={{0,2},{1,3},{2,0},{3,1},{4,6},{5,7},{6,4},{7,5},{8,10},{9,11},{10,... | collective-permute-start | bytes 1179656 | tf_op jit(solution)/shard_map/ppermute | solution.py:463
  141.4 9.4 %collective-permute-start.35 = (bf16[192,768]{1,0:T(8,128)(2,1)S(1)}, bf16[192,768]{1,0:T(8,128)(2,1)S(1)}, u32[]{:S(2)}, u32[]{:S(2)}) collective-permute-start(bf16[192,768]{1,0:T(8,128)(2,1)S(1)} %slice_bitcast_fusion), channel_id=1, source_target_pairs={{0,1},{1,0},{2,3},{3,2},{4,5},{5,4},{6,7},{7,6},{8,9},{9,8},{10,11... | collective-permute-start | bytes 884744 | tf_op jit(solution)/shard_map/ppermute | solution.py:463
  142.0 8.8 %collective-permute-start.37 = (bf16[112,768]{1,0:T(8,128)(2,1)S(1)}, bf16[112,768]{1,0:T(8,128)(2,1)S(1)}, u32[]{:S(2)}, u32[]{:S(2)}) collective-permute-start(bf16[112,768]{1,0:T(8,128)(2,1)S(1)} %get-tuple-element.282), channel_id=1, source_target_pairs={{0,8},{4,12},{8,0},{12,4},{16,24},{20,28},{24,16},{28,20},{1,9},{5... | collective-permute-start | bytes 516104 | tf_op jit(solution)/shard_map/ppermute | solution.py:475
  151.5 10.6 %collective-permute-start.42 = (bf16[304,768]{1,0:T(8,128)(2,1)S(1)}, bf16[304,768]{1,0:T(8,128)(2,1)S(1)}, u32[]{:S(2)}, u32[]{:S(2)}) collective-permute-start(bf16[304,768]{1,0:T(8,128)(2,1)S(1)} %grad_share.1.refs_0_), channel_id=1, source_target_pairs={{0,8},{4,12},{8,0},{12,4},{16,24},{20,28},{24,16},{28,20},{1,9},{5... | collective-permute-start | bytes 1400840 | tf_op jit(solution)/shard_map/ppermute | solution.py:475
  152.8 9.0 %collective-permute-start.43 = (bf16[256,768]{1,0:T(8,128)(2,1)S(1)}, bf16[256,768]{1,0:T(8,128)(2,1)S(1)}, u32[]{:S(2)}, u32[]{:S(2)}) collective-permute-start(bf16[256,768]{1,0:T(8,128)(2,1)S(1)} %fusion.refs_0_), channel_id=1, source_target_pairs={{0,1},{1,0},{2,3},{3,2},{4,5},{5,4},{6,7},{7,6},{8,9},{9,8},{10,11... | collective-permute-start | bytes 1179656 | tf_op jit(solution)/shard_map/ppermute | solution.py:463
  154.6 13.6 %collective-permute-start.44 = (bf16[304,768]{1,0:T(8,128)(2,1)S(1)}, bf16[304,768]{1,0:T(8,128)(2,1)S(1)}, u32[]{:S(2)}, u32[]{:S(2)}) collective-permute-start(bf16[304,768]{1,0:T(8,128)(2,1)S(1)} %grad_share.1.refs_0_), channel_id=1, source_target_pairs={{0,16},{4,20},{8,24},{12,28},{16,0},{20,4},{24,8},{28,12},{1,17},{... | collective-permute-start | bytes 1400840 | tf_op jit(solution)/shard_map/ppermute | solution.py:475
  156.1 19.6 %collective-permute-start.45 = (bf16[304,768]{1,0:T(8,128)(2,1)S(1)}, bf16[304,768]{1,0:T(8,128)(2,1)S(1)}, u32[]{:S(2)}, u32[]{:S(2)}) collective-permute-start(bf16[304,768]{1,0:T(8,128)(2,1)S(1)} %grad_share.1.refs_0_), channel_id=1, source_target_pairs={{0,24},{4,28},{8,16},{12,20},{16,8},{20,12},{24,0},{28,4},{1,25},{... | collective-permute-start | bytes 1400840 | tf_op jit(solution)/shard_map/ppermute | solution.py:475
  156.9 18.8 %collective-permute-start.46 = (bf16[304,768]{1,0:T(8,128)(2,1)S(1)}, bf16[304,768]{1,0:T(8,128)(2,1)S(1)}, u32[]{:S(2)}, u32[]{:S(2)}) collective-permute-start(bf16[304,768]{1,0:T(8,128)(2,1)S(1)} %grad_share.1.refs_0_), channel_id=1, source_target_pairs={{0,4},{4,0},{8,12},{12,8},{1,5},{5,1},{9,13},{13,9},{2,6},{6,2},{1... | collective-permute-start | bytes 1400840 | tf_op jit(solution)/shard_map/ppermute | solution.py:466
  163.6 12.1 %collective-permute-start.47 = (bf16[304,768]{1,0:T(8,128)(2,1)S(1)}, bf16[304,768]{1,0:T(8,128)(2,1)S(1)}, u32[]{:S(2)}, u32[]{:S(2)}) collective-permute-start(bf16[304,768]{1,0:T(8,128)(2,1)S(1)} %collective-permute-done.42.refs_1_), channel_id=1, source_target_pairs={{0,4},{4,0},{8,12},{12,8},{1,5},{5,1},{9,13},{13,9},{2,6},{6,2},{1... | collective-permute-start | bytes 1400840 | tf_op jit(solution)/shard_map/ppermute | solution.py:466
  (59 other events, 464.7 us)

commit v10 on v9

--- a/solution.py
+++ b/solution.py
@@ -413,19 +413,37 @@
     share[rows:, :] = total.astype(bf16)
 
 
+def widen(at, members, mine, other, g_in, g_outer, wide, sems):
+    first = at[1] == 0
+    rows = wide.shape[2]
+    copies = []
+    for c, s in enumerate(members):
+        here = pl.ds(pl.multiple_of((at[3] ^ s) * rows, rows), rows)
+        a, b = mine[c][:rows, :], other[c][:rows, :]
+        wide[0, c] = pick(first, a, b).astype(f32)
+        wide[1, c] = pick(first, b, a).astype(f32)
+        for k, ref in enumerate((g_in, g_outer)):
+            copies.append(pltpu.make_async_copy(wide.at[k, c], ref.at[here, :], sems.at[2 * c + k]))
+            copies[-1].start()
+    return copies
+
+
+def early_kernel(m, at, *refs):
+    count = m - 1
+    for copy in widen(at, range(count), refs[:count], refs[count : 2 * count], *refs[2 * count :]):
+        copy.wait()
+
+
 def final_kernel(m, at, *refs):
     mine, other = refs[:m], refs[m : 2 * m]
-    g_in, g_outer, g_out, g_q, g_k, g_v, *vectors, packed = refs[2 * m :]
+    g_in, g_outer, g_out, g_q, g_k, g_v, *vectors, packed, wide, sems = refs[2 * m + 2 :]
     first = at[1] == 0
-    rows = g_in.shape[0] // m
+    rows = wide.shape[2]
+    copies = widen(at, [m - 1], mine[m - 1 :], other[m - 1 :], g_in, g_outer, wide, sems)
     for s in range(m):
         i = at[3] ^ s
-        a, b = mine[s], other[s]
-        here = pl.ds(pl.multiple_of(i * rows, rows), rows)
-        g_in[here, :] = pick(first, a[:rows, :], b[:rows, :]).astype(f32)
-        g_outer[here, :] = pick(first, b[:rows, :], a[:rows, :]).astype(f32)
-        packed[0, i] = pick(first, a[rows:, :], b[rows:, :])
-        packed[1, i] = pick(first, b[rows:, :], a[rows:, :])
+        packed[0, i] = pick(first, mine[s][rows:, :], other[s][rows:, :])
+        packed[1, i] = pick(first, other[s][rows:, :], mine[s][rows:, :])
     width = g_q.shape[0]
     one = join(packed[0, i] for i in range(m)).astype(f32)
     two = join(packed[1, i] for i in range(m)).astype(f32)
@@ -443,6 +461,8 @@
         ref[...] = tail[i]
     b_q[...] = tail[8, :width]
     b_v[...] = jnp.concatenate(values, axis=1)[0]
+    for copy in copies:
+        copy.wait()
 
 
 def rows_kernel(at, *refs):
@@ -748,20 +768,37 @@
         others = [flip(v, 1) for v in [share, held] + shares_in[1:]]
         vector = shape((width,), f32)
         short = shape((local,), f32)
-        square = shape((width, units), f32)
         wide = shape((local, width), f32)
+        squares = (pltpu.HBM((width, units), f32), pltpu.HBM((units, width), f32))
+        rows1 = width // m
+
+        def grads_out(kernel, outs, arrays, before, members, scratch, us, name):
+            return pl.pallas_call(
+                kernel,
+                out_shape=squares + outs,
+                in_specs=[SMEM] + [VMEM] * len(arrays) + [HBM] * len(before),
+                out_specs=(HBM,) * 2 + (VMEM,) * len(outs),
+                scratch_shapes=scratch
+                + [pltpu.VMEM((2, members, rows1, width), f32), pltpu.SemaphoreType.DMA((2 * members,))],
+                input_output_aliases={1 + len(arrays) + k: k for k in range(len(before))},
+                compiler_params=pltpu.CompilerParams(vmem_limit_bytes=24 * MIB),
+                cost_estimate=pl.CostEstimate(
+                    flops=int(us * FLOPS_US), bytes_accessed=1, transcendentals=0
+                ),
+                name=name,
+            )(at, *arrays, *before)
+
+        early = grads_out(
+            functools.partial(early_kernel, m), (), (*mine[:-1], *others[:-1]), (), m - 1, [], 2.0,
+            "early_grads",
+        )
         (
             g_w_inner, g_w_outer, g_w_out, g_q, g_k, g_v, g_gain1, g_bias1, g_b_out, g_gain2, g_bias2,
             g_b_outer, g_b_inner, g_b_query, g_b_value,
-        ) = call(
-            functools.partial(final_kernel, m),
-            (square,) * 2 + (wide,) * 4 + (vector,) * 7 + (short,) * 2,
+        ) = grads_out(
+            functools.partial(final_kernel, m), (wide,) * 4 + (vector,) * 7 + (short,) * 2,
+            (*mine, *others), tuple(early), 1, [pltpu.VMEM((2, m, rows2 // m, width), bf16)], 2.0,
             "grads_out",
-            (at, *mine, *others),
-            us=4.0,
-            vmem=24,
-            scalars=1,
-            scratch=[pltpu.VMEM((2, m, rows2 // m, width), bf16)],
         )
         return (
             output, d_tokens, g_q.T, g_b_query, g_k.T, g_v.T, g_b_value, g_w_out, g_b_out, g_gain1,

time: 182 us -> 181 us (level)
  waiting for transfers between devices: 90.8 us -> 87.3 us
  Pallas kernels: 39.4 us -> 41.3 us
    pallas_call x0 -> x2, Pallas kernels: none -> 5.74 us  [grads_out(): pl.pallas_call(kernel, out_shape=squares + outs, in_specs=[SMEM] + [VMEM]...]
    pallas_call x18 -> x17, Pallas kernels: 31.3 us -> 27.4 us  [call(): pl.pallas_call(kernel, out_shape=outs, in_specs=[SMEM] * scalars + [VMEM]...]
    ppermute x21, waiting for transfers between devices: 51 us -> 48.6 us  [swap(): return lax.ppermute(v, 'tensor', [(i, i ^ bit) for i in range(n)])]
where the time goes in v10:
time: 181 us
  waiting for transfers between devices  87.3 us (48%)
  starting transfers between devices  45.1 us (25%)
  Pallas kernels  41.3 us (23%)
  local copies, waits for them, and re-layouts  4.24 us (2%)
    ppermute x21, waiting for transfers between devices, swap(): return lax.ppermute(v, 'tensor', [(i, i ^ bit) for i in range(n)])  48.6 us
    pallas_call x17, Pallas kernels, call(): pl.pallas_call(kernel, out_shape=outs, in_specs=[SMEM] * scalars + [VMEM]...  27.4 us
    ppermute x9, waiting for transfers between devices, flip_member(): return lax.ppermute(v, ('dp', 'blk'), perm)  27 us
    ppermute x21, starting transfers between devices, swap(): return lax.ppermute(v, 'tensor', [(i, i ^ bit) for i in range(n)])  23.1 us
    ppermute x9, starting transfers between devices, flip_member(): return lax.ppermute(v, ('dp', 'blk'), perm)  11.3 us
    ppermute x17, waiting for transfers between devices, flip(): return lax.ppermute(v, 'blk', [(i, i ^ bit) for i in range(n_blk)])  10.3 us
    ppermute x17, starting transfers between devices, flip(): return lax.ppermute(v, 'blk', [(i, i ^ bit) for i in range(n_blk)])  7 us
    pallas_call x2, Pallas kernels, grads_out(): pl.pallas_call(kernel, out_shape=squares + outs, in_specs=[SMEM] + [VMEM]...  5.74 us
  transfers between devices with their start and end apart: 50, of which 26 were waited for; matrix products, arithmetic and copies ran while one was open for 1% of the time, Pallas kernels for 16%

profile of v10, /device:TPU:0, one launch (start us, length us, event | category | flops | bytes accessed | tf_op | source)
XLA Modules:
  0.0 181.0 jit_solution(17449120047548109174)
XLA Ops:
  1.5 2.5 %front.1 = (bf16[512,384]{1,0:T(8,128)(2,1)S(1)}, bf16[240,768]{1,0:T(8,128)(2,1)S(1)}, bf16[48,768]{1,0:T(8,128)(2,1)S(1)}) custom-call(s32[5]{0:T(128)S(1)} %stack.23.at, bf16[512,768]{1,0:T(8,128)(2,1)} %bitcast.39, bf16[192,768]{1,0:T(8,128)(2,1)} %bitcast.45, bf16[192,768]{1,0:T(8,128)(2,1)} %bitcast.48, bf16[768,768]{1,0:T(8,128)(2,1)} %w_in.9, ...), custom_call_target="tpu_custom_call" | custom-call | tf_op jit(solution)/shard_map/front/pallas_call | solution.py:536
  4.0 3.0 %collective-permute-start = (bf16[512,384]{1,0:T(8,128)(2,1)S(1)}, bf16[512,384]{1,0:T(8,128)(2,1)S(1)}, u32[]{:S(2)}, u32[]{:S(2)}) collective-permute-start(bf16[512,384]{1,0:T(8,128)(2,1)S(1)} %get-tuple-element.151.refs_0_), channel_id=1, source_target_pairs={{0,8},{4,12},{8,0},{12,4},{1,9},{5,13},{9,1},{13,5},{2,10},{6,14},... | collective-permute-start | bytes 1179656 | tf_op jit(solution)/shard_map/ppermute | solution.py:486
  8.6 2.5 %collective-permute-start.4 = (bf16[48,768]{1,0:T(8,128)(2,1)S(1)}, bf16[48,768]{1,0:T(8,128)(2,1)S(1)}, u32[]{:S(2)}, u32[]{:S(2)}) collective-permute-start(bf16[48,768]{1,0:T(8,128)(2,1)S(1)} %get-tuple-element.154), channel_id=1, source_target_pairs={{0,3},{1,2},{2,1},{3,0},{4,7},{5,6},{6,5},{7,4},{8,11},{9,10},{10,... | collective-permute-start | bytes 221192 | tf_op jit(solution)/shard_map/ppermute | solution.py:483
  11.2 1.8 collective-permute-start.1
  13.0 6.5 %collective-permute-done.1 = f32[768]{0:T(1024)S(1)} collective-permute-done((f32[768]{0:T(1024)S(1)}, f32[768]{0:T(1024)S(1)}, u32[]{:S(2)}, u32[]{:S(2)}) %collective-permute-start.1) | collective-permute-done | bytes 3104 | tf_op jit(solution)/shard_map/ppermute | solution.py:483
  19.5 2.0 %collective-permute-done.4 = bf16[48,768]{1,0:T(8,128)(2,1)S(1)} collective-permute-done((bf16[48,768]{1,0:T(8,128)(2,1)S(1)}, bf16[48,768]{1,0:T(8,128)(2,1)S(1)}, u32[]{:S(2)}, u32[]{:S(2)}) %collective-permute-start.4) | collective-permute-done | bytes 73760 | tf_op jit(solution)/shard_map/ppermute | solution.py:483
  26.0 5.6 %attend.1 = (bf16[384,128]{1,0:T(8,128)(2,1)S(1)}, bf16[384,128]{1,0:T(8,128)(2,1)S(1)}, bf16[768,512]{1,0:T(8,128)(2,1)}, bf16[768,512]{1,0:T(8,128)(2,1)}, bf16[768,128]{1,0:T(8,128)(2,1)}) custom-call(s32[5]{0:T(128)S(1)} %stack.23.at, s32[4]{0:T(128)S(1)} %copy-done.28, s32[4,4]{1,0:T(4,128)S(1)} %copy-done.26, bf16[512,384]{1,0:T(8,128)(2,1)S(1)} %query_rows.1.q, ...), custom_call_target="tpu_custom_call" | custom-call | flops 49999998976 | bytes 1 | tf_op jit(solution)/shard_map/attend/pallas_call | solution.py:572
  31.6 3.0 %collective-permute-start.10 = (bf16[384,128]{1,0:T(8,128)(2,1)S(1)}, bf16[384,128]{1,0:T(8,128)(2,1)S(1)}, u32[]{:S(2)}, u32[]{:S(2)}) collective-permute-start(bf16[384,128]{1,0:T(8,128)(2,1)S(1)} %get-tuple-element.159), channel_id=1, source_target_pairs={{0,3},{1,2},{2,1},{3,0},{4,7},{5,6},{6,5},{7,4},{8,11},{9,10},{10,... | collective-permute-start | bytes 294920 | tf_op jit(solution)/shard_map/ppermute | solution.py:483
  44.5 2.0 %collective-permute-done.15.refs_5_ = bf16[192,768]{1,0:T(8,128)(2,1)} collective-permute-done((bf16[192,768]{1,0:T(8,128)(2,1)}, bf16[192,768]{1,0:T(8,128)(2,1)}, u32[]{:S(2)}, u32[]{:S(2)}) %collective-permute-start.15) | collective-permute-done | bytes 294944 | tf_op jit(solution)/shard_map/ppermute | solution.py:486
  48.1 2.3 %ffn.2 = (bf16[128,768]{1,0:T(8,128)(2,1)S(1)}, f32[128,768]{1,0:T(8,128)S(1)}, f32[128,128]{1,0:T(8,128)S(1)}, bf16[128,768]{1,0:T(8,128)(2,1)S(1)}, bf16[128,7...) custom-call(s32[5]{0:T(128)S(1)} %stack.23.at, ...), custom_call_target="tpu_custom_call" | custom-call | flops 2400000000 | bytes 1 | tf_op jit(solution)/shard_map/ffn/pallas_call | solution.py:73
  51.7 2.3 %ffn.3 = (bf16[128,768]{1,0:T(8,128)(2,1)S(1)}, f32[128,768]{1,0:T(8,128)S(1)}, f32[128,128]{1,0:T(8,128)S(1)}, bf16[128,768]{1,0:T(8,128)(2,1)S(1)}, bf16[128,7...) custom-call(s32[5]{0:T(128)S(1)} %stack.23.at, bf16[512,768]{1,0:T(8,128)(2,1)S(1)} %bitcast.42, ...), custom_call_target="tpu_custom_call" | custom-call | flops 2400000000 | bytes 1 | tf_op jit(solution)/shard_map/ffn/pallas_call | solution.py:73
  54.1 1.7 collective-permute-start.18
  55.8 11.7 %collective-permute-done.17.theirs = bf16[128,768]{1,0:T(8,128)(2,1)S(1)} collective-permute-done((bf16[128,768]{1,0:T(8,128)(2,1)S(1)}, bf16[128,768]{1,0:T(8,128)(2,1)S(1)}, u32[]{:S(2)}, u32[]{:S(2)}) %collective-permute-start.17) | collective-permute-done | bytes 196640 | tf_op jit(solution)/shard_map/ppermute | solution.py:483
  67.5 2.7 %ffn_back.2 = (bf16[128,768]{1,0:T(8,128)(2,1)S(1)}, bf16[128,768]{1,0:T(8,128)(2,1)S(1)}, bf16[128,768]{1,0:T(8,128)(2,1)S(1)}, bf16[128,768]{1,0:T(8,128)(2,1)...) custom-call(s32[5]{0:T(128)S(1)} %stack.23.at, bf16[512,768]{1,0:T(8,128)(2,1)S(1)} %bitcast.52, ...), custom_call_target="tpu_custom_call" | custom-call | flops 2700000000 | bytes 1 | tf_op jit(solution)/shard_map/ffn_back/pallas_call | solution.py:73
  71.0 2.7 %ffn_back.3 = (bf16[128,768]{1,0:T(8,128)(2,1)S(1)}, bf16[128,768]{1,0:T(8,128)(2,1)S(1)}, bf16[128,768]{1,0:T(8,128)(2,1)S(1)}, bf16[128,768]{1,0:T(8,128)(2,1)...) custom-call(s32[5]{0:T(128)S(1)} %stack.23.at, bf16[512,768]{1,0:T(8,128)(2,1)S(1)} %bitcast.53, ...), custom_call_target="tpu_custom_call" | custom-call | flops 2700000000 | bytes 1 | tf_op jit(solution)/shard_map/ffn_back/pallas_call | solution.py:73
  73.8 2.2 %collective-permute-start.20 = (bf16[128,768]{1,0:T(8,128)(2,1)S(1)}, bf16[128,768]{1,0:T(8,128)(2,1)S(1)}, u32[]{:S(2)}, u32[]{:S(2)}) collective-permute-start(bf16[128,768]{1,0:T(8,128)(2,1)S(1)} %get-tuple-element.185.mine), channel_id=1, source_target_pairs={{0,2},{1,3},{2,0},{3,1},{4,6},{5,7},{6,4},{7,5},{8,10},{9,11},{10,... | collective-permute-start | bytes 589832 | tf_op jit(solution)/shard_map/ppermute | solution.py:483
  76.0 2.2 %ffn_grads.1 = (bf16[4,2,192,768]{3,2,1,0:T(8,128)(2,1)S(1)}, bf16[4,2,192,768]{3,2,1,0:T(8,128)(2,1)S(1)}) custom-call(s32[5]{0:T(128)S(1)} %stack.23.at, bf16[128,768]{1,0:T(8,128)(2,1)S(1)} %get-tuple-element.196.refs_0_, bf16[128,768]{1,0:T(8,128)(2,1)S(1)} %get-tuple-element.197.refs_1_, bf16[128,768]{1,0:T(8,128)(2,1)S(1)} %get-tuple-element.198.refs_2_, ...), custom_call_target="tpu_custom_call" | custom-call | flops 49999998976 | bytes 1 | tf_op jit(solution)/shard_map/ffn_grads/pallas_call | solution.py:73
  78.3 7.1 %collective-permute-done.19.theirs = bf16[128,768]{1,0:T(8,128)(2,1)S(1)} collective-permute-done((bf16[128,768]{1,0:T(8,128)(2,1)S(1)}, bf16[128,768]{1,0:T(8,128)(2,1)S(1)}, u32[]{:S(2)}, u32[]{:S(2)}) %collective-permute-start.19) | collective-permute-done | bytes 196640 | tf_op jit(solution)/shard_map/ppermute | solution.py:483
  86.7 2.8 %collective-permute-done.20.theirs = bf16[128,768]{1,0:T(8,128)(2,1)S(1)} collective-permute-done((bf16[128,768]{1,0:T(8,128)(2,1)S(1)}, bf16[128,768]{1,0:T(8,128)(2,1)S(1)}, u32[]{:S(2)}, u32[]{:S(2)}) %collective-permute-start.20) | collective-permute-done | bytes 196640 | tf_op jit(solution)/shard_map/ppermute | solution.py:483
  91.2 2.7 %attend_back.2 = (bf16[256,192]{1,0:T(8,128)(2,1)S(1)}, bf16[2,2,384,128]{3,2,1,0:T(8,128)(2,1)S(1)}, bf16[2,2,384,128]{3,2,1,0:T(8,128)(2,1)S(1)}) custom-call(s32[5]{0:T(128)S(1)} %stack.23.at, bf16[192,128]{1,0:T(8,128)(2,1)S(1)} %get-tuple-element.184.first, bf16[192,128]{1,0:T(8,128)(2,1)S(1)} %get-tuple-element.189.second, ...), custom_call_target="tpu_custom_call" | custom-call | flops 49999998976 | bytes 1 | tf_op jit(solution)/shard_map/attend_back/pallas_call | solution.py:73
  95.1 2.7 %attend_back.3 = (bf16[256,192]{1,0:T(8,128)(2,1)S(1)}, bf16[2,2,384,128]{3,2,1,0:T(8,128)(2,1)S(1)}, bf16[2,2,384,128]{3,2,1,0:T(8,128)(2,1)S(1)}) custom-call(s32[5]{0:T(128)S(1)} %stack.23.at, bf16[192,128]{1,0:T(8,128)(2,1)S(1)} %collective-permute-done.21.first, bf16[192,128]{1,0:T(8,128)(2,1)S(1)} %collective-permute-done.22.second, ...), custom_call_target="tpu_custom_call" | custom-call | flops 49999998976 | bytes 1 | tf_op jit(solution)/shard_map/attend_back/pallas_call | solution.py:73
  103.9 3.6 %collective-permute-done.27.far = bf16[2,384,128]{2,1,0:T(8,128)(2,1)S(1)} collective-permute-done((bf16[2,384,128]{2,1,0:T(8,128)(2,1)S(1)}, bf16[2,384,128]{2,1,0:T(8,128)(2,1)S(1)}, u32[]{:S(2)}, u32[]{:S(2)}) %collective-permute-start.27) | collective-permute-done | bytes 196640 | tf_op jit(solution)/shard_map/ppermute | solution.py:486
  107.5 3.4 %collective-permute-done.25.far = bf16[2,384,128]{2,1,0:T(8,128)(2,1)S(1)} collective-permute-done((bf16[2,384,128]{2,1,0:T(8,128)(2,1)S(1)}, bf16[2,384,128]{2,1,0:T(8,128)(2,1)S(1)}, u32[]{:S(2)}, u32[]{:S(2)}) %collective-permute-start.25) | collective-permute-done | bytes 196640 | tf_op jit(solution)/shard_map/ppermute | solution.py:486
  117.1 4.8 %collective-permute-done.28 = bf16[256,768]{1,0:T(8,128)(2,1)S(1)} collective-permute-done((bf16[256,768]{1,0:T(8,128)(2,1)S(1)}, bf16[256,768]{1,0:T(8,128)(2,1)S(1)}, u32[]{:S(2)}, u32[]{:S(2)}) %collective-permute-start.28) | collective-permute-done | bytes 393248 | tf_op jit(solution)/shard_map/ppermute | solution.py:483
  125.2 3.2 %collective-permute-done.32 = bf16[2,192,768]{2,1,0:T(8,128)(2,1)S(1)} collective-permute-done((bf16[2,192,768]{2,1,0:T(8,128)(2,1)S(1)}, bf16[2,192,768]{2,1,0:T(8,128)(2,1)S(1)}, u32[]{:S(2)}, u32[]{:S(2)}) %collective-permute-start.32) | collective-permute-done | bytes 589856 | tf_op jit(solution)/shard_map/ppermute | solution.py:495
  130.2 11.0 %collective-permute-done.34 = bf16[2,192,768]{2,1,0:T(8,128)(2,1)S(1)} collective-permute-done((bf16[2,192,768]{2,1,0:T(8,128)(2,1)S(1)}, bf16[2,192,768]{2,1,0:T(8,128)(2,1)S(1)}, u32[]{:S(2)}, u32[]{:S(2)}) %collective-permute-start.34) | collective-permute-done | bytes 589856 | tf_op jit(solution)/shard_map/ppermute | solution.py:495
  147.1 3.9 %collective-permute-done.35.near1 = bf16[192,768]{1,0:T(8,128)(2,1)S(1)} collective-permute-done((bf16[192,768]{1,0:T(8,128)(2,1)S(1)}, bf16[192,768]{1,0:T(8,128)(2,1)S(1)}, u32[]{:S(2)}, u32[]{:S(2)}) %collective-permute-start.35) | collective-permute-done | bytes 294944 | tf_op jit(solution)/shard_map/ppermute | solution.py:483
  157.7 3.6 %collective-permute-done.43.refs_1_ = bf16[256,768]{1,0:T(8,128)(2,1)S(1)} collective-permute-done((bf16[256,768]{1,0:T(8,128)(2,1)S(1)}, bf16[256,768]{1,0:T(8,128)(2,1)S(1)}, u32[]{:S(2)}, u32[]{:S(2)}) %collective-permute-start.43) | collective-permute-done | bytes 393248 | tf_op jit(solution)/shard_map/ppermute | solution.py:483
  163.0 3.9 %collective-permute-done.44.refs_2_ = bf16[304,768]{1,0:T(8,128)(2,1)S(1)} collective-permute-done((bf16[304,768]{1,0:T(8,128)(2,1)S(1)}, bf16[304,768]{1,0:T(8,128)(2,1)S(1)}, u32[]{:S(2)}, u32[]{:S(2)}) %collective-permute-start.44) | collective-permute-done | bytes 466976 | tf_op jit(solution)/shard_map/ppermute | solution.py:495
  167.4 7.7 %collective-permute-done.45.refs_3_ = bf16[304,768]{1,0:T(8,128)(2,1)S(1)} collective-permute-done((bf16[304,768]{1,0:T(8,128)(2,1)S(1)}, bf16[304,768]{1,0:T(8,128)(2,1)S(1)}, u32[]{:S(2)}, u32[]{:S(2)}) %collective-permute-start.45) | collective-permute-done | bytes 466976 | tf_op jit(solution)/shard_map/ppermute | solution.py:495
  175.1 2.5 %early_grads.1 = (f32[768,768]{1,0:T(8,128)}, f32[768,768]{1,0:T(8,128)}) custom-call(s32[5]{0:T(128)S(1)} %stack.23.at, bf16[304,768]{1,0:T(8,128)(2,1)S(1)} %grad_share.1.refs_0_, bf16[304,768]{1,0:T(8,128)(2,1)S(1)} %collective-permute-done.42.refs_1_, bf16[304,768]{1,0:T(8,128)(2,1)S(1)} %collective-permute-done.44.refs_2_, ...), custom_call_target="tpu_custom_call" | custom-call | flops 2000000000 | bytes 1 | tf_op jit(solution)/shard_map/early_grads/pallas_call | solution.py:776
  177.6 3.3 %grads_out.1 = (f32[768,768]{1,0:T(8,128)}, f32[768,768]{1,0:T(8,128)}, f32[192,768]{1,0:T(8,128)}, f32[192,768]{1,0:T(8,128)}, f32[192,768]{1,0:T(8,128)}, /*in...) custom-call(s32[5]{0:T(128)S(1)} %stack.23.at, ...), custom_call_target="tpu_custom_call", output_to_operand_aliasing={{0}: (9, {}), {1}: (10, {})} | custom-call | flops 2000000000 | bytes 1 | tf_op jit(solution)/shard_map/grads_out/pallas_call | solution.py:776
  (192 shorter events, 56.4 us)
Async XLA Ops:
  4.0 17.5 %collective-permute-start = (bf16[512,384]{1,0:T(8,128)(2,1)S(1)}, bf16[512,384]{1,0:T(8,128)(2,1)S(1)}, u32[]{:S(2)}, u32[]{:S(2)}) collective-permute-start(bf16[512,384]{1,0:T(8,128)(2,1)S(1)} %get-tuple-element.151.refs_0_), channel_id=1, source_target_pairs={{0,8},{4,12},{8,0},{12,4},{1,9},{5,13},{9,1},{13,5},{2,10},{6,14},... | collective-permute-start | bytes 1179656 | tf_op jit(solution)/shard_map/ppermute | solution.py:486
  7.0 14.5 %collective-permute-start.2 = (bf16[240,768]{1,0:T(8,128)(2,1)S(1)}, bf16[240,768]{1,0:T(8,128)(2,1)S(1)}, u32[]{:S(2)}, u32[]{:S(2)}) collective-permute-start(bf16[240,768]{1,0:T(8,128)(2,1)S(1)} %get-tuple-element.153), channel_id=1, source_target_pairs={{0,1},{1,0},{2,3},{3,2},{4,5},{5,4},{6,7},{7,6},{8,9},{9,8},{10,11... | collective-permute-start | bytes 1105928 | tf_op jit(solution)/shard_map/ppermute | solution.py:483
  8.6 12.9 %collective-permute-start.4 = (bf16[48,768]{1,0:T(8,128)(2,1)S(1)}, bf16[48,768]{1,0:T(8,128)(2,1)S(1)}, u32[]{:S(2)}, u32[]{:S(2)}) collective-permute-start(bf16[48,768]{1,0:T(8,128)(2,1)S(1)} %get-tuple-element.154), channel_id=1, source_target_pairs={{0,3},{1,2},{2,1},{3,0},{4,7},{5,6},{6,5},{7,4},{8,11},{9,10},{10,... | collective-permute-start | bytes 221192 | tf_op jit(solution)/shard_map/ppermute | solution.py:483
  11.0 10.4 %collective-permute-start.3 = (bf16[48,768]{1,0:T(8,128)(2,1)S(1)}, bf16[48,768]{1,0:T(8,128)(2,1)S(1)}, u32[]{:S(2)}, u32[]{:S(2)}) collective-permute-start(bf16[48,768]{1,0:T(8,128)(2,1)S(1)} %get-tuple-element.154), channel_id=1, source_target_pairs={{0,2},{1,3},{2,0},{3,1},{4,6},{5,7},{6,4},{7,5},{8,10},{9,11},{10,... | collective-permute-start | bytes 221192 | tf_op jit(solution)/shard_map/ppermute | solution.py:483
  11.2 8.3 %collective-permute-start.1 = (f32[768]{0:T(1024)S(1)}, f32[768]{0:T(1024)S(1)}, u32[]{:S(2)}, u32[]{:S(2)}) collective-permute-start(f32[768]{0:T(1024)S(1)} %copy-done.34), channel_id=1, source_target_pairs={{0,1},{1,0},{2,3},{3,2},{4,5},{5,4},{6,7},{7,6},{8,9},{9,8},{10,11... | collective-permute-start | bytes 9224 | tf_op jit(solution)/shard_map/ppermute | solution.py:483
  22.1 12.4 %collective-permute-start.13 = (bf16[192,768]{1,0:T(8,128)(2,1)S(1)}, bf16[192,768]{1,0:T(8,128)(2,1)S(1)}, u32[]{:S(2)}, u32[]{:S(2)}) collective-permute-start(bf16[192,768]{1,0:T(8,128)(2,1)S(1)} %slice.18), channel_id=1, source_target_pairs={{0,24},{4,28},{8,16},{12,20},{16,8},{20,12},{24,0},{28,4},{1,25},{... | collective-permute-start | bytes 884744 | tf_op jit(solution)/shard_map/ppermute | solution.py:563
  23.6 14.4 %collective-permute-start.12 = (bf16[192,768]{1,0:T(8,128)(2,1)S(1)}, bf16[192,768]{1,0:T(8,128)(2,1)}, u32[]{:S(2)}, u32[]{:S(2)}) collective-permute-start(bf16[192,768]{1,0:T(8,128)(2,1)S(1)} %slice.18), channel_id=1, source_target_pairs={{0,16},{4,20},{8,24},{12,28},{16,0},{20,4},{24,8},{28,12},{1,17},{... | collective-permute-start | bytes 884744 | tf_op jit(solution)/shard_map/ppermute | solution.py:563
  24.3 19.4 %collective-permute-start.11 = (bf16[336,768]{1,0:T(8,128)(2,1)S(1)}, bf16[336,768]{1,0:T(8,128)(2,1)S(1)}, u32[]{:S(2)}, u32[]{:S(2)}) collective-permute-start(bf16[336,768]{1,0:T(8,128)(2,1)S(1)} %constant_dynamic-update-slice_fusion.refs_0_), channel_id=1, source_target_pairs={{0,8},{4,12},{8,0},{12,4},{16,24},{20,28},{24,16},{28,20},{1,9},{5... | collective-permute-start | bytes 1548296 | tf_op jit(solution)/shard_map/ppermute | solution.py:563
  34.6 8.5 %collective-permute-start.9 = (bf16[384,128]{1,0:T(8,128)(2,1)S(1)}, bf16[384,128]{1,0:T(8,128)(2,1)S(1)}, u32[]{:S(2)}, u32[]{:S(2)}) collective-permute-start(bf16[384,128]{1,0:T(8,128)(2,1)S(1)} %get-tuple-element.160.refs_0_), channel_id=1, source_target_pairs={{0,2},{1,3},{2,0},{3,1},{4,6},{5,7},{6,4},{7,5},{8,10},{9,11},{10,... | collective-permute-start | bytes 294920 | tf_op jit(solution)/shard_map/ppermute | solution.py:483
  50.4 17.1 %collective-permute-start.17 = (bf16[128,768]{1,0:T(8,128)(2,1)S(1)}, bf16[128,768]{1,0:T(8,128)(2,1)S(1)}, u32[]{:S(2)}, u32[]{:S(2)}) collective-permute-start(bf16[128,768]{1,0:T(8,128)(2,1)S(1)} %get-tuple-element.173.mine), channel_id=1, source_target_pairs={{0,2},{1,3},{2,0},{3,1},{4,6},{5,7},{6,4},{7,5},{8,10},{9,11},{10,... | collective-permute-start | bytes 589832 | tf_op jit(solution)/shard_map/ppermute | solution.py:483
  54.1 17.0 %collective-permute-start.18 = (bf16[128,768]{1,0:T(8,128)(2,1)S(1)}, bf16[128,768]{1,0:T(8,128)(2,1)S(1)}, u32[]{:S(2)}, u32[]{:S(2)}) collective-permute-start(bf16[128,768]{1,0:T(8,128)(2,1)S(1)} %get-tuple-element.178.mine), channel_id=1, source_target_pairs={{0,2},{1,3},{2,0},{3,1},{4,6},{5,7},{6,4},{7,5},{8,10},{9,11},{10,... | collective-permute-start | bytes 589832 | tf_op jit(solution)/shard_map/ppermute | solution.py:483
  70.2 15.2 %collective-permute-start.19 = (bf16[128,768]{1,0:T(8,128)(2,1)S(1)}, bf16[128,768]{1,0:T(8,128)(2,1)S(1)}, u32[]{:S(2)}, u32[]{:S(2)}) collective-permute-start(bf16[128,768]{1,0:T(8,128)(2,1)S(1)} %get-tuple-element.180.mine), channel_id=1, source_target_pairs={{0,2},{1,3},{2,0},{3,1},{4,6},{5,7},{6,4},{7,5},{8,10},{9,11},{10,... | collective-permute-start | bytes 589832 | tf_op jit(solution)/shard_map/ppermute | solution.py:483
  73.8 15.7 %collective-permute-start.20 = (bf16[128,768]{1,0:T(8,128)(2,1)S(1)}, bf16[128,768]{1,0:T(8,128)(2,1)S(1)}, u32[]{:S(2)}, u32[]{:S(2)}) collective-permute-start(bf16[128,768]{1,0:T(8,128)(2,1)S(1)} %get-tuple-element.185.mine), channel_id=1, source_target_pairs={{0,2},{1,3},{2,0},{3,1},{4,6},{5,7},{6,4},{7,5},{8,10},{9,11},{10,... | collective-permute-start | bytes 589832 | tf_op jit(solution)/shard_map/ppermute | solution.py:483
  78.2 15.7 %collective-permute-start.23 = (bf16[4,2,192,768]{3,2,1,0:T(8,128)(2,1)S(1)}, bf16[4,2,192,768]{3,2,1,0:T(8,128)(2,1)S(1)}, u32[]{:S(2)}, u32[]{:S(2)}) collective-permute-start(bf16[4,2,192,768]{3,2,1,0:T(8,128)(2,1)S(1)} %get-tuple-element.209), channel_id=1, source_target_pairs={{0,4},{4,0},{8,12},{12,8},{1,5},{5,1},{9,13},{13,9},{2,6},{6,2},{1... | collective-permute-start | bytes 7077896 | tf_op jit(solution)/shard_map/ppermute | solution.py:486
  100.3 10.6 %collective-permute-start.25 = (bf16[2,384,128]{2,1,0:T(8,128)(2,1)S(1)}, bf16[2,384,128]{2,1,0:T(8,128)(2,1)S(1)}, u32[]{:S(2)}, u32[]{:S(2)}) collective-permute-start(bf16[2,384,128]{2,1,0:T(8,128)(2,1)S(1)} %fusion.5), channel_id=1, source_target_pairs={{0,8},{4,12},{8,0},{12,4},{1,9},{5,13},{9,1},{13,5},{2,10},{6,14},... | collective-permute-start | bytes 589832 | tf_op jit(solution)/shard_map/ppermute | solution.py:486
  101.9 13.2 %collective-permute-start.29 = (bf16[144,768]{1,0:T(8,128)(2,1)S(1)}, bf16[144,768]{1,0:T(8,128)(2,1)S(1)}, u32[]{:S(2)}, u32[]{:S(2)}) collective-permute-start(bf16[144,768]{1,0:T(8,128)(2,1)S(1)} %get-tuple-element.230.refs_0_), channel_id=1, source_target_pairs={{0,1},{1,0},{2,3},{3,2},{4,5},{5,4},{6,7},{7,6},{8,9},{9,8},{10,11... | collective-permute-start | bytes 663560 | tf_op jit(solution)/shard_map/ppermute | solution.py:483
  103.5 13.7 %collective-permute-start.30 = (bf16[144,768]{1,0:T(8,128)(2,1)S(1)}, bf16[144,768]{1,0:T(8,128)(2,1)S(1)}, u32[]{:S(2)}, u32[]{:S(2)}) collective-permute-start(bf16[144,768]{1,0:T(8,128)(2,1)S(1)} %get-tuple-element.231.refs_1_), channel_id=1, source_target_pairs={{0,1},{1,0},{2,3},{3,2},{4,5},{5,4},{6,7},{7,6},{8,9},{9,8},{10,11... | collective-permute-start | bytes 663560 | tf_op jit(solution)/shard_map/ppermute | solution.py:483
  111.4 10.5 %collective-permute-start.28 = (bf16[256,768]{1,0:T(8,128)(2,1)S(1)}, bf16[256,768]{1,0:T(8,128)(2,1)S(1)}, u32[]{:S(2)}, u32[]{:S(2)}) collective-permute-start(bf16[256,768]{1,0:T(8,128)(2,1)S(1)} %get-tuple-element.229), channel_id=1, source_target_pairs={{0,1},{1,0},{2,3},{3,2},{4,5},{5,4},{6,7},{7,6},{8,9},{9,8},{10,11... | collective-permute-start | bytes 1179656 | tf_op jit(solution)/shard_map/ppermute | solution.py:483
  113.1 15.4 %collective-permute-start.32 = (bf16[2,192,768]{2,1,0:T(8,128)(2,1)S(1)}, bf16[2,192,768]{2,1,0:T(8,128)(2,1)S(1)}, u32[]{:S(2)}, u32[]{:S(2)}) collective-permute-start(bf16[2,192,768]{2,1,0:T(8,128)(2,1)S(1)} %get-tuple-element.234), channel_id=1, source_target_pairs={{0,8},{4,12},{8,0},{12,4},{16,24},{20,28},{24,16},{28,20},{1,9},{5... | collective-permute-start | bytes 1769480 | tf_op jit(solution)/shard_map/ppermute | solution.py:495
  113.6 16.3 %collective-permute-start.33 = (bf16[2,192,768]{2,1,0:T(8,128)(2,1)S(1)}, bf16[2,192,768]{2,1,0:T(8,128)(2,1)S(1)}, u32[]{:S(2)}, u32[]{:S(2)}) collective-permute-start(bf16[2,192,768]{2,1,0:T(8,128)(2,1)S(1)} %get-tuple-element.235), channel_id=1, source_target_pairs={{0,16},{4,20},{8,24},{12,28},{16,0},{20,4},{24,8},{28,12},{1,17},{... | collective-permute-start | bytes 1769480 | tf_op jit(solution)/shard_map/ppermute | solution.py:495
  115.1 26.1 %collective-permute-start.34 = (bf16[2,192,768]{2,1,0:T(8,128)(2,1)S(1)}, bf16[2,192,768]{2,1,0:T(8,128)(2,1)S(1)}, u32[]{:S(2)}, u32[]{:S(2)}) collective-permute-start(bf16[2,192,768]{2,1,0:T(8,128)(2,1)S(1)} %get-tuple-element.236), channel_id=1, source_target_pairs={{0,24},{4,28},{8,16},{12,20},{16,8},{20,12},{24,0},{28,4},{1,25},{... | collective-permute-start | bytes 1769480 | tf_op jit(solution)/shard_map/ppermute | solution.py:495
  123.5 18.5 %collective-permute-start.36 = (bf16[448,768]{1,0:T(8,128)(2,1)S(1)}, bf16[448,768]{1,0:T(8,128)(2,1)S(1)}, u32[]{:S(2)}, u32[]{:S(2)}) collective-permute-start(bf16[448,768]{1,0:T(8,128)(2,1)S(1)} %get-tuple-element.249), channel_id=1, source_target_pairs={{0,4},{4,0},{8,12},{12,8},{1,5},{5,1},{9,13},{13,9},{2,6},{6,2},{1... | collective-permute-start | bytes 2064392 | tf_op jit(solution)/shard_map/ppermute | solution.py:486
  123.6 20.1 %collective-permute-start.40 = (bf16[128,768]{1,0:T(8,128)(2,1)S(1)}, bf16[128,768]{1,0:T(8,128)(2,1)S(1)}, u32[]{:S(2)}, u32[]{:S(2)}) collective-permute-start(bf16[128,768]{1,0:T(8,128)(2,1)S(1)} %get-tuple-element.174.refs_0_), channel_id=1, source_target_pairs={{0,1},{1,0},{2,3},{3,2},{4,5},{5,4},{6,7},{7,6},{8,9},{9,8},{10,11... | collective-permute-start | bytes 589832 | tf_op jit(solution)/shard_map/ppermute | solution.py:483
  128.4 15.8 %collective-permute-start.41 = (bf16[128,768]{1,0:T(8,128)(2,1)S(1)}, bf16[128,768]{1,0:T(8,128)(2,1)S(1)}, u32[]{:S(2)}, u32[]{:S(2)}) collective-permute-start(bf16[128,768]{1,0:T(8,128)(2,1)S(1)} %get-tuple-element.179.refs_1_), channel_id=1, source_target_pairs={{0,1},{1,0},{2,3},{3,2},{4,5},{5,4},{6,7},{7,6},{8,9},{9,8},{10,11... | collective-permute-start | bytes 589832 | tf_op jit(solution)/shard_map/ppermute | solution.py:483
  129.9 17.3 %collective-permute-start.31 = (bf16[256,768]{1,0:T(8,128)(2,1)S(1)}, bf16[256,768]{1,0:T(8,128)(2,1)S(1)}, u32[]{:S(2)}, u32[]{:S(2)}) collective-permute-start(bf16[256,768]{1,0:T(8,128)(2,1)S(1)} %add_convert_fusion.5), channel_id=1, source_target_pairs={{0,2},{1,3},{2,0},{3,1},{4,6},{5,7},{6,4},{7,5},{8,10},{9,11},{10,... | collective-permute-start | bytes 1179656 | tf_op jit(solution)/shard_map/ppermute | solution.py:483
  141.5 9.5 %collective-permute-start.35 = (bf16[192,768]{1,0:T(8,128)(2,1)S(1)}, bf16[192,768]{1,0:T(8,128)(2,1)S(1)}, u32[]{:S(2)}, u32[]{:S(2)}) collective-permute-start(bf16[192,768]{1,0:T(8,128)(2,1)S(1)} %slice_bitcast_fusion), channel_id=1, source_target_pairs={{0,1},{1,0},{2,3},{3,2},{4,5},{5,4},{6,7},{7,6},{8,9},{9,8},{10,11... | collective-permute-start | bytes 884744 | tf_op jit(solution)/shard_map/ppermute | solution.py:483
  142.2 8.8 %collective-permute-start.39 = (bf16[112,768]{1,0:T(8,128)(2,1)S(1)}, bf16[112,768]{1,0:T(8,128)(2,1)S(1)}, u32[]{:S(2)}, u32[]{:S(2)}) collective-permute-start(bf16[112,768]{1,0:T(8,128)(2,1)S(1)} %get-tuple-element.284), channel_id=1, source_target_pairs={{0,24},{4,28},{8,16},{12,20},{16,8},{20,12},{24,0},{28,4},{1,25},{... | collective-permute-start | bytes 516104 | tf_op jit(solution)/shard_map/ppermute | solution.py:495
  151.2 10.3 %collective-permute-start.42 = (bf16[304,768]{1,0:T(8,128)(2,1)S(1)}, bf16[304,768]{1,0:T(8,128)(2,1)S(1)}, u32[]{:S(2)}, u32[]{:S(2)}) collective-permute-start(bf16[304,768]{1,0:T(8,128)(2,1)S(1)} %grad_share.1.refs_0_), channel_id=1, source_target_pairs={{0,8},{4,12},{8,0},{12,4},{16,24},{20,28},{24,16},{28,20},{1,9},{5... | collective-permute-start | bytes 1400840 | tf_op jit(solution)/shard_map/ppermute | solution.py:495
  152.6 8.7 %collective-permute-start.43 = (bf16[256,768]{1,0:T(8,128)(2,1)S(1)}, bf16[256,768]{1,0:T(8,128)(2,1)S(1)}, u32[]{:S(2)}, u32[]{:S(2)}) collective-permute-start(bf16[256,768]{1,0:T(8,128)(2,1)S(1)} %fusion.refs_0_), channel_id=1, source_target_pairs={{0,1},{1,0},{2,3},{3,2},{4,5},{5,4},{6,7},{7,6},{8,9},{9,8},{10,11... | collective-permute-start | bytes 1179656 | tf_op jit(solution)/shard_map/ppermute | solution.py:483
  153.3 13.6 %collective-permute-start.44 = (bf16[304,768]{1,0:T(8,128)(2,1)S(1)}, bf16[304,768]{1,0:T(8,128)(2,1)S(1)}, u32[]{:S(2)}, u32[]{:S(2)}) collective-permute-start(bf16[304,768]{1,0:T(8,128)(2,1)S(1)} %grad_share.1.refs_0_), channel_id=1, source_target_pairs={{0,16},{4,20},{8,24},{12,28},{16,0},{20,4},{24,8},{28,12},{1,17},{... | collective-permute-start | bytes 1400840 | tf_op jit(solution)/shard_map/ppermute | solution.py:495
  154.7 20.3 %collective-permute-start.46 = (bf16[304,768]{1,0:T(8,128)(2,1)S(1)}, bf16[304,768]{1,0:T(8,128)(2,1)S(1)}, u32[]{:S(2)}, u32[]{:S(2)}) collective-permute-start(bf16[304,768]{1,0:T(8,128)(2,1)S(1)} %grad_share.1.refs_0_), channel_id=1, source_target_pairs={{0,4},{4,0},{8,12},{12,8},{1,5},{5,1},{9,13},{13,9},{2,6},{6,2},{1... | collective-permute-start | bytes 1400840 | tf_op jit(solution)/shard_map/ppermute | solution.py:486
  154.8 20.3 %collective-permute-start.45 = (bf16[304,768]{1,0:T(8,128)(2,1)S(1)}, bf16[304,768]{1,0:T(8,128)(2,1)S(1)}, u32[]{:S(2)}, u32[]{:S(2)}) collective-permute-start(bf16[304,768]{1,0:T(8,128)(2,1)S(1)} %grad_share.1.refs_0_), channel_id=1, source_target_pairs={{0,24},{4,28},{8,16},{12,20},{16,8},{20,12},{24,0},{28,4},{1,25},{... | collective-permute-start | bytes 1400840 | tf_op jit(solution)/shard_map/ppermute | solution.py:495
  (59 other events, 458.1 us)

commit v11 on v10

--- a/solution.py
+++ b/solution.py
@@ -739,8 +739,9 @@
         got1, _, _ = fence((got1, keep2, pair))
         total1 = fence(add(pieces1[0], got1))
         near1 = swap(total1[1], 1)
-        crossed, near1, got2, *ends = fence((swap(pair, 2), near1, got2, *outs[2:]))
+        crossed, *ends = fence((swap(pair, 2), *outs[2:]))
         outs[2:] = ends
+        near1, got2 = fence((near1, got2))
         d_tok = pair.astype(f32) + crossed.astype(f32) + jnp.concatenate(dres1, axis=0)
         d_tok = d_tok.astype(bf16)
         share = call(

time: 181 us -> 181 us (level)
  no operation moved by 1% of the time
where the time goes in v11:
time: 181 us
  waiting for transfers between devices  87.2 us (48%)
  starting transfers between devices  45.1 us (25%)
  Pallas kernels  41.2 us (23%)
  local copies, waits for them, and re-layouts  4.24 us (2%)
    ppermute x21, waiting for transfers between devices, swap(): return lax.ppermute(v, 'tensor', [(i, i ^ bit) for i in range(n)])  48.6 us
    pallas_call x17, Pallas kernels, call(): pl.pallas_call(kernel, out_shape=outs, in_specs=[SMEM] * scalars + [VMEM]...  27.4 us
    ppermute x9, waiting for transfers between devices, flip_member(): return lax.ppermute(v, ('dp', 'blk'), perm)  27 us
    ppermute x21, starting transfers between devices, swap(): return lax.ppermute(v, 'tensor', [(i, i ^ bit) for i in range(n)])  23.2 us
    ppermute x9, starting transfers between devices, flip_member(): return lax.ppermute(v, ('dp', 'blk'), perm)  11.3 us
    ppermute x17, waiting for transfers between devices, flip(): return lax.ppermute(v, 'blk', [(i, i ^ bit) for i in range(n_blk)])  10.3 us
    ppermute x17, starting transfers between devices, flip(): return lax.ppermute(v, 'blk', [(i, i ^ bit) for i in range(n_blk)])  7 us
    pallas_call x2, Pallas kernels, grads_out(): pl.pallas_call(kernel, out_shape=squares + outs, in_specs=[SMEM] + [VMEM]...  5.72 us
  transfers between devices with their start and end apart: 50, of which 26 were waited for; matrix products, arithmetic and copies ran while one was open for 1% of the time, Pallas kernels for 16%

profile of v11, /device:TPU:0, one launch (start us, length us, event | category | flops | bytes accessed | tf_op | source)
XLA Modules:
  0.0 181.0 jit_solution(13942101713224718984)
XLA Ops:
  1.5 2.5 %front.1 = (bf16[512,384]{1,0:T(8,128)(2,1)S(1)}, bf16[240,768]{1,0:T(8,128)(2,1)S(1)}, bf16[48,768]{1,0:T(8,128)(2,1)S(1)}) custom-call(s32[5]{0:T(128)S(1)} %stack.23.at, bf16[512,768]{1,0:T(8,128)(2,1)} %bitcast.39, bf16[192,768]{1,0:T(8,128)(2,1)} %bitcast.45, bf16[192,768]{1,0:T(8,128)(2,1)} %bitcast.48, bf16[768,768]{1,0:T(8,128)(2,1)} %w_in.9, ...), custom_call_target="tpu_custom_call" | custom-call | tf_op jit(solution)/shard_map/front/pallas_call | solution.py:536
  4.0 3.0 %collective-permute-start = (bf16[512,384]{1,0:T(8,128)(2,1)S(1)}, bf16[512,384]{1,0:T(8,128)(2,1)S(1)}, u32[]{:S(2)}, u32[]{:S(2)}) collective-permute-start(bf16[512,384]{1,0:T(8,128)(2,1)S(1)} %get-tuple-element.151.refs_0_), channel_id=1, source_target_pairs={{0,8},{4,12},{8,0},{12,4},{1,9},{5,13},{9,1},{13,5},{2,10},{6,14},... | collective-permute-start | bytes 1179656 | tf_op jit(solution)/shard_map/ppermute | solution.py:486
  8.6 2.5 %collective-permute-start.4 = (bf16[48,768]{1,0:T(8,128)(2,1)S(1)}, bf16[48,768]{1,0:T(8,128)(2,1)S(1)}, u32[]{:S(2)}, u32[]{:S(2)}) collective-permute-start(bf16[48,768]{1,0:T(8,128)(2,1)S(1)} %get-tuple-element.154), channel_id=1, source_target_pairs={{0,3},{1,2},{2,1},{3,0},{4,7},{5,6},{6,5},{7,4},{8,11},{9,10},{10,... | collective-permute-start | bytes 221192 | tf_op jit(solution)/shard_map/ppermute | solution.py:483
  11.2 1.8 collective-permute-start.1
  13.0 6.5 %collective-permute-done.1 = f32[768]{0:T(1024)S(1)} collective-permute-done((f32[768]{0:T(1024)S(1)}, f32[768]{0:T(1024)S(1)}, u32[]{:S(2)}, u32[]{:S(2)}) %collective-permute-start.1) | collective-permute-done | bytes 3104 | tf_op jit(solution)/shard_map/ppermute | solution.py:483
  19.5 2.0 %collective-permute-done.4 = bf16[48,768]{1,0:T(8,128)(2,1)S(1)} collective-permute-done((bf16[48,768]{1,0:T(8,128)(2,1)S(1)}, bf16[48,768]{1,0:T(8,128)(2,1)S(1)}, u32[]{:S(2)}, u32[]{:S(2)}) %collective-permute-start.4) | collective-permute-done | bytes 73760 | tf_op jit(solution)/shard_map/ppermute | solution.py:483
  26.0 5.6 %attend.1 = (bf16[384,128]{1,0:T(8,128)(2,1)S(1)}, bf16[384,128]{1,0:T(8,128)(2,1)S(1)}, bf16[768,512]{1,0:T(8,128)(2,1)}, bf16[768,512]{1,0:T(8,128)(2,1)}, bf16[768,128]{1,0:T(8,128)(2,1)}) custom-call(s32[5]{0:T(128)S(1)} %stack.23.at, s32[4]{0:T(128)S(1)} %copy-done.28, s32[4,4]{1,0:T(4,128)S(1)} %copy-done.26, bf16[512,384]{1,0:T(8,128)(2,1)S(1)} %query_rows.1.q, ...), custom_call_target="tpu_custom_call" | custom-call | flops 49999998976 | bytes 1 | tf_op jit(solution)/shard_map/attend/pallas_call | solution.py:572
  31.6 3.0 %collective-permute-start.10 = (bf16[384,128]{1,0:T(8,128)(2,1)S(1)}, bf16[384,128]{1,0:T(8,128)(2,1)S(1)}, u32[]{:S(2)}, u32[]{:S(2)}) collective-permute-start(bf16[384,128]{1,0:T(8,128)(2,1)S(1)} %get-tuple-element.159), channel_id=1, source_target_pairs={{0,3},{1,2},{2,1},{3,0},{4,7},{5,6},{6,5},{7,4},{8,11},{9,10},{10,... | collective-permute-start | bytes 294920 | tf_op jit(solution)/shard_map/ppermute | solution.py:483
  44.5 2.0 %collective-permute-done.15.refs_5_ = bf16[192,768]{1,0:T(8,128)(2,1)} collective-permute-done((bf16[192,768]{1,0:T(8,128)(2,1)}, bf16[192,768]{1,0:T(8,128)(2,1)}, u32[]{:S(2)}, u32[]{:S(2)}) %collective-permute-start.15) | collective-permute-done | bytes 294944 | tf_op jit(solution)/shard_map/ppermute | solution.py:486
  48.1 2.3 %ffn.2 = (bf16[128,768]{1,0:T(8,128)(2,1)S(1)}, f32[128,768]{1,0:T(8,128)S(1)}, f32[128,128]{1,0:T(8,128)S(1)}, bf16[128,768]{1,0:T(8,128)(2,1)S(1)}, bf16[128,7...) custom-call(s32[5]{0:T(128)S(1)} %stack.23.at, ...), custom_call_target="tpu_custom_call" | custom-call | flops 2400000000 | bytes 1 | tf_op jit(solution)/shard_map/ffn/pallas_call | solution.py:73
  51.7 2.3 %ffn.3 = (bf16[128,768]{1,0:T(8,128)(2,1)S(1)}, f32[128,768]{1,0:T(8,128)S(1)}, f32[128,128]{1,0:T(8,128)S(1)}, bf16[128,768]{1,0:T(8,128)(2,1)S(1)}, bf16[128,7...) custom-call(s32[5]{0:T(128)S(1)} %stack.23.at, bf16[512,768]{1,0:T(8,128)(2,1)S(1)} %bitcast.42, ...), custom_call_target="tpu_custom_call" | custom-call | flops 2400000000 | bytes 1 | tf_op jit(solution)/shard_map/ffn/pallas_call | solution.py:73
  54.1 1.7 collective-permute-start.18
  55.8 11.7 %collective-permute-done.17.theirs = bf16[128,768]{1,0:T(8,128)(2,1)S(1)} collective-permute-done((bf16[128,768]{1,0:T(8,128)(2,1)S(1)}, bf16[128,768]{1,0:T(8,128)(2,1)S(1)}, u32[]{:S(2)}, u32[]{:S(2)}) %collective-permute-start.17) | collective-permute-done | bytes 196640 | tf_op jit(solution)/shard_map/ppermute | solution.py:483
  67.5 2.7 %ffn_back.2 = (bf16[128,768]{1,0:T(8,128)(2,1)S(1)}, bf16[128,768]{1,0:T(8,128)(2,1)S(1)}, bf16[128,768]{1,0:T(8,128)(2,1)S(1)}, bf16[128,768]{1,0:T(8,128)(2,1)...) custom-call(s32[5]{0:T(128)S(1)} %stack.23.at, bf16[512,768]{1,0:T(8,128)(2,1)S(1)} %bitcast.52, ...), custom_call_target="tpu_custom_call" | custom-call | flops 2700000000 | bytes 1 | tf_op jit(solution)/shard_map/ffn_back/pallas_call | solution.py:73
  71.0 2.7 %ffn_back.3 = (bf16[128,768]{1,0:T(8,128)(2,1)S(1)}, bf16[128,768]{1,0:T(8,128)(2,1)S(1)}, bf16[128,768]{1,0:T(8,128)(2,1)S(1)}, bf16[128,768]{1,0:T(8,128)(2,1)...) custom-call(s32[5]{0:T(128)S(1)} %stack.23.at, bf16[512,768]{1,0:T(8,128)(2,1)S(1)} %bitcast.53, ...), custom_call_target="tpu_custom_call" | custom-call | flops 2700000000 | bytes 1 | tf_op jit(solution)/shard_map/ffn_back/pallas_call | solution.py:73
  73.8 2.2 %collective-permute-start.20 = (bf16[128,768]{1,0:T(8,128)(2,1)S(1)}, bf16[128,768]{1,0:T(8,128)(2,1)S(1)}, u32[]{:S(2)}, u32[]{:S(2)}) collective-permute-start(bf16[128,768]{1,0:T(8,128)(2,1)S(1)} %get-tuple-element.185.mine), channel_id=1, source_target_pairs={{0,2},{1,3},{2,0},{3,1},{4,6},{5,7},{6,4},{7,5},{8,10},{9,11},{10,... | collective-permute-start | bytes 589832 | tf_op jit(solution)/shard_map/ppermute | solution.py:483
  76.0 2.2 %ffn_grads.1 = (bf16[4,2,192,768]{3,2,1,0:T(8,128)(2,1)S(1)}, bf16[4,2,192,768]{3,2,1,0:T(8,128)(2,1)S(1)}) custom-call(s32[5]{0:T(128)S(1)} %stack.23.at, bf16[128,768]{1,0:T(8,128)(2,1)S(1)} %get-tuple-element.196.refs_0_, bf16[128,768]{1,0:T(8,128)(2,1)S(1)} %get-tuple-element.197.refs_1_, bf16[128,768]{1,0:T(8,128)(2,1)S(1)} %get-tuple-element.198.refs_2_, ...), custom_call_target="tpu_custom_call" | custom-call | flops 49999998976 | bytes 1 | tf_op jit(solution)/shard_map/ffn_grads/pallas_call | solution.py:73
  78.3 7.1 %collective-permute-done.19.theirs = bf16[128,768]{1,0:T(8,128)(2,1)S(1)} collective-permute-done((bf16[128,768]{1,0:T(8,128)(2,1)S(1)}, bf16[128,768]{1,0:T(8,128)(2,1)S(1)}, u32[]{:S(2)}, u32[]{:S(2)}) %collective-permute-start.19) | collective-permute-done | bytes 196640 | tf_op jit(solution)/shard_map/ppermute | solution.py:483
  86.7 2.8 %collective-permute-done.20.theirs = bf16[128,768]{1,0:T(8,128)(2,1)S(1)} collective-permute-done((bf16[128,768]{1,0:T(8,128)(2,1)S(1)}, bf16[128,768]{1,0:T(8,128)(2,1)S(1)}, u32[]{:S(2)}, u32[]{:S(2)}) %collective-permute-start.20) | collective-permute-done | bytes 196640 | tf_op jit(solution)/shard_map/ppermute | solution.py:483
  91.2 2.7 %attend_back.2 = (bf16[256,192]{1,0:T(8,128)(2,1)S(1)}, bf16[2,2,384,128]{3,2,1,0:T(8,128)(2,1)S(1)}, bf16[2,2,384,128]{3,2,1,0:T(8,128)(2,1)S(1)}) custom-call(s32[5]{0:T(128)S(1)} %stack.23.at, bf16[192,128]{1,0:T(8,128)(2,1)S(1)} %get-tuple-element.184.first, bf16[192,128]{1,0:T(8,128)(2,1)S(1)} %get-tuple-element.189.second, ...), custom_call_target="tpu_custom_call" | custom-call | flops 49999998976 | bytes 1 | tf_op jit(solution)/shard_map/attend_back/pallas_call | solution.py:73
  95.1 2.7 %attend_back.3 = (bf16[256,192]{1,0:T(8,128)(2,1)S(1)}, bf16[2,2,384,128]{3,2,1,0:T(8,128)(2,1)S(1)}, bf16[2,2,384,128]{3,2,1,0:T(8,128)(2,1)S(1)}) custom-call(s32[5]{0:T(128)S(1)} %stack.23.at, bf16[192,128]{1,0:T(8,128)(2,1)S(1)} %collective-permute-done.21.first, bf16[192,128]{1,0:T(8,128)(2,1)S(1)} %collective-permute-done.22.second, ...), custom_call_target="tpu_custom_call" | custom-call | flops 49999998976 | bytes 1 | tf_op jit(solution)/shard_map/attend_back/pallas_call | solution.py:73
  103.9 3.6 %collective-permute-done.27.far = bf16[2,384,128]{2,1,0:T(8,128)(2,1)S(1)} collective-permute-done((bf16[2,384,128]{2,1,0:T(8,128)(2,1)S(1)}, bf16[2,384,128]{2,1,0:T(8,128)(2,1)S(1)}, u32[]{:S(2)}, u32[]{:S(2)}) %collective-permute-start.27) | collective-permute-done | bytes 196640 | tf_op jit(solution)/shard_map/ppermute | solution.py:486
  107.5 3.4 %collective-permute-done.25.far = bf16[2,384,128]{2,1,0:T(8,128)(2,1)S(1)} collective-permute-done((bf16[2,384,128]{2,1,0:T(8,128)(2,1)S(1)}, bf16[2,384,128]{2,1,0:T(8,128)(2,1)S(1)}, u32[]{:S(2)}, u32[]{:S(2)}) %collective-permute-start.25) | collective-permute-done | bytes 196640 | tf_op jit(solution)/shard_map/ppermute | solution.py:486
  117.1 4.8 %collective-permute-done.28 = bf16[256,768]{1,0:T(8,128)(2,1)S(1)} collective-permute-done((bf16[256,768]{1,0:T(8,128)(2,1)S(1)}, bf16[256,768]{1,0:T(8,128)(2,1)S(1)}, u32[]{:S(2)}, u32[]{:S(2)}) %collective-permute-start.28) | collective-permute-done | bytes 393248 | tf_op jit(solution)/shard_map/ppermute | solution.py:483
  125.2 3.2 %collective-permute-done.34 = bf16[2,192,768]{2,1,0:T(8,128)(2,1)S(1)} collective-permute-done((bf16[2,192,768]{2,1,0:T(8,128)(2,1)S(1)}, bf16[2,192,768]{2,1,0:T(8,128)(2,1)S(1)}, u32[]{:S(2)}, u32[]{:S(2)}) %collective-permute-start.34) | collective-permute-done | bytes 589856 | tf_op jit(solution)/shard_map/ppermute | solution.py:495
  130.2 11.0 %collective-permute-done.36 = bf16[2,192,768]{2,1,0:T(8,128)(2,1)S(1)} collective-permute-done((bf16[2,192,768]{2,1,0:T(8,128)(2,1)S(1)}, bf16[2,192,768]{2,1,0:T(8,128)(2,1)S(1)}, u32[]{:S(2)}, u32[]{:S(2)}) %collective-permute-start.36) | collective-permute-done | bytes 589856 | tf_op jit(solution)/shard_map/ppermute | solution.py:495
  147.1 3.9 %collective-permute-done.37.near1 = bf16[192,768]{1,0:T(8,128)(2,1)S(1)} collective-permute-done((bf16[192,768]{1,0:T(8,128)(2,1)S(1)}, bf16[192,768]{1,0:T(8,128)(2,1)S(1)}, u32[]{:S(2)}, u32[]{:S(2)}) %collective-permute-start.37) | collective-permute-done | bytes 294944 | tf_op jit(solution)/shard_map/ppermute | solution.py:483
  157.7 3.6 %collective-permute-done.43.refs_1_ = bf16[256,768]{1,0:T(8,128)(2,1)S(1)} collective-permute-done((bf16[256,768]{1,0:T(8,128)(2,1)S(1)}, bf16[256,768]{1,0:T(8,128)(2,1)S(1)}, u32[]{:S(2)}, u32[]{:S(2)}) %collective-permute-start.43) | collective-permute-done | bytes 393248 | tf_op jit(solution)/shard_map/ppermute | solution.py:483
  163.0 3.9 %collective-permute-done.44.refs_2_ = bf16[304,768]{1,0:T(8,128)(2,1)S(1)} collective-permute-done((bf16[304,768]{1,0:T(8,128)(2,1)S(1)}, bf16[304,768]{1,0:T(8,128)(2,1)S(1)}, u32[]{:S(2)}, u32[]{:S(2)}) %collective-permute-start.44) | collective-permute-done | bytes 466976 | tf_op jit(solution)/shard_map/ppermute | solution.py:495
  167.4 7.7 %collective-permute-done.45.refs_3_ = bf16[304,768]{1,0:T(8,128)(2,1)S(1)} collective-permute-done((bf16[304,768]{1,0:T(8,128)(2,1)S(1)}, bf16[304,768]{1,0:T(8,128)(2,1)S(1)}, u32[]{:S(2)}, u32[]{:S(2)}) %collective-permute-start.45) | collective-permute-done | bytes 466976 | tf_op jit(solution)/shard_map/ppermute | solution.py:495
  175.1 2.5 %early_grads.1 = (f32[768,768]{1,0:T(8,128)}, f32[768,768]{1,0:T(8,128)}) custom-call(s32[5]{0:T(128)S(1)} %stack.23.at, bf16[304,768]{1,0:T(8,128)(2,1)S(1)} %grad_share.1.refs_0_, bf16[304,768]{1,0:T(8,128)(2,1)S(1)} %collective-permute-done.42.refs_1_, bf16[304,768]{1,0:T(8,128)(2,1)S(1)} %collective-permute-done.44.refs_2_, ...), custom_call_target="tpu_custom_call" | custom-call | flops 2000000000 | bytes 1 | tf_op jit(solution)/shard_map/early_grads/pallas_call | solution.py:777
  177.6 3.2 %grads_out.1 = (f32[768,768]{1,0:T(8,128)}, f32[768,768]{1,0:T(8,128)}, f32[192,768]{1,0:T(8,128)}, f32[192,768]{1,0:T(8,128)}, f32[192,768]{1,0:T(8,128)}, /*in...) custom-call(s32[5]{0:T(128)S(1)} %stack.23.at, ...), custom_call_target="tpu_custom_call", output_to_operand_aliasing={{0}: (9, {}), {1}: (10, {})} | custom-call | flops 2000000000 | bytes 1 | tf_op jit(solution)/shard_map/grads_out/pallas_call | solution.py:777
  (192 shorter events, 56.4 us)
Async XLA Ops:
  4.0 17.5 %collective-permute-start = (bf16[512,384]{1,0:T(8,128)(2,1)S(1)}, bf16[512,384]{1,0:T(8,128)(2,1)S(1)}, u32[]{:S(2)}, u32[]{:S(2)}) collective-permute-start(bf16[512,384]{1,0:T(8,128)(2,1)S(1)} %get-tuple-element.151.refs_0_), channel_id=1, source_target_pairs={{0,8},{4,12},{8,0},{12,4},{1,9},{5,13},{9,1},{13,5},{2,10},{6,14},... | collective-permute-start | bytes 1179656 | tf_op jit(solution)/shard_map/ppermute | solution.py:486
  7.0 14.5 %collective-permute-start.2 = (bf16[240,768]{1,0:T(8,128)(2,1)S(1)}, bf16[240,768]{1,0:T(8,128)(2,1)S(1)}, u32[]{:S(2)}, u32[]{:S(2)}) collective-permute-start(bf16[240,768]{1,0:T(8,128)(2,1)S(1)} %get-tuple-element.153), channel_id=1, source_target_pairs={{0,1},{1,0},{2,3},{3,2},{4,5},{5,4},{6,7},{7,6},{8,9},{9,8},{10,11... | collective-permute-start | bytes 1105928 | tf_op jit(solution)/shard_map/ppermute | solution.py:483
  8.6 12.9 %collective-permute-start.4 = (bf16[48,768]{1,0:T(8,128)(2,1)S(1)}, bf16[48,768]{1,0:T(8,128)(2,1)S(1)}, u32[]{:S(2)}, u32[]{:S(2)}) collective-permute-start(bf16[48,768]{1,0:T(8,128)(2,1)S(1)} %get-tuple-element.154), channel_id=1, source_target_pairs={{0,3},{1,2},{2,1},{3,0},{4,7},{5,6},{6,5},{7,4},{8,11},{9,10},{10,... | collective-permute-start | bytes 221192 | tf_op jit(solution)/shard_map/ppermute | solution.py:483
  11.0 10.4 %collective-permute-start.3 = (bf16[48,768]{1,0:T(8,128)(2,1)S(1)}, bf16[48,768]{1,0:T(8,128)(2,1)S(1)}, u32[]{:S(2)}, u32[]{:S(2)}) collective-permute-start(bf16[48,768]{1,0:T(8,128)(2,1)S(1)} %get-tuple-element.154), channel_id=1, source_target_pairs={{0,2},{1,3},{2,0},{3,1},{4,6},{5,7},{6,4},{7,5},{8,10},{9,11},{10,... | collective-permute-start | bytes 221192 | tf_op jit(solution)/shard_map/ppermute | solution.py:483
  11.2 8.3 %collective-permute-start.1 = (f32[768]{0:T(1024)S(1)}, f32[768]{0:T(1024)S(1)}, u32[]{:S(2)}, u32[]{:S(2)}) collective-permute-start(f32[768]{0:T(1024)S(1)} %copy-done.34), channel_id=1, source_target_pairs={{0,1},{1,0},{2,3},{3,2},{4,5},{5,4},{6,7},{7,6},{8,9},{9,8},{10,11... | collective-permute-start | bytes 9224 | tf_op jit(solution)/shard_map/ppermute | solution.py:483
  22.1 12.4 %collective-permute-start.13 = (bf16[192,768]{1,0:T(8,128)(2,1)S(1)}, bf16[192,768]{1,0:T(8,128)(2,1)S(1)}, u32[]{:S(2)}, u32[]{:S(2)}) collective-permute-start(bf16[192,768]{1,0:T(8,128)(2,1)S(1)} %slice.18), channel_id=1, source_target_pairs={{0,24},{4,28},{8,16},{12,20},{16,8},{20,12},{24,0},{28,4},{1,25},{... | collective-permute-start | bytes 884744 | tf_op jit(solution)/shard_map/ppermute | solution.py:563
  23.6 14.4 %collective-permute-start.12 = (bf16[192,768]{1,0:T(8,128)(2,1)S(1)}, bf16[192,768]{1,0:T(8,128)(2,1)}, u32[]{:S(2)}, u32[]{:S(2)}) collective-permute-start(bf16[192,768]{1,0:T(8,128)(2,1)S(1)} %slice.18), channel_id=1, source_target_pairs={{0,16},{4,20},{8,24},{12,28},{16,0},{20,4},{24,8},{28,12},{1,17},{... | collective-permute-start | bytes 884744 | tf_op jit(solution)/shard_map/ppermute | solution.py:563
  24.3 19.4 %collective-permute-start.11 = (bf16[336,768]{1,0:T(8,128)(2,1)S(1)}, bf16[336,768]{1,0:T(8,128)(2,1)S(1)}, u32[]{:S(2)}, u32[]{:S(2)}) collective-permute-start(bf16[336,768]{1,0:T(8,128)(2,1)S(1)} %constant_dynamic-update-slice_fusion.refs_0_), channel_id=1, source_target_pairs={{0,8},{4,12},{8,0},{12,4},{16,24},{20,28},{24,16},{28,20},{1,9},{5... | collective-permute-start | bytes 1548296 | tf_op jit(solution)/shard_map/ppermute | solution.py:563
  34.6 8.5 %collective-permute-start.9 = (bf16[384,128]{1,0:T(8,128)(2,1)S(1)}, bf16[384,128]{1,0:T(8,128)(2,1)S(1)}, u32[]{:S(2)}, u32[]{:S(2)}) collective-permute-start(bf16[384,128]{1,0:T(8,128)(2,1)S(1)} %get-tuple-element.160.refs_0_), channel_id=1, source_target_pairs={{0,2},{1,3},{2,0},{3,1},{4,6},{5,7},{6,4},{7,5},{8,10},{9,11},{10,... | collective-permute-start | bytes 294920 | tf_op jit(solution)/shard_map/ppermute | solution.py:483
  50.4 17.1 %collective-permute-start.17 = (bf16[128,768]{1,0:T(8,128)(2,1)S(1)}, bf16[128,768]{1,0:T(8,128)(2,1)S(1)}, u32[]{:S(2)}, u32[]{:S(2)}) collective-permute-start(bf16[128,768]{1,0:T(8,128)(2,1)S(1)} %get-tuple-element.173.mine), channel_id=1, source_target_pairs={{0,2},{1,3},{2,0},{3,1},{4,6},{5,7},{6,4},{7,5},{8,10},{9,11},{10,... | collective-permute-start | bytes 589832 | tf_op jit(solution)/shard_map/ppermute | solution.py:483
  54.1 17.0 %collective-permute-start.18 = (bf16[128,768]{1,0:T(8,128)(2,1)S(1)}, bf16[128,768]{1,0:T(8,128)(2,1)S(1)}, u32[]{:S(2)}, u32[]{:S(2)}) collective-permute-start(bf16[128,768]{1,0:T(8,128)(2,1)S(1)} %get-tuple-element.178.mine), channel_id=1, source_target_pairs={{0,2},{1,3},{2,0},{3,1},{4,6},{5,7},{6,4},{7,5},{8,10},{9,11},{10,... | collective-permute-start | bytes 589832 | tf_op jit(solution)/shard_map/ppermute | solution.py:483
  70.2 15.2 %collective-permute-start.19 = (bf16[128,768]{1,0:T(8,128)(2,1)S(1)}, bf16[128,768]{1,0:T(8,128)(2,1)S(1)}, u32[]{:S(2)}, u32[]{:S(2)}) collective-permute-start(bf16[128,768]{1,0:T(8,128)(2,1)S(1)} %get-tuple-element.180.mine), channel_id=1, source_target_pairs={{0,2},{1,3},{2,0},{3,1},{4,6},{5,7},{6,4},{7,5},{8,10},{9,11},{10,... | collective-permute-start | bytes 589832 | tf_op jit(solution)/shard_map/ppermute | solution.py:483
  73.8 15.7 %collective-permute-start.20 = (bf16[128,768]{1,0:T(8,128)(2,1)S(1)}, bf16[128,768]{1,0:T(8,128)(2,1)S(1)}, u32[]{:S(2)}, u32[]{:S(2)}) collective-permute-start(bf16[128,768]{1,0:T(8,128)(2,1)S(1)} %get-tuple-element.185.mine), channel_id=1, source_target_pairs={{0,2},{1,3},{2,0},{3,1},{4,6},{5,7},{6,4},{7,5},{8,10},{9,11},{10,... | collective-permute-start | bytes 589832 | tf_op jit(solution)/shard_map/ppermute | solution.py:483
  78.2 15.7 %collective-permute-start.23 = (bf16[4,2,192,768]{3,2,1,0:T(8,128)(2,1)S(1)}, bf16[4,2,192,768]{3,2,1,0:T(8,128)(2,1)S(1)}, u32[]{:S(2)}, u32[]{:S(2)}) collective-permute-start(bf16[4,2,192,768]{3,2,1,0:T(8,128)(2,1)S(1)} %get-tuple-element.209), channel_id=1, source_target_pairs={{0,4},{4,0},{8,12},{12,8},{1,5},{5,1},{9,13},{13,9},{2,6},{6,2},{1... | collective-permute-start | bytes 7077896 | tf_op jit(solution)/shard_map/ppermute | solution.py:486
  100.3 10.6 %collective-permute-start.25 = (bf16[2,384,128]{2,1,0:T(8,128)(2,1)S(1)}, bf16[2,384,128]{2,1,0:T(8,128)(2,1)S(1)}, u32[]{:S(2)}, u32[]{:S(2)}) collective-permute-start(bf16[2,384,128]{2,1,0:T(8,128)(2,1)S(1)} %fusion.5), channel_id=1, source_target_pairs={{0,8},{4,12},{8,0},{12,4},{1,9},{5,13},{9,1},{13,5},{2,10},{6,14},... | collective-permute-start | bytes 589832 | tf_op jit(solution)/shard_map/ppermute | solution.py:486
  101.9 13.2 %collective-permute-start.29 = (bf16[144,768]{1,0:T(8,128)(2,1)S(1)}, bf16[144,768]{1,0:T(8,128)(2,1)S(1)}, u32[]{:S(2)}, u32[]{:S(2)}) collective-permute-start(bf16[144,768]{1,0:T(8,128)(2,1)S(1)} %get-tuple-element.230.refs_0_), channel_id=1, source_target_pairs={{0,1},{1,0},{2,3},{3,2},{4,5},{5,4},{6,7},{7,6},{8,9},{9,8},{10,11... | collective-permute-start | bytes 663560 | tf_op jit(solution)/shard_map/ppermute | solution.py:483
  103.5 13.7 %collective-permute-start.30 = (bf16[144,768]{1,0:T(8,128)(2,1)S(1)}, bf16[144,768]{1,0:T(8,128)(2,1)S(1)}, u32[]{:S(2)}, u32[]{:S(2)}) collective-permute-start(bf16[144,768]{1,0:T(8,128)(2,1)S(1)} %get-tuple-element.231.refs_1_), channel_id=1, source_target_pairs={{0,1},{1,0},{2,3},{3,2},{4,5},{5,4},{6,7},{7,6},{8,9},{9,8},{10,11... | collective-permute-start | bytes 663560 | tf_op jit(solution)/shard_map/ppermute | solution.py:483
  111.4 10.5 %collective-permute-start.28 = (bf16[256,768]{1,0:T(8,128)(2,1)S(1)}, bf16[256,768]{1,0:T(8,128)(2,1)S(1)}, u32[]{:S(2)}, u32[]{:S(2)}) collective-permute-start(bf16[256,768]{1,0:T(8,128)(2,1)S(1)} %get-tuple-element.229), channel_id=1, source_target_pairs={{0,1},{1,0},{2,3},{3,2},{4,5},{5,4},{6,7},{7,6},{8,9},{9,8},{10,11... | collective-permute-start | bytes 1179656 | tf_op jit(solution)/shard_map/ppermute | solution.py:483
  113.1 15.4 %collective-permute-start.34 = (bf16[2,192,768]{2,1,0:T(8,128)(2,1)S(1)}, bf16[2,192,768]{2,1,0:T(8,128)(2,1)S(1)}, u32[]{:S(2)}, u32[]{:S(2)}) collective-permute-start(bf16[2,192,768]{2,1,0:T(8,128)(2,1)S(1)} %get-tuple-element.239), channel_id=1, source_target_pairs={{0,8},{4,12},{8,0},{12,4},{16,24},{20,28},{24,16},{28,20},{1,9},{5... | collective-permute-start | bytes 1769480 | tf_op jit(solution)/shard_map/ppermute | solution.py:495
  113.6 16.3 %collective-permute-start.35 = (bf16[2,192,768]{2,1,0:T(8,128)(2,1)S(1)}, bf16[2,192,768]{2,1,0:T(8,128)(2,1)S(1)}, u32[]{:S(2)}, u32[]{:S(2)}) collective-permute-start(bf16[2,192,768]{2,1,0:T(8,128)(2,1)S(1)} %get-tuple-element.240), channel_id=1, source_target_pairs={{0,16},{4,20},{8,24},{12,28},{16,0},{20,4},{24,8},{28,12},{1,17},{... | collective-permute-start | bytes 1769480 | tf_op jit(solution)/shard_map/ppermute | solution.py:495
  115.1 26.1 %collective-permute-start.36 = (bf16[2,192,768]{2,1,0:T(8,128)(2,1)S(1)}, bf16[2,192,768]{2,1,0:T(8,128)(2,1)S(1)}, u32[]{:S(2)}, u32[]{:S(2)}) collective-permute-start(bf16[2,192,768]{2,1,0:T(8,128)(2,1)S(1)} %get-tuple-element.241), channel_id=1, source_target_pairs={{0,24},{4,28},{8,16},{12,20},{16,8},{20,12},{24,0},{28,4},{1,25},{... | collective-permute-start | bytes 1769480 | tf_op jit(solution)/shard_map/ppermute | solution.py:495
  123.5 18.5 %collective-permute-start.38 = (bf16[448,768]{1,0:T(8,128)(2,1)S(1)}, bf16[448,768]{1,0:T(8,128)(2,1)S(1)}, u32[]{:S(2)}, u32[]{:S(2)}) collective-permute-start(bf16[448,768]{1,0:T(8,128)(2,1)S(1)} %get-tuple-element.254), channel_id=1, source_target_pairs={{0,4},{4,0},{8,12},{12,8},{1,5},{5,1},{9,13},{13,9},{2,6},{6,2},{1... | collective-permute-start | bytes 2064392 | tf_op jit(solution)/shard_map/ppermute | solution.py:486
  123.6 20.1 %collective-permute-start.32 = (bf16[128,768]{1,0:T(8,128)(2,1)S(1)}, bf16[128,768]{1,0:T(8,128)(2,1)S(1)}, u32[]{:S(2)}, u32[]{:S(2)}) collective-permute-start(bf16[128,768]{1,0:T(8,128)(2,1)S(1)} %get-tuple-element.174.refs_0_), channel_id=1, source_target_pairs={{0,1},{1,0},{2,3},{3,2},{4,5},{5,4},{6,7},{7,6},{8,9},{9,8},{10,11... | collective-permute-start | bytes 589832 | tf_op jit(solution)/shard_map/ppermute | solution.py:483
  128.4 15.8 %collective-permute-start.33 = (bf16[128,768]{1,0:T(8,128)(2,1)S(1)}, bf16[128,768]{1,0:T(8,128)(2,1)S(1)}, u32[]{:S(2)}, u32[]{:S(2)}) collective-permute-start(bf16[128,768]{1,0:T(8,128)(2,1)S(1)} %get-tuple-element.179.refs_1_), channel_id=1, source_target_pairs={{0,1},{1,0},{2,3},{3,2},{4,5},{5,4},{6,7},{7,6},{8,9},{9,8},{10,11... | collective-permute-start | bytes 589832 | tf_op jit(solution)/shard_map/ppermute | solution.py:483
  129.9 17.3 %collective-permute-start.31 = (bf16[256,768]{1,0:T(8,128)(2,1)S(1)}, bf16[256,768]{1,0:T(8,128)(2,1)S(1)}, u32[]{:S(2)}, u32[]{:S(2)}) collective-permute-start(bf16[256,768]{1,0:T(8,128)(2,1)S(1)} %add_convert_fusion.5), channel_id=1, source_target_pairs={{0,2},{1,3},{2,0},{3,1},{4,6},{5,7},{6,4},{7,5},{8,10},{9,11},{10,... | collective-permute-start | bytes 1179656 | tf_op jit(solution)/shard_map/ppermute | solution.py:483
  141.5 9.5 %collective-permute-start.37 = (bf16[192,768]{1,0:T(8,128)(2,1)S(1)}, bf16[192,768]{1,0:T(8,128)(2,1)S(1)}, u32[]{:S(2)}, u32[]{:S(2)}) collective-permute-start(bf16[192,768]{1,0:T(8,128)(2,1)S(1)} %slice_bitcast_fusion), channel_id=1, source_target_pairs={{0,1},{1,0},{2,3},{3,2},{4,5},{5,4},{6,7},{7,6},{8,9},{9,8},{10,11... | collective-permute-start | bytes 884744 | tf_op jit(solution)/shard_map/ppermute | solution.py:483
  142.2 8.8 %collective-permute-start.41 = (bf16[112,768]{1,0:T(8,128)(2,1)S(1)}, bf16[112,768]{1,0:T(8,128)(2,1)S(1)}, u32[]{:S(2)}, u32[]{:S(2)}) collective-permute-start(bf16[112,768]{1,0:T(8,128)(2,1)S(1)} %get-tuple-element.284), channel_id=1, source_target_pairs={{0,24},{4,28},{8,16},{12,20},{16,8},{20,12},{24,0},{28,4},{1,25},{... | collective-permute-start | bytes 516104 | tf_op jit(solution)/shard_map/ppermute | solution.py:495
  151.1 10.3 %collective-permute-start.42 = (bf16[304,768]{1,0:T(8,128)(2,1)S(1)}, bf16[304,768]{1,0:T(8,128)(2,1)S(1)}, u32[]{:S(2)}, u32[]{:S(2)}) collective-permute-start(bf16[304,768]{1,0:T(8,128)(2,1)S(1)} %grad_share.1.refs_0_), channel_id=1, source_target_pairs={{0,8},{4,12},{8,0},{12,4},{16,24},{20,28},{24,16},{28,20},{1,9},{5... | collective-permute-start | bytes 1400840 | tf_op jit(solution)/shard_map/ppermute | solution.py:495
  152.6 8.7 %collective-permute-start.43 = (bf16[256,768]{1,0:T(8,128)(2,1)S(1)}, bf16[256,768]{1,0:T(8,128)(2,1)S(1)}, u32[]{:S(2)}, u32[]{:S(2)}) collective-permute-start(bf16[256,768]{1,0:T(8,128)(2,1)S(1)} %fusion.refs_0_), channel_id=1, source_target_pairs={{0,1},{1,0},{2,3},{3,2},{4,5},{5,4},{6,7},{7,6},{8,9},{9,8},{10,11... | collective-permute-start | bytes 1179656 | tf_op jit(solution)/shard_map/ppermute | solution.py:483
  153.3 13.6 %collective-permute-start.44 = (bf16[304,768]{1,0:T(8,128)(2,1)S(1)}, bf16[304,768]{1,0:T(8,128)(2,1)S(1)}, u32[]{:S(2)}, u32[]{:S(2)}) collective-permute-start(bf16[304,768]{1,0:T(8,128)(2,1)S(1)} %grad_share.1.refs_0_), channel_id=1, source_target_pairs={{0,16},{4,20},{8,24},{12,28},{16,0},{20,4},{24,8},{28,12},{1,17},{... | collective-permute-start | bytes 1400840 | tf_op jit(solution)/shard_map/ppermute | solution.py:495
  154.8 20.3 %collective-permute-start.45 = (bf16[304,768]{1,0:T(8,128)(2,1)S(1)}, bf16[304,768]{1,0:T(8,128)(2,1)S(1)}, u32[]{:S(2)}, u32[]{:S(2)}) collective-permute-start(bf16[304,768]{1,0:T(8,128)(2,1)S(1)} %grad_share.1.refs_0_), channel_id=1, source_target_pairs={{0,24},{4,28},{8,16},{12,20},{16,8},{20,12},{24,0},{28,4},{1,25},{... | collective-permute-start | bytes 1400840 | tf_op jit(solution)/shard_map/ppermute | solution.py:495
  157.7 17.4 %collective-permute-start.46 = (bf16[304,768]{1,0:T(8,128)(2,1)S(1)}, bf16[304,768]{1,0:T(8,128)(2,1)S(1)}, u32[]{:S(2)}, u32[]{:S(2)}) collective-permute-start(bf16[304,768]{1,0:T(8,128)(2,1)S(1)} %grad_share.1.refs_0_), channel_id=1, source_target_pairs={{0,4},{4,0},{8,12},{12,8},{1,5},{5,1},{9,13},{13,9},{2,6},{6,2},{1... | collective-permute-start | bytes 1400840 | tf_op jit(solution)/shard_map/ppermute | solution.py:486
  (59 other events, 458.1 us)

commit v12 on v11

--- a/solution.py
+++ b/solution.py
@@ -20,8 +20,8 @@
 ATTEND_US = 50.0
 BACK_US = 50.0
 FILL_US = 50.0
-INPUT_US = 50.0
-GRADS_US = 1.0
+INPUT_US = 10.0
+GRADS_US = 4.0
 PACKED = BLOCK + HEAD_DIM
 
 

time: 181 us -> 181 us (level)
  no operation moved by 1% of the time
where the time goes in v12:
time: 181 us
  waiting for transfers between devices  87.2 us (48%)
  starting transfers between devices  45.1 us (25%)
  Pallas kernels  41.2 us (23%)
  local copies, waits for them, and re-layouts  4.24 us (2%)
    ppermute x21, waiting for transfers between devices, swap(): return lax.ppermute(v, 'tensor', [(i, i ^ bit) for i in range(n)])  48.5 us
    pallas_call x17, Pallas kernels, call(): pl.pallas_call(kernel, out_shape=outs, in_specs=[SMEM] * scalars + [VMEM]...  27.4 us
    ppermute x9, waiting for transfers between devices, flip_member(): return lax.ppermute(v, ('dp', 'blk'), perm)  27 us
    ppermute x21, starting transfers between devices, swap(): return lax.ppermute(v, 'tensor', [(i, i ^ bit) for i in range(n)])  23.2 us
    ppermute x9, starting transfers between devices, flip_member(): return lax.ppermute(v, ('dp', 'blk'), perm)  11.4 us
    ppermute x17, waiting for transfers between devices, flip(): return lax.ppermute(v, 'blk', [(i, i ^ bit) for i in range(n_blk)])  10.3 us
    ppermute x17, starting transfers between devices, flip(): return lax.ppermute(v, 'blk', [(i, i ^ bit) for i in range(n_blk)])  7 us
    pallas_call x2, Pallas kernels, grads_out(): pl.pallas_call(kernel, out_shape=squares + outs, in_specs=[SMEM] + [VMEM]...  5.72 us
  transfers between devices with their start and end apart: 50, of which 26 were waited for; matrix products, arithmetic and copies ran while one was open for 1% of the time, Pallas kernels for 16%

profile of v12, /device:TPU:0, one launch (start us, length us, event | category | flops | bytes accessed | tf_op | source)
XLA Modules:
  0.0 181.0 jit_solution(5777307120137531093)
XLA Ops:
  1.5 2.5 %front.1 = (bf16[512,384]{1,0:T(8,128)(2,1)S(1)}, bf16[240,768]{1,0:T(8,128)(2,1)S(1)}, bf16[48,768]{1,0:T(8,128)(2,1)S(1)}) custom-call(s32[5]{0:T(128)S(1)} %stack.23.at, bf16[512,768]{1,0:T(8,128)(2,1)} %bitcast.39, bf16[192,768]{1,0:T(8,128)(2,1)} %bitcast.45, bf16[192,768]{1,0:T(8,128)(2,1)} %bitcast.48, bf16[768,768]{1,0:T(8,128)(2,1)} %w_in.9, ...), custom_call_target="tpu_custom_call" | custom-call | tf_op jit(solution)/shard_map/front/pallas_call | solution.py:536
  4.0 3.0 %collective-permute-start = (bf16[512,384]{1,0:T(8,128)(2,1)S(1)}, bf16[512,384]{1,0:T(8,128)(2,1)S(1)}, u32[]{:S(2)}, u32[]{:S(2)}) collective-permute-start(bf16[512,384]{1,0:T(8,128)(2,1)S(1)} %get-tuple-element.151.refs_0_), channel_id=1, source_target_pairs={{0,8},{4,12},{8,0},{12,4},{1,9},{5,13},{9,1},{13,5},{2,10},{6,14},... | collective-permute-start | bytes 1179656 | tf_op jit(solution)/shard_map/ppermute | solution.py:486
  8.6 2.5 %collective-permute-start.4 = (bf16[48,768]{1,0:T(8,128)(2,1)S(1)}, bf16[48,768]{1,0:T(8,128)(2,1)S(1)}, u32[]{:S(2)}, u32[]{:S(2)}) collective-permute-start(bf16[48,768]{1,0:T(8,128)(2,1)S(1)} %get-tuple-element.154), channel_id=1, source_target_pairs={{0,3},{1,2},{2,1},{3,0},{4,7},{5,6},{6,5},{7,4},{8,11},{9,10},{10,... | collective-permute-start | bytes 221192 | tf_op jit(solution)/shard_map/ppermute | solution.py:483
  11.2 1.8 collective-permute-start.1
  13.0 6.5 %collective-permute-done.1 = f32[768]{0:T(1024)S(1)} collective-permute-done((f32[768]{0:T(1024)S(1)}, f32[768]{0:T(1024)S(1)}, u32[]{:S(2)}, u32[]{:S(2)}) %collective-permute-start.1) | collective-permute-done | bytes 3104 | tf_op jit(solution)/shard_map/ppermute | solution.py:483
  19.5 2.0 %collective-permute-done.4 = bf16[48,768]{1,0:T(8,128)(2,1)S(1)} collective-permute-done((bf16[48,768]{1,0:T(8,128)(2,1)S(1)}, bf16[48,768]{1,0:T(8,128)(2,1)S(1)}, u32[]{:S(2)}, u32[]{:S(2)}) %collective-permute-start.4) | collective-permute-done | bytes 73760 | tf_op jit(solution)/shard_map/ppermute | solution.py:483
  26.0 5.6 %attend.1 = (bf16[384,128]{1,0:T(8,128)(2,1)S(1)}, bf16[384,128]{1,0:T(8,128)(2,1)S(1)}, bf16[768,512]{1,0:T(8,128)(2,1)}, bf16[768,512]{1,0:T(8,128)(2,1)}, bf16[768,128]{1,0:T(8,128)(2,1)}) custom-call(s32[5]{0:T(128)S(1)} %stack.23.at, s32[4]{0:T(128)S(1)} %copy-done.28, s32[4,4]{1,0:T(4,128)S(1)} %copy-done.26, bf16[512,384]{1,0:T(8,128)(2,1)S(1)} %query_rows.1.q, ...), custom_call_target="tpu_custom_call" | custom-call | flops 49999998976 | bytes 1 | tf_op jit(solution)/shard_map/attend/pallas_call | solution.py:572
  31.6 3.0 %collective-permute-start.10 = (bf16[384,128]{1,0:T(8,128)(2,1)S(1)}, bf16[384,128]{1,0:T(8,128)(2,1)S(1)}, u32[]{:S(2)}, u32[]{:S(2)}) collective-permute-start(bf16[384,128]{1,0:T(8,128)(2,1)S(1)} %get-tuple-element.159), channel_id=1, source_target_pairs={{0,3},{1,2},{2,1},{3,0},{4,7},{5,6},{6,5},{7,4},{8,11},{9,10},{10,... | collective-permute-start | bytes 294920 | tf_op jit(solution)/shard_map/ppermute | solution.py:483
  44.5 2.0 %collective-permute-done.15.refs_5_ = bf16[192,768]{1,0:T(8,128)(2,1)} collective-permute-done((bf16[192,768]{1,0:T(8,128)(2,1)}, bf16[192,768]{1,0:T(8,128)(2,1)}, u32[]{:S(2)}, u32[]{:S(2)}) %collective-permute-start.15) | collective-permute-done | bytes 294944 | tf_op jit(solution)/shard_map/ppermute | solution.py:486
  48.1 2.3 %ffn.2 = (bf16[128,768]{1,0:T(8,128)(2,1)S(1)}, f32[128,768]{1,0:T(8,128)S(1)}, f32[128,128]{1,0:T(8,128)S(1)}, bf16[128,768]{1,0:T(8,128)(2,1)S(1)}, bf16[128,7...) custom-call(s32[5]{0:T(128)S(1)} %stack.23.at, ...), custom_call_target="tpu_custom_call" | custom-call | flops 2400000000 | bytes 1 | tf_op jit(solution)/shard_map/ffn/pallas_call | solution.py:73
  51.7 2.3 %ffn.3 = (bf16[128,768]{1,0:T(8,128)(2,1)S(1)}, f32[128,768]{1,0:T(8,128)S(1)}, f32[128,128]{1,0:T(8,128)S(1)}, bf16[128,768]{1,0:T(8,128)(2,1)S(1)}, bf16[128,7...) custom-call(s32[5]{0:T(128)S(1)} %stack.23.at, bf16[512,768]{1,0:T(8,128)(2,1)S(1)} %bitcast.42, ...), custom_call_target="tpu_custom_call" | custom-call | flops 2400000000 | bytes 1 | tf_op jit(solution)/shard_map/ffn/pallas_call | solution.py:73
  54.1 1.7 collective-permute-start.18
  55.8 11.7 %collective-permute-done.17.theirs = bf16[128,768]{1,0:T(8,128)(2,1)S(1)} collective-permute-done((bf16[128,768]{1,0:T(8,128)(2,1)S(1)}, bf16[128,768]{1,0:T(8,128)(2,1)S(1)}, u32[]{:S(2)}, u32[]{:S(2)}) %collective-permute-start.17) | collective-permute-done | bytes 196640 | tf_op jit(solution)/shard_map/ppermute | solution.py:483
  67.5 2.7 %ffn_back.2 = (bf16[128,768]{1,0:T(8,128)(2,1)S(1)}, bf16[128,768]{1,0:T(8,128)(2,1)S(1)}, bf16[128,768]{1,0:T(8,128)(2,1)S(1)}, bf16[128,768]{1,0:T(8,128)(2,1)...) custom-call(s32[5]{0:T(128)S(1)} %stack.23.at, bf16[512,768]{1,0:T(8,128)(2,1)S(1)} %bitcast.52, ...), custom_call_target="tpu_custom_call" | custom-call | flops 2700000000 | bytes 1 | tf_op jit(solution)/shard_map/ffn_back/pallas_call | solution.py:73
  71.0 2.7 %ffn_back.3 = (bf16[128,768]{1,0:T(8,128)(2,1)S(1)}, bf16[128,768]{1,0:T(8,128)(2,1)S(1)}, bf16[128,768]{1,0:T(8,128)(2,1)S(1)}, bf16[128,768]{1,0:T(8,128)(2,1)...) custom-call(s32[5]{0:T(128)S(1)} %stack.23.at, bf16[512,768]{1,0:T(8,128)(2,1)S(1)} %bitcast.53, ...), custom_call_target="tpu_custom_call" | custom-call | flops 2700000000 | bytes 1 | tf_op jit(solution)/shard_map/ffn_back/pallas_call | solution.py:73
  73.8 2.2 %collective-permute-start.20 = (bf16[128,768]{1,0:T(8,128)(2,1)S(1)}, bf16[128,768]{1,0:T(8,128)(2,1)S(1)}, u32[]{:S(2)}, u32[]{:S(2)}) collective-permute-start(bf16[128,768]{1,0:T(8,128)(2,1)S(1)} %get-tuple-element.185.mine), channel_id=1, source_target_pairs={{0,2},{1,3},{2,0},{3,1},{4,6},{5,7},{6,4},{7,5},{8,10},{9,11},{10,... | collective-permute-start | bytes 589832 | tf_op jit(solution)/shard_map/ppermute | solution.py:483
  76.0 2.2 %ffn_grads.1 = (bf16[4,2,192,768]{3,2,1,0:T(8,128)(2,1)S(1)}, bf16[4,2,192,768]{3,2,1,0:T(8,128)(2,1)S(1)}) custom-call(s32[5]{0:T(128)S(1)} %stack.23.at, bf16[128,768]{1,0:T(8,128)(2,1)S(1)} %get-tuple-element.196.refs_0_, bf16[128,768]{1,0:T(8,128)(2,1)S(1)} %get-tuple-element.197.refs_1_, bf16[128,768]{1,0:T(8,128)(2,1)S(1)} %get-tuple-element.198.refs_2_, ...), custom_call_target="tpu_custom_call" | custom-call | flops 49999998976 | bytes 1 | tf_op jit(solution)/shard_map/ffn_grads/pallas_call | solution.py:73
  78.3 7.1 %collective-permute-done.19.theirs = bf16[128,768]{1,0:T(8,128)(2,1)S(1)} collective-permute-done((bf16[128,768]{1,0:T(8,128)(2,1)S(1)}, bf16[128,768]{1,0:T(8,128)(2,1)S(1)}, u32[]{:S(2)}, u32[]{:S(2)}) %collective-permute-start.19) | collective-permute-done | bytes 196640 | tf_op jit(solution)/shard_map/ppermute | solution.py:483
  86.7 2.8 %collective-permute-done.20.theirs = bf16[128,768]{1,0:T(8,128)(2,1)S(1)} collective-permute-done((bf16[128,768]{1,0:T(8,128)(2,1)S(1)}, bf16[128,768]{1,0:T(8,128)(2,1)S(1)}, u32[]{:S(2)}, u32[]{:S(2)}) %collective-permute-start.20) | collective-permute-done | bytes 196640 | tf_op jit(solution)/shard_map/ppermute | solution.py:483
  91.2 2.7 %attend_back.2 = (bf16[256,192]{1,0:T(8,128)(2,1)S(1)}, bf16[2,2,384,128]{3,2,1,0:T(8,128)(2,1)S(1)}, bf16[2,2,384,128]{3,2,1,0:T(8,128)(2,1)S(1)}) custom-call(s32[5]{0:T(128)S(1)} %stack.23.at, bf16[192,128]{1,0:T(8,128)(2,1)S(1)} %get-tuple-element.184.first, bf16[192,128]{1,0:T(8,128)(2,1)S(1)} %get-tuple-element.189.second, ...), custom_call_target="tpu_custom_call" | custom-call | flops 49999998976 | bytes 1 | tf_op jit(solution)/shard_map/attend_back/pallas_call | solution.py:73
  95.1 2.7 %attend_back.3 = (bf16[256,192]{1,0:T(8,128)(2,1)S(1)}, bf16[2,2,384,128]{3,2,1,0:T(8,128)(2,1)S(1)}, bf16[2,2,384,128]{3,2,1,0:T(8,128)(2,1)S(1)}) custom-call(s32[5]{0:T(128)S(1)} %stack.23.at, bf16[192,128]{1,0:T(8,128)(2,1)S(1)} %collective-permute-done.21.first, bf16[192,128]{1,0:T(8,128)(2,1)S(1)} %collective-permute-done.22.second, ...), custom_call_target="tpu_custom_call" | custom-call | flops 49999998976 | bytes 1 | tf_op jit(solution)/shard_map/attend_back/pallas_call | solution.py:73
  103.9 3.6 %collective-permute-done.27.far = bf16[2,384,128]{2,1,0:T(8,128)(2,1)S(1)} collective-permute-done((bf16[2,384,128]{2,1,0:T(8,128)(2,1)S(1)}, bf16[2,384,128]{2,1,0:T(8,128)(2,1)S(1)}, u32[]{:S(2)}, u32[]{:S(2)}) %collective-permute-start.27) | collective-permute-done | bytes 196640 | tf_op jit(solution)/shard_map/ppermute | solution.py:486
  107.5 3.4 %collective-permute-done.25.far = bf16[2,384,128]{2,1,0:T(8,128)(2,1)S(1)} collective-permute-done((bf16[2,384,128]{2,1,0:T(8,128)(2,1)S(1)}, bf16[2,384,128]{2,1,0:T(8,128)(2,1)S(1)}, u32[]{:S(2)}, u32[]{:S(2)}) %collective-permute-start.25) | collective-permute-done | bytes 196640 | tf_op jit(solution)/shard_map/ppermute | solution.py:486
  117.2 4.7 %collective-permute-done.28 = bf16[256,768]{1,0:T(8,128)(2,1)S(1)} collective-permute-done((bf16[256,768]{1,0:T(8,128)(2,1)S(1)}, bf16[256,768]{1,0:T(8,128)(2,1)S(1)}, u32[]{:S(2)}, u32[]{:S(2)}) %collective-permute-start.28) | collective-permute-done | bytes 393248 | tf_op jit(solution)/shard_map/ppermute | solution.py:483
  125.2 3.2 %collective-permute-done.34 = bf16[2,192,768]{2,1,0:T(8,128)(2,1)S(1)} collective-permute-done((bf16[2,192,768]{2,1,0:T(8,128)(2,1)S(1)}, bf16[2,192,768]{2,1,0:T(8,128)(2,1)S(1)}, u32[]{:S(2)}, u32[]{:S(2)}) %collective-permute-start.34) | collective-permute-done | bytes 589856 | tf_op jit(solution)/shard_map/ppermute | solution.py:495
  130.2 11.0 %collective-permute-done.36 = bf16[2,192,768]{2,1,0:T(8,128)(2,1)S(1)} collective-permute-done((bf16[2,192,768]{2,1,0:T(8,128)(2,1)S(1)}, bf16[2,192,768]{2,1,0:T(8,128)(2,1)S(1)}, u32[]{:S(2)}, u32[]{:S(2)}) %collective-permute-start.36) | collective-permute-done | bytes 589856 | tf_op jit(solution)/shard_map/ppermute | solution.py:495
  147.1 3.9 %collective-permute-done.37.near1 = bf16[192,768]{1,0:T(8,128)(2,1)S(1)} collective-permute-done((bf16[192,768]{1,0:T(8,128)(2,1)S(1)}, bf16[192,768]{1,0:T(8,128)(2,1)S(1)}, u32[]{:S(2)}, u32[]{:S(2)}) %collective-permute-start.37) | collective-permute-done | bytes 294944 | tf_op jit(solution)/shard_map/ppermute | solution.py:483
  157.7 3.6 %collective-permute-done.43.refs_1_ = bf16[256,768]{1,0:T(8,128)(2,1)S(1)} collective-permute-done((bf16[256,768]{1,0:T(8,128)(2,1)S(1)}, bf16[256,768]{1,0:T(8,128)(2,1)S(1)}, u32[]{:S(2)}, u32[]{:S(2)}) %collective-permute-start.43) | collective-permute-done | bytes 393248 | tf_op jit(solution)/shard_map/ppermute | solution.py:483
  163.0 3.9 %collective-permute-done.44.refs_2_ = bf16[304,768]{1,0:T(8,128)(2,1)S(1)} collective-permute-done((bf16[304,768]{1,0:T(8,128)(2,1)S(1)}, bf16[304,768]{1,0:T(8,128)(2,1)S(1)}, u32[]{:S(2)}, u32[]{:S(2)}) %collective-permute-start.44) | collective-permute-done | bytes 466976 | tf_op jit(solution)/shard_map/ppermute | solution.py:495
  167.4 7.7 %collective-permute-done.45.refs_3_ = bf16[304,768]{1,0:T(8,128)(2,1)S(1)} collective-permute-done((bf16[304,768]{1,0:T(8,128)(2,1)S(1)}, bf16[304,768]{1,0:T(8,128)(2,1)S(1)}, u32[]{:S(2)}, u32[]{:S(2)}) %collective-permute-start.45) | collective-permute-done | bytes 466976 | tf_op jit(solution)/shard_map/ppermute | solution.py:495
  175.1 2.5 %early_grads.1 = (f32[768,768]{1,0:T(8,128)}, f32[768,768]{1,0:T(8,128)}) custom-call(s32[5]{0:T(128)S(1)} %stack.23.at, bf16[304,768]{1,0:T(8,128)(2,1)S(1)} %grad_share.1.refs_0_, bf16[304,768]{1,0:T(8,128)(2,1)S(1)} %collective-permute-done.42.refs_1_, bf16[304,768]{1,0:T(8,128)(2,1)S(1)} %collective-permute-done.44.refs_2_, ...), custom_call_target="tpu_custom_call" | custom-call | flops 2000000000 | bytes 1 | tf_op jit(solution)/shard_map/early_grads/pallas_call | solution.py:777
  177.6 3.2 %grads_out.1 = (f32[768,768]{1,0:T(8,128)}, f32[768,768]{1,0:T(8,128)}, f32[192,768]{1,0:T(8,128)}, f32[192,768]{1,0:T(8,128)}, f32[192,768]{1,0:T(8,128)}, /*in...) custom-call(s32[5]{0:T(128)S(1)} %stack.23.at, ...), custom_call_target="tpu_custom_call", output_to_operand_aliasing={{0}: (9, {}), {1}: (10, {})} | custom-call | flops 2000000000 | bytes 1 | tf_op jit(solution)/shard_map/grads_out/pallas_call | solution.py:777
  (192 shorter events, 56.5 us)
Async XLA Ops:
  4.0 17.5 %collective-permute-start = (bf16[512,384]{1,0:T(8,128)(2,1)S(1)}, bf16[512,384]{1,0:T(8,128)(2,1)S(1)}, u32[]{:S(2)}, u32[]{:S(2)}) collective-permute-start(bf16[512,384]{1,0:T(8,128)(2,1)S(1)} %get-tuple-element.151.refs_0_), channel_id=1, source_target_pairs={{0,8},{4,12},{8,0},{12,4},{1,9},{5,13},{9,1},{13,5},{2,10},{6,14},... | collective-permute-start | bytes 1179656 | tf_op jit(solution)/shard_map/ppermute | solution.py:486
  7.0 14.5 %collective-permute-start.2 = (bf16[240,768]{1,0:T(8,128)(2,1)S(1)}, bf16[240,768]{1,0:T(8,128)(2,1)S(1)}, u32[]{:S(2)}, u32[]{:S(2)}) collective-permute-start(bf16[240,768]{1,0:T(8,128)(2,1)S(1)} %get-tuple-element.153), channel_id=1, source_target_pairs={{0,1},{1,0},{2,3},{3,2},{4,5},{5,4},{6,7},{7,6},{8,9},{9,8},{10,11... | collective-permute-start | bytes 1105928 | tf_op jit(solution)/shard_map/ppermute | solution.py:483
  8.6 12.9 %collective-permute-start.4 = (bf16[48,768]{1,0:T(8,128)(2,1)S(1)}, bf16[48,768]{1,0:T(8,128)(2,1)S(1)}, u32[]{:S(2)}, u32[]{:S(2)}) collective-permute-start(bf16[48,768]{1,0:T(8,128)(2,1)S(1)} %get-tuple-element.154), channel_id=1, source_target_pairs={{0,3},{1,2},{2,1},{3,0},{4,7},{5,6},{6,5},{7,4},{8,11},{9,10},{10,... | collective-permute-start | bytes 221192 | tf_op jit(solution)/shard_map/ppermute | solution.py:483
  11.0 10.4 %collective-permute-start.3 = (bf16[48,768]{1,0:T(8,128)(2,1)S(1)}, bf16[48,768]{1,0:T(8,128)(2,1)S(1)}, u32[]{:S(2)}, u32[]{:S(2)}) collective-permute-start(bf16[48,768]{1,0:T(8,128)(2,1)S(1)} %get-tuple-element.154), channel_id=1, source_target_pairs={{0,2},{1,3},{2,0},{3,1},{4,6},{5,7},{6,4},{7,5},{8,10},{9,11},{10,... | collective-permute-start | bytes 221192 | tf_op jit(solution)/shard_map/ppermute | solution.py:483
  11.2 8.3 %collective-permute-start.1 = (f32[768]{0:T(1024)S(1)}, f32[768]{0:T(1024)S(1)}, u32[]{:S(2)}, u32[]{:S(2)}) collective-permute-start(f32[768]{0:T(1024)S(1)} %copy-done.34), channel_id=1, source_target_pairs={{0,1},{1,0},{2,3},{3,2},{4,5},{5,4},{6,7},{7,6},{8,9},{9,8},{10,11... | collective-permute-start | bytes 9224 | tf_op jit(solution)/shard_map/ppermute | solution.py:483
  22.1 12.4 %collective-permute-start.13 = (bf16[192,768]{1,0:T(8,128)(2,1)S(1)}, bf16[192,768]{1,0:T(8,128)(2,1)S(1)}, u32[]{:S(2)}, u32[]{:S(2)}) collective-permute-start(bf16[192,768]{1,0:T(8,128)(2,1)S(1)} %slice.18), channel_id=1, source_target_pairs={{0,24},{4,28},{8,16},{12,20},{16,8},{20,12},{24,0},{28,4},{1,25},{... | collective-permute-start | bytes 884744 | tf_op jit(solution)/shard_map/ppermute | solution.py:563
  23.6 14.4 %collective-permute-start.12 = (bf16[192,768]{1,0:T(8,128)(2,1)S(1)}, bf16[192,768]{1,0:T(8,128)(2,1)}, u32[]{:S(2)}, u32[]{:S(2)}) collective-permute-start(bf16[192,768]{1,0:T(8,128)(2,1)S(1)} %slice.18), channel_id=1, source_target_pairs={{0,16},{4,20},{8,24},{12,28},{16,0},{20,4},{24,8},{28,12},{1,17},{... | collective-permute-start | bytes 884744 | tf_op jit(solution)/shard_map/ppermute | solution.py:563
  24.3 19.4 %collective-permute-start.11 = (bf16[336,768]{1,0:T(8,128)(2,1)S(1)}, bf16[336,768]{1,0:T(8,128)(2,1)S(1)}, u32[]{:S(2)}, u32[]{:S(2)}) collective-permute-start(bf16[336,768]{1,0:T(8,128)(2,1)S(1)} %constant_dynamic-update-slice_fusion.refs_0_), channel_id=1, source_target_pairs={{0,8},{4,12},{8,0},{12,4},{16,24},{20,28},{24,16},{28,20},{1,9},{5... | collective-permute-start | bytes 1548296 | tf_op jit(solution)/shard_map/ppermute | solution.py:563
  34.6 8.5 %collective-permute-start.9 = (bf16[384,128]{1,0:T(8,128)(2,1)S(1)}, bf16[384,128]{1,0:T(8,128)(2,1)S(1)}, u32[]{:S(2)}, u32[]{:S(2)}) collective-permute-start(bf16[384,128]{1,0:T(8,128)(2,1)S(1)} %get-tuple-element.160.refs_0_), channel_id=1, source_target_pairs={{0,2},{1,3},{2,0},{3,1},{4,6},{5,7},{6,4},{7,5},{8,10},{9,11},{10,... | collective-permute-start | bytes 294920 | tf_op jit(solution)/shard_map/ppermute | solution.py:483
  50.4 17.1 %collective-permute-start.17 = (bf16[128,768]{1,0:T(8,128)(2,1)S(1)}, bf16[128,768]{1,0:T(8,128)(2,1)S(1)}, u32[]{:S(2)}, u32[]{:S(2)}) collective-permute-start(bf16[128,768]{1,0:T(8,128)(2,1)S(1)} %get-tuple-element.173.mine), channel_id=1, source_target_pairs={{0,2},{1,3},{2,0},{3,1},{4,6},{5,7},{6,4},{7,5},{8,10},{9,11},{10,... | collective-permute-start | bytes 589832 | tf_op jit(solution)/shard_map/ppermute | solution.py:483
  54.1 17.0 %collective-permute-start.18 = (bf16[128,768]{1,0:T(8,128)(2,1)S(1)}, bf16[128,768]{1,0:T(8,128)(2,1)S(1)}, u32[]{:S(2)}, u32[]{:S(2)}) collective-permute-start(bf16[128,768]{1,0:T(8,128)(2,1)S(1)} %get-tuple-element.178.mine), channel_id=1, source_target_pairs={{0,2},{1,3},{2,0},{3,1},{4,6},{5,7},{6,4},{7,5},{8,10},{9,11},{10,... | collective-permute-start | bytes 589832 | tf_op jit(solution)/shard_map/ppermute | solution.py:483
  70.2 15.2 %collective-permute-start.19 = (bf16[128,768]{1,0:T(8,128)(2,1)S(1)}, bf16[128,768]{1,0:T(8,128)(2,1)S(1)}, u32[]{:S(2)}, u32[]{:S(2)}) collective-permute-start(bf16[128,768]{1,0:T(8,128)(2,1)S(1)} %get-tuple-element.180.mine), channel_id=1, source_target_pairs={{0,2},{1,3},{2,0},{3,1},{4,6},{5,7},{6,4},{7,5},{8,10},{9,11},{10,... | collective-permute-start | bytes 589832 | tf_op jit(solution)/shard_map/ppermute | solution.py:483
  73.8 15.7 %collective-permute-start.20 = (bf16[128,768]{1,0:T(8,128)(2,1)S(1)}, bf16[128,768]{1,0:T(8,128)(2,1)S(1)}, u32[]{:S(2)}, u32[]{:S(2)}) collective-permute-start(bf16[128,768]{1,0:T(8,128)(2,1)S(1)} %get-tuple-element.185.mine), channel_id=1, source_target_pairs={{0,2},{1,3},{2,0},{3,1},{4,6},{5,7},{6,4},{7,5},{8,10},{9,11},{10,... | collective-permute-start | bytes 589832 | tf_op jit(solution)/shard_map/ppermute | solution.py:483
  78.2 15.7 %collective-permute-start.23 = (bf16[4,2,192,768]{3,2,1,0:T(8,128)(2,1)S(1)}, bf16[4,2,192,768]{3,2,1,0:T(8,128)(2,1)S(1)}, u32[]{:S(2)}, u32[]{:S(2)}) collective-permute-start(bf16[4,2,192,768]{3,2,1,0:T(8,128)(2,1)S(1)} %get-tuple-element.209), channel_id=1, source_target_pairs={{0,4},{4,0},{8,12},{12,8},{1,5},{5,1},{9,13},{13,9},{2,6},{6,2},{1... | collective-permute-start | bytes 7077896 | tf_op jit(solution)/shard_map/ppermute | solution.py:486
  100.3 10.6 %collective-permute-start.25 = (bf16[2,384,128]{2,1,0:T(8,128)(2,1)S(1)}, bf16[2,384,128]{2,1,0:T(8,128)(2,1)S(1)}, u32[]{:S(2)}, u32[]{:S(2)}) collective-permute-start(bf16[2,384,128]{2,1,0:T(8,128)(2,1)S(1)} %fusion.5), channel_id=1, source_target_pairs={{0,8},{4,12},{8,0},{12,4},{1,9},{5,13},{9,1},{13,5},{2,10},{6,14},... | collective-permute-start | bytes 589832 | tf_op jit(solution)/shard_map/ppermute | solution.py:486
  101.9 13.8 %collective-permute-start.29 = (bf16[144,768]{1,0:T(8,128)(2,1)S(1)}, bf16[144,768]{1,0:T(8,128)(2,1)S(1)}, u32[]{:S(2)}, u32[]{:S(2)}) collective-permute-start(bf16[144,768]{1,0:T(8,128)(2,1)S(1)} %get-tuple-element.230.refs_0_), channel_id=1, source_target_pairs={{0,1},{1,0},{2,3},{3,2},{4,5},{5,4},{6,7},{7,6},{8,9},{9,8},{10,11... | collective-permute-start | bytes 663560 | tf_op jit(solution)/shard_map/ppermute | solution.py:483
  103.5 13.8 %collective-permute-start.30 = (bf16[144,768]{1,0:T(8,128)(2,1)S(1)}, bf16[144,768]{1,0:T(8,128)(2,1)S(1)}, u32[]{:S(2)}, u32[]{:S(2)}) collective-permute-start(bf16[144,768]{1,0:T(8,128)(2,1)S(1)} %get-tuple-element.231.refs_1_), channel_id=1, source_target_pairs={{0,1},{1,0},{2,3},{3,2},{4,5},{5,4},{6,7},{7,6},{8,9},{9,8},{10,11... | collective-permute-start | bytes 663560 | tf_op jit(solution)/shard_map/ppermute | solution.py:483
  111.4 10.5 %collective-permute-start.28 = (bf16[256,768]{1,0:T(8,128)(2,1)S(1)}, bf16[256,768]{1,0:T(8,128)(2,1)S(1)}, u32[]{:S(2)}, u32[]{:S(2)}) collective-permute-start(bf16[256,768]{1,0:T(8,128)(2,1)S(1)} %get-tuple-element.229), channel_id=1, source_target_pairs={{0,1},{1,0},{2,3},{3,2},{4,5},{5,4},{6,7},{7,6},{8,9},{9,8},{10,11... | collective-permute-start | bytes 1179656 | tf_op jit(solution)/shard_map/ppermute | solution.py:483
  113.1 15.4 %collective-permute-start.34 = (bf16[2,192,768]{2,1,0:T(8,128)(2,1)S(1)}, bf16[2,192,768]{2,1,0:T(8,128)(2,1)S(1)}, u32[]{:S(2)}, u32[]{:S(2)}) collective-permute-start(bf16[2,192,768]{2,1,0:T(8,128)(2,1)S(1)} %get-tuple-element.239), channel_id=1, source_target_pairs={{0,8},{4,12},{8,0},{12,4},{16,24},{20,28},{24,16},{28,20},{1,9},{5... | collective-permute-start | bytes 1769480 | tf_op jit(solution)/shard_map/ppermute | solution.py:495
  113.6 16.3 %collective-permute-start.35 = (bf16[2,192,768]{2,1,0:T(8,128)(2,1)S(1)}, bf16[2,192,768]{2,1,0:T(8,128)(2,1)S(1)}, u32[]{:S(2)}, u32[]{:S(2)}) collective-permute-start(bf16[2,192,768]{2,1,0:T(8,128)(2,1)S(1)} %get-tuple-element.240), channel_id=1, source_target_pairs={{0,16},{4,20},{8,24},{12,28},{16,0},{20,4},{24,8},{28,12},{1,17},{... | collective-permute-start | bytes 1769480 | tf_op jit(solution)/shard_map/ppermute | solution.py:495
  115.6 25.5 %collective-permute-start.36 = (bf16[2,192,768]{2,1,0:T(8,128)(2,1)S(1)}, bf16[2,192,768]{2,1,0:T(8,128)(2,1)S(1)}, u32[]{:S(2)}, u32[]{:S(2)}) collective-permute-start(bf16[2,192,768]{2,1,0:T(8,128)(2,1)S(1)} %get-tuple-element.241), channel_id=1, source_target_pairs={{0,24},{4,28},{8,16},{12,20},{16,8},{20,12},{24,0},{28,4},{1,25},{... | collective-permute-start | bytes 1769480 | tf_op jit(solution)/shard_map/ppermute | solution.py:495
  123.5 18.5 %collective-permute-start.38 = (bf16[448,768]{1,0:T(8,128)(2,1)S(1)}, bf16[448,768]{1,0:T(8,128)(2,1)S(1)}, u32[]{:S(2)}, u32[]{:S(2)}) collective-permute-start(bf16[448,768]{1,0:T(8,128)(2,1)S(1)} %get-tuple-element.254), channel_id=1, source_target_pairs={{0,4},{4,0},{8,12},{12,8},{1,5},{5,1},{9,13},{13,9},{2,6},{6,2},{1... | collective-permute-start | bytes 2064392 | tf_op jit(solution)/shard_map/ppermute | solution.py:486
  123.6 20.1 %collective-permute-start.32 = (bf16[128,768]{1,0:T(8,128)(2,1)S(1)}, bf16[128,768]{1,0:T(8,128)(2,1)S(1)}, u32[]{:S(2)}, u32[]{:S(2)}) collective-permute-start(bf16[128,768]{1,0:T(8,128)(2,1)S(1)} %get-tuple-element.174.refs_0_), channel_id=1, source_target_pairs={{0,1},{1,0},{2,3},{3,2},{4,5},{5,4},{6,7},{7,6},{8,9},{9,8},{10,11... | collective-permute-start | bytes 589832 | tf_op jit(solution)/shard_map/ppermute | solution.py:483
  128.4 15.8 %collective-permute-start.33 = (bf16[128,768]{1,0:T(8,128)(2,1)S(1)}, bf16[128,768]{1,0:T(8,128)(2,1)S(1)}, u32[]{:S(2)}, u32[]{:S(2)}) collective-permute-start(bf16[128,768]{1,0:T(8,128)(2,1)S(1)} %get-tuple-element.179.refs_1_), channel_id=1, source_target_pairs={{0,1},{1,0},{2,3},{3,2},{4,5},{5,4},{6,7},{7,6},{8,9},{9,8},{10,11... | collective-permute-start | bytes 589832 | tf_op jit(solution)/shard_map/ppermute | solution.py:483
  129.9 17.3 %collective-permute-start.31 = (bf16[256,768]{1,0:T(8,128)(2,1)S(1)}, bf16[256,768]{1,0:T(8,128)(2,1)S(1)}, u32[]{:S(2)}, u32[]{:S(2)}) collective-permute-start(bf16[256,768]{1,0:T(8,128)(2,1)S(1)} %add_convert_fusion.5), channel_id=1, source_target_pairs={{0,2},{1,3},{2,0},{3,1},{4,6},{5,7},{6,4},{7,5},{8,10},{9,11},{10,... | collective-permute-start | bytes 1179656 | tf_op jit(solution)/shard_map/ppermute | solution.py:483
  141.5 9.5 %collective-permute-start.37 = (bf16[192,768]{1,0:T(8,128)(2,1)S(1)}, bf16[192,768]{1,0:T(8,128)(2,1)S(1)}, u32[]{:S(2)}, u32[]{:S(2)}) collective-permute-start(bf16[192,768]{1,0:T(8,128)(2,1)S(1)} %slice_bitcast_fusion), channel_id=1, source_target_pairs={{0,1},{1,0},{2,3},{3,2},{4,5},{5,4},{6,7},{7,6},{8,9},{9,8},{10,11... | collective-permute-start | bytes 884744 | tf_op jit(solution)/shard_map/ppermute | solution.py:483
  142.2 8.8 %collective-permute-start.41 = (bf16[112,768]{1,0:T(8,128)(2,1)S(1)}, bf16[112,768]{1,0:T(8,128)(2,1)S(1)}, u32[]{:S(2)}, u32[]{:S(2)}) collective-permute-start(bf16[112,768]{1,0:T(8,128)(2,1)S(1)} %get-tuple-element.284), channel_id=1, source_target_pairs={{0,24},{4,28},{8,16},{12,20},{16,8},{20,12},{24,0},{28,4},{1,25},{... | collective-permute-start | bytes 516104 | tf_op jit(solution)/shard_map/ppermute | solution.py:495
  151.1 10.3 %collective-permute-start.42 = (bf16[304,768]{1,0:T(8,128)(2,1)S(1)}, bf16[304,768]{1,0:T(8,128)(2,1)S(1)}, u32[]{:S(2)}, u32[]{:S(2)}) collective-permute-start(bf16[304,768]{1,0:T(8,128)(2,1)S(1)} %grad_share.1.refs_0_), channel_id=1, source_target_pairs={{0,8},{4,12},{8,0},{12,4},{16,24},{20,28},{24,16},{28,20},{1,9},{5... | collective-permute-start | bytes 1400840 | tf_op jit(solution)/shard_map/ppermute | solution.py:495
  152.6 8.7 %collective-permute-start.43 = (bf16[256,768]{1,0:T(8,128)(2,1)S(1)}, bf16[256,768]{1,0:T(8,128)(2,1)S(1)}, u32[]{:S(2)}, u32[]{:S(2)}) collective-permute-start(bf16[256,768]{1,0:T(8,128)(2,1)S(1)} %fusion.refs_0_), channel_id=1, source_target_pairs={{0,1},{1,0},{2,3},{3,2},{4,5},{5,4},{6,7},{7,6},{8,9},{9,8},{10,11... | collective-permute-start | bytes 1179656 | tf_op jit(solution)/shard_map/ppermute | solution.py:483
  153.3 13.6 %collective-permute-start.44 = (bf16[304,768]{1,0:T(8,128)(2,1)S(1)}, bf16[304,768]{1,0:T(8,128)(2,1)S(1)}, u32[]{:S(2)}, u32[]{:S(2)}) collective-permute-start(bf16[304,768]{1,0:T(8,128)(2,1)S(1)} %grad_share.1.refs_0_), channel_id=1, source_target_pairs={{0,16},{4,20},{8,24},{12,28},{16,0},{20,4},{24,8},{28,12},{1,17},{... | collective-permute-start | bytes 1400840 | tf_op jit(solution)/shard_map/ppermute | solution.py:495
  154.8 20.3 %collective-permute-start.45 = (bf16[304,768]{1,0:T(8,128)(2,1)S(1)}, bf16[304,768]{1,0:T(8,128)(2,1)S(1)}, u32[]{:S(2)}, u32[]{:S(2)}) collective-permute-start(bf16[304,768]{1,0:T(8,128)(2,1)S(1)} %grad_share.1.refs_0_), channel_id=1, source_target_pairs={{0,24},{4,28},{8,16},{12,20},{16,8},{20,12},{24,0},{28,4},{1,25},{... | collective-permute-start | bytes 1400840 | tf_op jit(solution)/shard_map/ppermute | solution.py:495
  157.7 17.4 %collective-permute-start.46 = (bf16[304,768]{1,0:T(8,128)(2,1)S(1)}, bf16[304,768]{1,0:T(8,128)(2,1)S(1)}, u32[]{:S(2)}, u32[]{:S(2)}) collective-permute-start(bf16[304,768]{1,0:T(8,128)(2,1)S(1)} %grad_share.1.refs_0_), channel_id=1, source_target_pairs={{0,4},{4,0},{8,12},{12,8},{1,5},{5,1},{9,13},{13,9},{2,6},{6,2},{1... | collective-permute-start | bytes 1400840 | tf_op jit(solution)/shard_map/ppermute | solution.py:486
  (59 other events, 459.6 us)
